TPU v7x, 256 devices: a whole 4x4x8 slice. The times are simulated.
256 devices in a mesh: dp: 32 (over z_hi, x, core), ctx: 8 (over y, z_lo).
Axes of the slice: x: 4, y: 4, z: 8 (z_hi: 4, z_lo: 2; z = z_hi * 2 + z_lo), core: 2. Of those that a mesh axis runs over, the one named last changes fastest.
Arguments:
- layer_input: bfloat16 [32, 2048, 4096], P('dp', 'ctx'), may hold values from -6 to 6
- queries: bfloat16 [32, 2048, 1024], P('dp', 'ctx'), may hold values from -6 to 6
- key_head: bfloat16 [32, 2048, 128], P('dp', 'ctx'), may hold values from -6 to 6
- shared_value_head: bfloat16 [32, 2048, 128], P('dp', 'ctx'), may hold values from -6 to 6
- grad_output: bfloat16 [32, 2048, 1024], P('dp', 'ctx'), may hold values from -6 to 6
- doc_ids: int32 [32, 2048], P('dp'), may hold values from 0 to 3, never falling along the last dimension, each value on 1 to 2045 neighbouring positions
Outputs:
- grad_query: bfloat16 [32, 2048, 1024], P('dp', 'ctx')
- grad_key: bfloat16 [32, 2048, 128], P('dp', 'ctx')
- grad_value: bfloat16 [32, 2048, 128], P('dp', 'ctx')
- query_weight_grad: float32 [4096, 1024], P(('dp', 'ctx'))
- key_weight_grad: float32 [4096, 128], P(('dp', 'ctx'))
- value_weight_grad: float32 [4096, 128], P(('dp', 'ctx'))
Inputs may be any that keep to these rules, and one draw needn't show every extreme that they name: `doc_ids`: along each row the document number never falls and starts at 0; every one of the 4 documents holds 1 to 2045 tokens.
All inputs are finite; a program needn't handle non-finite values.
Results may differ from a plain program's by a relative error of at most 0.019.
Values may be sent and summed in bfloat16 or wider, within the bound.
No kernel may reach another device: no remote copies, remote signals or barrier semaphores. Data moves between devices by JAX's collectives and lax.ppermute only.
A program may use at most 128 MiB of HBM per device.

v0:
```python
import math

import jax
import jax.numpy as jnp
from jax import lax
from jax.sharding import PartitionSpec as P

NEG = -1e30


def local(layer_input, queries, key_head, shared_value_head, grad_output, doc_ids):
    tok_rows = queries.shape[1]
    head_size = key_head.shape[2]
    heads = queries.shape[2] // head_size
    scale = head_size ** (-0.5)
    dp_count = lax.axis_size("dp")
    ctx_place = lax.axis_index("ctx")
    keys_all, values_all = (
        lax.all_gather(key_head, "ctx", axis=1, tiled=True),
        lax.all_gather(shared_value_head, "ctx", axis=1, tiled=True),
    )
    keys_all = keys_all[0]
    values_all = values_all[0]
    seq = keys_all.shape[0]
    documents = doc_ids[0]
    first_row = ctx_place * tok_rows
    local_docs = lax.dynamic_slice_in_dim(documents, first_row, tok_rows)
    local_places = first_row + jnp.arange(tok_rows)
    places = jnp.arange(seq)
    allowed = (local_docs[:, None] == documents[None, :]) & (
        places[None, :] <= local_places[:, None]
    )
    qmat = queries[0].reshape(tok_rows, heads, head_size)
    output_gradient = grad_output[0].reshape(tok_rows, heads, head_size)
    scores = jnp.einsum("xua,ia->uxi", qmat, keys_all, preferred_element_type=jnp.float32) * scale
    scores = jnp.where(allowed[None], scores, NEG)
    summit = jnp.max(scores, axis=-1, keepdims=True)
    raised = jnp.exp(scores - summit)
    prob = raised / jnp.sum(raised, axis=-1, keepdims=True)
    probability_reduced = prob.astype(jnp.bfloat16)
    rebuilt_probabilities = jnp.einsum(
        "jgl,lw->jgw", probability_reduced, values_all, preferred_element_type=jnp.float32
    )
    delta = jnp.einsum("thd,htd->ht", output_gradient.astype(jnp.float32), rebuilt_probabilities)
    probability_gradient = jnp.einsum(
        "xua,ia->uxi", output_gradient, values_all, preferred_element_type=jnp.float32
    )
    score_gradient = (prob * (probability_gradient - delta[..., None])).astype(jnp.bfloat16)
    grad_q = (
        jnp.einsum("hts,sd->thd", score_gradient, keys_all, preferred_element_type=jnp.float32)
        * scale
    ).astype(jnp.bfloat16)
    grad_q = grad_q.reshape(tok_rows, heads * head_size)
    key_part = (
        jnp.einsum("hts,thd->sd", score_gradient, qmat, preferred_element_type=jnp.float32) * scale
    )
    value_part = jnp.einsum(
        "hts,thd->sd", probability_reduced, output_gradient, preferred_element_type=jnp.float32
    )
    kv_grads = lax.psum_scatter(
        jnp.concatenate([key_part, value_part], axis=1).astype(jnp.bfloat16),
        "ctx",
        scatter_dimension=0,
        tiled=True,
    ).astype(jnp.float32)
    grad_k = kv_grads[:, :head_size].astype(jnp.bfloat16)
    grad_v = kv_grads[:, head_size:].astype(jnp.bfloat16)
    grad_rows = jnp.concatenate([grad_q, grad_k, grad_v], axis=1)
    features = layer_input[0]
    weight_block = lax.psum_scatter(
        lax.dot_general(
            features, grad_rows, (((0,), (0,)), ((), ())), preferred_element_type=jnp.float32
        ),
        ("dp", "ctx"),
        scatter_dimension=0,
        tiled=True,
    )
    factor = 1.0 / math.sqrt(dp_count * seq)
    weight_block = weight_block * factor
    query_width = heads * head_size
    return (
        grad_q[None],
        grad_k[None],
        grad_v[None],
        weight_block[:, :query_width],
        weight_block[:, query_width : query_width + head_size],
        weight_block[:, query_width + head_size :],
    )


def solution(mesh):
    placed = (
        P("dp", "ctx", None),
        P("dp", "ctx", None),
        P("dp", "ctx", None),
        P("dp", "ctx", None),
        P("dp", "ctx", None),
        P("dp", None),
    )
    return jax.shard_map(
        local,
        mesh=mesh,
        in_specs=placed,
        out_specs=(
            P("dp", "ctx", None),
            P("dp", "ctx", None),
            P("dp", "ctx", None),
            P(("dp", "ctx"), None),
            P(("dp", "ctx"), None),
            P(("dp", "ctx"), None),
        ),
        check_vma=False,
    )
```

profile of v0, /device:TPU:32, one launch (start us, length us, event | category | flops | bytes accessed | tf_op | source)
XLA Modules:
  0.0 1517.4 jit_solution(16757180800837014644)
XLA Ops:
  7.2 32.7 %all_gather.6 = bf16[1,2048,128]{2,1,0:T(8,128)(2,1)} all-gather(bf16[1,256,128]{2,1,0:T(8,128)(2,1)} %param.8), channel_id=1, replica_groups=mesh['dp'=32,'ctx'=8] {'ctx'}, dimensions={1}, use_global_device_ids=true | all-gather | bytes 589824 | tf_op jit(solution)/shard_map/all_gather | solution.py:19
  39.9 32.4 %all_gather.7 = bf16[1,2048,128]{2,1,0:T(8,128)(2,1)} all-gather(bf16[1,256,128]{2,1,0:T(8,128)(2,1)} %param.9), channel_id=1, replica_groups=mesh['dp'=32,'ctx'=8] {'ctx'}, dimensions={1}, use_global_device_ids=true | all-gather | bytes 589824 | tf_op jit(solution)/shard_map/all_gather | solution.py:20
  72.3 1.2 copy.53
  73.6 1.1 copy.54
  74.7 1.1 copy.33
  76.6 9.1 fusion.21
  85.7 1.2 fusion.12
  86.9 18.0 %fusion.27 = (f32[8,256]{1,0:T(8,128)S(1)}, f32[8,256,2048]{1,2,0:T(8,128)}) fusion(f32[2048,256,8]{1,0,2:T(8,128)} %fusion.21, pred[256,2048]{0,1:T(8,128)(4,1)} %fusion.12), kind=kOutput, calls=%fused_computation.43 | output fusion | flops 25167872 | bytes 34086912 | tf_op jit(solution)/shard_map/sub | solution.py:38
  104.8 6.8 fusion.7
  111.7 3.6 fusion.9
  115.3 2.4 fusion.17
  118.5 8.5 fusion.2
  127.0 2.8 fusion.10
  130.2 1.1 pad_maximum_fusion
  131.4 4.7 fusion.13
  136.1 38.0 %reduce-scatter.5.cloned.1.call-done = bf16[256,256]{0,1:T(8,128)(2,1)} async-done(((bf16[2048,256]{0,1:T(8,128)(2,1)}), bf16[256,256]{0,1:T(8,128)(2,1)}) %reduce-scatter.5.cloned.1.call-update) | async-done | bytes 131088 | tf_op jit(solution)/shard_map/reduce_scatter | solution.py:60
  174.1 9.6 convolution_bitcast_fusion
  183.7 22.5 %copy.51 = f32[4096,1280]{1,0:T(8,128)} copy(f32[4096,1280]{0,1:T(8,128)} %convolution_bitcast_fusion) | data formatting | bytes 41943040
  206.2 1.0 copy.34
  207.2 0.7 copy.36
  208.0 0.7 copy.35
  208.7 1298.5 %reduce-scatter.7.cloned.1.call-done = f32[16,1280]{1,0:T(8,128)} async-done(((f32[4096,1280]{1,0:T(8,128)}), f32[16,1280]{1,0:T(8,128)}) %reduce-scatter.7.cloned.1.call-update) | async-done | bytes 81936
  1507.2 1.1 copy.52
  1508.4 0.8 copy.37
  (30 shorter events, 3.4 us)
Async XLA Ops:
  7.2 166.9 %copy-start = (bf16[1,256,4096]{2,1,0:T(8,128)(2,1)S(1)}, bf16[1,256,4096]{2,1,0:T(8,128)(2,1)}, u32[]{:S(2)}) copy-start(bf16[1,256,4096]{2,1,0:T(8,128)(2,1)} %param.6) | copy-start | bytes 6291460
  7.2 166.9 %reduce-scatter.5.cloned.1.call-start = ((), (), s32[]{:S(2)}) async-start(), calls=%async_computation.2 | async-start | bytes 1179648 | tf_op jit(solution)/shard_map/reduce_scatter | solution.py:60
  76.6 9.1 copy-start.6
  104.8 6.8 copy-start.4
  111.7 3.6 copy-start.3
  126.9 3.2 copy-start.7
  126.9 3.2 copy-start.5
  127.0 4.4 copy-start.1
  131.3 1375.8 %reduce-scatter.7.cloned.1.call-start = ((), (), s32[]{:S(2)}) async-start(), calls=%async_computation.3 | async-start | bytes 21053440
  206.2 1.0 copy-start.2
Sparse Core Ops, SparseCore 0:
  131.4 42.6 reduce-scatter.4
  206.3 1300.7 reduce-scatter.6
where the time goes:
time: 1530 us; the launch traced here: 1520 us
  waiting for transfers between devices  1340 us (88%)
  blocking collectives  65.1 us (4%)
  matrix products  40.7 us (3%)
  local copies, waits for them, and re-layouts  33 us (2%)
  other arithmetic  27.9 us (2%)
    unnamed x3, waiting for transfers between devices  1300 us
    reduce_scatter x1, waiting for transfers between devices, local(): lax.psum_scatter(jnp.concatenate([key_part, value_part], axis=1).astype(j...  38 us
    all_gather x1, blocking collectives, local(): lax.all_gather(key_head, 'ctx', axis=1, tiled=True)  32.7 us
    all_gather x1, blocking collectives, local(): lax.all_gather(shared_value_head, 'ctx', axis=1, tiled=True)  32.4 us
  transfers between devices with their start and end apart: 2, of which 2 were waited for; matrix products, arithmetic and copies ran while one was open for 0% of the time, Pallas kernels for 0%

commit v1 on v0

v1 whole, which is shorter than its diff:
```python
import math

import jax
import jax.numpy as jnp
from jax import lax
from jax.sharding import Mesh, PartitionSpec as P

NEG = -1e30
AXES = ("zh", "x", "core", "y", "zl")
SIZES = (4, 4, 2, 4, 2)
GROUP = ("x", "core")
CTX = ("y", "zl")
BF = jnp.bfloat16
F32 = jnp.float32


def shifted(value, axes, count, step, wrap):
    pairs = []
    for src in range(count):
        dst = src + step
        if wrap:
            pairs.append((src, dst % count))
        elif 0 <= dst < count:
            pairs.append((src, dst))
    return lax.ppermute(value, axes, pairs)


def attention(q, do, kv, docs, place):
    rows = q.shape[0]
    hd = kv[0].shape[1] // 2
    heads = q.shape[1] // hd
    scale = hd ** (-0.5)
    blocks = len(kv)
    kv = jnp.concatenate(kv, axis=0)
    keys, values = kv[:, :hd], kv[:, hd:]
    first = place * rows
    my_places = first + jnp.arange(rows)
    my_docs = lax.dynamic_slice_in_dim(docs, first, rows)
    starts = jnp.sum(docs[None, :] < my_docs[:, None], axis=1)
    key_places = (
        (place - jnp.arange(blocks))[:, None] * rows + jnp.arange(rows)[None, :]
    ).reshape(-1)
    allowed = (key_places[None, :] >= starts[:, None]) & (
        key_places[None, :] <= my_places[:, None]
    )
    q = q.reshape(rows, heads, hd)
    do = do.reshape(rows, heads, hd)
    scores = jnp.einsum("xua,ia->uxi", q, keys, preferred_element_type=F32) * scale
    scores = jnp.where(allowed[None], scores, NEG)
    top = jnp.max(scores, axis=-1, keepdims=True)
    raised = jnp.exp(scores - top)
    prob = raised / jnp.sum(raised, axis=-1, keepdims=True)
    prob_low = prob.astype(BF)
    dprob = jnp.einsum("xua,ia->uxi", do, values, preferred_element_type=F32)
    delta = jnp.sum(prob * dprob, axis=-1, keepdims=True)
    dscore = (prob * (dprob - delta)).astype(BF)
    dq = jnp.einsum("hts,sd->thd", dscore, keys, preferred_element_type=F32) * scale
    dk = jnp.einsum("hts,thd->sd", dscore, q, preferred_element_type=F32) * scale
    dv = jnp.einsum("hts,thd->sd", prob_low, do, preferred_element_type=F32)
    dkv = jnp.concatenate([dk, dv], axis=1).reshape(blocks, rows, 2 * hd)
    return dq.astype(BF).reshape(rows, heads * hd), [dkv[d] for d in range(blocks)]


def local(layer_input, queries, key_head, value_head, grad_output, doc_ids):
    x, q, k, v, do, docs = (
        a[0] for a in (layer_input, queries, key_head, value_head, grad_output, doc_ids)
    )
    rows, hd = k.shape
    dim = x.shape[1]
    ctx = lax.axis_size(CTX)
    group = lax.axis_size(GROUP)
    z_hi = lax.axis_size("zh")
    place = lax.axis_index(CTX)
    me = lax.axis_index(GROUP)

    kv = jnp.concatenate([k, v], axis=1)
    kv_blocks = [kv] + [shifted(kv, CTX, ctx, d, False) for d in range(1, ctx)]

    wide = dim // (z_hi * group)
    split = x.reshape(rows, z_hi, group, wide).transpose(2, 0, 1, 3).reshape(group, rows, z_hi * wide)
    features = lax.all_to_all(split, GROUP, 0, 0, tiled=True).reshape(group * rows, z_hi * wide)

    dq, dkv = attention(q, do, kv_blocks, docs, place)

    total = dkv[0]
    for d in range(1, ctx):
        total = total + shifted(dkv[d].astype(BF), CTX, ctx, -d, False).astype(F32)
    dkv_own = total.astype(BF)

    grads = jnp.concatenate([dq, dkv_own], axis=1)
    grads_all = lax.all_gather(grads, GROUP, axis=0, tiled=True)
    part = lax.dot_general(
        features, grads_all, (((0,), (0,)), ((), ())), preferred_element_type=F32
    ).astype(BF)
    n = part.shape[1]
    y, zl = lax.axis_size("y"), lax.axis_size("zl")
    keep = wide // (y * zl)
    part = part.reshape(z_hi, y, zl * keep * n).transpose(1, 0, 2)
    part = lax.all_to_all(part, "y", 0, 0, tiled=True)
    part = jnp.sum(part.astype(F32), axis=0).astype(BF)
    part = part.reshape(z_hi * zl, keep, n)
    part = lax.all_to_all(part, ("zh", "zl"), 0, 0, tiled=True)
    tokens = rows * ctx * group * z_hi
    weight = jnp.sum(part.astype(F32), axis=0) * (1.0 / math.sqrt(tokens))
    width = q.shape[1]
    return (
        dq[None],
        dkv_own[None, :, :hd],
        dkv_own[None, :, hd:],
        weight[:, :width],
        weight[:, width : width + hd],
        weight[:, width + hd :],
    )


def solution(mesh):
    fine = Mesh(mesh.devices.reshape(SIZES), AXES)
    dp = ("zh", "x", "core")
    tok = P(dp, CTX, None)
    row = P(dp + CTX, None)
    return jax.shard_map(
        local,
        mesh=fine,
        in_specs=(tok, tok, tok, tok, tok, P(dp, None)),
        out_specs=(tok, tok, tok, row, row, row),
        check_vma=False,
    )
```

time: 1530 us -> 235 us (0.15)
  waiting for transfers between devices: 1340 us -> 39.1 us
  starting transfers between devices: 0.08 us -> 33.7 us
    unnamed x3 -> x1, waiting for transfers between devices: 1300 us -> 0.02 us
    all_gather x2 -> x0, blocking collectives: 65.1 us -> none  [the longest x1 32.7 us: local(): lax.all_gather(key_head, 'ctx', axis=1, tiled=True)]
    all_to_all x0 -> x2, blocking collectives: none -> 62.5 us  [the longest x1 41.5 us: local(): lax.all_to_all(split, GROUP, 0, 0, tiled=True)]
    reduce_scatter x1 -> x0, waiting for transfers between devices: 38 us -> none  [local(): lax.psum_scatter(jnp.concatenate([key_part, value_part], axis=1).astype(j...]
    ppermute x0 -> x14, starting transfers between devices: none -> 25.6 us  [shifted(): return lax.ppermute(value, axes, pairs)]
    unnamed x25 -> x13, local copies, waits for them, and re-layouts: 29.8 us -> 9.15 us
    ppermute x0 -> x14, waiting for transfers between devices: none -> 17.4 us  [shifted(): return lax.ppermute(value, axes, pairs)]
    dot_general x7 -> x6, matrix products: 40.7 us -> 34.1 us  [the longest x1 13 us: attention(): dprob = jnp.einsum('xua,ia->uxi', do, values, preferred_element_type=F32)]
  transfers between devices with their start and end apart: 2 -> 16, of which waited for: 2 -> 5; matrix products, arithmetic and copies ran while one was open for 0% -> 6% of each run, Pallas kernels for 0% -> 0%
where the time goes in v1:
time: 235 us; the launch traced here: 234 us
  blocking collectives  62.5 us (27%)
  waiting for transfers between devices  39.1 us (17%)
  matrix products  34.1 us (15%)
  starting transfers between devices  33.7 us (14%)
  other arithmetic  29.9 us (13%)
  local copies, waits for them, and re-layouts  19.8 us (8%)
  between operations  14.4 us (6%)
    all_to_all x1, blocking collectives, local(): lax.all_to_all(split, GROUP, 0, 0, tiled=True)  41.5 us
    ppermute x14, starting transfers between devices, shifted(): return lax.ppermute(value, axes, pairs)  25.6 us
    all_to_all x1, blocking collectives, local(): part = lax.all_to_all(part, 'y', 0, 0, tiled=True)  21 us
    sub x1, other arithmetic, attention(): raised = jnp.exp(scores - top)  17.8 us
    ppermute x14, waiting for transfers between devices, shifted(): return lax.ppermute(value, axes, pairs)  17.4 us
    dot_general x1, matrix products, attention(): dprob = jnp.einsum('xua,ia->uxi', do, values, preferred_element_type=F32)  13 us
    all_gather x1, waiting for transfers between devices, local(): grads_all = lax.all_gather(grads, GROUP, axis=0, tiled=True)  12.8 us
    unnamed x13, local copies, waits for them, and re-layouts  9.15 us
  transfers between devices with their start and end apart: 16, of which 5 were waited for; matrix products, arithmetic and copies ran while one was open for 6% of the time, Pallas kernels for 0%

profile of v1, /device:TPU:32, one launch (start us, length us, event | category | flops | bytes accessed | tf_op | source)
XLA Modules:
  0.0 233.7 jit_solution(12957721022645573969)
XLA Ops:
  8.1 3.0 %collective-permute-start = (bf16[256,256]{1,0:T(8,128)(2,1)S(1)}, bf16[256,256]{1,0:T(8,128)(2,1)S(1)}, u32[]{:S(2)}, u32[]{:S(2)}) collective-permute-start(bf16[256,256]{1,0:T(8,128)(2,1)S(1)} %get-tuple-element.45), channel_id=1, source_target_pairs={{0,1},{1,2},{2,3},{3,4},{4,5},{5,6},{6,7},{8,9},{9,10},{10,11},{11... | collective-permute-start | bytes 393224 | tf_op jit(solution)/shard_map/ppermute | solution.py:25
  11.1 3.5 %collective-permute-start.1 = (bf16[256,256]{1,0:T(8,128)(2,1)S(1)}, bf16[256,256]{1,0:T(8,128)(2,1)S(1)}, u32[]{:S(2)}, u32[]{:S(2)}) collective-permute-start(bf16[256,256]{1,0:T(8,128)(2,1)S(1)} %get-tuple-element.45), channel_id=1, source_target_pairs={{0,2},{1,3},{2,4},{3,5},{4,6},{5,7},{8,10},{9,11},{10,12},{11,13},... | collective-permute-start | bytes 393224 | tf_op jit(solution)/shard_map/ppermute | solution.py:25
  14.6 5.2 %collective-permute-start.2 = (bf16[256,256]{1,0:T(8,128)(2,1)S(1)}, bf16[256,256]{1,0:T(8,128)(2,1)S(1)}, u32[]{:S(2)}, u32[]{:S(2)}) collective-permute-start(bf16[256,256]{1,0:T(8,128)(2,1)S(1)} %get-tuple-element.45), channel_id=1, source_target_pairs={{0,3},{1,4},{2,5},{3,6},{4,7},{8,11},{9,12},{10,13},{11,14},{12,15... | collective-permute-start | bytes 393224 | tf_op jit(solution)/shard_map/ppermute | solution.py:25
  29.5 4.5 %collective-permute-done.5 = bf16[256,256]{1,0:T(8,128)(2,1)S(1)} collective-permute-done((bf16[256,256]{1,0:T(8,128)(2,1)S(1)}, bf16[256,256]{1,0:T(8,128)(2,1)S(1)}, u32[]{:S(2)}, u32[]{:S(2)}) %collective-permute-start.5) | collective-permute-done | bytes 131104 | tf_op jit(solution)/shard_map/ppermute | solution.py:25
  34.0 8.1 %fusion.18 = f32[2048,256,8]{1,0,2:T(8,128)} fusion(bf16[256,8,128]{0,2,1:T(8,128)(2,1)S(1)} %bitcast.75, bf16[2048,256]{1,0:T(8,128)(2,1)S(1)} %constant_dynamic-update-slice_fusion), kind=kOutput, calls=%fused_computation.33 | convolution fusion | flops 1073741824 | bytes 17825792 | tf_op jit(solution)/shard_map/xua,ia->uxi/dot_general | solution.py:48
  42.0 17.8 %fusion.32 = (f32[8,256]{1,0:T(8,128)S(1)}, f32[8,256,2048]{1,2,0:T(8,128)}) fusion(f32[2048,256,8]{1,0,2:T(8,128)} %fusion.18, pred[256,2048]{0,1:T(8,128)(4,1)S(1)} %compare_and_fusion), kind=kOutput, calls=%fused_computation.63 | output fusion | flops 25167872 | bytes 34086912 | tf_op jit(solution)/shard_map/sub | solution.py:51
  59.8 13.0 %fusion.1 = (f32[8,256]{1,0:T(8,128)S(1)}, f32[2048,256,8]{1,0,2:T(8,128)}) fusion(f32[8,256,2048]{1,2,0:T(8,128)} %get-tuple-element.50, f32[8,256]{1,0:T(8,128)S(1)} %get-tuple-element.49, bf16[256,8,128]{0,2,1:T(8,128)(2,1)S(1)} %bitcast.78, bf16[2048,256]{1,0:T(8,128)(2,1)S(1)} %constant_dynamic-update-slice_fusion), kind=kOutput, calls=%fused_computation.3 | convolution fusion | flops 1086322688 | bytes 34619392 | tf_op jit(solution)/shard_map/xua,ia->uxi/dot_general | solution.py:54
  72.8 3.3 %copy-done = f32[8,256,2048]{1,2,0:T(8,128)S(1)} copy-done((f32[8,256,2048]{1,2,0:T(8,128)S(1)}, f32[8,256,2048]{1,2,0:T(8,128)}, u32[]{:S(2)}) %copy-start) | copy-done | bytes 16777240
  76.2 2.9 %fusion.12 = f32[2048,128]{0,1:T(8,128)S(1)} fusion(bf16[256,8,128]{0,2,1:T(8,128)(2,1)S(1)} %bitcast.79, f32[8,256,2048]{1,2,0:T(8,128)S(1)} %copy-done, f32[8,256]{1,0:T(8,128)S(1)} %get-tuple-element.49), kind=kOutput, calls=%fused_computation.22 | convolution fusion | flops 1082130432 | bytes 18358272 | tf_op jit(solution)/shard_map/hts,thd->sd/dot_general | solution.py:59
  79.1 7.4 %fusion.3 = bf16[8,256,2048]{1,2,0:T(8,128)(2,1)S(1)} fusion(f32[2048,256,8]{1,0,2:T(8,128)} %get-tuple-element.52, f32[8,256]{1,0:T(8,128)S(1)} %get-tuple-element.51, f32[8,256,2048]{1,2,0:T(8,128)S(1)} %copy-done, f32[8,256]{1,0:T(8,128)S(1)} %get-tuple-element.49), kind=kLoop, calls=%fused_computation.5 | loop fusion | flops 16777216 | bytes 41959424 | tf_op jit(solution)/shard_map/convert_element_type | solution.py:56
  86.4 2.8 %fusion.11 = f32[2048,128]{0,1:T(8,128)S(1)} fusion(bf16[8,256,2048]{1,2,0:T(8,128)(2,1)S(1)} %fusion.3, bf16[256,8,128]{0,2,1:T(8,128)(2,1)S(1)} %bitcast.76), kind=kOutput, calls=%fused_computation.21 | convolution fusion | flops 1074003968 | bytes 9961472 | tf_op jit(solution)/shard_map/hts,thd->sd/dot_general | solution.py:58
  94.1 1.5 collective-permute-start.9
  96.9 8.5 %collective-permute-done.12 = bf16[256,256]{0,1:T(8,128)(2,1)S(1)} collective-permute-done((bf16[256,256]{0,1:T(8,128)(2,1)S(1)}, bf16[256,256]{0,1:T(8,128)(2,1)S(1)}, u32[]{:S(2)}, u32[]{:S(2)}) %collective-permute-start.12) | collective-permute-done | bytes 131104 | tf_op jit(solution)/shard_map/ppermute | solution.py:25
  105.4 2.1 collective-permute-start.7
  107.5 1.3 fusion.16
  108.8 4.3 %collective-permute-done.7 = bf16[256,256]{0,1:T(8,128)(2,1)S(1)} collective-permute-done((bf16[256,256]{0,1:T(8,128)(2,1)S(1)}, bf16[256,256]{0,1:T(8,128)(2,1)S(1)}, u32[]{:S(2)}, u32[]{:S(2)}) %collective-permute-start.7) | collective-permute-done | bytes 131104 | tf_op jit(solution)/shard_map/ppermute | solution.py:25
  114.2 3.3 %copy.74 = bf16[1,256,4096]{1,2,0:T(8,128)(2,1)S(1)} copy(bf16[1,256,4096]{2,1,0:T(8,128)(2,1)} %param.6) | data formatting | bytes 4194304 | tf_op args[0]
  117.7 41.5 %all_to_all.15 = bf16[8,256,512]{1,2,0:T(8,128)(2,1)S(1)} all-to-all(bf16[8,256,512]{1,2,0:T(8,128)(2,1)S(1)} %bitcast.70), channel_id=1, replica_groups=mesh['zh'=4,'x'=4,'core'=2,'y'=4,'zl'=2] {'x','core'}, dimensions={0} | all-to-all | bytes 4194304 | tf_op jit(solution)/shard_map/all_to_all | solution.py:81
  159.1 2.4 %copy.76 = bf16[8,256,512]{2,1,0:T(8,128)(2,1)} copy(bf16[8,256,512]{1,2,0:T(8,128)(2,1)S(1)} %all_to_all.15) | data formatting | bytes 4194304 | tf_op jit(solution)/shard_map/all_to_all | solution.py:81
  161.6 12.8 %all-gather.2.cloned.1.call-done = bf16[2048,1280]{0,1:T(8,128)(2,1)} async-done(((bf16[256,1280]{0,1:T(8,128)(2,1)}), bf16[2048,1280]{0,1:T(8,128)(2,1)}) %all-gather.2.cloned.1.call-update) | async-done | bytes 5242896 | tf_op jit(solution)/shard_map/all_gather | solution.py:91
  174.4 6.0 %fusion.10 = bf16[512,1280]{0,1:T(8,128)(2,1)S(1)} fusion(bf16[2048,1280]{0,1:T(8,128)(2,1)} %all-gather.2.cloned.1.call-done, bf16[2048,512]{1,0:T(8,128)(2,1)} %bitcast.77), kind=kOutput, calls=%fused_computation.16 | convolution fusion | flops 2685009920 | bytes 8650752 | tf_op jit(solution)/shard_map/dot_general | solution.py:92
  183.1 21.0 %all_to_all.16 = bf16[4,4,40960]{2,1,0:T(4,128)(2,1)S(1)} all-to-all(bf16[4,4,40960]{2,1,0:T(4,128)(2,1)S(1)} %copy.78), channel_id=1, replica_groups=mesh['zh'=4,'x'=4,'core'=2,'y'=4,'zl'=2] {'y'}, dimensions={0} | all-to-all | bytes 2621440 | tf_op jit(solution)/shard_map/all_to_all | solution.py:99
  206.0 8.1 %all-to-all-start.2 = ((bf16[8,16,1280]{2,1,0:T(8,128)(2,1)}), bf16[8,16,1280]{2,1,0:T(8,128)(2,1)S(1)}, u32[]{:S(2)}, u32[]{:S(2)}) async-start(bf16[8,16,1280]{2,1,0:T(8,128)(2,1)} %reshape.132), calls=%async_computation.2 | async-start | bytes 655360 | tf_op jit(solution)/shard_map/all_to_all | solution.py:102
  216.6 8.9 %all-to-all-done.2 = bf16[8,16,1280]{2,1,0:T(8,128)(2,1)S(1)} async-done(((bf16[8,16,1280]{2,1,0:T(8,128)(2,1)}), bf16[8,16,1280]{2,1,0:T(8,128)(2,1)S(1)}, u32[]{:S(2)}, u32[]{:S(2)}) %all-to-all-start.2) | async-done | bytes 327712 | tf_op jit(solution)/shard_map/all_to_all | solution.py:102
  (58 shorter events, 26.1 us)
Async XLA Ops:
  7.2 167.2 %all-gather.2.cloned.1.call-start = ((), (), s32[]{:S(2)}) async-start(), calls=%async_computation.3 | async-start | bytes 5898240 | tf_op jit(solution)/shard_map/all_gather | solution.py:91
  8.1 19.2 %collective-permute-start = (bf16[256,256]{1,0:T(8,128)(2,1)S(1)}, bf16[256,256]{1,0:T(8,128)(2,1)S(1)}, u32[]{:S(2)}, u32[]{:S(2)}) collective-permute-start(bf16[256,256]{1,0:T(8,128)(2,1)S(1)} %get-tuple-element.45), channel_id=1, source_target_pairs={{0,1},{1,2},{2,3},{3,4},{4,5},{5,6},{6,7},{8,9},{9,10},{10,11},{11... | collective-permute-start | bytes 393224 | tf_op jit(solution)/shard_map/ppermute | solution.py:25
  11.1 17.5 %collective-permute-start.1 = (bf16[256,256]{1,0:T(8,128)(2,1)S(1)}, bf16[256,256]{1,0:T(8,128)(2,1)S(1)}, u32[]{:S(2)}, u32[]{:S(2)}) collective-permute-start(bf16[256,256]{1,0:T(8,128)(2,1)S(1)} %get-tuple-element.45), channel_id=1, source_target_pairs={{0,2},{1,3},{2,4},{3,5},{4,6},{5,7},{8,10},{9,11},{10,12},{11,13},... | collective-permute-start | bytes 393224 | tf_op jit(solution)/shard_map/ppermute | solution.py:25
  14.6 14.7 %collective-permute-start.2 = (bf16[256,256]{1,0:T(8,128)(2,1)S(1)}, bf16[256,256]{1,0:T(8,128)(2,1)S(1)}, u32[]{:S(2)}, u32[]{:S(2)}) collective-permute-start(bf16[256,256]{1,0:T(8,128)(2,1)S(1)} %get-tuple-element.45), channel_id=1, source_target_pairs={{0,3},{1,4},{2,5},{3,6},{4,7},{8,11},{9,12},{10,13},{11,14},{12,15... | collective-permute-start | bytes 393224 | tf_op jit(solution)/shard_map/ppermute | solution.py:25
  19.8 9.6 %collective-permute-start.3 = (bf16[256,256]{1,0:T(8,128)(2,1)S(1)}, bf16[256,256]{1,0:T(8,128)(2,1)S(1)}, u32[]{:S(2)}, u32[]{:S(2)}) collective-permute-start(bf16[256,256]{1,0:T(8,128)(2,1)S(1)} %get-tuple-element.45), channel_id=1, source_target_pairs={{0,4},{1,5},{2,6},{3,7},{8,12},{9,13},{10,14},{11,15},{16,20},{17,... | collective-permute-start | bytes 393224 | tf_op jit(solution)/shard_map/ppermute | solution.py:25
  21.1 8.3 %collective-permute-start.4 = (bf16[256,256]{1,0:T(8,128)(2,1)S(1)}, bf16[256,256]{1,0:T(8,128)(2,1)S(1)}, u32[]{:S(2)}, u32[]{:S(2)}) collective-permute-start(bf16[256,256]{1,0:T(8,128)(2,1)S(1)} %get-tuple-element.45), channel_id=1, source_target_pairs={{0,5},{1,6},{2,7},{8,13},{9,14},{10,15},{16,21},{17,22},{18,23},{2... | collective-permute-start | bytes 393224 | tf_op jit(solution)/shard_map/ppermute | solution.py:25
  27.3 6.6 %collective-permute-start.5 = (bf16[256,256]{1,0:T(8,128)(2,1)S(1)}, bf16[256,256]{1,0:T(8,128)(2,1)S(1)}, u32[]{:S(2)}, u32[]{:S(2)}) collective-permute-start(bf16[256,256]{1,0:T(8,128)(2,1)S(1)} %get-tuple-element.45), channel_id=1, source_target_pairs={{0,6},{1,7},{8,14},{9,15},{16,22},{17,23},{24,30},{25,31},{32,38},... | collective-permute-start | bytes 393224 | tf_op jit(solution)/shard_map/ppermute | solution.py:25
  28.7 5.3 %collective-permute-start.6 = (bf16[256,256]{1,0:T(8,128)(2,1)S(1)}, bf16[256,256]{1,0:T(8,128)(2,1)S(1)}, u32[]{:S(2)}, u32[]{:S(2)}) collective-permute-start(bf16[256,256]{1,0:T(8,128)(2,1)S(1)} %get-tuple-element.45), channel_id=1, source_target_pairs={{0,7},{8,15},{16,23},{24,31},{32,39},{40,47},{48,55},{56,63},{64,7... | collective-permute-start | bytes 393224 | tf_op jit(solution)/shard_map/ppermute | solution.py:25
  59.8 16.4 %copy-start = (f32[8,256,2048]{1,2,0:T(8,128)S(1)}, f32[8,256,2048]{1,2,0:T(8,128)}, u32[]{:S(2)}) copy-start(f32[8,256,2048]{1,2,0:T(8,128)} %get-tuple-element.50) | copy-start | bytes 50331652
  89.5 6.1 %collective-permute-start.13 = (bf16[256,256]{0,1:T(8,128)(2,1)S(1)}, bf16[256,256]{0,1:T(8,128)(2,1)S(1)}, u32[]{:S(2)}, u32[]{:S(2)}) collective-permute-start(bf16[256,256]{0,1:T(8,128)(2,1)S(1)} %get-tuple-element.37), channel_id=1, source_target_pairs={{7,0},{15,8},{23,16},{31,24},{39,32},{47,40},{55,48},{63,56},{71,6... | collective-permute-start | bytes 393224 | tf_op jit(solution)/shard_map/ppermute | solution.py:25
  90.2 15.2 %collective-permute-start.12 = (bf16[256,256]{0,1:T(8,128)(2,1)S(1)}, bf16[256,256]{0,1:T(8,128)(2,1)S(1)}, u32[]{:S(2)}, u32[]{:S(2)}) collective-permute-start(bf16[256,256]{0,1:T(8,128)(2,1)S(1)} %get-tuple-element.38), channel_id=1, source_target_pairs={{6,0},{7,1},{14,8},{15,9},{22,16},{23,17},{30,24},{31,25},{38,32},... | collective-permute-start | bytes 393224 | tf_op jit(solution)/shard_map/ppermute | solution.py:25
  91.5 17.3 %collective-permute-start.11 = (bf16[256,256]{0,1:T(8,128)(2,1)S(1)}, bf16[256,256]{0,1:T(8,128)(2,1)S(1)}, u32[]{:S(2)}, u32[]{:S(2)}) collective-permute-start(bf16[256,256]{0,1:T(8,128)(2,1)S(1)} %get-tuple-element.39), channel_id=1, source_target_pairs={{5,0},{6,1},{7,2},{13,8},{14,9},{15,10},{21,16},{22,17},{23,18},{2... | collective-permute-start | bytes 393224 | tf_op jit(solution)/shard_map/ppermute | solution.py:25
  92.8 16.0 %collective-permute-start.10 = (bf16[256,256]{0,1:T(8,128)(2,1)S(1)}, bf16[256,256]{0,1:T(8,128)(2,1)S(1)}, u32[]{:S(2)}, u32[]{:S(2)}) collective-permute-start(bf16[256,256]{0,1:T(8,128)(2,1)S(1)} %get-tuple-element.40), channel_id=1, source_target_pairs={{4,0},{5,1},{6,2},{7,3},{12,8},{13,9},{14,10},{15,11},{20,16},{21,... | collective-permute-start | bytes 393224 | tf_op jit(solution)/shard_map/ppermute | solution.py:25
  94.1 14.7 %collective-permute-start.9 = (bf16[256,256]{0,1:T(8,128)(2,1)S(1)}, bf16[256,256]{0,1:T(8,128)(2,1)S(1)}, u32[]{:S(2)}, u32[]{:S(2)}) collective-permute-start(bf16[256,256]{0,1:T(8,128)(2,1)S(1)} %get-tuple-element.41), channel_id=1, source_target_pairs={{3,0},{4,1},{5,2},{6,3},{7,4},{11,8},{12,9},{13,10},{14,11},{15,12... | collective-permute-start | bytes 393224 | tf_op jit(solution)/shard_map/ppermute | solution.py:25
  95.6 13.2 %collective-permute-start.8 = (bf16[256,256]{0,1:T(8,128)(2,1)S(1)}, bf16[256,256]{0,1:T(8,128)(2,1)S(1)}, u32[]{:S(2)}, u32[]{:S(2)}) collective-permute-start(bf16[256,256]{0,1:T(8,128)(2,1)S(1)} %get-tuple-element.42), channel_id=1, source_target_pairs={{2,0},{3,1},{4,2},{5,3},{6,4},{7,5},{10,8},{11,9},{12,10},{13,11},... | collective-permute-start | bytes 393224 | tf_op jit(solution)/shard_map/ppermute | solution.py:25
  105.4 7.7 %collective-permute-start.7 = (bf16[256,256]{0,1:T(8,128)(2,1)S(1)}, bf16[256,256]{0,1:T(8,128)(2,1)S(1)}, u32[]{:S(2)}, u32[]{:S(2)}) collective-permute-start(bf16[256,256]{0,1:T(8,128)(2,1)S(1)} %get-tuple-element.36), channel_id=1, source_target_pairs={{1,0},{2,1},{3,2},{4,3},{5,4},{6,5},{7,6},{9,8},{10,9},{11,10},{12... | collective-permute-start | bytes 393224 | tf_op jit(solution)/shard_map/ppermute | solution.py:25
  206.0 19.5 %all-to-all-start.2 = ((bf16[8,16,1280]{2,1,0:T(8,128)(2,1)}), bf16[8,16,1280]{2,1,0:T(8,128)(2,1)S(1)}, u32[]{:S(2)}, u32[]{:S(2)}) async-start(bf16[8,16,1280]{2,1,0:T(8,128)(2,1)} %reshape.132), calls=%async_computation.2 | async-start | bytes 655360 | tf_op jit(solution)/shard_map/all_to_all | solution.py:102
Sparse Core Ops, SparseCore 0:
  114.4 60.0 all-gather.1

commit v2 on v1

v2 whole, which is shorter than its diff:
```python
import functools
import math

import jax
import jax.numpy as jnp
from jax import lax
from jax.experimental import pallas as pl
from jax.experimental.pallas import tpu as pltpu
from jax.sharding import Mesh, PartitionSpec as P

NEG = -1e30
AXES = ("zh", "x", "core", "y", "zl")
SIZES = (4, 4, 2, 4, 2)
CTX = ("y", "zl")
BF = jnp.bfloat16
F32 = jnp.float32
NT = (((1,), (1,)), ((), ()))
NN = (((1,), (0,)), ((), ()))
TN = (((0,), (0,)), ((), ()))


def dot(a, b, dims):
    return lax.dot_general(a, b, dims, preferred_element_type=F32)


def shifted(value, axes, count, step, wrap):
    pairs = []
    for src in range(count):
        dst = src + step
        if wrap:
            pairs.append((src, dst % count))
        elif 0 <= dst < count:
            pairs.append((src, dst))
    return lax.ppermute(value, axes, pairs)


def attention_kernel(blocks, per, scale, info, starts_ref, q_ref, do_ref, *refs):
    kv_refs, refs = refs[:blocks], refs[blocks:]
    dq_ref, refs = refs[0], refs[1:]
    out_refs, refs = refs[:blocks], refs[blocks:]
    kv_s, kt_s, acc_s, e_s, dp_s, md_s, stat_s, dqt_s = refs
    rows = q_ref.shape[0]
    hd = kt_s.shape[1]
    used, place, limit = info[0], info[1], info[2]
    step = pl.program_id(0)
    power = scale * math.log2(math.e)

    @pl.when(step == 0)
    def _():
        acc_s[...] = jnp.zeros_like(acc_s)
        for d in range(blocks):

            @pl.when(d < used)
            def _():
                kv_s[d] = kv_refs[d][...]
                kt_s[d] = kv_refs[d][:, :hd].astype(F32).T.astype(BF)

    for h in range(per):
        stat_s[0, h] = jnp.full((1, rows), NEG, F32)
        stat_s[1, h] = jnp.zeros((1, rows), F32)
        stat_s[2, h] = jnp.zeros((1, rows), F32)
    dqt_s[...] = jnp.zeros_like(dqt_s)

    def forward(d, masked):
        kd = kv_s[d, :, :hd]
        vd = kv_s[d, :, hd:]
        if masked:
            base = (place - d) * rows
            kp = lax.broadcasted_iota(jnp.int32, (rows, rows), 0) + base
            qp = lax.broadcasted_iota(jnp.int32, (rows, rows), 1) + place * rows
            ok = (kp >= starts_ref[...]) & (kp <= qp)
        for h in range(per):
            cols = slice(h * hd, (h + 1) * hd)
            s = dot(kd, q_ref[:, cols], NT)
            if masked:
                s = jnp.where(ok, s, NEG)
            old = stat_s[0, h]
            top = jnp.maximum(old, jnp.max(s, axis=0, keepdims=True))
            e = jnp.exp2(s * power - top * power)
            alpha = jnp.exp2((old - top) * power)
            dp = dot(vd, do_ref[:, cols], NT)
            stat_s[0, h] = top
            stat_s[1, h] = stat_s[1, h] * alpha + jnp.sum(e, axis=0, keepdims=True)
            stat_s[2, h] = stat_s[2, h] * alpha + jnp.sum(e * dp, axis=0, keepdims=True)
            e_s[d, h] = e
            dp_s[d, h] = dp
            md_s[d, h] = top

    def first(d, carry):
        masked = (d == 0) | ((place - d) * rows < limit)
        pl.when(masked)(lambda: forward(d, True))
        pl.when(jnp.logical_not(masked))(lambda: forward(d, False))
        return carry

    lax.fori_loop(0, used, first, 0)

    tops = [stat_s[0, h] for h in range(per)]
    inverse = [1.0 / stat_s[1, h] for h in range(per)]
    delta = [stat_s[2, h] * inverse[h] for h in range(per)]

    def second(d, carry):
        kt = kt_s[d]
        dk = jnp.zeros((rows, hd), F32)
        dv = jnp.zeros((rows, hd), F32)
        for h in range(per):
            cols = slice(h * hd, (h + 1) * hd)
            p = e_s[d, h] * (jnp.exp2((md_s[d, h] - tops[h]) * power) * inverse[h])
            ds = (p * (dp_s[d, h] - delta[h])).astype(BF)
            dv += dot(p.astype(BF), do_ref[:, cols], NN)
            dk += dot(ds, q_ref[:, cols], NN)
            dqt_s[h] += dot(kt, ds, NN)
        acc_s[d, :, :hd] += dk
        acc_s[d, :, hd:] += dv
        return carry

    lax.fori_loop(0, used, second, 0)

    for h in range(per):
        dq_ref[:, h * hd : (h + 1) * hd] = (dqt_s[h].T * scale).astype(BF)

    @pl.when(step == pl.num_programs(0) - 1)
    def _():
        for d in range(blocks):
            out_refs[d][:, :hd] = (acc_s[d, :, :hd] * scale).astype(BF)
            out_refs[d][:, hd:] = acc_s[d, :, hd:].astype(BF)


def attention(q, do, kv, docs, place):
    rows = q.shape[0]
    hd = kv[0].shape[1] // 2
    heads = q.shape[1] // hd
    blocks = len(kv)
    per = 2
    my_docs = lax.dynamic_slice_in_dim(docs, place * rows, rows)
    starts = jnp.sum((docs[:, None] < my_docs[None, :]).astype(jnp.int32), axis=0)
    info = jnp.stack([place - starts[0] // rows + 1, place, starts[rows - 1]])
    whole = lambda shape: pl.BlockSpec(shape, lambda g: (0,) * len(shape))
    slab = pl.BlockSpec((rows, per * hd), lambda g: (0, g))
    kv_shape = (rows, 2 * hd)
    outs = pl.pallas_call(
        functools.partial(attention_kernel, blocks, per, hd ** (-0.5)),
        grid=(heads // per,),
        in_specs=[pl.BlockSpec(memory_space=pltpu.SMEM), whole((1, rows)), slab, slab]
        + [whole(kv_shape)] * blocks,
        out_specs=[slab] + [whole(kv_shape)] * blocks,
        out_shape=[jax.ShapeDtypeStruct(q.shape, BF)]
        + [jax.ShapeDtypeStruct(kv_shape, BF)] * blocks,
        scratch_shapes=[
            pltpu.VMEM((blocks, rows, 2 * hd), BF),
            pltpu.VMEM((blocks, hd, rows), BF),
            pltpu.VMEM((blocks, rows, 2 * hd), F32),
            pltpu.VMEM((blocks, per, rows, rows), F32),
            pltpu.VMEM((blocks, per, rows, rows), F32),
            pltpu.VMEM((blocks, per, 1, rows), F32),
            pltpu.VMEM((3, per, 1, rows), F32),
            pltpu.VMEM((per, hd, rows), F32),
        ],
        compiler_params=pltpu.CompilerParams(vmem_limit_bytes=40 * 2**20),
        cost_estimate=pl.CostEstimate(
            flops=10 * heads * rows * rows * blocks * hd,
            bytes_accessed=8 * 2**20,
            transcendentals=heads * rows * rows * blocks,
        ),
        name="attention_backward",
    )(info, starts[None, :], q, do, *kv)
    return outs[0], outs[1:]


def local(layer_input, queries, key_head, value_head, grad_output, doc_ids):
    x, q, k, v, do, docs = (
        a[0] for a in (layer_input, queries, key_head, value_head, grad_output, doc_ids)
    )
    rows, hd = k.shape
    dim = x.shape[1]
    ctx = lax.axis_size(CTX)
    nx, nc, z_hi = lax.axis_size("x"), lax.axis_size("core"), lax.axis_size("zh")
    place = lax.axis_index(CTX)
    my_x, my_core = lax.axis_index("x"), lax.axis_index("core")
    wide = dim // (z_hi * nx * nc)

    kv = jnp.concatenate([k, v], axis=1)
    kv_blocks = [kv] + [shifted(kv, CTX, ctx, d, False) for d in range(1, ctx)]

    split = x.reshape(rows, z_hi, nx, nc, wide)

    def owned(core):
        part = lax.dynamic_index_in_dim(split, core, 3, keepdims=False)
        return part.transpose(2, 0, 1, 3).reshape(nx, rows, z_hi * wide)

    kept = owned(my_core)
    given = shifted(owned(1 - my_core), "core", nc, 1, True)
    both = jnp.stack([kept, given], axis=1).reshape(nx, nc * rows, z_hi * wide)
    features = []
    for s in range(nx):
        mine = lax.dynamic_index_in_dim(both, (my_x + s) % nx, 0, keepdims=False)
        features.append(shifted(mine, "x", nx, s, True) if s else mine)

    dq, dkv = attention(q, do, kv_blocks, docs, place)

    total = dkv[0].astype(F32)
    for d in range(1, ctx):
        total = total + shifted(dkv[d], CTX, ctx, -d, False).astype(F32)
    dkv_own = total.astype(BF)

    grads = jnp.concatenate([dq, dkv_own], axis=1)
    along = [grads] + [shifted(grads, "x", nx, s, True) for s in range(1, nx)]
    along = jnp.stack(along)
    other = shifted(along, "core", nc, 1, True)
    grads_all = jnp.stack([along, other], axis=1).reshape(nx * nc * rows, -1)
    part = dot(jnp.concatenate(features, axis=0), grads_all, TN).astype(BF)
    n = part.shape[1]
    y, zl = lax.axis_size("y"), lax.axis_size("zl")
    keep = wide // (y * zl)
    part = part.reshape(z_hi, y, zl * keep * n).transpose(1, 0, 2)
    part = lax.all_to_all(part, "y", 0, 0, tiled=True)
    part = jnp.sum(part.astype(F32), axis=0).astype(BF)
    part = part.reshape(z_hi * zl, keep, n)
    part = lax.all_to_all(part, ("zh", "zl"), 0, 0, tiled=True)
    tokens = rows * ctx * nx * nc * z_hi
    weight = jnp.sum(part.astype(F32), axis=0) * (1.0 / math.sqrt(tokens))
    width = q.shape[1]
    return (
        dq[None],
        dkv_own[None, :, :hd],
        dkv_own[None, :, hd:],
        weight[:, :width],
        weight[:, width : width + hd],
        weight[:, width + hd :],
    )


def solution(mesh):
    fine = Mesh(mesh.devices.reshape(SIZES), AXES)
    dp = ("zh", "x", "core")
    tok = P(dp, CTX, None)
    row = P(dp + CTX, None)
    return jax.shard_map(
        local,
        mesh=fine,
        in_specs=(tok, tok, tok, tok, tok, P(dp, None)),
        out_specs=(tok, tok, tok, row, row, row),
        check_vma=False,
    )
```

time: 235 us -> 203 us (0.86); the launches traced: 234 us -> 199 us
  blocking collectives: 62.5 us -> 21 us
  waiting for transfers between devices: 39.1 us -> 79.2 us
  matrix products: 34.1 us -> 2.93 us
  other arithmetic: 29.9 us -> 11.9 us
  starting transfers between devices: 33.7 us -> 47.2 us
  between operations: 14.4 us -> 3.46 us
  Pallas kernels: 0 us -> 8.81 us
  local copies, waits for them, and re-layouts: 19.8 us -> 24.6 us
    ppermute x14 -> x22, waiting for transfers between devices: 17.4 us -> 70 us  [shifted(): return lax.ppermute(value, axes, pairs)]
    all_to_all x1 -> x0, blocking collectives: 41.5 us -> none  [local(): lax.all_to_all(split, GROUP, 0, 0, tiled=True)]
    dot_general x6 -> x1, matrix products: 34.1 us -> 2.93 us  [dot(): return lax.dot_general(a, b, dims, preferred_element_type=F32)]
    sub x1 -> x0, other arithmetic: 17.8 us -> none  [attention(): raised = jnp.exp(scores - top)]
    all_gather x1 -> x0, waiting for transfers between devices: 12.8 us -> none  [local(): grads_all = lax.all_gather(grads, GROUP, axis=0, tiled=True)]
    ppermute x14 -> x22, starting transfers between devices: 25.6 us -> 37.5 us  [shifted(): return lax.ppermute(value, axes, pairs)]
    pallas_call x0 -> x1, Pallas kernels: none -> 8.81 us  [attention(): pl.pallas_call(functools.partial(attention_kernel, blocks, per, hd ** (-0...]
    another operation x1 -> x5, other arithmetic: 0.19 us -> 8.84 us  [the longest x2 3.93 us: local(): grads_all = jnp.stack([along, other], axis=1).reshape(nx * nc * rows, -1)]
  transfers between devices with their start and end apart: 16 -> 23, of which waited for: 5 -> 12; matrix products, arithmetic and copies ran while one was open for 6% -> 13% of each run, Pallas kernels for 0% -> 0%
where the time goes in v2:
time: 203 us; the launch traced here: 199 us
  waiting for transfers between devices  79.2 us (39%)
  starting transfers between devices  47.2 us (23%)
  local copies, waits for them, and re-layouts  24.6 us (12%)
  blocking collectives  21 us (10%)
  other arithmetic  11.9 us (6%)
  Pallas kernels  8.81 us (4%)
  between operations  3.46 us (2%)
  matrix products  2.93 us (1%)
    ppermute x22, waiting for transfers between devices, shifted(): return lax.ppermute(value, axes, pairs)  70 us
    ppermute x22, starting transfers between devices, shifted(): return lax.ppermute(value, axes, pairs)  37.5 us
    all_to_all x1, blocking collectives, local(): part = lax.all_to_all(part, 'y', 0, 0, tiled=True)  21 us
    all_to_all x1, starting transfers between devices, local(): part = lax.all_to_all(part, ('zh', 'zl'), 0, 0, tiled=True)  9.71 us
    all_to_all x1, waiting for transfers between devices, local(): part = lax.all_to_all(part, ('zh', 'zl'), 0, 0, tiled=True)  9.22 us
    pallas_call x1, Pallas kernels, attention(): pl.pallas_call(functools.partial(attention_kernel, blocks, per, hd ** (-0...  8.81 us
    unnamed x5, local copies, waits for them, and re-layouts  6.15 us
    transpose x3, local copies, waits for them, and re-layouts, owned(): return part.transpose(2, 0, 1, 3).reshape(nx, rows, z_hi * wide)  6.14 us
  transfers between devices with their start and end apart: 23, of which 12 were waited for; matrix products, arithmetic and copies ran while one was open for 13% of the time, Pallas kernels for 0%

profile of v2, /device:TPU:32, one launch (start us, length us, event | category | flops | bytes accessed | tf_op | source)
XLA Modules:
  0.0 199.0 jit_solution(12746665295593028173)
XLA Ops:
  1.5 3.0 %collective-permute-start = (bf16[256,256]{1,0:T(8,128)(2,1)S(1)}, bf16[256,256]{1,0:T(8,128)(2,1)S(1)}, u32[]{:S(2)}, u32[]{:S(2)}) collective-permute-start(bf16[256,256]{1,0:T(8,128)(2,1)S(1)} %pad_maximum_fusion.4.refs_0_), channel_id=1, source_target_pairs={{0,1},{1,2},{2,3},{3,4},{4,5},{5,6},{6,7},{8,9},{9,10},{10,11},{11... | collective-permute-start | bytes 393224 | tf_op jit(solution)/shard_map/ppermute | solution.py:34
  4.6 3.5 %collective-permute-start.1 = (bf16[256,256]{1,0:T(8,128)(2,1)S(1)}, bf16[256,256]{1,0:T(8,128)(2,1)S(1)}, u32[]{:S(2)}, u32[]{:S(2)}) collective-permute-start(bf16[256,256]{1,0:T(8,128)(2,1)S(1)} %pad_maximum_fusion.4.refs_0_), channel_id=1, source_target_pairs={{0,2},{1,3},{2,4},{3,5},{4,6},{5,7},{8,10},{9,11},{10,12},{11,13},... | collective-permute-start | bytes 393224 | tf_op jit(solution)/shard_map/ppermute | solution.py:34
  8.1 5.2 %collective-permute-start.2 = (bf16[256,256]{1,0:T(8,128)(2,1)S(1)}, bf16[256,256]{1,0:T(8,128)(2,1)S(1)}, u32[]{:S(2)}, u32[]{:S(2)}) collective-permute-start(bf16[256,256]{1,0:T(8,128)(2,1)S(1)} %pad_maximum_fusion.4.refs_0_), channel_id=1, source_target_pairs={{0,3},{1,4},{2,5},{3,6},{4,7},{8,11},{9,12},{10,13},{11,14},{12,15... | collective-permute-start | bytes 393224 | tf_op jit(solution)/shard_map/ppermute | solution.py:34
  26.3 8.8 %attention_backward.1 = (bf16[256,1024]{1,0:T(8,128)(2,1)}, bf16[256,256]{1,0:T(8,128)(2,1)S(1)}, bf16[256,256]{1,0:T(8,128)(2,1)S(1)}, bf16[256,256]{1,0:T(8,12...) custom-call(s32[3]{0:T(128)S(1)} %pad_add_fusion.info, ...), custom_call_target="tpu_custom_call" | custom-call | flops 5368709120 | bytes 8388608 | tf_op jit(solution)/shard_map/attention_backward/pallas_call | solution.py:140
  41.6 10.3 %collective-permute-done.10 = bf16[256,256]{1,0:T(8,128)(2,1)S(1)} collective-permute-done((bf16[256,256]{1,0:T(8,128)(2,1)S(1)}, bf16[256,256]{1,0:T(8,128)(2,1)S(1)}, u32[]{:S(2)}, u32[]{:S(2)}) %collective-permute-start.10) | collective-permute-done | bytes 131104 | tf_op jit(solution)/shard_map/ppermute | solution.py:34
  53.1 6.5 %collective-permute-done.11 = bf16[256,256]{1,0:T(8,128)(2,1)S(1)} collective-permute-done((bf16[256,256]{1,0:T(8,128)(2,1)S(1)}, bf16[256,256]{1,0:T(8,128)(2,1)S(1)}, u32[]{:S(2)}, u32[]{:S(2)}) %collective-permute-start.11) | collective-permute-done | bytes 131104 | tf_op jit(solution)/shard_map/ppermute | solution.py:34
  60.9 3.4 %collective-permute-done.12 = bf16[256,256]{1,0:T(8,128)(2,1)S(1)} collective-permute-done((bf16[256,256]{1,0:T(8,128)(2,1)S(1)}, bf16[256,256]{1,0:T(8,128)(2,1)S(1)}, u32[]{:S(2)}, u32[]{:S(2)}) %collective-permute-start.12) | collective-permute-done | bytes 131104 | tf_op jit(solution)/shard_map/ppermute | solution.py:34
  64.3 6.5 %collective-permute-done.8 = bf16[256,256]{1,0:T(8,128)(2,1)S(1)} collective-permute-done((bf16[256,256]{1,0:T(8,128)(2,1)S(1)}, bf16[256,256]{1,0:T(8,128)(2,1)S(1)}, u32[]{:S(2)}, u32[]{:S(2)}) %collective-permute-start.8) | collective-permute-done | bytes 131104 | tf_op jit(solution)/shard_map/ppermute | solution.py:34
  74.3 2.3 %collective-permute-start.19 = (bf16[256,1280]{1,0:T(8,128)(2,1)S(1)}, bf16[256,1280]{1,0:T(8,128)(2,1)S(1)}, u32[]{:S(2)}, u32[]{:S(2)}) collective-permute-start(bf16[256,1280]{1,0:T(8,128)(2,1)S(1)} %get-tuple-element.33), channel_id=1, source_target_pairs={{0,32},{16,48},{32,0},{48,16},{1,33},{17,49},{33,1},{49,17},{2,34}... | collective-permute-start | bytes 1966088 | tf_op jit(solution)/shard_map/ppermute | solution.py:34
  78.5 11.8 %collective-permute-done.18 = bf16[256,1280]{1,0:T(8,128)(2,1)S(1)} collective-permute-done((bf16[256,1280]{1,0:T(8,128)(2,1)S(1)}, bf16[256,1280]{1,0:T(8,128)(2,1)S(1)}, u32[]{:S(2)}, u32[]{:S(2)}) %collective-permute-start.18) | collective-permute-done | bytes 655392 | tf_op jit(solution)/shard_map/ppermute | solution.py:34
  90.3 11.0 %collective-permute-done.19 = bf16[256,1280]{1,0:T(8,128)(2,1)S(1)} collective-permute-done((bf16[256,1280]{1,0:T(8,128)(2,1)S(1)}, bf16[256,1280]{1,0:T(8,128)(2,1)S(1)}, u32[]{:S(2)}, u32[]{:S(2)}) %collective-permute-start.19) | collective-permute-done | bytes 655392 | tf_op jit(solution)/shard_map/ppermute | solution.py:34
  103.1 4.1 %copy.30 = bf16[1,256,4096]{1,2,0:T(8,128)(2,1)} copy(bf16[1,256,4096]{2,1,0:T(8,128)(2,1)} %param.6) | data formatting | bytes 4194304 | tf_op args[0]
  107.1 2.8 %dynamic-slice_bitcast_fusion.1 = (bf16[4,256,4,128]{1,3,0,2:T(8,128)(2,1)}, bf16[4,256,4,128]{1,3,0,2:T(8,128)(2,1)S(1)}) fusion(bf16[256,4,4,2,128]{0,4,3,2,1:T(8,128)(2,1)} %bitcast.52, s32[]{:T(128)S(6)} %select_n.48, s32[]{:T(128)S(6)} %select_n.49), kind=kLoop, calls=%fused_computation.14 | loop fusion | bytes 4194312 | tf_op jit(solution)/shard_map/transpose | solution.py:188
  111.5 2.3 %copy.32 = bf16[4,256,4,128]{1,3,2,0:T(8,128)(2,1)} copy(bf16[4,256,4,128]{1,3,0,2:T(8,128)(2,1)} %get-tuple-element.30) | data formatting | bytes 2097152 | tf_op jit(solution)/shard_map/transpose | solution.py:188
  114.1 3.1 %pad_maximum_fusion.2 = bf16[4,2,256,512]{2,3,0,1:T(8,128)(2,1)} fusion(bf16[4,1,256,512]{2,3,0,1:T(8,128)(2,1)} %bitcast.22, bf16[4,1,256,512]{2,3,0,1:T(8,128)(2,1)} %bitcast.56), kind=kLoop, calls=%fused_computation.3 | loop fusion | flops 1048576 | bytes 4194304 | tf_op jit(solution)/shard_map/stack | solution.py:192
  117.2 4.1 %copy.35 = bf16[4,2,256,512]{3,2,1,0:T(8,128)(2,1)} copy(bf16[4,2,256,512]{2,3,0,1:T(8,128)(2,1)} %pad_maximum_fusion.2) | data formatting | bytes 4194304 | tf_op jit(solution)/shard_map/stack | solution.py:192
  124.4 2.4 %collective-permute-start.16 = (bf16[512,512]{1,0:T(8,128)(2,1)S(1)}, bf16[512,512]{1,0:T(8,128)(2,1)S(1)}, u32[]{:S(2)}, u32[]{:S(2)}) collective-permute-start(bf16[512,512]{1,0:T(8,128)(2,1)S(1)} %get-tuple-element.28), channel_id=1, source_target_pairs={{0,32},{16,48},{32,0},{48,16},{1,33},{17,49},{33,1},{49,17},{2,34}... | collective-permute-start | bytes 1572872 | tf_op jit(solution)/shard_map/ppermute | solution.py:34
  128.3 2.2 %pad_maximum_fusion = bf16[4,2,256,1280]{3,2,0,1:T(8,128)(2,1)S(1)} fusion(bf16[4,1,256,1280]{3,2,0,1:T(8,128)(2,1)} %bitcast.33, bf16[4,1,256,1280]{3,2,0,1:T(8,128)(2,1)S(1)} %get-tuple-element.24), kind=kLoop, calls=%fused_computation | loop fusion | flops 2621440 | bytes 10485760 | tf_op jit(solution)/shard_map/stack | solution.py:209
  130.9 7.6 %collective-permute-done.15 = bf16[512,512]{1,0:T(8,128)(2,1)S(1)} collective-permute-done((bf16[512,512]{1,0:T(8,128)(2,1)S(1)}, bf16[512,512]{1,0:T(8,128)(2,1)S(1)}, u32[]{:S(2)}, u32[]{:S(2)}) %collective-permute-start.15) | collective-permute-done | bytes 524320 | tf_op jit(solution)/shard_map/ppermute | solution.py:34
  138.5 11.7 %collective-permute-done.16 = bf16[512,512]{1,0:T(8,128)(2,1)S(1)} collective-permute-done((bf16[512,512]{1,0:T(8,128)(2,1)S(1)}, bf16[512,512]{1,0:T(8,128)(2,1)S(1)}, u32[]{:S(2)}, u32[]{:S(2)}) %collective-permute-start.16) | collective-permute-done | bytes 524320 | tf_op jit(solution)/shard_map/ppermute | solution.py:34
  150.3 2.9 %convolution_convert_fusion = bf16[512,1280]{1,0:T(8,128)(2,1)S(1)} fusion(bf16[2048,1280]{1,0:T(8,128)(2,1)S(1)} %bitcast.54, bf16[512,512]{1,0:T(8,128)(2,1)S(1)} %collective-permute-done.17, bf16[512,512]{1,0:T(8,128)(2,1)S(1)} %collective-permute-done.16, bf16[512,512]{1,0:T(8,128)(2,1)S(1)} %collective-permute-done.15, ...), kind=kOutput, calls=%fused_computation.1 | convolution fusion | flops 2693398528 | bytes 8650752 | tf_op jit(solution)/shard_map/dot_general | solution.py:23
  155.3 21.0 %all_to_all.10 = bf16[4,4,40960]{2,1,0:T(4,128)(2,1)S(1)} all-to-all(bf16[4,4,40960]{2,1,0:T(4,128)(2,1)S(1)} %bitcast.55), channel_id=1, replica_groups=mesh['zh'=4,'x'=4,'core'=2,'y'=4,'zl'=2] {'y'}, dimensions={0} | all-to-all | bytes 2621440 | tf_op jit(solution)/shard_map/all_to_all | solution.py:215
  178.1 9.7 %all-to-all-start.1 = ((bf16[8,16,1280]{2,1,0:T(8,128)(2,1)}), bf16[8,16,1280]{2,1,0:T(8,128)(2,1)S(1)}, u32[]{:S(2)}, u32[]{:S(2)}) async-start(bf16[8,16,1280]{2,1,0:T(8,128)(2,1)} %reshape.34), calls=%async_computation.1 | async-start | bytes 655360 | tf_op jit(solution)/shard_map/all_to_all | solution.py:218
  188.5 9.2 %all-to-all-done.1 = bf16[8,16,1280]{2,1,0:T(8,128)(2,1)S(1)} async-done(((bf16[8,16,1280]{2,1,0:T(8,128)(2,1)}), bf16[8,16,1280]{2,1,0:T(8,128)(2,1)S(1)}, u32[]{:S(2)}, u32[]{:S(2)}) %all-to-all-start.1) | async-done | bytes 327712 | tf_op jit(solution)/shard_map/all_to_all | solution.py:218
  (55 shorter events, 40.2 us)
Async XLA Ops:
  1.5 16.0 %collective-permute-start = (bf16[256,256]{1,0:T(8,128)(2,1)S(1)}, bf16[256,256]{1,0:T(8,128)(2,1)S(1)}, u32[]{:S(2)}, u32[]{:S(2)}) collective-permute-start(bf16[256,256]{1,0:T(8,128)(2,1)S(1)} %pad_maximum_fusion.4.refs_0_), channel_id=1, source_target_pairs={{0,1},{1,2},{2,3},{3,4},{4,5},{5,6},{6,7},{8,9},{9,10},{10,11},{11... | collective-permute-start | bytes 393224 | tf_op jit(solution)/shard_map/ppermute | solution.py:34
  4.6 14.3 %collective-permute-start.1 = (bf16[256,256]{1,0:T(8,128)(2,1)S(1)}, bf16[256,256]{1,0:T(8,128)(2,1)S(1)}, u32[]{:S(2)}, u32[]{:S(2)}) collective-permute-start(bf16[256,256]{1,0:T(8,128)(2,1)S(1)} %pad_maximum_fusion.4.refs_0_), channel_id=1, source_target_pairs={{0,2},{1,3},{2,4},{3,5},{4,6},{5,7},{8,10},{9,11},{10,12},{11,13},... | collective-permute-start | bytes 393224 | tf_op jit(solution)/shard_map/ppermute | solution.py:34
  8.1 15.4 %collective-permute-start.2 = (bf16[256,256]{1,0:T(8,128)(2,1)S(1)}, bf16[256,256]{1,0:T(8,128)(2,1)S(1)}, u32[]{:S(2)}, u32[]{:S(2)}) collective-permute-start(bf16[256,256]{1,0:T(8,128)(2,1)S(1)} %pad_maximum_fusion.4.refs_0_), channel_id=1, source_target_pairs={{0,3},{1,4},{2,5},{3,6},{4,7},{8,11},{9,12},{10,13},{11,14},{12,15... | collective-permute-start | bytes 393224 | tf_op jit(solution)/shard_map/ppermute | solution.py:34
  13.2 10.3 %collective-permute-start.3 = (bf16[256,256]{1,0:T(8,128)(2,1)S(1)}, bf16[256,256]{1,0:T(8,128)(2,1)S(1)}, u32[]{:S(2)}, u32[]{:S(2)}) collective-permute-start(bf16[256,256]{1,0:T(8,128)(2,1)S(1)} %pad_maximum_fusion.4.refs_0_), channel_id=1, source_target_pairs={{0,4},{1,5},{2,6},{3,7},{8,12},{9,13},{10,14},{11,15},{16,20},{17,... | collective-permute-start | bytes 393224 | tf_op jit(solution)/shard_map/ppermute | solution.py:34
  14.5 9.0 %collective-permute-start.4 = (bf16[256,256]{1,0:T(8,128)(2,1)S(1)}, bf16[256,256]{1,0:T(8,128)(2,1)S(1)}, u32[]{:S(2)}, u32[]{:S(2)}) collective-permute-start(bf16[256,256]{1,0:T(8,128)(2,1)S(1)} %pad_maximum_fusion.4.refs_0_), channel_id=1, source_target_pairs={{0,5},{1,6},{2,7},{8,13},{9,14},{10,15},{16,21},{17,22},{18,23},{2... | collective-permute-start | bytes 393224 | tf_op jit(solution)/shard_map/ppermute | solution.py:34
  17.6 6.6 %collective-permute-start.5 = (bf16[256,256]{1,0:T(8,128)(2,1)S(1)}, bf16[256,256]{1,0:T(8,128)(2,1)S(1)}, u32[]{:S(2)}, u32[]{:S(2)}) collective-permute-start(bf16[256,256]{1,0:T(8,128)(2,1)S(1)} %pad_maximum_fusion.4.refs_0_), channel_id=1, source_target_pairs={{0,6},{1,7},{8,14},{9,15},{16,22},{17,23},{24,30},{25,31},{32,38},... | collective-permute-start | bytes 393224 | tf_op jit(solution)/shard_map/ppermute | solution.py:34
  18.9 5.3 %collective-permute-start.6 = (bf16[256,256]{1,0:T(8,128)(2,1)S(1)}, bf16[256,256]{1,0:T(8,128)(2,1)S(1)}, u32[]{:S(2)}, u32[]{:S(2)}) collective-permute-start(bf16[256,256]{1,0:T(8,128)(2,1)S(1)} %pad_maximum_fusion.4.refs_0_), channel_id=1, source_target_pairs={{0,7},{8,15},{16,23},{24,31},{32,39},{40,47},{48,55},{56,63},{64,7... | collective-permute-start | bytes 393224 | tf_op jit(solution)/shard_map/ppermute | solution.py:34
  24.2 1.0 copy-start
  35.1 16.8 %collective-permute-start.10 = (bf16[256,256]{1,0:T(8,128)(2,1)S(1)}, bf16[256,256]{1,0:T(8,128)(2,1)S(1)}, u32[]{:S(2)}, u32[]{:S(2)}) collective-permute-start(bf16[256,256]{1,0:T(8,128)(2,1)S(1)} %get-tuple-element.20), channel_id=1, source_target_pairs={{4,0},{5,1},{6,2},{7,3},{12,8},{13,9},{14,10},{15,11},{20,16},{21,... | collective-permute-start | bytes 393224 | tf_op jit(solution)/shard_map/ppermute | solution.py:34
  36.4 23.2 %collective-permute-start.11 = (bf16[256,256]{1,0:T(8,128)(2,1)S(1)}, bf16[256,256]{1,0:T(8,128)(2,1)S(1)}, u32[]{:S(2)}, u32[]{:S(2)}) collective-permute-start(bf16[256,256]{1,0:T(8,128)(2,1)S(1)} %get-tuple-element.21), channel_id=1, source_target_pairs={{5,0},{6,1},{7,2},{13,8},{14,9},{15,10},{21,16},{22,17},{23,18},{2... | collective-permute-start | bytes 393224 | tf_op jit(solution)/shard_map/ppermute | solution.py:34
  37.7 26.6 %collective-permute-start.12 = (bf16[256,256]{1,0:T(8,128)(2,1)S(1)}, bf16[256,256]{1,0:T(8,128)(2,1)S(1)}, u32[]{:S(2)}, u32[]{:S(2)}) collective-permute-start(bf16[256,256]{1,0:T(8,128)(2,1)S(1)} %get-tuple-element.22), channel_id=1, source_target_pairs={{6,0},{7,1},{14,8},{15,9},{22,16},{23,17},{30,24},{31,25},{38,32},... | collective-permute-start | bytes 393224 | tf_op jit(solution)/shard_map/ppermute | solution.py:34
  39.0 25.4 %collective-permute-start.13 = (bf16[256,256]{1,0:T(8,128)(2,1)S(1)}, bf16[256,256]{1,0:T(8,128)(2,1)S(1)}, u32[]{:S(2)}, u32[]{:S(2)}) collective-permute-start(bf16[256,256]{1,0:T(8,128)(2,1)S(1)} %get-tuple-element.23), channel_id=1, source_target_pairs={{7,0},{15,8},{23,16},{31,24},{39,32},{47,40},{55,48},{63,56},{71,6... | collective-permute-start | bytes 393224 | tf_op jit(solution)/shard_map/ppermute | solution.py:34
  39.6 24.7 %collective-permute-start.7 = (bf16[256,256]{1,0:T(8,128)(2,1)S(1)}, bf16[256,256]{1,0:T(8,128)(2,1)S(1)}, u32[]{:S(2)}, u32[]{:S(2)}) collective-permute-start(bf16[256,256]{1,0:T(8,128)(2,1)S(1)} %get-tuple-element.17), channel_id=1, source_target_pairs={{1,0},{2,1},{3,2},{4,3},{5,4},{6,5},{7,6},{9,8},{10,9},{11,10},{12... | collective-permute-start | bytes 393224 | tf_op jit(solution)/shard_map/ppermute | solution.py:34
  51.8 19.0 %collective-permute-start.8 = (bf16[256,256]{1,0:T(8,128)(2,1)S(1)}, bf16[256,256]{1,0:T(8,128)(2,1)S(1)}, u32[]{:S(2)}, u32[]{:S(2)}) collective-permute-start(bf16[256,256]{1,0:T(8,128)(2,1)S(1)} %get-tuple-element.18), channel_id=1, source_target_pairs={{2,0},{3,1},{4,2},{5,3},{6,4},{7,5},{10,8},{11,9},{12,10},{13,11},... | collective-permute-start | bytes 393224 | tf_op jit(solution)/shard_map/ppermute | solution.py:34
  59.6 11.2 %collective-permute-start.9 = (bf16[256,256]{1,0:T(8,128)(2,1)S(1)}, bf16[256,256]{1,0:T(8,128)(2,1)S(1)}, u32[]{:S(2)}, u32[]{:S(2)}) collective-permute-start(bf16[256,256]{1,0:T(8,128)(2,1)S(1)} %get-tuple-element.19), channel_id=1, source_target_pairs={{3,0},{4,1},{5,2},{6,3},{7,4},{11,8},{12,9},{13,10},{14,11},{15,12... | collective-permute-start | bytes 393224 | tf_op jit(solution)/shard_map/ppermute | solution.py:34
  72.1 18.2 %collective-permute-start.18 = (bf16[256,1280]{1,0:T(8,128)(2,1)S(1)}, bf16[256,1280]{1,0:T(8,128)(2,1)S(1)}, u32[]{:S(2)}, u32[]{:S(2)}) collective-permute-start(bf16[256,1280]{1,0:T(8,128)(2,1)S(1)} %get-tuple-element.33), channel_id=1, source_target_pairs={{0,16},{16,32},{32,48},{48,0},{1,17},{17,33},{33,49},{49,1},{2,18}... | collective-permute-start | bytes 1966088 | tf_op jit(solution)/shard_map/ppermute | solution.py:34
  74.3 27.0 %collective-permute-start.19 = (bf16[256,1280]{1,0:T(8,128)(2,1)S(1)}, bf16[256,1280]{1,0:T(8,128)(2,1)S(1)}, u32[]{:S(2)}, u32[]{:S(2)}) collective-permute-start(bf16[256,1280]{1,0:T(8,128)(2,1)S(1)} %get-tuple-element.33), channel_id=1, source_target_pairs={{0,32},{16,48},{32,0},{48,16},{1,33},{17,49},{33,1},{49,17},{2,34}... | collective-permute-start | bytes 1966088 | tf_op jit(solution)/shard_map/ppermute | solution.py:34
  76.6 24.8 %collective-permute-start.20 = (bf16[256,1280]{1,0:T(8,128)(2,1)S(1)}, bf16[256,1280]{1,0:T(8,128)(2,1)S(1)}, u32[]{:S(2)}, u32[]{:S(2)}) collective-permute-start(bf16[256,1280]{1,0:T(8,128)(2,1)S(1)} %get-tuple-element.33), channel_id=1, source_target_pairs={{0,48},{16,0},{32,16},{48,32},{1,49},{17,1},{33,17},{49,33},{2,50}... | collective-permute-start | bytes 1966088 | tf_op jit(solution)/shard_map/ppermute | solution.py:34
  103.1 25.3 %collective-permute-start.21 = (bf16[4,256,1280]{2,1,0:T(8,128)(2,1)}, bf16[4,256,1280]{2,1,0:T(8,128)(2,1)}, u32[]{:S(2)}, u32[]{:S(2)}) collective-permute-start(bf16[4,256,1280]{2,1,0:T(8,128)(2,1)} %get-tuple-element.25), channel_id=1, source_target_pairs={{0,8},{8,0},{1,9},{9,1},{2,10},{10,2},{3,11},{11,3},{4,12},{12,4},... | collective-permute-start | bytes 7864328 | tf_op jit(solution)/shard_map/ppermute | solution.py:34
  111.0 3.1 %collective-permute-start.14 = (bf16[4,256,512]{1,2,0:T(8,128)(2,1)}, bf16[4,256,512]{1,2,0:T(8,128)(2,1)}, u32[]{:S(2)}, u32[]{:S(2)}) collective-permute-start(bf16[4,256,512]{1,2,0:T(8,128)(2,1)} %bitcast.21), channel_id=1, source_target_pairs={{0,8},{8,0},{1,9},{9,1},{2,10},{10,2},{3,11},{11,3},{4,12},{12,4},... | collective-permute-start | bytes 3145736 | tf_op jit(solution)/shard_map/ppermute | solution.py:34
  123.0 15.5 %collective-permute-start.15 = (bf16[512,512]{1,0:T(8,128)(2,1)S(1)}, bf16[512,512]{1,0:T(8,128)(2,1)S(1)}, u32[]{:S(2)}, u32[]{:S(2)}) collective-permute-start(bf16[512,512]{1,0:T(8,128)(2,1)S(1)} %get-tuple-element.29), channel_id=1, source_target_pairs={{0,16},{16,32},{32,48},{48,0},{1,17},{17,33},{33,49},{49,1},{2,18}... | collective-permute-start | bytes 1572872 | tf_op jit(solution)/shard_map/ppermute | solution.py:34
  124.4 25.8 %collective-permute-start.16 = (bf16[512,512]{1,0:T(8,128)(2,1)S(1)}, bf16[512,512]{1,0:T(8,128)(2,1)S(1)}, u32[]{:S(2)}, u32[]{:S(2)}) collective-permute-start(bf16[512,512]{1,0:T(8,128)(2,1)S(1)} %get-tuple-element.28), channel_id=1, source_target_pairs={{0,32},{16,48},{32,0},{48,16},{1,33},{17,49},{33,1},{49,17},{2,34}... | collective-permute-start | bytes 1572872 | tf_op jit(solution)/shard_map/ppermute | solution.py:34
  126.8 23.5 %collective-permute-start.17 = (bf16[512,512]{1,0:T(8,128)(2,1)S(1)}, bf16[512,512]{1,0:T(8,128)(2,1)S(1)}, u32[]{:S(2)}, u32[]{:S(2)}) collective-permute-start(bf16[512,512]{1,0:T(8,128)(2,1)S(1)} %get-tuple-element.27), channel_id=1, source_target_pairs={{0,48},{16,0},{32,16},{48,32},{1,49},{17,1},{33,17},{49,33},{2,50}... | collective-permute-start | bytes 1572872 | tf_op jit(solution)/shard_map/ppermute | solution.py:34
  178.1 19.6 %all-to-all-start.1 = ((bf16[8,16,1280]{2,1,0:T(8,128)(2,1)}), bf16[8,16,1280]{2,1,0:T(8,128)(2,1)S(1)}, u32[]{:S(2)}, u32[]{:S(2)}) async-start(bf16[8,16,1280]{2,1,0:T(8,128)(2,1)} %reshape.34), calls=%async_computation.1 | async-start | bytes 655360 | tf_op jit(solution)/shard_map/all_to_all | solution.py:218
  (1 other events, 1.0 us)

commit v3 on v2

--- a/solution.py
+++ b/solution.py
@@ -166,56 +166,128 @@
     return outs[0], outs[1:]
 
 
+def split_kernel(info, *refs):
+    half = len(refs) // 2
+    for src, dst in zip(refs[:half], refs[half:]):
+        dst[...] = src[...]
+
+
+def split_features(x, my_x, z_hi, nx):
+    rows, dim = x.shape
+    wide = dim // (z_hi * nx)
+
+    def source(s):
+        return pl.BlockSpec((rows, wide), lambda g, info: (0, g * nx + (info[0] + s) % nx))
+
+    return pl.pallas_call(
+        split_kernel,
+        grid_spec=pltpu.PrefetchScalarGridSpec(
+            num_scalar_prefetch=1,
+            grid=(z_hi,),
+            in_specs=[source(s) for s in range(1, nx)],
+            out_specs=[pl.BlockSpec((rows, wide), lambda g, info: (0, g))] * (nx - 1),
+        ),
+        out_shape=[jax.ShapeDtypeStruct((rows, z_hi * wide), x.dtype)] * (nx - 1),
+        compiler_params=pltpu.CompilerParams(vmem_limit_bytes=16 * 2**20),
+        name="split_features",
+    )(my_x[None], *([x] * (nx - 1)))
+
+
+def weight_kernel(nx, z_hi, ny, info, x_ref, *refs):
+    f_refs, g_refs, out_ref, ft_s = refs[: nx - 1], refs[nx - 1 : 2 * nx - 1], refs[-2], refs[-1]
+    rows = x_ref.shape[0]
+    wide = x_ref.shape[1] // (z_hi * nx * 2)
+    my_x, which = info[0], info[1]
+
+    @pl.when(pl.program_id(0) == 0)
+    def _():
+        for s in range(nx):
+            for z in range(z_hi):
+                if s == 0:
+                    at = pl.multiple_of(((z * nx + my_x) * 2 + which) * wide, wide)
+                    block = x_ref[:, pl.ds(at, wide)]
+                else:
+                    at = pl.multiple_of((z * 2 + which) * wide, wide)
+                    block = f_refs[s - 1][:, pl.ds(at, wide)]
+                ft_s[z * wide : (z + 1) * wide, s * rows : (s + 1) * rows] = (
+                    block.astype(F32).T.astype(BF)
+                )
+
+    total = dot(ft_s[:, :rows], g_refs[0][...], NN)
+    for s in range(1, nx):
+        total += dot(ft_s[:, s * rows : (s + 1) * rows], g_refs[s][...], NN)
+    total = total.astype(BF)
+    part = wide // ny
+    for z in range(z_hi):
+        for y in range(ny):
+            at = z * wide + y * part
+            out_ref[y, z] = total[at : at + part]
+
+
+def weight_part(x, features, grads, my_x, which, z_hi, ny):
+    nx = len(grads)
+    rows, dim = x.shape
+    n = grads[0].shape[1]
+    wide = dim // (z_hi * nx * 2)
+    cols = min(n, 256)
+    whole = lambda shape: pl.BlockSpec(shape, lambda g: (0,) * len(shape))
+    return pl.pallas_call(
+        functools.partial(weight_kernel, nx, z_hi, ny),
+        grid=(n // cols,),
+        in_specs=[pl.BlockSpec(memory_space=pltpu.SMEM), whole(x.shape)]
+        + [whole(features[0].shape)] * (nx - 1)
+        + [pl.BlockSpec((rows, cols), lambda g: (0, g))] * nx,
+        out_specs=pl.BlockSpec((ny, z_hi, wide // ny, cols), lambda g: (0, 0, 0, g)),
+        out_shape=jax.ShapeDtypeStruct((ny, z_hi, wide // ny, n), BF),
+        scratch_shapes=[pltpu.VMEM((z_hi * wide, nx * rows), BF)],
+        compiler_params=pltpu.CompilerParams(vmem_limit_bytes=32 * 2**20),
+        cost_estimate=pl.CostEstimate(
+            flops=2 * z_hi * wide * nx * rows * n,
+            bytes_accessed=6 * 2**20,
+            transcendentals=0,
+        ),
+        name="weight_part",
+    )(jnp.stack([my_x, which]), x, *features, *grads)
+
+
 def local(layer_input, queries, key_head, value_head, grad_output, doc_ids):
     x, q, k, v, do, docs = (
         a[0] for a in (layer_input, queries, key_head, value_head, grad_output, doc_ids)
     )
     rows, hd = k.shape
-    dim = x.shape[1]
     ctx = lax.axis_size(CTX)
     nx, nc, z_hi = lax.axis_size("x"), lax.axis_size("core"), lax.axis_size("zh")
+    y, zl = lax.axis_size("y"), lax.axis_size("zl")
     place = lax.axis_index(CTX)
     my_x, my_core = lax.axis_index("x"), lax.axis_index("core")
-    wide = dim // (z_hi * nx * nc)
 
     kv = jnp.concatenate([k, v], axis=1)
     kv_blocks = [kv] + [shifted(kv, CTX, ctx, d, False) for d in range(1, ctx)]
-
-    split = x.reshape(rows, z_hi, nx, nc, wide)
-
-    def owned(core):
-        part = lax.dynamic_index_in_dim(split, core, 3, keepdims=False)
-        return part.transpose(2, 0, 1, 3).reshape(nx, rows, z_hi * wide)
-
-    kept = owned(my_core)
-    given = shifted(owned(1 - my_core), "core", nc, 1, True)
-    both = jnp.stack([kept, given], axis=1).reshape(nx, nc * rows, z_hi * wide)
-    features = []
-    for s in range(nx):
-        mine = lax.dynamic_index_in_dim(both, (my_x + s) % nx, 0, keepdims=False)
-        features.append(shifted(mine, "x", nx, s, True) if s else mine)
+    features = [
+        shifted(part, "x", nx, s + 1, True)
+        for s, part in enumerate(split_features(x, my_x, z_hi, nx))
+    ]
 
     dq, dkv = attention(q, do, kv_blocks, docs, place)
+    dq, *features = lax.optimization_barrier((dq, *features))
+
+    def term(grads):
+        along = [grads] + [shifted(grads, "x", nx, s, True) for s in range(1, nx)]
+        theirs = weight_part(x, features, along, my_x, 1 - my_core, z_hi, y)
+        theirs = shifted(theirs, "core", nc, 1, True)
+        mine = weight_part(x, features, along, my_x, my_core, z_hi, y)
+        return mine.astype(F32) + theirs.astype(F32)
 
     total = dkv[0].astype(F32)
     for d in range(1, ctx):
         total = total + shifted(dkv[d], CTX, ctx, -d, False).astype(F32)
     dkv_own = total.astype(BF)
 
-    grads = jnp.concatenate([dq, dkv_own], axis=1)
-    along = [grads] + [shifted(grads, "x", nx, s, True) for s in range(1, nx)]
-    along = jnp.stack(along)
-    other = shifted(along, "core", nc, 1, True)
-    grads_all = jnp.stack([along, other], axis=1).reshape(nx * nc * rows, -1)
-    part = dot(jnp.concatenate(features, axis=0), grads_all, TN).astype(BF)
-    n = part.shape[1]
-    y, zl = lax.axis_size("y"), lax.axis_size("zl")
-    keep = wide // (y * zl)
-    part = part.reshape(z_hi, y, zl * keep * n).transpose(1, 0, 2)
-    part = lax.all_to_all(part, "y", 0, 0, tiled=True)
+    part = jnp.concatenate([term(dq), term(dkv_own)], axis=-1).astype(BF)
+    n = part.shape[-1]
+    part = lax.all_to_all(part.reshape(y, -1, n), "y", 0, 0, tiled=True)
     part = jnp.sum(part.astype(F32), axis=0).astype(BF)
-    part = part.reshape(z_hi * zl, keep, n)
-    part = lax.all_to_all(part, ("zh", "zl"), 0, 0, tiled=True)
+    part = lax.all_to_all(part.reshape(z_hi * zl, -1, n), ("zh", "zl"), 0, 0, tiled=True)
     tokens = rows * ctx * nx * nc * z_hi
     weight = jnp.sum(part.astype(F32), axis=0) * (1.0 / math.sqrt(tokens))
     width = q.shape[1]

time: 203 us -> 172 us (0.85); the launches traced: 199 us -> 171 us
  waiting for transfers between devices: 79.2 us -> 40.6 us
  Pallas kernels: 8.81 us -> 19.8 us
  starting transfers between devices: 47.2 us -> 56.4 us
  other arithmetic: 11.9 us -> 5.47 us
  local copies, waits for them, and re-layouts: 24.6 us -> 19.6 us
  blocking collectives: 21 us -> 25.8 us
  matrix products: 2.93 us -> 0 us
    ppermute x22 -> x25, waiting for transfers between devices: 70 us -> 30.5 us  [shifted(): return lax.ppermute(value, axes, pairs)]
    pallas_call x0 -> x5, Pallas kernels: none -> 11 us  [the longest x4 10.2 us: weight_part(): pl.pallas_call(functools.partial(weight_kernel, nx, z_hi, ny), grid=(n //...]
    ppermute x22 -> x25, starting transfers between devices: 37.5 us -> 48.3 us  [shifted(): return lax.ppermute(value, axes, pairs)]
    unnamed x5 -> x50, local copies, waits for them, and re-layouts: 6.15 us -> 16.5 us
    another operation x4, other arithmetic: 8.12 us -> 0.64 us  [the longest x2 3.93 us: local(): grads_all = jnp.stack([along, other], axis=1).reshape(nx * nc * rows, -1)]
    transpose x3 -> x0, local copies, waits for them, and re-layouts: 6.14 us -> none  [owned(): return part.transpose(2, 0, 1, 3).reshape(nx, rows, z_hi * wide)]
    all_to_all x1, blocking collectives: 21 us -> 25.8 us  [local(): part = lax.all_to_all(part.reshape(y, -1, n), 'y', 0, 0, tiled=True)]
    another operation x2 -> x0, local copies, waits for them, and re-layouts: 4.48 us -> none  [the longest x1 4.13 us: local(): both = jnp.stack([kept, given], axis=1).reshape(nx, nc * rows, z_hi * wide)]
  transfers between devices with their start and end apart: 23 -> 26, of which waited for: 12 -> 15; matrix products, arithmetic and copies ran while one was open for 13% -> 3% of each run, Pallas kernels for 0% -> 12%
where the time goes in v3:
time: 172 us; the launch traced here: 171 us
  starting transfers between devices  56.4 us (33%)
  waiting for transfers between devices  40.6 us (24%)
  blocking collectives  25.8 us (15%)
  Pallas kernels  19.8 us (12%)
  local copies, waits for them, and re-layouts  19.6 us (11%)
  other arithmetic  5.47 us (3%)
  between operations  3.58 us (2%)
    ppermute x25, starting transfers between devices, shifted(): return lax.ppermute(value, axes, pairs)  48.3 us
    ppermute x25, waiting for transfers between devices, shifted(): return lax.ppermute(value, axes, pairs)  30.5 us
    all_to_all x1, blocking collectives, local(): part = lax.all_to_all(part.reshape(y, -1, n), 'y', 0, 0, tiled=True)  25.8 us
    unnamed x50, local copies, waits for them, and re-layouts  16.5 us
    pallas_call x4, Pallas kernels, weight_part(): pl.pallas_call(functools.partial(weight_kernel, nx, z_hi, ny), grid=(n //...  10.2 us
    all_to_all x1, waiting for transfers between devices, local(): lax.all_to_all(part.reshape(z_hi * zl, -1, n), ('zh', 'zl'), 0, 0, tiled=...  10.1 us
    pallas_call x1, Pallas kernels, attention(): pl.pallas_call(functools.partial(attention_kernel, blocks, per, hd ** (-0...  8.89 us
    all_to_all x1, starting transfers between devices, local(): lax.all_to_all(part.reshape(z_hi * zl, -1, n), ('zh', 'zl'), 0, 0, tiled=...  8.1 us
  transfers between devices with their start and end apart: 26, of which 15 were waited for; matrix products, arithmetic and copies ran while one was open for 3% of the time, Pallas kernels for 12%

profile of v3, /device:TPU:32, one launch (start us, length us, event | category | flops | bytes accessed | tf_op | source)
XLA Modules:
  0.0 171.3 jit_solution(14556460745012419895)
XLA Ops:
  2.2 5.5 %collective-permute-start.5 = (bf16[256,256]{1,0:T(8,128)(2,1)S(1)}, bf16[256,256]{1,0:T(8,128)(2,1)S(1)}, u32[]{:S(2)}, u32[]{:S(2)}) collective-permute-start(bf16[256,256]{1,0:T(8,128)(2,1)S(1)} %pad_maximum_fusion.1.refs_0_), channel_id=1, source_target_pairs={{0,6},{1,7},{8,14},{9,15},{16,22},{17,23},{24,30},{25,31},{32,38},... | collective-permute-start | bytes 393224 | tf_op jit(solution)/shard_map/ppermute | solution.py:34
  13.4 3.4 %collective-permute-start.1 = (bf16[256,256]{1,0:T(8,128)(2,1)S(1)}, bf16[256,256]{1,0:T(8,128)(2,1)S(1)}, u32[]{:S(2)}, u32[]{:S(2)}) collective-permute-start(bf16[256,256]{1,0:T(8,128)(2,1)S(1)} %pad_maximum_fusion.1.refs_0_), channel_id=1, source_target_pairs={{0,2},{1,3},{2,4},{3,5},{4,6},{5,7},{8,10},{9,11},{10,12},{11,13},... | collective-permute-start | bytes 393224 | tf_op jit(solution)/shard_map/ppermute | solution.py:34
  16.8 1.7 collective-permute-done.5.refs_6_
  18.5 1.9 %collective-permute-start = (bf16[256,256]{1,0:T(8,128)(2,1)S(1)}, bf16[256,256]{1,0:T(8,128)(2,1)S(1)}, u32[]{:S(2)}, u32[]{:S(2)}) collective-permute-start(bf16[256,256]{1,0:T(8,128)(2,1)S(1)} %pad_maximum_fusion.1.refs_0_), channel_id=1, source_target_pairs={{0,1},{1,2},{2,3},{3,4},{4,5},{5,6},{6,7},{8,9},{9,10},{10,11},{11... | collective-permute-start | bytes 393224 | tf_op jit(solution)/shard_map/ppermute | solution.py:34
  23.6 1.6 copy-done
  26.7 1.5 collective-permute-start.7
  28.8 2.7 %collective-permute-start.8 = (bf16[256,1024]{1,0:T(8,128)(2,1)S(1)}, bf16[256,1024]{1,0:T(8,128)(2,1)S(1)}, u32[]{:S(2)}, u32[]{:S(2)}) collective-permute-start(bf16[256,1024]{1,0:T(8,128)(2,1)S(1)} %get-tuple-element.24), channel_id=1, source_target_pairs={{0,32},{16,48},{32,0},{48,16},{1,33},{17,49},{33,1},{49,17},{2,34}... | collective-permute-start | bytes 1572872 | tf_op jit(solution)/shard_map/ppermute | solution.py:34
  41.1 8.9 %attention_backward.1 = (bf16[256,1024]{1,0:T(8,128)(2,1)}, bf16[256,256]{1,0:T(8,128)(2,1)S(1)}, bf16[256,256]{1,0:T(8,128)(2,1)}, bf16[256,256]{1,0:T(8,128)(2...) custom-call(s32[3]{0:T(128)S(1)} %pad_add_fusion.info, ...), custom_call_target="tpu_custom_call" | custom-call | flops 5368709120 | bytes 8388608 | tf_op jit(solution)/shard_map/attention_backward/pallas_call | solution.py:140
  55.1 2.6 %collective-permute-start.19 = (bf16[256,1024]{1,0:T(8,128)(2,1)}, bf16[256,1024]{1,0:T(8,128)(2,1)}, u32[]{:S(2)}, u32[]{:S(2)}) collective-permute-start(bf16[256,1024]{1,0:T(8,128)(2,1)} %get-tuple-element.26.refs_3_), channel_id=1, source_target_pairs={{0,48},{16,0},{32,16},{48,32},{1,49},{17,1},{33,17},{49,33},{2,50}... | collective-permute-start | bytes 1572872 | tf_op jit(solution)/shard_map/ppermute | solution.py:34
  57.7 1.8 %collective-permute-start.18 = (bf16[256,1024]{1,0:T(8,128)(2,1)}, bf16[256,1024]{1,0:T(8,128)(2,1)}, u32[]{:S(2)}, u32[]{:S(2)}) collective-permute-start(bf16[256,1024]{1,0:T(8,128)(2,1)} %get-tuple-element.26.refs_3_), channel_id=1, source_target_pairs={{0,32},{16,48},{32,0},{48,16},{1,33},{17,49},{33,1},{49,17},{2,34}... | collective-permute-start | bytes 1572872 | tf_op jit(solution)/shard_map/ppermute | solution.py:34
  59.5 3.6 %collective-permute-start.10 = (bf16[256,256]{1,0:T(8,128)(2,1)}, bf16[256,256]{1,0:T(8,128)(2,1)S(1)}, u32[]{:S(2)}, u32[]{:S(2)}) collective-permute-start(bf16[256,256]{1,0:T(8,128)(2,1)} %get-tuple-element.28), channel_id=1, source_target_pairs={{1,0},{2,1},{3,2},{4,3},{5,4},{6,5},{7,6},{9,8},{10,9},{11,10},{12... | collective-permute-start | bytes 393224 | tf_op jit(solution)/shard_map/ppermute | solution.py:34
  64.5 3.1 %collective-permute-done.10 = bf16[256,256]{1,0:T(8,128)(2,1)S(1)} collective-permute-done((bf16[256,256]{1,0:T(8,128)(2,1)}, bf16[256,256]{1,0:T(8,128)(2,1)S(1)}, u32[]{:S(2)}, u32[]{:S(2)}) %collective-permute-start.10) | collective-permute-done | bytes 131104 | tf_op jit(solution)/shard_map/ppermute | solution.py:34
  71.6 9.1 %collective-permute-done.19.refs_6_ = bf16[256,1024]{1,0:T(8,128)(2,1)} collective-permute-done((bf16[256,1024]{1,0:T(8,128)(2,1)}, bf16[256,1024]{1,0:T(8,128)(2,1)}, u32[]{:S(2)}, u32[]{:S(2)}) %collective-permute-start.19) | collective-permute-done | bytes 524320 | tf_op jit(solution)/shard_map/ppermute | solution.py:34
  87.1 4.0 %weight_part.5 = bf16[4,4,32,1024]{3,2,1,0:T(8,128)(2,1)S(1)} custom-call(s32[2]{0:T(128)S(1)} %pad_add_fusion.2.info, bf16[256,4096]{1,0:T(8,128)(2,1)S(1)} %bitcast.25, bf16[256,1024]{1,0:T(8,128)(2,1)S(1)} %collective-permute-done.7.refs_0_, bf16[256,1024]{1,0:T(8,128)(2,1)S(1)} %collective-permute-done.8.refs_1_, bf16[256,1024]{1,0:T(8,128)(2,1)S(1)} %copy-done.3, ...), custom_call_target="tpu_custom_call" | custom-call | flops 1073741824 | bytes 6291456 | tf_op jit(solution)/shard_map/weight_part/pallas_call | solution.py:234
  91.2 1.7 %collective-permute-done.13 = bf16[256,256]{1,0:T(8,128)(2,1)S(1)} collective-permute-done((bf16[256,256]{1,0:T(8,128)(2,1)}, bf16[256,256]{1,0:T(8,128)(2,1)S(1)}, u32[]{:S(2)}, u32[]{:S(2)}) %collective-permute-start.13) | collective-permute-done | bytes 131104 | tf_op jit(solution)/shard_map/ppermute | solution.py:34
  92.9 1.7 collective-permute-done.14
  94.5 2.9 %collective-permute-done.15 = bf16[256,256]{1,0:T(8,128)(2,1)S(1)} collective-permute-done((bf16[256,256]{1,0:T(8,128)(2,1)}, bf16[256,256]{1,0:T(8,128)(2,1)S(1)}, u32[]{:S(2)}, u32[]{:S(2)}) %collective-permute-start.15) | collective-permute-done | bytes 131104 | tf_op jit(solution)/shard_map/ppermute | solution.py:34
  98.6 10.6 %collective-permute-start.23 = (bf16[256,256]{1,0:T(8,128)(2,1)S(1)}, bf16[256,256]{1,0:T(8,128)(2,1)S(1)}, u32[]{:S(2)}, u32[]{:S(2)}) collective-permute-start(bf16[256,256]{1,0:T(8,128)(2,1)S(1)} %add_convert_fusion.2.refs_3_), channel_id=1, source_target_pairs={{0,48},{16,0},{32,16},{48,32},{1,49},{17,1},{33,17},{49,33},{2,50}... | collective-permute-start | bytes 393224 | tf_op jit(solution)/shard_map/ppermute | solution.py:34
  110.4 2.6 %collective-permute-done.23.refs_6_ = bf16[256,256]{1,0:T(8,128)(2,1)S(1)} collective-permute-done((bf16[256,256]{1,0:T(8,128)(2,1)S(1)}, bf16[256,256]{1,0:T(8,128)(2,1)S(1)}, u32[]{:S(2)}, u32[]{:S(2)}) %collective-permute-start.23) | collective-permute-done | bytes 131104 | tf_op jit(solution)/shard_map/ppermute | solution.py:34
  113.1 2.6 %collective-permute-done.22.refs_5_ = bf16[256,256]{1,0:T(8,128)(2,1)S(1)} collective-permute-done((bf16[256,256]{1,0:T(8,128)(2,1)S(1)}, bf16[256,256]{1,0:T(8,128)(2,1)S(1)}, u32[]{:S(2)}, u32[]{:S(2)}) %collective-permute-start.22) | collective-permute-done | bytes 131104 | tf_op jit(solution)/shard_map/ppermute | solution.py:34
  119.9 4.0 %weight_part.4 = bf16[4,4,32,1024]{3,2,1,0:T(8,128)(2,1)S(1)} custom-call(s32[2]{0:T(128)S(1)} %pad_add_fusion.1.info, bf16[256,4096]{1,0:T(8,128)(2,1)S(1)} %bitcast.28, bf16[256,1024]{1,0:T(8,128)(2,1)S(1)} %collective-permute-done.7.refs_0_, bf16[256,1024]{1,0:T(8,128)(2,1)S(1)} %collective-permute-done.8.refs_1_, bf16[256,1024]{1,0:T(8,128)(2,1)S(1)} %copy-done.3, ...), custom_call_target="tpu_custom_call" | custom-call | flops 1073741824 | bytes 6291456 | tf_op jit(solution)/shard_map/weight_part/pallas_call | solution.py:234
  124.4 25.8 %all_to_all.10 = bf16[4,128,1280]{2,1,0:T(8,128)(2,1)S(1)} all-to-all(bf16[4,128,1280]{2,1,0:T(8,128)(2,1)S(1)} %pad_maximum_fusion), channel_id=1, replica_groups=mesh['zh'=4,'x'=4,'core'=2,'y'=4,'zl'=2] {'y'}, dimensions={0} | all-to-all | bytes 2621440 | tf_op jit(solution)/shard_map/all_to_all | solution.py:288
  151.1 8.1 %all-to-all-start.1 = ((bf16[8,16,1280]{2,1,0:T(8,128)(2,1)}), bf16[8,16,1280]{2,1,0:T(8,128)(2,1)S(1)}, u32[]{:S(2)}, u32[]{:S(2)}) async-start(bf16[8,16,1280]{2,1,0:T(8,128)(2,1)} %bitcast.19), calls=%async_computation.1 | async-start | bytes 655360 | tf_op jit(solution)/shard_map/all_to_all | solution.py:290
  159.9 10.1 %all-to-all-done.1 = bf16[8,16,1280]{2,1,0:T(8,128)(2,1)S(1)} async-done(((bf16[8,16,1280]{2,1,0:T(8,128)(2,1)}), bf16[8,16,1280]{2,1,0:T(8,128)(2,1)S(1)}, u32[]{:S(2)}, u32[]{:S(2)}) %all-to-all-start.1) | async-done | bytes 327712 | tf_op jit(solution)/shard_map/all_to_all | solution.py:290
  (102 shorter events, 46.3 us)
Async XLA Ops:
  1.5 11.9 %collective-permute-start.6 = (bf16[256,256]{1,0:T(8,128)(2,1)S(1)}, bf16[256,256]{1,0:T(8,128)(2,1)S(1)}, u32[]{:S(2)}, u32[]{:S(2)}) collective-permute-start(bf16[256,256]{1,0:T(8,128)(2,1)S(1)} %pad_maximum_fusion.1.refs_0_), channel_id=1, source_target_pairs={{0,7},{8,15},{16,23},{24,31},{32,39},{40,47},{48,55},{56,63},{64,7... | collective-permute-start | bytes 393224 | tf_op jit(solution)/shard_map/ppermute | solution.py:34
  2.2 16.3 %collective-permute-start.5 = (bf16[256,256]{1,0:T(8,128)(2,1)S(1)}, bf16[256,256]{1,0:T(8,128)(2,1)S(1)}, u32[]{:S(2)}, u32[]{:S(2)}) collective-permute-start(bf16[256,256]{1,0:T(8,128)(2,1)S(1)} %pad_maximum_fusion.1.refs_0_), channel_id=1, source_target_pairs={{0,6},{1,7},{8,14},{9,15},{16,22},{17,23},{24,30},{25,31},{32,38},... | collective-permute-start | bytes 393224 | tf_op jit(solution)/shard_map/ppermute | solution.py:34
  7.8 18.3 %collective-permute-start.4 = (bf16[256,256]{1,0:T(8,128)(2,1)S(1)}, bf16[256,256]{1,0:T(8,128)(2,1)S(1)}, u32[]{:S(2)}, u32[]{:S(2)}) collective-permute-start(bf16[256,256]{1,0:T(8,128)(2,1)S(1)} %pad_maximum_fusion.1.refs_0_), channel_id=1, source_target_pairs={{0,5},{1,6},{2,7},{8,13},{9,14},{10,15},{16,21},{17,22},{18,23},{2... | collective-permute-start | bytes 393224 | tf_op jit(solution)/shard_map/ppermute | solution.py:34
  9.1 19.1 %collective-permute-start.3 = (bf16[256,256]{1,0:T(8,128)(2,1)S(1)}, bf16[256,256]{1,0:T(8,128)(2,1)S(1)}, u32[]{:S(2)}, u32[]{:S(2)}) collective-permute-start(bf16[256,256]{1,0:T(8,128)(2,1)S(1)} %pad_maximum_fusion.1.refs_0_), channel_id=1, source_target_pairs={{0,4},{1,5},{2,6},{3,7},{8,12},{9,13},{10,14},{11,15},{16,20},{17,... | collective-permute-start | bytes 393224 | tf_op jit(solution)/shard_map/ppermute | solution.py:34
  10.4 21.2 %collective-permute-start.2 = (bf16[256,256]{1,0:T(8,128)(2,1)S(1)}, bf16[256,256]{1,0:T(8,128)(2,1)S(1)}, u32[]{:S(2)}, u32[]{:S(2)}) collective-permute-start(bf16[256,256]{1,0:T(8,128)(2,1)S(1)} %pad_maximum_fusion.1.refs_0_), channel_id=1, source_target_pairs={{0,3},{1,4},{2,5},{3,6},{4,7},{8,11},{9,12},{10,13},{11,14},{12,15... | collective-permute-start | bytes 393224 | tf_op jit(solution)/shard_map/ppermute | solution.py:34
  13.4 21.0 %collective-permute-start.1 = (bf16[256,256]{1,0:T(8,128)(2,1)S(1)}, bf16[256,256]{1,0:T(8,128)(2,1)S(1)}, u32[]{:S(2)}, u32[]{:S(2)}) collective-permute-start(bf16[256,256]{1,0:T(8,128)(2,1)S(1)} %pad_maximum_fusion.1.refs_0_), channel_id=1, source_target_pairs={{0,2},{1,3},{2,4},{3,5},{4,6},{5,7},{8,10},{9,11},{10,12},{11,13},... | collective-permute-start | bytes 393224 | tf_op jit(solution)/shard_map/ppermute | solution.py:34
  18.5 16.5 %collective-permute-start = (bf16[256,256]{1,0:T(8,128)(2,1)S(1)}, bf16[256,256]{1,0:T(8,128)(2,1)S(1)}, u32[]{:S(2)}, u32[]{:S(2)}) collective-permute-start(bf16[256,256]{1,0:T(8,128)(2,1)S(1)} %pad_maximum_fusion.1.refs_0_), channel_id=1, source_target_pairs={{0,1},{1,2},{2,3},{3,4},{4,5},{5,6},{6,7},{8,9},{9,10},{10,11},{11... | collective-permute-start | bytes 393224 | tf_op jit(solution)/shard_map/ppermute | solution.py:34
  26.7 26.6 %collective-permute-start.7 = (bf16[256,1024]{1,0:T(8,128)(2,1)S(1)}, bf16[256,1024]{1,0:T(8,128)(2,1)S(1)}, u32[]{:S(2)}, u32[]{:S(2)}) collective-permute-start(bf16[256,1024]{1,0:T(8,128)(2,1)S(1)} %get-tuple-element.23), channel_id=1, source_target_pairs={{0,16},{16,32},{32,48},{48,0},{1,17},{17,33},{33,49},{49,1},{2,18}... | collective-permute-start | bytes 1572872 | tf_op jit(solution)/shard_map/ppermute | solution.py:34
  28.8 25.1 %collective-permute-start.8 = (bf16[256,1024]{1,0:T(8,128)(2,1)S(1)}, bf16[256,1024]{1,0:T(8,128)(2,1)S(1)}, u32[]{:S(2)}, u32[]{:S(2)}) collective-permute-start(bf16[256,1024]{1,0:T(8,128)(2,1)S(1)} %get-tuple-element.24), channel_id=1, source_target_pairs={{0,32},{16,48},{32,0},{48,16},{1,33},{17,49},{33,1},{49,17},{2,34}... | collective-permute-start | bytes 1572872 | tf_op jit(solution)/shard_map/ppermute | solution.py:34
  32.2 22.0 %collective-permute-start.9 = (bf16[256,1024]{1,0:T(8,128)(2,1)S(1)}, bf16[256,1024]{1,0:T(8,128)(2,1)S(1)}, u32[]{:S(2)}, u32[]{:S(2)}) collective-permute-start(bf16[256,1024]{1,0:T(8,128)(2,1)S(1)} %get-tuple-element.25), channel_id=1, source_target_pairs={{0,48},{16,0},{32,16},{48,32},{1,49},{17,1},{33,17},{49,33},{2,50}... | collective-permute-start | bytes 1572872 | tf_op jit(solution)/shard_map/ppermute | solution.py:34
  55.1 25.6 %collective-permute-start.19 = (bf16[256,1024]{1,0:T(8,128)(2,1)}, bf16[256,1024]{1,0:T(8,128)(2,1)}, u32[]{:S(2)}, u32[]{:S(2)}) collective-permute-start(bf16[256,1024]{1,0:T(8,128)(2,1)} %get-tuple-element.26.refs_3_), channel_id=1, source_target_pairs={{0,48},{16,0},{32,16},{48,32},{1,49},{17,1},{33,17},{49,33},{2,50}... | collective-permute-start | bytes 1572872 | tf_op jit(solution)/shard_map/ppermute | solution.py:34
  57.7 24.2 %collective-permute-start.18 = (bf16[256,1024]{1,0:T(8,128)(2,1)}, bf16[256,1024]{1,0:T(8,128)(2,1)}, u32[]{:S(2)}, u32[]{:S(2)}) collective-permute-start(bf16[256,1024]{1,0:T(8,128)(2,1)} %get-tuple-element.26.refs_3_), channel_id=1, source_target_pairs={{0,32},{16,48},{32,0},{48,16},{1,33},{17,49},{33,1},{49,17},{2,34}... | collective-permute-start | bytes 1572872 | tf_op jit(solution)/shard_map/ppermute | solution.py:34
  59.5 24.8 %collective-permute-start.17 = (bf16[256,1024]{1,0:T(8,128)(2,1)}, bf16[256,1024]{1,0:T(8,128)(2,1)}, u32[]{:S(2)}, u32[]{:S(2)}) collective-permute-start(bf16[256,1024]{1,0:T(8,128)(2,1)} %get-tuple-element.26.refs_3_), channel_id=1, source_target_pairs={{0,16},{16,32},{32,48},{48,0},{1,17},{17,33},{33,49},{49,1},{2,18}... | collective-permute-start | bytes 1572872 | tf_op jit(solution)/shard_map/ppermute | solution.py:34
  59.5 8.0 %collective-permute-start.10 = (bf16[256,256]{1,0:T(8,128)(2,1)}, bf16[256,256]{1,0:T(8,128)(2,1)S(1)}, u32[]{:S(2)}, u32[]{:S(2)}) collective-permute-start(bf16[256,256]{1,0:T(8,128)(2,1)} %get-tuple-element.28), channel_id=1, source_target_pairs={{1,0},{2,1},{3,2},{4,3},{5,4},{6,5},{7,6},{9,8},{10,9},{11,10},{12... | collective-permute-start | bytes 393224 | tf_op jit(solution)/shard_map/ppermute | solution.py:34
  63.2 7.1 %collective-permute-start.11 = (bf16[256,256]{1,0:T(8,128)(2,1)}, bf16[256,256]{1,0:T(8,128)(2,1)S(1)}, u32[]{:S(2)}, u32[]{:S(2)}) collective-permute-start(bf16[256,256]{1,0:T(8,128)(2,1)} %get-tuple-element.29), channel_id=1, source_target_pairs={{2,0},{3,1},{4,2},{5,3},{6,4},{7,5},{10,8},{11,9},{12,10},{13,11},... | collective-permute-start | bytes 393224 | tf_op jit(solution)/shard_map/ppermute | solution.py:34
  67.5 23.5 %collective-permute-start.12 = (bf16[256,256]{1,0:T(8,128)(2,1)}, bf16[256,256]{1,0:T(8,128)(2,1)S(1)}, u32[]{:S(2)}, u32[]{:S(2)}) collective-permute-start(bf16[256,256]{1,0:T(8,128)(2,1)} %copy-done.23), channel_id=1, source_target_pairs={{3,0},{4,1},{5,2},{6,3},{7,4},{11,8},{12,9},{13,10},{14,11},{15,12... | collective-permute-start | bytes 393224 | tf_op jit(solution)/shard_map/ppermute | solution.py:34
  70.3 22.6 %collective-permute-start.13 = (bf16[256,256]{1,0:T(8,128)(2,1)}, bf16[256,256]{1,0:T(8,128)(2,1)S(1)}, u32[]{:S(2)}, u32[]{:S(2)}) collective-permute-start(bf16[256,256]{1,0:T(8,128)(2,1)} %copy-done.20), channel_id=1, source_target_pairs={{4,0},{5,1},{6,2},{7,3},{12,8},{13,9},{14,10},{15,11},{20,16},{21,... | collective-permute-start | bytes 393224 | tf_op jit(solution)/shard_map/ppermute | solution.py:34
  80.7 13.9 %collective-permute-start.14 = (bf16[256,256]{1,0:T(8,128)(2,1)}, bf16[256,256]{1,0:T(8,128)(2,1)S(1)}, u32[]{:S(2)}, u32[]{:S(2)}) collective-permute-start(bf16[256,256]{1,0:T(8,128)(2,1)} %copy-done.17), channel_id=1, source_target_pairs={{5,0},{6,1},{7,2},{13,8},{14,9},{15,10},{21,16},{22,17},{23,18},{2... | collective-permute-start | bytes 393224 | tf_op jit(solution)/shard_map/ppermute | solution.py:34
  81.9 15.5 %collective-permute-start.15 = (bf16[256,256]{1,0:T(8,128)(2,1)}, bf16[256,256]{1,0:T(8,128)(2,1)S(1)}, u32[]{:S(2)}, u32[]{:S(2)}) collective-permute-start(bf16[256,256]{1,0:T(8,128)(2,1)} %copy-done.16), channel_id=1, source_target_pairs={{6,0},{7,1},{14,8},{15,9},{22,16},{23,17},{30,24},{31,25},{38,32},... | collective-permute-start | bytes 393224 | tf_op jit(solution)/shard_map/ppermute | solution.py:34
  84.3 13.2 %collective-permute-start.16 = (bf16[256,256]{1,0:T(8,128)(2,1)}, bf16[256,256]{1,0:T(8,128)(2,1)S(1)}, u32[]{:S(2)}, u32[]{:S(2)}) collective-permute-start(bf16[256,256]{1,0:T(8,128)(2,1)} %copy-done.15), channel_id=1, source_target_pairs={{7,0},{15,8},{23,16},{31,24},{39,32},{47,40},{55,48},{63,56},{71,6... | collective-permute-start | bytes 393224 | tf_op jit(solution)/shard_map/ppermute | solution.py:34
  91.1 32.8 %collective-permute-start.20 = (bf16[4,4,32,1024]{3,2,1,0:T(8,128)(2,1)S(1)}, bf16[4,4,32,1024]{3,2,1,0:T(8,128)(2,1)S(1)}, u32[]{:S(2)}, u32[]{:S(2)}) collective-permute-start(bf16[4,4,32,1024]{3,2,1,0:T(8,128)(2,1)S(1)} %weight_part.5), channel_id=1, source_target_pairs={{0,8},{8,0},{1,9},{9,1},{2,10},{10,2},{3,11},{11,3},{4,12},{12,4},... | collective-permute-start | bytes 3145736 | tf_op jit(solution)/shard_map/ppermute | solution.py:34
  98.6 14.5 %collective-permute-start.23 = (bf16[256,256]{1,0:T(8,128)(2,1)S(1)}, bf16[256,256]{1,0:T(8,128)(2,1)S(1)}, u32[]{:S(2)}, u32[]{:S(2)}) collective-permute-start(bf16[256,256]{1,0:T(8,128)(2,1)S(1)} %add_convert_fusion.2.refs_3_), channel_id=1, source_target_pairs={{0,48},{16,0},{32,16},{48,32},{1,49},{17,1},{33,17},{49,33},{2,50}... | collective-permute-start | bytes 393224 | tf_op jit(solution)/shard_map/ppermute | solution.py:34
  110.4 6.6 %collective-permute-start.21 = (bf16[256,256]{1,0:T(8,128)(2,1)S(1)}, bf16[256,256]{1,0:T(8,128)(2,1)S(1)}, u32[]{:S(2)}, u32[]{:S(2)}) collective-permute-start(bf16[256,256]{1,0:T(8,128)(2,1)S(1)} %add_convert_fusion.2.refs_3_), channel_id=1, source_target_pairs={{0,16},{16,32},{32,48},{48,0},{1,17},{17,33},{33,49},{49,1},{2,18}... | collective-permute-start | bytes 393224 | tf_op jit(solution)/shard_map/ppermute | solution.py:34
  151.1 18.9 %all-to-all-start.1 = ((bf16[8,16,1280]{2,1,0:T(8,128)(2,1)}), bf16[8,16,1280]{2,1,0:T(8,128)(2,1)S(1)}, u32[]{:S(2)}, u32[]{:S(2)}) async-start(bf16[8,16,1280]{2,1,0:T(8,128)(2,1)} %bitcast.19), calls=%async_computation.1 | async-start | bytes 655360 | tf_op jit(solution)/shard_map/all_to_all | solution.py:290
  (27 other events, 117.7 us)

commit v4 on v3

v4 whole, which is shorter than its diff:
```python
import functools
import math

import jax
import jax.numpy as jnp
from jax import lax
from jax.experimental import pallas as pl
from jax.experimental.pallas import tpu as pltpu
from jax.sharding import Mesh, PartitionSpec as P

NEG = -1e30
AXES = ("zh", "x", "core", "y", "zl")
SIZES = (4, 4, 2, 4, 2)
CTX = ("y", "zl")
HALVES = 2
BF = jnp.bfloat16
F32 = jnp.float32
NN = (((1,), (0,)), ((), ()))


def dot(a, b):
    return lax.dot_general(a, b, NN, preferred_element_type=F32)


def shifted(value, axis, count, step, wrap=True):
    pairs = []
    for src in range(count):
        dst = src + step
        if wrap:
            pairs.append((src, dst % count))
        elif 0 <= dst < count:
            pairs.append((src, dst))
    return lax.ppermute(value, axis, pairs)


def whole(shape):
    return pl.BlockSpec(shape, lambda *g: (0,) * len(shape))


def attention_kernel(ny, per, scale, last, info, starts_ref, q_ref, do_ref, *refs):
    kv_refs, refs = refs[:ny], refs[ny:]
    if last:
        old_refs, refs = refs[:ny], refs[ny:]
    dq_ref, refs = refs[0], refs[1:]
    out_refs, refs = refs[:ny], refs[ny:]
    kv_s, kt_s, acc_s, e_s, dp_s, md_s, stat_s, dqt_s, qt_s, dot_s, p_s, ds_s, qk_s, dk_s, sem = refs
    rows = q_ref.shape[0]
    hd = kt_s.shape[1]
    used, place, limit = info[0], info[1], info[2]
    power = scale * math.log2(math.e)
    farthest = place // 2 - (place - used + 1) // 2

    for s in range(ny):

        @pl.when(s <= farthest)
        def _():
            pltpu.make_async_copy(kv_refs[s], kv_s.at[pl.ds(2 * s, 2)], sem.at[s]).start()

    for s in range(ny):
        for k in range(2):
            if last:
                acc_s[2 * s + k] = old_refs[s][k].astype(F32)
            else:
                acc_s[2 * s + k] = jnp.zeros(acc_s.shape[1:], F32)
    for h in range(per):
        cols = slice(h * hd, (h + 1) * hd)
        span = slice(h * rows, (h + 1) * rows)
        qk_s[span] = q_ref[:, cols]
        dk_s[span] = do_ref[:, cols]
        qt_s[h] = q_ref[:, cols].T
        dot_s[h] = do_ref[:, cols].T
        stat_s[0, h] = jnp.full((1, rows), NEG, F32)
        stat_s[1, h] = jnp.zeros((1, rows), F32)
        stat_s[2, h] = jnp.zeros((1, rows), F32)
    dqt_s[...] = jnp.zeros_like(dqt_s)

    for s in range(ny):

        @pl.when(s <= farthest)
        def _():
            pltpu.make_async_copy(kv_refs[s], kv_s.at[pl.ds(2 * s, 2)], sem.at[s]).wait()
            for k in range(2):
                kt_s[2 * s + k] = kv_s[2 * s + k, :, :hd].T

    def slot(d):
        block = place - d
        return 2 * (place // 2 - block // 2) + (d % 2)

    def forward(d, masked):
        at = slot(d)
        kd = kv_s[at, :, :hd]
        vd = kv_s[at, :, hd:]
        if masked:
            kp = lax.broadcasted_iota(jnp.int32, (rows, rows), 0) + (place - d) * rows
            qp = lax.broadcasted_iota(jnp.int32, (rows, rows), 1) + place * rows
            ok = (kp >= starts_ref[...]) & (kp <= qp)
        for h in range(per):
            s = dot(kd, qt_s[h])
            if masked:
                s = jnp.where(ok, s, NEG)
            old = stat_s[0, h]
            top = jnp.maximum(old, jnp.max(s, axis=0, keepdims=True))
            e = jnp.exp2(s * power - top * power)
            alpha = jnp.exp2((old - top) * power)
            dp = dot(vd, dot_s[h])
            stat_s[0, h] = top
            stat_s[1, h] = stat_s[1, h] * alpha + jnp.sum(e, axis=0, keepdims=True)
            stat_s[2, h] = stat_s[2, h] * alpha + jnp.sum(e * dp, axis=0, keepdims=True)
            e_s[d, h] = e
            dp_s[d, h] = dp
            md_s[d, h] = top

    def first(d, carry):
        masked = (d == 0) | ((place - d) * rows < limit)
        pl.when(masked)(lambda: forward(d, True))
        pl.when(jnp.logical_not(masked))(lambda: forward(d, False))
        return carry

    lax.fori_loop(0, used, first, 0)

    tops = [stat_s[0, h] for h in range(per)]
    inverse = [1.0 / stat_s[1, h] for h in range(per)]
    delta = [stat_s[2, h] * inverse[h] for h in range(per)]

    def second(d, carry):
        at = slot(d)
        for h in range(per):
            p = e_s[d, h] * (jnp.exp2((md_s[d, h] - tops[h]) * power) * inverse[h])
            p_s[:, h * rows : (h + 1) * rows] = p.astype(BF)
            ds_s[:, h * rows : (h + 1) * rows] = (p * (dp_s[d, h] - delta[h])).astype(BF)
        acc_s[at, :, hd:] += dot(p_s[...], dk_s[...])
        acc_s[at, :, :hd] += dot(ds_s[...], qk_s[...])
        dqt_s[...] += dot(kt_s[at], ds_s[...])
        return carry

    lax.fori_loop(0, used, second, 0)

    for h in range(per):
        dq_ref[:, h * hd : (h + 1) * hd] = (dqt_s[:, h * rows : (h + 1) * rows].T * scale).astype(BF)
    for s in range(ny):
        for k in range(2):
            at = 2 * s + k
            dk = acc_s[at, :, :hd]
            out_refs[s][k, :, :hd] = (dk * scale if last else dk).astype(BF)
            out_refs[s][k, :, hd:] = acc_s[at, :, hd:].astype(BF)


def attention_half(q, do, kv, info, starts, half, old):
    rows = q.shape[0]
    hd = kv[0].shape[2] // 2
    width = q.shape[1] // HALVES
    per = width // hd
    ny = len(kv)
    blocks = 2 * ny
    last = old is not None
    slab = pl.BlockSpec((rows, width), lambda g: (0, half))
    pair = kv[0].shape
    outs = pl.pallas_call(
        functools.partial(attention_kernel, ny, per, hd ** (-0.5), last),
        grid=(1,),
        in_specs=[pl.BlockSpec(memory_space=pltpu.SMEM), whole((1, rows)), slab, slab]
        + [pl.BlockSpec(memory_space=pl.ANY)] * ny
        + ([whole(pair)] * ny if last else []),
        out_specs=[whole((rows, width))] + [whole(pair)] * ny,
        out_shape=[jax.ShapeDtypeStruct((rows, width), BF)] + [jax.ShapeDtypeStruct(pair, BF)] * ny,
        scratch_shapes=[
            pltpu.VMEM((blocks, rows, 2 * hd), BF),
            pltpu.VMEM((blocks, hd, rows), BF),
            pltpu.VMEM((blocks, rows, 2 * hd), F32),
            pltpu.VMEM((blocks, per, rows, rows), F32),
            pltpu.VMEM((blocks, per, rows, rows), F32),
            pltpu.VMEM((blocks, per, 1, rows), F32),
            pltpu.VMEM((3, per, 1, rows), F32),
            pltpu.VMEM((hd, per * rows), F32),
            pltpu.VMEM((per, hd, rows), BF),
            pltpu.VMEM((per, hd, rows), BF),
            pltpu.VMEM((rows, per * rows), BF),
            pltpu.VMEM((rows, per * rows), BF),
            pltpu.VMEM((per * rows, hd), BF),
            pltpu.VMEM((per * rows, hd), BF),
            pltpu.SemaphoreType.DMA((ny,)),
        ],
        compiler_params=pltpu.CompilerParams(vmem_limit_bytes=28 * 2**20),
        cost_estimate=pl.CostEstimate(
            flops=10 * per * rows * rows * blocks * hd * 2,
            bytes_accessed=4 * 2**20,
            transcendentals=per * rows * rows * blocks,
        ),
        name="attention_backward",
    )(info, starts, q, do, *kv, *(old or []))
    return outs[0], outs[1:]


def split_kernel(info, *refs):
    half = len(refs) // 2
    for src, dst in zip(refs[:half], refs[half:]):
        dst[...] = src[...].T


def split_features(x, my_x, z_hi, nx):
    rows, dim = x.shape
    wide = dim // (z_hi * nx)

    def source(s):
        return pl.BlockSpec((rows, wide), lambda g, info: (0, g * nx + (info[0] + s) % nx))

    return pl.pallas_call(
        split_kernel,
        grid_spec=pltpu.PrefetchScalarGridSpec(
            num_scalar_prefetch=1,
            grid=(z_hi,),
            in_specs=[source(s) for s in range(nx)],
            out_specs=[pl.BlockSpec((wide, rows), lambda g, info: (g, 0))] * nx,
        ),
        out_shape=[jax.ShapeDtypeStruct((z_hi * wide, rows), x.dtype)] * nx,
        compiler_params=pltpu.CompilerParams(vmem_limit_bytes=16 * 2**20),
        name="split_features",
    )(my_x[None], *([x] * nx))


def weight_kernel(nx, parts, z_hi, ny, info, *refs):
    f_refs, g_refs, (out_ref, ft_s, total_s) = refs[:nx], refs[nx:-3], refs[-3:]
    rows = f_refs[0].shape[1]
    wide = f_refs[0].shape[0] // (z_hi * 2)
    which, my_y = info[0], info[1]
    step = pl.program_id(0)
    each = pl.num_programs(0) // parts

    @pl.when(step == 0)
    def _():
        for s in range(nx):
            for z in range(z_hi):
                at = pl.multiple_of((z * 2 + which) * wide, wide)
                ft_s[z * wide : (z + 1) * wide, s * rows : (s + 1) * rows] = f_refs[s][pl.ds(at, wide)]

    for i in range(parts):

        @pl.when(step // each == i)
        def _():
            total = dot(ft_s[:, :rows], g_refs[i * nx][...])
            for s in range(1, nx):
                total += dot(ft_s[:, s * rows : (s + 1) * rows], g_refs[i * nx + s][...])
            total_s[...] = total.astype(BF)

    part = wide // ny
    for z in range(z_hi):
        for r in range(ny):
            at = pl.multiple_of(z * wide + (my_y + r) % ny * part, part)
            out_ref[r, z] = total_s[pl.ds(at, part)]


def weight_part(features, grads, which, my_y, z_hi, ny):
    nx = len(features)
    parts = len(grads)
    rows, n = grads[0][0].shape
    wide = features[0].shape[0] // (z_hi * 2)
    cols = min(n, 256)
    each = n // cols

    def block(i):
        return pl.BlockSpec((rows, cols), lambda g: (0, jnp.clip(g - i * each, 0, each - 1)))

    return pl.pallas_call(
        functools.partial(weight_kernel, nx, parts, z_hi, ny),
        grid=(parts * each,),
        in_specs=[pl.BlockSpec(memory_space=pltpu.SMEM)]
        + [whole(features[0].shape)] * nx
        + [block(i) for i in range(parts) for _ in range(nx)],
        out_specs=pl.BlockSpec((ny, z_hi, wide // ny, cols), lambda g: (0, 0, 0, g)),
        out_shape=jax.ShapeDtypeStruct((ny, z_hi, wide // ny, parts * n), BF),
        scratch_shapes=[
            pltpu.VMEM((z_hi * wide, nx * rows), BF),
            pltpu.VMEM((z_hi * wide, cols), BF),
        ],
        compiler_params=pltpu.CompilerParams(vmem_limit_bytes=24 * 2**20),
        cost_estimate=pl.CostEstimate(
            flops=2 * z_hi * wide * nx * rows * parts * n,
            bytes_accessed=6 * 2**20,
            transcendentals=0,
        ),
        name="weight_part",
    )(jnp.stack([which, my_y]), *features, *[g for group in grads for g in group])


def local(layer_input, queries, key_head, value_head, grad_output, doc_ids):
    x, q, k, v, do, docs = (
        a[0] for a in (layer_input, queries, key_head, value_head, grad_output, doc_ids)
    )
    rows, hd = k.shape
    ctx = lax.axis_size(CTX)
    nx, nc, z_hi = lax.axis_size("x"), lax.axis_size("core"), lax.axis_size("zh")
    ny, zl = lax.axis_size("y"), lax.axis_size("zl")
    place = lax.axis_index(CTX)
    my_x, my_core, my_y = lax.axis_index("x"), lax.axis_index("core"), lax.axis_index("y")

    kv = jnp.concatenate([k, v], axis=1)
    pair = jnp.stack([kv, shifted(kv, "zl", zl, 1)])
    kv_pairs = [pair] + [shifted(pair, "y", ny, s, False) for s in range(1, ny)]
    features = [
        shifted(part, "x", nx, s) if s else part
        for s, part in enumerate(split_features(x, my_x, z_hi, nx))
    ]

    my_docs = lax.dynamic_slice_in_dim(docs, place * rows, rows)
    starts = jnp.sum((docs[:, None] < my_docs[None, :]).astype(jnp.int32), axis=0)
    info = jnp.stack([place - starts[0] // rows + 1, place, starts[rows - 1]])
    starts = starts[None, :]

    def along_x(grads):
        return [grads] + [shifted(grads, "x", nx, s) for s in range(1, nx)]

    def term(grads):
        theirs = weight_part(features, grads, 1 - my_core, my_y, z_hi, ny)
        theirs = shifted(theirs, "core", nc, 1)
        mine = weight_part(features, grads, my_core, my_y, z_hi, ny)
        return [(mine[r].astype(F32) + theirs[r].astype(F32)).astype(BF) for r in range(ny)]

    def along_y(pieces):
        total = pieces[0].astype(F32)
        for r in range(1, ny):
            total = total + shifted(pieces[r], "y", ny, r).astype(F32)
        return total.astype(BF)

    dq_first, dkv = attention_half(q, do, kv_pairs, info, starts, 0, None)
    dq_first, *features = lax.optimization_barrier((dq_first, *features))
    first = along_x(dq_first)
    dq_second, dkv = attention_half(q, do, kv_pairs, info, starts, 1, dkv)
    dq_second, dkv, first = lax.optimization_barrier((dq_second, dkv, first))
    second = along_x(dq_second)

    total = dkv[0].astype(F32)
    for s in range(1, ny):
        total = total + shifted(dkv[s], "y", ny, -s, False).astype(F32)
    other = shifted(total[1].astype(BF), "zl", zl, 1)
    dkv_own = (total[0] + other.astype(F32)).astype(BF)

    pieces = term([first, second])
    pieces, along = lax.optimization_barrier((pieces, along_x(dkv_own)))
    part = jnp.concatenate([along_y(pieces), along_y(term([along]))], axis=-1)
    n = part.shape[-1]
    part = lax.all_to_all(part.reshape(z_hi * zl, -1, n), ("zh", "zl"), 0, 0, tiled=True)
    tokens = rows * ctx * nx * nc * z_hi
    weight = jnp.sum(part.astype(F32), axis=0) * (1.0 / math.sqrt(tokens))
    width = q.shape[1]
    dq = jnp.concatenate([dq_first, dq_second], axis=1)
    return (
        dq[None],
        dkv_own[None, :, :hd],
        dkv_own[None, :, hd:],
        weight[:, :width],
        weight[:, width : width + hd],
        weight[:, width + hd :],
    )


def solution(mesh):
    fine = Mesh(mesh.devices.reshape(SIZES), AXES)
    dp = ("zh", "x", "core")
    tok = P(dp, CTX, None)
    row = P(dp + CTX, None)
    return jax.shard_map(
        local,
        mesh=fine,
        in_specs=(tok, tok, tok, tok, tok, P(dp, None)),
        out_specs=(tok, tok, tok, row, row, row),
        check_vma=False,
    )
```

time: 172 us -> 143 us (0.83)
  blocking collectives: 25.8 us -> 0 us
  local copies, waits for them, and re-layouts: 19.6 us -> 12.3 us
  waiting for transfers between devices: 40.6 us -> 44.9 us
    all_to_all x1 -> x0, blocking collectives: 25.8 us -> none  [local(): part = lax.all_to_all(part.reshape(y, -1, n), 'y', 0, 0, tiled=True)]
    unnamed x50 -> x36, local copies, waits for them, and re-layouts: 16.5 us -> 9.82 us
    ppermute x25 -> x28, waiting for transfers between devices: 30.5 us -> 36.1 us  [shifted(): return lax.ppermute(value, axis, pairs)]
    pallas_call x5 -> x6, Pallas kernels: 19.1 us -> 17 us  [the longest x4 9.88 us: weight_part(): pl.pallas_call(functools.partial(weight_kernel, nx, parts, z_hi, ny), gri...]
    ppermute x25 -> x28, starting transfers between devices: 48.3 us -> 47.3 us  [shifted(): return lax.ppermute(value, axis, pairs)]
  transfers between devices with their start and end apart: 26 -> 29, of which waited for: 15 -> 15; matrix products, arithmetic and copies ran while one was open for 3% -> 3% of each run, Pallas kernels for 12% -> 13%
where the time goes in v4:
time: 143 us; the launch traced here: 141 us
  starting transfers between devices  56.4 us (39%)
  waiting for transfers between devices  44.9 us (31%)
  Pallas kernels  19.2 us (13%)
  local copies, waits for them, and re-layouts  12.3 us (9%)
  other arithmetic  4.65 us (3%)
  between operations  3.56 us (2%)
    ppermute x28, starting transfers between devices, shifted(): return lax.ppermute(value, axis, pairs)  47.3 us
    ppermute x28, waiting for transfers between devices, shifted(): return lax.ppermute(value, axis, pairs)  36.1 us
    pallas_call x4, Pallas kernels, weight_part(): pl.pallas_call(functools.partial(weight_kernel, nx, parts, z_hi, ny), gri...  9.88 us
    unnamed x36, local copies, waits for them, and re-layouts  9.82 us
    all_to_all x1, starting transfers between devices, local(): lax.all_to_all(part.reshape(z_hi * zl, -1, n), ('zh', 'zl'), 0, 0, tiled=...  9.11 us
    all_to_all x1, waiting for transfers between devices, local(): lax.all_to_all(part.reshape(z_hi * zl, -1, n), ('zh', 'zl'), 0, 0, tiled=...  8.81 us
    pallas_call x2, Pallas kernels, attention_half(): pl.pallas_call(functools.partial(attention_kernel, ny, per, hd ** (-0.5),...  7.11 us
  transfers between devices with their start and end apart: 29, of which 15 were waited for; matrix products, arithmetic and copies ran while one was open for 3% of the time, Pallas kernels for 13%

profile of v4, /device:TPU:32, one launch (start us, length us, event | category | flops | bytes accessed | tf_op | source)
XLA Modules:
  0.0 141.1 jit_solution(1876998229751696752)
XLA Ops:
  5.1 2.2 %split_features.1 = (bf16[1024,256]{1,0:T(8,128)(2,1)S(1)}, bf16[1024,256]{1,0:T(8,128)(2,1)}, bf16[1024,256]{1,0:T(8,128)(2,1)}, bf16[1024,256]{1,0:T(8,128)(2,1)S(1)}) custom-call(s32[1]{0:T(128)} %bitcast.12.info, bf16[256,4096]{1,0:T(8,128)(2,1)S(1)} %bitcast.52, bf16[256,4096]{1,0:T(8,128)(2,1)S(1)} %bitcast.53, bf16[256,4096]{1,0:T(8,128)(2,1)S(1)} %bitcast.54, ...), custom_call_target="tpu_custom_call" | custom-call | tf_op jit(solution)/shard_map/split_features/pallas_call | solution.py:207
  8.1 2.5 %collective-permute-start.5 = (bf16[1024,256]{1,0:T(8,128)(2,1)}, bf16[1024,256]{1,0:T(8,128)(2,1)S(1)}, u32[]{:S(2)}, u32[]{:S(2)}) collective-permute-start(bf16[1024,256]{1,0:T(8,128)(2,1)} %get-tuple-element.45), channel_id=1, source_target_pairs={{0,32},{16,48},{32,0},{48,16},{1,33},{17,49},{33,1},{49,17},{2,34}... | collective-permute-start | bytes 1572872 | tf_op jit(solution)/shard_map/ppermute | solution.py:33
  10.6 3.5 %collective-permute-start.1 = (bf16[2,256,256]{2,1,0:T(8,128)(2,1)S(1)}, bf16[2,256,256]{2,1,0:T(8,128)(2,1)S(1)}, u32[]{:S(2)}, u32[]{:S(2)}) collective-permute-start(bf16[2,256,256]{2,1,0:T(8,128)(2,1)S(1)} %pad_maximum_fusion.1.refs_0_), channel_id=1, source_target_pairs={{0,2},{2,4},{4,6},{1,3},{3,5},{5,7},{8,10},{10,12},{12,14},{9,11},... | collective-permute-start | bytes 786440 | tf_op jit(solution)/shard_map/ppermute | solution.py:33
  14.1 4.8 %collective-permute-start.2 = (bf16[2,256,256]{2,1,0:T(8,128)(2,1)S(1)}, bf16[2,256,256]{2,1,0:T(8,128)(2,1)S(1)}, u32[]{:S(2)}, u32[]{:S(2)}) collective-permute-start(bf16[2,256,256]{2,1,0:T(8,128)(2,1)S(1)} %pad_maximum_fusion.1.refs_0_), channel_id=1, source_target_pairs={{0,4},{2,6},{1,5},{3,7},{8,12},{10,14},{9,13},{11,15},{16,20},{18,... | collective-permute-start | bytes 786440 | tf_op jit(solution)/shard_map/ppermute | solution.py:33
  19.0 2.0 %collective-permute-start.3 = (bf16[2,256,256]{2,1,0:T(8,128)(2,1)S(1)}, bf16[2,256,256]{2,1,0:T(8,128)(2,1)}, u32[]{:S(2)}, u32[]{:S(2)}) collective-permute-start(bf16[2,256,256]{2,1,0:T(8,128)(2,1)S(1)} %pad_maximum_fusion.1.refs_0_), channel_id=1, source_target_pairs={{0,6},{1,7},{8,14},{9,15},{16,22},{17,23},{24,30},{25,31},{32,38},... | collective-permute-start | bytes 786440 | tf_op jit(solution)/shard_map/ppermute | solution.py:33
  29.7 3.5 %attention_backward.2 = (bf16[256,512]{1,0:T(8,128)(2,1)S(1)}, bf16[2,256,256]{2,1,0:T(8,128)(2,1)S(1)}, bf16[2,256,256]{2,1,0:T(8,128)(2,1)S(1)}, bf16[2,256,25...) custom-call(s32[3]{0:T(128)S(1)} %pad_add_fusion.info, s32[1,256]{1,0:T(1,128)S(1)} %bitcast.56, ...), custom_call_target="tpu_custom_call" | custom-call | flops 5368709120 | bytes 4194304 | tf_op jit(solution)/shard_map/attention_backward/pallas_call | solution.py:158
  33.6 3.7 %collective-permute-done.6.refs_3_ = bf16[1024,256]{1,0:T(8,128)(2,1)S(1)} collective-permute-done((bf16[1024,256]{1,0:T(8,128)(2,1)}, bf16[1024,256]{1,0:T(8,128)(2,1)S(1)}, u32[]{:S(2)}, u32[]{:S(2)}) %collective-permute-start.6) | collective-permute-done | bytes 524320 | tf_op jit(solution)/shard_map/ppermute | solution.py:33
  37.3 4.1 %collective-permute-start.8 = (bf16[256,512]{1,0:T(8,128)(2,1)S(1)}, bf16[256,512]{1,0:T(8,128)(2,1)S(1)}, u32[]{:S(2)}, u32[]{:S(2)}) collective-permute-start(bf16[256,512]{1,0:T(8,128)(2,1)S(1)} %get-tuple-element.66.refs_4_), channel_id=1, source_target_pairs={{0,32},{16,48},{32,0},{48,16},{1,33},{17,49},{33,1},{49,17},{2,34}... | collective-permute-start | bytes 786440 | tf_op jit(solution)/shard_map/ppermute | solution.py:33
  43.3 3.6 %attention_backward.3 = (bf16[256,512]{1,0:T(8,128)(2,1)S(1)}, bf16[2,256,256]{2,1,0:T(8,128)(2,1)S(1)}, bf16[2,256,256]{2,1,0:T(8,128)(2,1)S(1)}, bf16[2,256,25...) custom-call(s32[3]{0:T(128)S(1)} %pad_add_fusion.info, s32[1,256]{1,0:T(1,128)S(1)} %bitcast.57, ...), custom_call_target="tpu_custom_call" | custom-call | flops 5368709120 | bytes 4194304 | tf_op jit(solution)/shard_map/attention_backward/pallas_call | solution.py:158
  51.8 2.9 %collective-permute-start.15 = (bf16[256,512]{1,0:T(8,128)(2,1)S(1)}, bf16[256,512]{1,0:T(8,128)(2,1)}, u32[]{:S(2)}, u32[]{:S(2)}) collective-permute-start(bf16[256,512]{1,0:T(8,128)(2,1)S(1)} %get-tuple-element.57.refs_8_), channel_id=1, source_target_pairs={{0,32},{16,48},{32,0},{48,16},{1,33},{17,49},{33,1},{49,17},{2,34}... | collective-permute-start | bytes 786440 | tf_op jit(solution)/shard_map/ppermute | solution.py:33
  57.4 2.3 %collective-permute-done.14.refs_9_ = bf16[256,512]{1,0:T(8,128)(2,1)} collective-permute-done((bf16[256,512]{1,0:T(8,128)(2,1)S(1)}, bf16[256,512]{1,0:T(8,128)(2,1)}, u32[]{:S(2)}, u32[]{:S(2)}) %collective-permute-start.14) | collective-permute-done | bytes 262176 | tf_op jit(solution)/shard_map/ppermute | solution.py:33
  61.1 4.6 %collective-permute-done.15.refs_10_ = bf16[256,512]{1,0:T(8,128)(2,1)} collective-permute-done((bf16[256,512]{1,0:T(8,128)(2,1)S(1)}, bf16[256,512]{1,0:T(8,128)(2,1)}, u32[]{:S(2)}, u32[]{:S(2)}) %collective-permute-start.15) | collective-permute-done | bytes 262176 | tf_op jit(solution)/shard_map/ppermute | solution.py:33
  65.6 3.9 %weight_part.5 = bf16[4,4,32,1024]{3,2,1,0:T(8,128)(2,1)S(1)} custom-call(s32[2]{0:T(128)S(1)} %pad_add_fusion.2.info, bf16[1024,256]{1,0:T(8,128)(2,1)S(1)} %get-tuple-element.62.refs_0_, bf16[1024,256]{1,0:T(8,128)(2,1)S(1)} %collective-permute-done.4.refs_1_, bf16[1024,256]{1,0:T(8,128)(2,1)S(1)} %collective-permute-done.5.refs_2_, ...), custom_call_target="tpu_custom_call" | custom-call | flops 1073741824 | bytes 6291456 | tf_op jit(solution)/shard_map/weight_part/pallas_call | solution.py:263
  69.7 5.7 %collective-permute-done.12 = bf16[2,256,256]{2,1,0:T(8,128)(2,1)S(1)} collective-permute-done((bf16[2,256,256]{2,1,0:T(8,128)(2,1)}, bf16[2,256,256]{2,1,0:T(8,128)(2,1)S(1)}, u32[]{:S(2)}, u32[]{:S(2)}) %collective-permute-start.12) | collective-permute-done | bytes 262176 | tf_op jit(solution)/shard_map/ppermute | solution.py:33
  75.7 3.9 %weight_part.4 = bf16[4,4,32,1024]{3,2,1,0:T(8,128)(2,1)S(1)} custom-call(s32[2]{0:T(128)S(1)} %pad_add_fusion.1.info, bf16[1024,256]{1,0:T(8,128)(2,1)S(1)} %get-tuple-element.62.refs_0_, bf16[1024,256]{1,0:T(8,128)(2,1)S(1)} %collective-permute-done.4.refs_1_, bf16[1024,256]{1,0:T(8,128)(2,1)S(1)} %collective-permute-done.5.refs_2_, ...), custom_call_target="tpu_custom_call" | custom-call | flops 1073741824 | bytes 6291456 | tf_op jit(solution)/shard_map/weight_part/pallas_call | solution.py:263
  84.5 3.8 %collective-permute-done.18.refs_5_ = bf16[256,256]{1,0:T(8,128)(2,1)S(1)} collective-permute-done((bf16[256,256]{1,0:T(8,128)(2,1)S(1)}, bf16[256,256]{1,0:T(8,128)(2,1)S(1)}, u32[]{:S(2)}, u32[]{:S(2)}) %collective-permute-start.18) | collective-permute-done | bytes 131104 | tf_op jit(solution)/shard_map/ppermute | solution.py:33
  90.3 9.8 %collective-permute-start.23 = (bf16[4,32,1024]{2,1,0:T(8,128)(2,1)S(1)}, bf16[4,32,1024]{2,1,0:T(8,128)(2,1)S(1)}, u32[]{:S(2)}, u32[]{:S(2)}) collective-permute-start(bf16[4,32,1024]{2,1,0:T(8,128)(2,1)S(1)} %get-tuple-element.73), channel_id=1, source_target_pairs={{0,6},{2,0},{4,2},{6,4},{1,7},{3,1},{5,3},{7,5},{8,14},{10,8},{12,... | collective-permute-start | bytes 786440 | tf_op jit(solution)/shard_map/ppermute | solution.py:33
  102.3 2.2 %collective-permute-start.27 = (bf16[4,32,256]{2,1,0:T(8,128)(2,1)S(1)}, bf16[4,32,256]{2,1,0:T(8,128)(2,1)S(1)}, u32[]{:S(2)}, u32[]{:S(2)}) collective-permute-start(bf16[4,32,256]{2,1,0:T(8,128)(2,1)S(1)} %get-tuple-element.83), channel_id=1, source_target_pairs={{0,6},{2,0},{4,2},{6,4},{1,7},{3,1},{5,3},{7,5},{8,14},{10,8},{12,... | collective-permute-start | bytes 196616 | tf_op jit(solution)/shard_map/ppermute | solution.py:33
  104.5 2.3 %collective-permute-start.26 = (bf16[4,32,256]{2,1,0:T(8,128)(2,1)S(1)}, bf16[4,32,256]{2,1,0:T(8,128)(2,1)S(1)}, u32[]{:S(2)}, u32[]{:S(2)}) collective-permute-start(bf16[4,32,256]{2,1,0:T(8,128)(2,1)S(1)} %get-tuple-element.84), channel_id=1, source_target_pairs={{0,4},{2,6},{4,0},{6,2},{1,5},{3,7},{5,1},{7,3},{8,12},{10,14},{12... | collective-permute-start | bytes 196616 | tf_op jit(solution)/shard_map/ppermute | solution.py:33
  106.8 6.8 %collective-permute-done.23 = bf16[4,32,1024]{2,1,0:T(8,128)(2,1)S(1)} collective-permute-done((bf16[4,32,1024]{2,1,0:T(8,128)(2,1)S(1)}, bf16[4,32,1024]{2,1,0:T(8,128)(2,1)S(1)}, u32[]{:S(2)}, u32[]{:S(2)}) %collective-permute-start.23) | collective-permute-done | bytes 262176 | tf_op jit(solution)/shard_map/ppermute | solution.py:33
  113.6 2.1 %collective-permute-done.21 = bf16[4,32,1024]{2,1,0:T(8,128)(2,1)S(1)} collective-permute-done((bf16[4,32,1024]{2,1,0:T(8,128)(2,1)S(1)}, bf16[4,32,1024]{2,1,0:T(8,128)(2,1)S(1)}, u32[]{:S(2)}, u32[]{:S(2)}) %collective-permute-start.21) | collective-permute-done | bytes 262176 | tf_op jit(solution)/shard_map/ppermute | solution.py:33
  117.0 2.5 %collective-permute-done.25 = bf16[4,32,256]{2,1,0:T(8,128)(2,1)S(1)} collective-permute-done((bf16[4,32,256]{2,1,0:T(8,128)(2,1)S(1)}, bf16[4,32,256]{2,1,0:T(8,128)(2,1)S(1)}, u32[]{:S(2)}, u32[]{:S(2)}) %collective-permute-start.25) | collective-permute-done | bytes 65568 | tf_op jit(solution)/shard_map/ppermute | solution.py:33
  120.3 9.1 %all-to-all-start = ((bf16[8,16,1280]{2,1,0:T(8,128)(2,1)}), bf16[8,16,1280]{2,1,0:T(8,128)(2,1)S(1)}, u32[]{:S(2)}, u32[]{:S(2)}) async-start(bf16[8,16,1280]{2,1,0:T(8,128)(2,1)} %bitcast.30), calls=%async_computation | async-start | bytes 655360 | tf_op jit(solution)/shard_map/all_to_all | solution.py:341
  130.9 8.8 %all-to-all-done = bf16[8,16,1280]{2,1,0:T(8,128)(2,1)S(1)} async-done(((bf16[8,16,1280]{2,1,0:T(8,128)(2,1)}), bf16[8,16,1280]{2,1,0:T(8,128)(2,1)S(1)}, u32[]{:S(2)}, u32[]{:S(2)}) %all-to-all-start) | async-done | bytes 327712 | tf_op jit(solution)/shard_map/all_to_all | solution.py:341
  (99 shorter events, 36.8 us)
Async XLA Ops:
  1.5 9.0 %collective-permute-start = (bf16[256,256]{1,0:T(8,128)(2,1)S(1)}, bf16[256,256]{1,0:T(8,128)(2,1)S(1)}, u32[]{:S(2)}, u32[]{:S(2)}) collective-permute-start(bf16[256,256]{1,0:T(8,128)(2,1)S(1)} %get-tuple-element.88), channel_id=1, source_target_pairs={{0,1},{1,0},{2,3},{3,2},{4,5},{5,4},{6,7},{7,6},{8,9},{9,8},{10,11... | collective-permute-start | bytes 393224 | tf_op jit(solution)/shard_map/ppermute | solution.py:33
  8.1 25.2 %collective-permute-start.4 = (bf16[1024,256]{1,0:T(8,128)(2,1)}, bf16[1024,256]{1,0:T(8,128)(2,1)S(1)}, u32[]{:S(2)}, u32[]{:S(2)}) collective-permute-start(bf16[1024,256]{1,0:T(8,128)(2,1)} %get-tuple-element.44), channel_id=1, source_target_pairs={{0,16},{16,32},{32,48},{48,0},{1,17},{17,33},{33,49},{49,1},{2,18}... | collective-permute-start | bytes 1572872 | tf_op jit(solution)/shard_map/ppermute | solution.py:33
  8.1 25.5 %collective-permute-start.5 = (bf16[1024,256]{1,0:T(8,128)(2,1)}, bf16[1024,256]{1,0:T(8,128)(2,1)S(1)}, u32[]{:S(2)}, u32[]{:S(2)}) collective-permute-start(bf16[1024,256]{1,0:T(8,128)(2,1)} %get-tuple-element.45), channel_id=1, source_target_pairs={{0,32},{16,48},{32,0},{48,16},{1,33},{17,49},{33,1},{49,17},{2,34}... | collective-permute-start | bytes 1572872 | tf_op jit(solution)/shard_map/ppermute | solution.py:33
  10.6 13.9 %collective-permute-start.1 = (bf16[2,256,256]{2,1,0:T(8,128)(2,1)S(1)}, bf16[2,256,256]{2,1,0:T(8,128)(2,1)S(1)}, u32[]{:S(2)}, u32[]{:S(2)}) collective-permute-start(bf16[2,256,256]{2,1,0:T(8,128)(2,1)S(1)} %pad_maximum_fusion.1.refs_0_), channel_id=1, source_target_pairs={{0,2},{2,4},{4,6},{1,3},{3,5},{5,7},{8,10},{10,12},{12,14},{9,11},... | collective-permute-start | bytes 786440 | tf_op jit(solution)/shard_map/ppermute | solution.py:33
  14.1 12.6 %collective-permute-start.2 = (bf16[2,256,256]{2,1,0:T(8,128)(2,1)S(1)}, bf16[2,256,256]{2,1,0:T(8,128)(2,1)S(1)}, u32[]{:S(2)}, u32[]{:S(2)}) collective-permute-start(bf16[2,256,256]{2,1,0:T(8,128)(2,1)S(1)} %pad_maximum_fusion.1.refs_0_), channel_id=1, source_target_pairs={{0,4},{2,6},{1,5},{3,7},{8,12},{10,14},{9,13},{11,15},{16,20},{18,... | collective-permute-start | bytes 786440 | tf_op jit(solution)/shard_map/ppermute | solution.py:33
  19.0 8.7 %collective-permute-start.3 = (bf16[2,256,256]{2,1,0:T(8,128)(2,1)S(1)}, bf16[2,256,256]{2,1,0:T(8,128)(2,1)}, u32[]{:S(2)}, u32[]{:S(2)}) collective-permute-start(bf16[2,256,256]{2,1,0:T(8,128)(2,1)S(1)} %pad_maximum_fusion.1.refs_0_), channel_id=1, source_target_pairs={{0,6},{1,7},{8,14},{9,15},{16,22},{17,23},{24,30},{25,31},{32,38},... | collective-permute-start | bytes 786440 | tf_op jit(solution)/shard_map/ppermute | solution.py:33
  24.5 12.7 %collective-permute-start.6 = (bf16[1024,256]{1,0:T(8,128)(2,1)}, bf16[1024,256]{1,0:T(8,128)(2,1)S(1)}, u32[]{:S(2)}, u32[]{:S(2)}) collective-permute-start(bf16[1024,256]{1,0:T(8,128)(2,1)} %copy-done.8), channel_id=1, source_target_pairs={{0,48},{16,0},{32,16},{48,32},{1,49},{17,1},{33,17},{49,33},{2,50}... | collective-permute-start | bytes 1572872 | tf_op jit(solution)/shard_map/ppermute | solution.py:33
  37.3 12.4 %collective-permute-start.7 = (bf16[256,512]{1,0:T(8,128)(2,1)S(1)}, bf16[256,512]{1,0:T(8,128)(2,1)S(1)}, u32[]{:S(2)}, u32[]{:S(2)}) collective-permute-start(bf16[256,512]{1,0:T(8,128)(2,1)S(1)} %get-tuple-element.66.refs_4_), channel_id=1, source_target_pairs={{0,16},{16,32},{32,48},{48,0},{1,17},{17,33},{33,49},{49,1},{2,18}... | collective-permute-start | bytes 786440 | tf_op jit(solution)/shard_map/ppermute | solution.py:33
  37.3 13.6 %collective-permute-start.8 = (bf16[256,512]{1,0:T(8,128)(2,1)S(1)}, bf16[256,512]{1,0:T(8,128)(2,1)S(1)}, u32[]{:S(2)}, u32[]{:S(2)}) collective-permute-start(bf16[256,512]{1,0:T(8,128)(2,1)S(1)} %get-tuple-element.66.refs_4_), channel_id=1, source_target_pairs={{0,32},{16,48},{32,0},{48,16},{1,33},{17,49},{33,1},{49,17},{2,34}... | collective-permute-start | bytes 786440 | tf_op jit(solution)/shard_map/ppermute | solution.py:33
  41.4 9.5 %collective-permute-start.9 = (bf16[256,512]{1,0:T(8,128)(2,1)S(1)}, bf16[256,512]{1,0:T(8,128)(2,1)S(1)}, u32[]{:S(2)}, u32[]{:S(2)}) collective-permute-start(bf16[256,512]{1,0:T(8,128)(2,1)S(1)} %get-tuple-element.66.refs_4_), channel_id=1, source_target_pairs={{0,48},{16,0},{32,16},{48,32},{1,49},{17,1},{33,17},{49,33},{2,50}... | collective-permute-start | bytes 786440 | tf_op jit(solution)/shard_map/ppermute | solution.py:33
  50.9 8.8 %collective-permute-start.14 = (bf16[256,512]{1,0:T(8,128)(2,1)S(1)}, bf16[256,512]{1,0:T(8,128)(2,1)}, u32[]{:S(2)}, u32[]{:S(2)}) collective-permute-start(bf16[256,512]{1,0:T(8,128)(2,1)S(1)} %get-tuple-element.57.refs_8_), channel_id=1, source_target_pairs={{0,16},{16,32},{32,48},{48,0},{1,17},{17,33},{33,49},{49,1},{2,18}... | collective-permute-start | bytes 786440 | tf_op jit(solution)/shard_map/ppermute | solution.py:33
  51.8 13.8 %collective-permute-start.15 = (bf16[256,512]{1,0:T(8,128)(2,1)S(1)}, bf16[256,512]{1,0:T(8,128)(2,1)}, u32[]{:S(2)}, u32[]{:S(2)}) collective-permute-start(bf16[256,512]{1,0:T(8,128)(2,1)S(1)} %get-tuple-element.57.refs_8_), channel_id=1, source_target_pairs={{0,32},{16,48},{32,0},{48,16},{1,33},{17,49},{33,1},{49,17},{2,34}... | collective-permute-start | bytes 786440 | tf_op jit(solution)/shard_map/ppermute | solution.py:33
  54.7 10.9 %collective-permute-start.16 = (bf16[256,512]{1,0:T(8,128)(2,1)S(1)}, bf16[256,512]{1,0:T(8,128)(2,1)}, u32[]{:S(2)}, u32[]{:S(2)}) collective-permute-start(bf16[256,512]{1,0:T(8,128)(2,1)S(1)} %get-tuple-element.57.refs_8_), channel_id=1, source_target_pairs={{0,48},{16,0},{32,16},{48,32},{1,49},{17,1},{33,17},{49,33},{2,50}... | collective-permute-start | bytes 786440 | tf_op jit(solution)/shard_map/ppermute | solution.py:33
  54.8 20.6 %collective-permute-start.12 = (bf16[2,256,256]{2,1,0:T(8,128)(2,1)}, bf16[2,256,256]{2,1,0:T(8,128)(2,1)S(1)}, u32[]{:S(2)}, u32[]{:S(2)}) collective-permute-start(bf16[2,256,256]{2,1,0:T(8,128)(2,1)} %copy-done.16), channel_id=1, source_target_pairs={{6,0},{7,1},{14,8},{15,9},{22,16},{23,17},{30,24},{31,25},{38,32},... | collective-permute-start | bytes 786440 | tf_op jit(solution)/shard_map/ppermute | solution.py:33
  56.1 19.3 %collective-permute-start.11 = (bf16[2,256,256]{2,1,0:T(8,128)(2,1)}, bf16[2,256,256]{2,1,0:T(8,128)(2,1)S(1)}, u32[]{:S(2)}, u32[]{:S(2)}) collective-permute-start(bf16[2,256,256]{2,1,0:T(8,128)(2,1)} %copy-done.15), channel_id=1, source_target_pairs={{4,0},{6,2},{5,1},{7,3},{12,8},{14,10},{13,9},{15,11},{20,16},{22,... | collective-permute-start | bytes 786440 | tf_op jit(solution)/shard_map/ppermute | solution.py:33
  59.7 15.6 %collective-permute-start.10 = (bf16[2,256,256]{2,1,0:T(8,128)(2,1)}, bf16[2,256,256]{2,1,0:T(8,128)(2,1)S(1)}, u32[]{:S(2)}, u32[]{:S(2)}) collective-permute-start(bf16[2,256,256]{2,1,0:T(8,128)(2,1)} %copy-done.14), channel_id=1, source_target_pairs={{2,0},{4,2},{6,4},{3,1},{5,3},{7,5},{10,8},{12,10},{14,12},{11,9},... | collective-permute-start | bytes 786440 | tf_op jit(solution)/shard_map/ppermute | solution.py:33
  69.6 14.5 %collective-permute-start.17 = (bf16[4,4,32,1024]{3,2,1,0:T(8,128)(2,1)S(1)}, bf16[4,4,32,1024]{3,2,1,0:T(8,128)(2,1)S(1)}, u32[]{:S(2)}, u32[]{:S(2)}) collective-permute-start(bf16[4,4,32,1024]{3,2,1,0:T(8,128)(2,1)S(1)} %weight_part.5), channel_id=1, source_target_pairs={{0,8},{8,0},{1,9},{9,1},{2,10},{10,2},{3,11},{11,3},{4,12},{12,4},... | collective-permute-start | bytes 3145736 | tf_op jit(solution)/shard_map/ppermute | solution.py:33
  90.2 12.0 %collective-permute-start.24 = (bf16[4,4,32,256]{3,2,1,0:T(8,128)(2,1)S(1)}, bf16[4,4,32,256]{3,2,1,0:T(8,128)(2,1)S(1)}, u32[]{:S(2)}, u32[]{:S(2)}) collective-permute-start(bf16[4,4,32,256]{3,2,1,0:T(8,128)(2,1)S(1)} %weight_part.7), channel_id=1, source_target_pairs={{0,8},{8,0},{1,9},{9,1},{2,10},{10,2},{3,11},{11,3},{4,12},{12,4},... | collective-permute-start | bytes 786440 | tf_op jit(solution)/shard_map/ppermute | solution.py:33
  90.3 23.3 %collective-permute-start.23 = (bf16[4,32,1024]{2,1,0:T(8,128)(2,1)S(1)}, bf16[4,32,1024]{2,1,0:T(8,128)(2,1)S(1)}, u32[]{:S(2)}, u32[]{:S(2)}) collective-permute-start(bf16[4,32,1024]{2,1,0:T(8,128)(2,1)S(1)} %get-tuple-element.73), channel_id=1, source_target_pairs={{0,6},{2,0},{4,2},{6,4},{1,7},{3,1},{5,3},{7,5},{8,14},{10,8},{12,... | collective-permute-start | bytes 786440 | tf_op jit(solution)/shard_map/ppermute | solution.py:33
  100.1 13.5 %collective-permute-start.22 = (bf16[4,32,1024]{2,1,0:T(8,128)(2,1)S(1)}, bf16[4,32,1024]{2,1,0:T(8,128)(2,1)S(1)}, u32[]{:S(2)}, u32[]{:S(2)}) collective-permute-start(bf16[4,32,1024]{2,1,0:T(8,128)(2,1)S(1)} %get-tuple-element.72), channel_id=1, source_target_pairs={{0,4},{2,6},{4,0},{6,2},{1,5},{3,7},{5,1},{7,3},{8,12},{10,14},{12... | collective-permute-start | bytes 786440 | tf_op jit(solution)/shard_map/ppermute | solution.py:33
  100.1 15.6 %collective-permute-start.21 = (bf16[4,32,1024]{2,1,0:T(8,128)(2,1)S(1)}, bf16[4,32,1024]{2,1,0:T(8,128)(2,1)S(1)}, u32[]{:S(2)}, u32[]{:S(2)}) collective-permute-start(bf16[4,32,1024]{2,1,0:T(8,128)(2,1)S(1)} %get-tuple-element.71), channel_id=1, source_target_pairs={{0,2},{2,4},{4,6},{6,0},{1,3},{3,5},{5,7},{7,1},{8,10},{10,12},{12... | collective-permute-start | bytes 786440 | tf_op jit(solution)/shard_map/ppermute | solution.py:33
  102.3 13.7 %collective-permute-start.27 = (bf16[4,32,256]{2,1,0:T(8,128)(2,1)S(1)}, bf16[4,32,256]{2,1,0:T(8,128)(2,1)S(1)}, u32[]{:S(2)}, u32[]{:S(2)}) collective-permute-start(bf16[4,32,256]{2,1,0:T(8,128)(2,1)S(1)} %get-tuple-element.83), channel_id=1, source_target_pairs={{0,6},{2,0},{4,2},{6,4},{1,7},{3,1},{5,3},{7,5},{8,14},{10,8},{12,... | collective-permute-start | bytes 196616 | tf_op jit(solution)/shard_map/ppermute | solution.py:33
  104.5 12.5 %collective-permute-start.26 = (bf16[4,32,256]{2,1,0:T(8,128)(2,1)S(1)}, bf16[4,32,256]{2,1,0:T(8,128)(2,1)S(1)}, u32[]{:S(2)}, u32[]{:S(2)}) collective-permute-start(bf16[4,32,256]{2,1,0:T(8,128)(2,1)S(1)} %get-tuple-element.84), channel_id=1, source_target_pairs={{0,4},{2,6},{4,0},{6,2},{1,5},{3,7},{5,1},{7,3},{8,12},{10,14},{12... | collective-permute-start | bytes 196616 | tf_op jit(solution)/shard_map/ppermute | solution.py:33
  120.3 19.4 %all-to-all-start = ((bf16[8,16,1280]{2,1,0:T(8,128)(2,1)}), bf16[8,16,1280]{2,1,0:T(8,128)(2,1)S(1)}, u32[]{:S(2)}, u32[]{:S(2)}) async-start(bf16[8,16,1280]{2,1,0:T(8,128)(2,1)} %bitcast.30), calls=%async_computation | async-start | bytes 655360 | tf_op jit(solution)/shard_map/all_to_all | solution.py:341
  (23 other events, 143.8 us)

commit v5 on v4

--- a/solution.py
+++ b/solution.py
@@ -12,7 +12,6 @@
 AXES = ("zh", "x", "core", "y", "zl")
 SIZES = (4, 4, 2, 4, 2)
 CTX = ("y", "zl")
-HALVES = 2
 BF = jnp.bfloat16
 F32 = jnp.float32
 NN = (((1,), (0,)), ((), ()))
@@ -33,14 +32,16 @@
     return lax.ppermute(value, axis, pairs)
 
 
+def plus(a, b):
+    return (a.astype(F32) + b.astype(F32)).astype(BF)
+
+
 def whole(shape):
     return pl.BlockSpec(shape, lambda *g: (0,) * len(shape))
 
 
-def attention_kernel(ny, per, scale, last, info, starts_ref, q_ref, do_ref, *refs):
+def attention_kernel(ny, per, scale, info, starts_ref, q_ref, do_ref, *refs):
     kv_refs, refs = refs[:ny], refs[ny:]
-    if last:
-        old_refs, refs = refs[:ny], refs[ny:]
     dq_ref, refs = refs[0], refs[1:]
     out_refs, refs = refs[:ny], refs[ny:]
     kv_s, kt_s, acc_s, e_s, dp_s, md_s, stat_s, dqt_s, qt_s, dot_s, p_s, ds_s, qk_s, dk_s, sem = refs
@@ -56,12 +57,7 @@
         def _():
             pltpu.make_async_copy(kv_refs[s], kv_s.at[pl.ds(2 * s, 2)], sem.at[s]).start()
 
-    for s in range(ny):
-        for k in range(2):
-            if last:
-                acc_s[2 * s + k] = old_refs[s][k].astype(F32)
-            else:
-                acc_s[2 * s + k] = jnp.zeros(acc_s.shape[1:], F32)
+    acc_s[...] = jnp.zeros_like(acc_s)
     for h in range(per):
         cols = slice(h * hd, (h + 1) * hd)
         span = slice(h * rows, (h + 1) * rows)
@@ -140,27 +136,24 @@
     for s in range(ny):
         for k in range(2):
             at = 2 * s + k
-            dk = acc_s[at, :, :hd]
-            out_refs[s][k, :, :hd] = (dk * scale if last else dk).astype(BF)
+            out_refs[s][k, :, :hd] = (acc_s[at, :, :hd] * scale).astype(BF)
             out_refs[s][k, :, hd:] = acc_s[at, :, hd:].astype(BF)
 
 
-def attention_half(q, do, kv, info, starts, half, old):
+def attention(q, do, kv, info, starts):
     rows = q.shape[0]
     hd = kv[0].shape[2] // 2
-    width = q.shape[1] // HALVES
+    width = q.shape[1]
     per = width // hd
     ny = len(kv)
     blocks = 2 * ny
-    last = old is not None
-    slab = pl.BlockSpec((rows, width), lambda g: (0, half))
+    slab = whole((rows, width))
     pair = kv[0].shape
     outs = pl.pallas_call(
-        functools.partial(attention_kernel, ny, per, hd ** (-0.5), last),
+        functools.partial(attention_kernel, ny, per, hd ** (-0.5)),
         grid=(1,),
         in_specs=[pl.BlockSpec(memory_space=pltpu.SMEM), whole((1, rows)), slab, slab]
-        + [pl.BlockSpec(memory_space=pl.ANY)] * ny
-        + ([whole(pair)] * ny if last else []),
+        + [pl.BlockSpec(memory_space=pl.ANY)] * ny,
         out_specs=[whole((rows, width))] + [whole(pair)] * ny,
         out_shape=[jax.ShapeDtypeStruct((rows, width), BF)] + [jax.ShapeDtypeStruct(pair, BF)] * ny,
         scratch_shapes=[
@@ -180,14 +173,14 @@
             pltpu.VMEM((per * rows, hd), BF),
             pltpu.SemaphoreType.DMA((ny,)),
         ],
-        compiler_params=pltpu.CompilerParams(vmem_limit_bytes=28 * 2**20),
+        compiler_params=pltpu.CompilerParams(vmem_limit_bytes=52 * 2**20),
         cost_estimate=pl.CostEstimate(
-            flops=10 * per * rows * rows * blocks * hd * 2,
+            flops=10 * per * rows * rows * blocks * hd,
             bytes_accessed=4 * 2**20,
             transcendentals=per * rows * rows * blocks,
         ),
         name="attention_backward",
-    )(info, starts, q, do, *kv, *(old or []))
+    )(info, starts, q, do, *kv)
     return outs[0], outs[1:]
 
 
@@ -218,13 +211,14 @@
     )(my_x[None], *([x] * nx))
 
 
-def weight_kernel(nx, parts, z_hi, ny, info, *refs):
+def weight_kernel(nx, z_hi, ny, info, *refs):
     f_refs, g_refs, (out_ref, ft_s, total_s) = refs[:nx], refs[nx:-3], refs[-3:]
+    own_ref, left_ref, far_refs, right_ref = g_refs[0], g_refs[1], g_refs[2:4], g_refs[4]
     rows = f_refs[0].shape[1]
     wide = f_refs[0].shape[0] // (z_hi * 2)
     which, my_y = info[0], info[1]
     step = pl.program_id(0)
-    each = pl.num_programs(0) // parts
+    half = pl.num_programs(0) // 2
 
     @pl.when(step == 0)
     def _():
@@ -233,13 +227,15 @@
                 at = pl.multiple_of((z * 2 + which) * wide, wide)
                 ft_s[z * wide : (z + 1) * wide, s * rows : (s + 1) * rows] = f_refs[s][pl.ds(at, wide)]
 
-    for i in range(parts):
-
-        @pl.when(step // each == i)
+    def product(s, ref):
+        return dot(ft_s[:, s * rows : (s + 1) * rows], ref[...])
+
+    for i in range(2):
+
+        @pl.when(step // half == i)
         def _():
-            total = dot(ft_s[:, :rows], g_refs[i * nx][...])
-            for s in range(1, nx):
-                total += dot(ft_s[:, s * rows : (s + 1) * rows], g_refs[i * nx + s][...])
+            total = product(0, own_ref) + product(1, left_ref)
+            total = total + product(2, far_refs[i]) + product(3, right_ref)
             total_s[...] = total.astype(BF)
 
     part = wide // ny
@@ -250,36 +246,38 @@
 
 
 def weight_part(features, grads, which, my_y, z_hi, ny):
+    own, left, far, right = grads
     nx = len(features)
-    parts = len(grads)
-    rows, n = grads[0][0].shape
+    rows, n = own.shape
     wide = features[0].shape[0] // (z_hi * 2)
-    cols = min(n, 256)
-    each = n // cols
-
-    def block(i):
-        return pl.BlockSpec((rows, cols), lambda g: (0, jnp.clip(g - i * each, 0, each - 1)))
-
+    cols = min(n // 2, 256)
+    half = n // 2 // cols
+    skip = half if far[1].shape[1] < n else 0
+    block = pl.BlockSpec((rows, cols), lambda g: (0, g))
+    halves = [
+        pl.BlockSpec((rows, cols), lambda g: (0, jnp.minimum(g, half - 1))),
+        pl.BlockSpec((rows, cols), lambda g: (0, jnp.maximum(g - skip, 0))),
+    ]
     return pl.pallas_call(
-        functools.partial(weight_kernel, nx, parts, z_hi, ny),
-        grid=(parts * each,),
+        functools.partial(weight_kernel, nx, z_hi, ny),
+        grid=(2 * half,),
         in_specs=[pl.BlockSpec(memory_space=pltpu.SMEM)]
         + [whole(features[0].shape)] * nx
-        + [block(i) for i in range(parts) for _ in range(nx)],
+        + [block, block, *halves, block],
         out_specs=pl.BlockSpec((ny, z_hi, wide // ny, cols), lambda g: (0, 0, 0, g)),
-        out_shape=jax.ShapeDtypeStruct((ny, z_hi, wide // ny, parts * n), BF),
+        out_shape=jax.ShapeDtypeStruct((ny, z_hi, wide // ny, n), BF),
         scratch_shapes=[
             pltpu.VMEM((z_hi * wide, nx * rows), BF),
             pltpu.VMEM((z_hi * wide, cols), BF),
         ],
         compiler_params=pltpu.CompilerParams(vmem_limit_bytes=24 * 2**20),
         cost_estimate=pl.CostEstimate(
-            flops=2 * z_hi * wide * nx * rows * parts * n,
+            flops=2 * z_hi * wide * nx * rows * n,
             bytes_accessed=6 * 2**20,
             transcendentals=0,
         ),
         name="weight_part",
-    )(jnp.stack([which, my_y]), *features, *[g for group in grads for g in group])
+    )(jnp.stack([which, my_y]), *features, own, left, *far, right)
 
 
 def local(layer_input, queries, key_head, value_head, grad_output, doc_ids):
@@ -295,19 +293,17 @@
 
     kv = jnp.concatenate([k, v], axis=1)
     pair = jnp.stack([kv, shifted(kv, "zl", zl, 1)])
-    kv_pairs = [pair] + [shifted(pair, "y", ny, s, False) for s in range(1, ny)]
-    features = [
-        shifted(part, "x", nx, s) if s else part
-        for s, part in enumerate(split_features(x, my_x, z_hi, nx))
-    ]
+    before, after = shifted(pair, "y", ny, 1), shifted(pair, "y", ny, -1)
+    parts = split_features(x, my_x, z_hi, nx)
+    before, after, parts = lax.optimization_barrier((before, after, parts))
+    far = jnp.stack([shifted(before[0], "y", ny, 1), shifted(after[1], "y", ny, -1)])
+    kv_pairs = [pair, before, far, after]
+    features = [shifted(part, "x", nx, s) if s else part for s, part in enumerate(parts)]
 
     my_docs = lax.dynamic_slice_in_dim(docs, place * rows, rows)
     starts = jnp.sum((docs[:, None] < my_docs[None, :]).astype(jnp.int32), axis=0)
     info = jnp.stack([place - starts[0] // rows + 1, place, starts[rows - 1]])
     starts = starts[None, :]
-
-    def along_x(grads):
-        return [grads] + [shifted(grads, "x", nx, s) for s in range(1, nx)]
 
     def term(grads):
         theirs = weight_part(features, grads, 1 - my_core, my_y, z_hi, ny)
@@ -315,34 +311,48 @@
         mine = weight_part(features, grads, my_core, my_y, z_hi, ny)
         return [(mine[r].astype(F32) + theirs[r].astype(F32)).astype(BF) for r in range(ny)]
 
-    def along_y(pieces):
-        total = pieces[0].astype(F32)
-        for r in range(1, ny):
-            total = total + shifted(pieces[r], "y", ny, r).astype(F32)
-        return total.astype(BF)
-
-    dq_first, dkv = attention_half(q, do, kv_pairs, info, starts, 0, None)
-    dq_first, *features = lax.optimization_barrier((dq_first, *features))
-    first = along_x(dq_first)
-    dq_second, dkv = attention_half(q, do, kv_pairs, info, starts, 1, dkv)
-    dq_second, dkv, first = lax.optimization_barrier((dq_second, dkv, first))
-    second = along_x(dq_second)
-
-    total = dkv[0].astype(F32)
-    for s in range(1, ny):
-        total = total + shifted(dkv[s], "y", ny, -s, False).astype(F32)
+    def far_y(pieces):
+        half = pieces[2].shape[0] // 2
+        ahead = shifted(pieces[2][:half], "y", ny, 1)
+        behind = shifted(pieces[2][half:], "y", ny, -1)
+        ahead = jnp.concatenate([plus(pieces[1][:half], ahead), pieces[1][half:]])
+        behind = jnp.concatenate([pieces[3][:half], plus(pieces[3][half:], behind)])
+        return pieces[0], ahead, behind
+
+    def near_y(pieces):
+        own, ahead, behind = pieces
+        total = own.astype(F32) + shifted(ahead, "y", ny, 1).astype(F32)
+        return total + shifted(behind, "y", ny, -1).astype(F32)
+
+    dq, dkv = attention(q, do, kv_pairs, info, starts)
+    dq, dkv, features = lax.optimization_barrier((dq, dkv, features))
+    left, right = shifted(dq, "x", nx, 1), shifted(dq, "x", nx, -1)
+    total = near_y(far_y([dkv[0], dkv[3], dkv[2], dkv[1]]))
+    left, right, total = lax.optimization_barrier((left, right, total))
+    half = dq.shape[1] // 2
+    far = shifted(left[:, :half], "x", nx, 1), shifted(right[:, half:], "x", nx, -1)
     other = shifted(total[1].astype(BF), "zl", zl, 1)
     dkv_own = (total[0] + other.astype(F32)).astype(BF)
 
-    pieces = term([first, second])
-    pieces, along = lax.optimization_barrier((pieces, along_x(dkv_own)))
-    part = jnp.concatenate([along_y(pieces), along_y(term([along]))], axis=-1)
+    pieces = far_y(term((dq, left, far, right)))
+    along = [shifted(dkv_own, "x", nx, s) for s in range(1, nx)]
+    pieces, along = lax.optimization_barrier((pieces, along))
+    part = near_y(pieces).astype(BF)
+    narrow = near_y(far_y(term((dkv_own, along[0], (along[1], along[1]), along[2])))).astype(BF)
+    part = jnp.concatenate([part, narrow], axis=-1)
     n = part.shape[-1]
-    part = lax.all_to_all(part.reshape(z_hi * zl, -1, n), ("zh", "zl"), 0, 0, tiled=True)
+    part = part.reshape(z_hi, zl, -1, n)
+    my_zl, my_zh = lax.axis_index("zl"), lax.axis_index("zh")
+    kept = lax.dynamic_index_in_dim(part, my_zl, 1, keepdims=False)
+    given = shifted(lax.dynamic_index_in_dim(part, 1 - my_zl, 1, keepdims=False), "zl", zl, 1)
+    part = (kept.astype(F32) + given.astype(F32)).astype(BF)
+    weight = 0.0
+    for s in range(z_hi):
+        piece = lax.dynamic_index_in_dim(part, (my_zh + s) % z_hi, 0, keepdims=False)
+        weight = weight + (shifted(piece, "zh", z_hi, s) if s else piece).astype(F32)
     tokens = rows * ctx * nx * nc * z_hi
-    weight = jnp.sum(part.astype(F32), axis=0) * (1.0 / math.sqrt(tokens))
+    weight = weight * (1.0 / math.sqrt(tokens))
     width = q.shape[1]
-    dq = jnp.concatenate([dq_first, dq_second], axis=1)
     return (
         dq[None],
         dkv_own[None, :, :hd],

time: 143 us -> 154 us (1.077)
  waiting for transfers between devices: 44.9 us -> 54.3 us
  other arithmetic: 4.65 us -> 8.13 us
  local copies, waits for them, and re-layouts: 12.3 us -> 9.22 us
    ppermute x28 -> x34, waiting for transfers between devices: 36.1 us -> 54.3 us  [shifted(): return lax.ppermute(value, axis, pairs)]
    ppermute x28 -> x34, starting transfers between devices: 47.3 us -> 56.6 us  [shifted(): return lax.ppermute(value, axis, pairs)]
    all_to_all x1 -> x0, starting transfers between devices: 9.11 us -> none  [local(): lax.all_to_all(part.reshape(z_hi * zl, -1, n), ('zh', 'zl'), 0, 0, tiled=...]
    all_to_all x1 -> x0, waiting for transfers between devices: 8.81 us -> none  [local(): lax.all_to_all(part.reshape(z_hi * zl, -1, n), ('zh', 'zl'), 0, 0, tiled=...]
    unnamed x36 -> x18, local copies, waits for them, and re-layouts: 9.82 us -> 5.14 us
    pallas_call x6 -> x5, Pallas kernels: 17 us -> 17.7 us  [the longest x4 10.9 us: weight_part(): pl.pallas_call(functools.partial(weight_kernel, nx, z_hi, ny), grid=(2 *...]
  transfers between devices with their start and end apart: 29 -> 34, of which waited for: 15 -> 16; matrix products, arithmetic and copies ran while one was open for 3% -> 5% of each run, Pallas kernels for 13% -> 10%
where the time goes in v5:
time: 154 us; the launch traced here: 152 us
  starting transfers between devices  56.6 us (37%)
  waiting for transfers between devices  54.3 us (35%)
  Pallas kernels  20 us (13%)
  local copies, waits for them, and re-layouts  9.22 us (6%)
  other arithmetic  8.13 us (5%)
  between operations  3.63 us (2%)
    ppermute x34, starting transfers between devices, shifted(): return lax.ppermute(value, axis, pairs)  56.6 us
    ppermute x34, waiting for transfers between devices, shifted(): return lax.ppermute(value, axis, pairs)  54.3 us
    pallas_call x4, Pallas kernels, weight_part(): pl.pallas_call(functools.partial(weight_kernel, nx, z_hi, ny), grid=(2 *...  10.9 us
    pallas_call x1, Pallas kernels, attention(): pl.pallas_call(functools.partial(attention_kernel, ny, per, hd ** (-0.5))...  6.8 us
    unnamed x18, local copies, waits for them, and re-layouts  5.14 us
  transfers between devices with their start and end apart: 34, of which 16 were waited for; matrix products, arithmetic and copies ran while one was open for 5% of the time, Pallas kernels for 10%

profile of v5, /device:TPU:32, one launch (start us, length us, event | category | flops | bytes accessed | tf_op | source)
XLA Modules:
  0.0 151.8 jit_solution(9075429074619667773)
XLA Ops:
  3.5 3.4 %collective-permute-done = bf16[256,256]{1,0:T(8,128)(2,1)S(1)} collective-permute-done((bf16[256,256]{1,0:T(8,128)(2,1)S(1)}, bf16[256,256]{1,0:T(8,128)(2,1)S(1)}, u32[]{:S(2)}, u32[]{:S(2)}) %collective-permute-start) | collective-permute-done | bytes 131104 | tf_op jit(solution)/shard_map/ppermute | solution.py:32
  15.4 3.1 %collective-permute-start.4 = (bf16[256,256]{1,0:T(8,128)(2,1)S(1)}, bf16[256,256]{1,0:T(8,128)(2,1)S(1)}, u32[]{:S(2)}, u32[]{:S(2)}) collective-permute-start(bf16[256,256]{1,0:T(8,128)(2,1)S(1)} %slice_bitcast_fusion.6), channel_id=1, source_target_pairs={{0,6},{2,0},{4,2},{6,4},{1,7},{3,1},{5,3},{7,5},{8,14},{10,8},{12,... | collective-permute-start | bytes 393224 | tf_op jit(solution)/shard_map/ppermute | solution.py:32
  24.1 2.7 %collective-permute-start.6 = (bf16[1024,256]{1,0:T(8,128)(2,1)}, bf16[1024,256]{1,0:T(8,128)(2,1)S(1)}, u32[]{:S(2)}, u32[]{:S(2)}) collective-permute-start(bf16[1024,256]{1,0:T(8,128)(2,1)} %get-tuple-element.52), channel_id=1, source_target_pairs={{0,32},{16,48},{32,0},{48,16},{1,33},{17,49},{33,1},{49,17},{2,34}... | collective-permute-start | bytes 1572872 | tf_op jit(solution)/shard_map/ppermute | solution.py:32
  29.2 6.8 %attention_backward.1 = (bf16[256,1024]{1,0:T(8,128)(2,1)}, bf16[2,256,256]{2,1,0:T(8,128)(2,1)S(1)}, bf16[2,256,256]{2,1,0:T(8,128)(2,1)S(1)}, bf16[2,256,256]{2,1,0:T(8,128)(2,1)S(1)}, bf16[2,256,256]{2,1,0:T(8,128)(2,1)S(1)}) custom-call(s32[3]{0:T(128)S(1)} %pad_add_fusion.info, s32[1,256]{1,0:T(1,128)S(1)} %bitcast.100, bf16[256,1024]{1,0:T(8,128)(2,1)} %bitcast.109, ...), custom_call_target="tpu_custom_call" | custom-call | flops 5368709120 | bytes 4194304 | tf_op jit(solution)/shard_map/attention_backward/pallas_call | solution.py:152
  37.9 9.8 %collective-permute-done.6.refs_2_ = bf16[1024,256]{1,0:T(8,128)(2,1)S(1)} collective-permute-done((bf16[1024,256]{1,0:T(8,128)(2,1)}, bf16[1024,256]{1,0:T(8,128)(2,1)S(1)}, u32[]{:S(2)}, u32[]{:S(2)}) %collective-permute-start.6) | collective-permute-done | bytes 524320 | tf_op jit(solution)/shard_map/ppermute | solution.py:32
  47.7 3.1 %collective-permute-start.12 = (bf16[1,256,256]{2,1,0:T(8,128)(2,1)S(1)}, bf16[1,256,256]{2,1,0:T(8,128)(2,1)S(1)}, u32[]{:S(2)}, u32[]{:S(2)}) collective-permute-start(bf16[1,256,256]{2,1,0:T(8,128)(2,1)S(1)} %get-tuple-element.82), channel_id=1, source_target_pairs={{0,6},{2,0},{4,2},{6,4},{1,7},{3,1},{5,3},{7,5},{8,14},{10,8},{12,... | collective-permute-start | bytes 393224 | tf_op jit(solution)/shard_map/ppermute | solution.py:32
  54.3 3.3 %collective-permute-start.13 = (bf16[2,256,256]{2,1,0:T(8,128)(2,1)S(1)}, bf16[2,256,256]{2,1,0:T(8,128)(2,1)S(1)}, u32[]{:S(2)}, u32[]{:S(2)}) collective-permute-start(bf16[2,256,256]{2,1,0:T(8,128)(2,1)S(1)} %pad_maximum_fusion.4), channel_id=1, source_target_pairs={{0,6},{2,0},{4,2},{6,4},{1,7},{3,1},{5,3},{7,5},{8,14},{10,8},{12,... | collective-permute-start | bytes 786440 | tf_op jit(solution)/shard_map/ppermute | solution.py:32
  57.6 2.8 %collective-permute-done.10 = bf16[1,256,256]{2,1,0:T(8,128)(2,1)S(1)} collective-permute-done((bf16[1,256,256]{2,1,0:T(8,128)(2,1)S(1)}, bf16[1,256,256]{2,1,0:T(8,128)(2,1)S(1)}, u32[]{:S(2)}, u32[]{:S(2)}) %collective-permute-start.10) | collective-permute-done | bytes 131104 | tf_op jit(solution)/shard_map/ppermute | solution.py:32
  61.5 6.6 %collective-permute-done.11 = bf16[2,256,256]{2,1,0:T(8,128)(2,1)S(1)} collective-permute-done((bf16[2,256,256]{2,1,0:T(8,128)(2,1)S(1)}, bf16[2,256,256]{2,1,0:T(8,128)(2,1)S(1)}, u32[]{:S(2)}, u32[]{:S(2)}) %collective-permute-start.11) | collective-permute-done | bytes 262176 | tf_op jit(solution)/shard_map/ppermute | solution.py:32
  70.4 3.2 %collective-permute-start.16 = (bf16[256,512]{1,0:T(8,128)(2,1)}, bf16[256,512]{1,0:T(8,128)(2,1)}, u32[]{:S(2)}, u32[]{:S(2)}) collective-permute-start(bf16[256,512]{1,0:T(8,128)(2,1)} %slice.185), channel_id=1, source_target_pairs={{0,48},{16,0},{32,16},{48,32},{1,49},{17,1},{33,17},{49,33},{2,50}... | collective-permute-start | bytes 786440 | tf_op jit(solution)/shard_map/ppermute | solution.py:32
  73.7 3.8 %collective-permute-done.15.refs_6_ = bf16[256,512]{1,0:T(8,128)(2,1)S(1)} collective-permute-done((bf16[256,512]{1,0:T(8,128)(2,1)}, bf16[256,512]{1,0:T(8,128)(2,1)S(1)}, u32[]{:S(2)}, u32[]{:S(2)}) %collective-permute-start.15) | collective-permute-done | bytes 262176 | tf_op jit(solution)/shard_map/ppermute | solution.py:32
  78.9 3.8 %weight_part.5 = bf16[4,4,32,1024]{3,2,1,0:T(8,128)(2,1)S(1)} custom-call(s32[2]{0:T(128)S(1)} %pad_add_fusion.2.info, bf16[1024,256]{1,0:T(8,128)(2,1)S(1)} %get-tuple-element.60.refs_0_, bf16[1024,256]{1,0:T(8,128)(2,1)S(1)} %collective-permute-done.5.refs_1_, bf16[1024,256]{1,0:T(8,128)(2,1)S(1)} %collective-permute-done.6.refs_2_, ...), custom_call_target="tpu_custom_call" | custom-call | flops 1073741824 | bytes 6291456 | tf_op jit(solution)/shard_map/weight_part/pallas_call | solution.py:261
  83.6 5.2 %collective-permute-done.14 = bf16[256,256]{1,0:T(8,128)(2,1)S(1)} collective-permute-done((bf16[256,256]{1,0:T(8,128)(2,1)S(1)}, bf16[256,256]{1,0:T(8,128)(2,1)S(1)}, u32[]{:S(2)}, u32[]{:S(2)}) %collective-permute-start.14) | collective-permute-done | bytes 131104 | tf_op jit(solution)/shard_map/ppermute | solution.py:32
  89.4 4.6 %collective-permute-start.21 = (bf16[256,256]{1,0:T(8,128)(2,1)S(1)}, bf16[256,256]{1,0:T(8,128)(2,1)S(1)}, u32[]{:S(2)}, u32[]{:S(2)}) collective-permute-start(bf16[256,256]{1,0:T(8,128)(2,1)S(1)} %fusion.4.refs_4_), channel_id=1, source_target_pairs={{0,32},{16,48},{32,0},{48,16},{1,33},{17,49},{33,1},{49,17},{2,34}... | collective-permute-start | bytes 393224 | tf_op jit(solution)/shard_map/ppermute | solution.py:32
  95.0 3.7 %weight_part.4 = bf16[4,4,32,1024]{3,2,1,0:T(8,128)(2,1)S(1)} custom-call(s32[2]{0:T(128)S(1)} %pad_add_fusion.1.info, bf16[1024,256]{1,0:T(8,128)(2,1)S(1)} %get-tuple-element.60.refs_0_, bf16[1024,256]{1,0:T(8,128)(2,1)S(1)} %collective-permute-done.5.refs_1_, bf16[1024,256]{1,0:T(8,128)(2,1)S(1)} %collective-permute-done.6.refs_2_, ...), custom_call_target="tpu_custom_call" | custom-call | flops 1073741824 | bytes 6291456 | tf_op jit(solution)/shard_map/weight_part/pallas_call | solution.py:261
  99.3 3.2 %collective-permute-start.19 = (bf16[2,32,1024]{2,1,0:T(8,128)(2,1)S(1)}, bf16[2,32,1024]{2,1,0:T(8,128)(2,1)S(1)}, u32[]{:S(2)}, u32[]{:S(2)}) collective-permute-start(bf16[2,32,1024]{2,1,0:T(8,128)(2,1)S(1)} %get-tuple-element.79), channel_id=1, source_target_pairs={{0,6},{2,0},{4,2},{6,4},{1,7},{3,1},{5,3},{7,5},{8,14},{10,8},{12,... | collective-permute-start | bytes 393224 | tf_op jit(solution)/shard_map/ppermute | solution.py:32
  102.5 2.9 %collective-permute-done.18 = bf16[2,32,1024]{2,1,0:T(8,128)(2,1)S(1)} collective-permute-done((bf16[2,32,1024]{2,1,0:T(8,128)(2,1)S(1)}, bf16[2,32,1024]{2,1,0:T(8,128)(2,1)S(1)}, u32[]{:S(2)}, u32[]{:S(2)}) %collective-permute-start.18) | collective-permute-done | bytes 131104 | tf_op jit(solution)/shard_map/ppermute | solution.py:32
  109.4 3.2 %collective-permute-start.24 = (bf16[4,32,1024]{2,1,0:T(8,128)(2,1)}, bf16[4,32,1024]{2,1,0:T(8,128)(2,1)S(1)}, u32[]{:S(2)}, u32[]{:S(2)}) collective-permute-start(bf16[4,32,1024]{2,1,0:T(8,128)(2,1)} %pad_maximum_fusion.6), channel_id=1, source_target_pairs={{0,6},{2,0},{4,2},{6,4},{1,7},{3,1},{5,3},{7,5},{8,14},{10,8},{12,... | collective-permute-start | bytes 786440 | tf_op jit(solution)/shard_map/ppermute | solution.py:32
  116.2 3.3 %collective-permute-start.28 = (bf16[2,32,256]{2,1,0:T(8,128)(2,1)S(1)}, bf16[2,32,256]{2,1,0:T(8,128)(2,1)S(1)}, u32[]{:S(2)}, u32[]{:S(2)}) collective-permute-start(bf16[2,32,256]{2,1,0:T(8,128)(2,1)S(1)} %get-tuple-element.93), channel_id=1, source_target_pairs={{0,6},{2,0},{4,2},{6,4},{1,7},{3,1},{5,3},{7,5},{8,14},{10,8},{12,... | collective-permute-start | bytes 98312 | tf_op jit(solution)/shard_map/ppermute | solution.py:32
  121.1 3.6 %collective-permute-start.29 = (bf16[4,32,256]{2,1,0:T(8,128)(2,1)S(1)}, bf16[4,32,256]{2,1,0:T(8,128)(2,1)S(1)}, u32[]{:S(2)}, u32[]{:S(2)}) collective-permute-start(bf16[4,32,256]{2,1,0:T(8,128)(2,1)S(1)} %pad_maximum_fusion.9), channel_id=1, source_target_pairs={{0,6},{2,0},{4,2},{6,4},{1,7},{3,1},{5,3},{7,5},{8,14},{10,8},{12,... | collective-permute-start | bytes 196616 | tf_op jit(solution)/shard_map/ppermute | solution.py:32
  126.6 3.7 %collective-permute-done.27 = bf16[4,32,256]{2,1,0:T(8,128)(2,1)S(1)} collective-permute-done((bf16[4,32,256]{2,1,0:T(8,128)(2,1)S(1)}, bf16[4,32,256]{2,1,0:T(8,128)(2,1)S(1)}, u32[]{:S(2)}, u32[]{:S(2)}) %collective-permute-start.27) | collective-permute-done | bytes 65568 | tf_op jit(solution)/shard_map/ppermute | solution.py:32
  131.9 4.7 %collective-permute-done.30 = bf16[4,16,1280]{2,1,0:T(8,128)(2,1)S(1)} collective-permute-done((bf16[4,16,1280]{2,1,0:T(8,128)(2,1)S(1)}, bf16[4,16,1280]{2,1,0:T(8,128)(2,1)S(1)}, u32[]{:S(2)}, u32[]{:S(2)}) %collective-permute-start.30) | collective-permute-done | bytes 163872 | tf_op jit(solution)/shard_map/ppermute | solution.py:32
  136.7 5.9 %collective-permute-start.33 = (bf16[16,1280]{1,0:T(8,128)(2,1)S(1)}, bf16[16,1280]{1,0:T(8,128)(2,1)S(1)}, u32[]{:S(2)}, u32[]{:S(2)}) collective-permute-start(bf16[16,1280]{1,0:T(8,128)(2,1)S(1)} %get-tuple-element.84), channel_id=1, source_target_pairs={{0,192},{64,0},{128,64},{192,128},{1,193},{65,1},{129,65},{193,129... | collective-permute-start | bytes 122888 | tf_op jit(solution)/shard_map/ppermute | solution.py:32
  146.7 3.9 %collective-permute-done.32 = bf16[16,1280]{1,0:T(8,128)(2,1)S(1)} collective-permute-done((bf16[16,1280]{1,0:T(8,128)(2,1)S(1)}, bf16[16,1280]{1,0:T(8,128)(2,1)S(1)}, u32[]{:S(2)}, u32[]{:S(2)}) %collective-permute-start.32) | collective-permute-done | bytes 40992 | tf_op jit(solution)/shard_map/ppermute | solution.py:32
  (116 shorter events, 47.7 us)
Async XLA Ops:
  6.9 8.5 %collective-permute-start.1 = (bf16[2,256,256]{2,1,0:T(8,128)(2,1)S(1)}, bf16[2,256,256]{2,1,0:T(8,128)(2,1)S(1)}, u32[]{:S(2)}, u32[]{:S(2)}) collective-permute-start(bf16[2,256,256]{2,1,0:T(8,128)(2,1)S(1)} %pad_maximum_fusion.1.refs_0_), channel_id=1, source_target_pairs={{0,2},{2,4},{4,6},{6,0},{1,3},{3,5},{5,7},{7,1},{8,10},{10,12},{12... | collective-permute-start | bytes 786440 | tf_op jit(solution)/shard_map/ppermute | solution.py:32
  8.5 6.9 %collective-permute-start.2 = (bf16[2,256,256]{2,1,0:T(8,128)(2,1)S(1)}, bf16[2,256,256]{2,1,0:T(8,128)(2,1)S(1)}, u32[]{:S(2)}, u32[]{:S(2)}) collective-permute-start(bf16[2,256,256]{2,1,0:T(8,128)(2,1)S(1)} %pad_maximum_fusion.1.refs_0_), channel_id=1, source_target_pairs={{0,6},{2,0},{4,2},{6,4},{1,7},{3,1},{5,3},{7,5},{8,14},{10,8},{12,... | collective-permute-start | bytes 786440 | tf_op jit(solution)/shard_map/ppermute | solution.py:32
  15.4 12.8 %collective-permute-start.4 = (bf16[256,256]{1,0:T(8,128)(2,1)S(1)}, bf16[256,256]{1,0:T(8,128)(2,1)S(1)}, u32[]{:S(2)}, u32[]{:S(2)}) collective-permute-start(bf16[256,256]{1,0:T(8,128)(2,1)S(1)} %slice_bitcast_fusion.6), channel_id=1, source_target_pairs={{0,6},{2,0},{4,2},{6,4},{1,7},{3,1},{5,3},{7,5},{8,14},{10,8},{12,... | collective-permute-start | bytes 393224 | tf_op jit(solution)/shard_map/ppermute | solution.py:32
  18.6 9.7 %collective-permute-start.3 = (bf16[256,256]{1,0:T(8,128)(2,1)S(1)}, bf16[256,256]{1,0:T(8,128)(2,1)}, u32[]{:S(2)}, u32[]{:S(2)}) collective-permute-start(bf16[256,256]{1,0:T(8,128)(2,1)S(1)} %slice_bitcast_fusion.7), channel_id=1, source_target_pairs={{0,2},{2,4},{4,6},{6,0},{1,3},{3,5},{5,7},{7,1},{8,10},{10,12},{12... | collective-permute-start | bytes 393224 | tf_op jit(solution)/shard_map/ppermute | solution.py:32
  22.6 15.3 %collective-permute-start.5 = (bf16[1024,256]{1,0:T(8,128)(2,1)}, bf16[1024,256]{1,0:T(8,128)(2,1)S(1)}, u32[]{:S(2)}, u32[]{:S(2)}) collective-permute-start(bf16[1024,256]{1,0:T(8,128)(2,1)} %get-tuple-element.51), channel_id=1, source_target_pairs={{0,16},{16,32},{32,48},{48,0},{1,17},{17,33},{33,49},{49,1},{2,18}... | collective-permute-start | bytes 1572872 | tf_op jit(solution)/shard_map/ppermute | solution.py:32
  24.1 23.6 %collective-permute-start.6 = (bf16[1024,256]{1,0:T(8,128)(2,1)}, bf16[1024,256]{1,0:T(8,128)(2,1)S(1)}, u32[]{:S(2)}, u32[]{:S(2)}) collective-permute-start(bf16[1024,256]{1,0:T(8,128)(2,1)} %get-tuple-element.52), channel_id=1, source_target_pairs={{0,32},{16,48},{32,0},{48,16},{1,33},{17,49},{33,1},{49,17},{2,34}... | collective-permute-start | bytes 1572872 | tf_op jit(solution)/shard_map/ppermute | solution.py:32
  26.8 20.9 %collective-permute-start.7 = (bf16[1024,256]{1,0:T(8,128)(2,1)S(1)}, bf16[1024,256]{1,0:T(8,128)(2,1)S(1)}, u32[]{:S(2)}, u32[]{:S(2)}) collective-permute-start(bf16[1024,256]{1,0:T(8,128)(2,1)S(1)} %get-tuple-element.53), channel_id=1, source_target_pairs={{0,48},{16,0},{32,16},{48,32},{1,49},{17,1},{33,17},{49,33},{2,50}... | collective-permute-start | bytes 1572872 | tf_op jit(solution)/shard_map/ppermute | solution.py:32
  47.7 6.5 %collective-permute-start.12 = (bf16[1,256,256]{2,1,0:T(8,128)(2,1)S(1)}, bf16[1,256,256]{2,1,0:T(8,128)(2,1)S(1)}, u32[]{:S(2)}, u32[]{:S(2)}) collective-permute-start(bf16[1,256,256]{2,1,0:T(8,128)(2,1)S(1)} %get-tuple-element.82), channel_id=1, source_target_pairs={{0,6},{2,0},{4,2},{6,4},{1,7},{3,1},{5,3},{7,5},{8,14},{10,8},{12,... | collective-permute-start | bytes 393224 | tf_op jit(solution)/shard_map/ppermute | solution.py:32
  50.8 18.1 %collective-permute-start.8 = (bf16[256,1024]{1,0:T(8,128)(2,1)}, bf16[256,1024]{1,0:T(8,128)(2,1)S(1)}, u32[]{:S(2)}, u32[]{:S(2)}) collective-permute-start(bf16[256,1024]{1,0:T(8,128)(2,1)} %get-tuple-element.54.refs_4_), channel_id=1, source_target_pairs={{0,16},{16,32},{32,48},{48,0},{1,17},{17,33},{33,49},{49,1},{2,18}... | collective-permute-start | bytes 1572872 | tf_op jit(solution)/shard_map/ppermute | solution.py:32
  51.9 17.1 %collective-permute-start.9 = (bf16[256,1024]{1,0:T(8,128)(2,1)}, bf16[256,1024]{1,0:T(8,128)(2,1)S(1)}, u32[]{:S(2)}, u32[]{:S(2)}) collective-permute-start(bf16[256,1024]{1,0:T(8,128)(2,1)} %get-tuple-element.54.refs_4_), channel_id=1, source_target_pairs={{0,48},{16,0},{32,16},{48,32},{1,49},{17,1},{33,17},{49,33},{2,50}... | collective-permute-start | bytes 1572872 | tf_op jit(solution)/shard_map/ppermute | solution.py:32
  54.1 6.3 %collective-permute-start.10 = (bf16[1,256,256]{2,1,0:T(8,128)(2,1)S(1)}, bf16[1,256,256]{2,1,0:T(8,128)(2,1)S(1)}, u32[]{:S(2)}, u32[]{:S(2)}) collective-permute-start(bf16[1,256,256]{2,1,0:T(8,128)(2,1)S(1)} %get-tuple-element.81), channel_id=1, source_target_pairs={{0,2},{2,4},{4,6},{6,0},{1,3},{3,5},{5,7},{7,1},{8,10},{10,12},{12... | collective-permute-start | bytes 393224 | tf_op jit(solution)/shard_map/ppermute | solution.py:32
  54.3 7.2 %collective-permute-start.13 = (bf16[2,256,256]{2,1,0:T(8,128)(2,1)S(1)}, bf16[2,256,256]{2,1,0:T(8,128)(2,1)S(1)}, u32[]{:S(2)}, u32[]{:S(2)}) collective-permute-start(bf16[2,256,256]{2,1,0:T(8,128)(2,1)S(1)} %pad_maximum_fusion.4), channel_id=1, source_target_pairs={{0,6},{2,0},{4,2},{6,4},{1,7},{3,1},{5,3},{7,5},{8,14},{10,8},{12,... | collective-permute-start | bytes 786440 | tf_op jit(solution)/shard_map/ppermute | solution.py:32
  60.4 7.7 %collective-permute-start.11 = (bf16[2,256,256]{2,1,0:T(8,128)(2,1)S(1)}, bf16[2,256,256]{2,1,0:T(8,128)(2,1)S(1)}, u32[]{:S(2)}, u32[]{:S(2)}) collective-permute-start(bf16[2,256,256]{2,1,0:T(8,128)(2,1)S(1)} %pad_maximum_fusion.3), channel_id=1, source_target_pairs={{0,2},{2,4},{4,6},{6,0},{1,3},{3,5},{5,7},{7,1},{8,10},{10,12},{12... | collective-permute-start | bytes 786440 | tf_op jit(solution)/shard_map/ppermute | solution.py:32
  69.7 7.8 %collective-permute-start.15 = (bf16[256,512]{1,0:T(8,128)(2,1)}, bf16[256,512]{1,0:T(8,128)(2,1)S(1)}, u32[]{:S(2)}, u32[]{:S(2)}) collective-permute-start(bf16[256,512]{1,0:T(8,128)(2,1)} %slice.184), channel_id=1, source_target_pairs={{0,16},{16,32},{32,48},{48,0},{1,17},{17,33},{33,49},{49,1},{2,18}... | collective-permute-start | bytes 786440 | tf_op jit(solution)/shard_map/ppermute | solution.py:32
  70.4 7.4 %collective-permute-start.16 = (bf16[256,512]{1,0:T(8,128)(2,1)}, bf16[256,512]{1,0:T(8,128)(2,1)}, u32[]{:S(2)}, u32[]{:S(2)}) collective-permute-start(bf16[256,512]{1,0:T(8,128)(2,1)} %slice.185), channel_id=1, source_target_pairs={{0,48},{16,0},{32,16},{48,32},{1,49},{17,1},{33,17},{49,33},{2,50}... | collective-permute-start | bytes 786440 | tf_op jit(solution)/shard_map/ppermute | solution.py:32
  82.7 16.1 %collective-permute-start.17 = (bf16[4,4,32,1024]{3,2,1,0:T(8,128)(2,1)S(1)}, bf16[4,4,32,1024]{3,2,1,0:T(8,128)(2,1)S(1)}, u32[]{:S(2)}, u32[]{:S(2)}) collective-permute-start(bf16[4,4,32,1024]{3,2,1,0:T(8,128)(2,1)S(1)} %weight_part.5), channel_id=1, source_target_pairs={{0,8},{8,0},{1,9},{9,1},{2,10},{10,2},{3,11},{11,3},{4,12},{12,4},... | collective-permute-start | bytes 3145736 | tf_op jit(solution)/shard_map/ppermute | solution.py:32
  88.8 18.2 %collective-permute-start.20 = (bf16[256,256]{1,0:T(8,128)(2,1)S(1)}, bf16[256,256]{1,0:T(8,128)(2,1)S(1)}, u32[]{:S(2)}, u32[]{:S(2)}) collective-permute-start(bf16[256,256]{1,0:T(8,128)(2,1)S(1)} %fusion.4.refs_4_), channel_id=1, source_target_pairs={{0,16},{16,32},{32,48},{48,0},{1,17},{17,33},{33,49},{49,1},{2,18}... | collective-permute-start | bytes 393224 | tf_op jit(solution)/shard_map/ppermute | solution.py:32
  89.4 17.6 %collective-permute-start.21 = (bf16[256,256]{1,0:T(8,128)(2,1)S(1)}, bf16[256,256]{1,0:T(8,128)(2,1)S(1)}, u32[]{:S(2)}, u32[]{:S(2)}) collective-permute-start(bf16[256,256]{1,0:T(8,128)(2,1)S(1)} %fusion.4.refs_4_), channel_id=1, source_target_pairs={{0,32},{16,48},{32,0},{48,16},{1,33},{17,49},{33,1},{49,17},{2,34}... | collective-permute-start | bytes 393224 | tf_op jit(solution)/shard_map/ppermute | solution.py:32
  94.1 13.0 %collective-permute-start.22 = (bf16[256,256]{1,0:T(8,128)(2,1)S(1)}, bf16[256,256]{1,0:T(8,128)(2,1)S(1)}, u32[]{:S(2)}, u32[]{:S(2)}) collective-permute-start(bf16[256,256]{1,0:T(8,128)(2,1)S(1)} %fusion.4.refs_4_), channel_id=1, source_target_pairs={{0,48},{16,0},{32,16},{48,32},{1,49},{17,1},{33,17},{49,33},{2,50}... | collective-permute-start | bytes 393224 | tf_op jit(solution)/shard_map/ppermute | solution.py:32
  109.4 15.4 %collective-permute-start.24 = (bf16[4,32,1024]{2,1,0:T(8,128)(2,1)}, bf16[4,32,1024]{2,1,0:T(8,128)(2,1)S(1)}, u32[]{:S(2)}, u32[]{:S(2)}) collective-permute-start(bf16[4,32,1024]{2,1,0:T(8,128)(2,1)} %pad_maximum_fusion.6), channel_id=1, source_target_pairs={{0,6},{2,0},{4,2},{6,4},{1,7},{3,1},{5,3},{7,5},{8,14},{10,8},{12,... | collective-permute-start | bytes 786440 | tf_op jit(solution)/shard_map/ppermute | solution.py:32
  112.6 12.3 %collective-permute-start.23 = (bf16[4,32,1024]{2,1,0:T(8,128)(2,1)}, bf16[4,32,1024]{2,1,0:T(8,128)(2,1)S(1)}, u32[]{:S(2)}, u32[]{:S(2)}) collective-permute-start(bf16[4,32,1024]{2,1,0:T(8,128)(2,1)} %pad_maximum_fusion.5), channel_id=1, source_target_pairs={{0,2},{2,4},{4,6},{6,0},{1,3},{3,5},{5,7},{7,1},{8,10},{10,12},{12... | collective-permute-start | bytes 786440 | tf_op jit(solution)/shard_map/ppermute | solution.py:32
  136.7 9.9 %collective-permute-start.33 = (bf16[16,1280]{1,0:T(8,128)(2,1)S(1)}, bf16[16,1280]{1,0:T(8,128)(2,1)S(1)}, u32[]{:S(2)}, u32[]{:S(2)}) collective-permute-start(bf16[16,1280]{1,0:T(8,128)(2,1)S(1)} %get-tuple-element.84), channel_id=1, source_target_pairs={{0,192},{64,0},{128,64},{192,128},{1,193},{65,1},{129,65},{193,129... | collective-permute-start | bytes 122888 | tf_op jit(solution)/shard_map/ppermute | solution.py:32
  142.6 7.9 %collective-permute-start.32 = (bf16[16,1280]{1,0:T(8,128)(2,1)S(1)}, bf16[16,1280]{1,0:T(8,128)(2,1)S(1)}, u32[]{:S(2)}, u32[]{:S(2)}) collective-permute-start(bf16[16,1280]{1,0:T(8,128)(2,1)S(1)} %get-tuple-element.85), channel_id=1, source_target_pairs={{0,128},{64,192},{128,0},{192,64},{1,129},{65,193},{129,1},{193,65... | collective-permute-start | bytes 122888 | tf_op jit(solution)/shard_map/ppermute | solution.py:32
  143.6 6.9 %collective-permute-start.31 = (bf16[16,1280]{1,0:T(8,128)(2,1)S(1)}, bf16[16,1280]{1,0:T(8,128)(2,1)S(1)}, u32[]{:S(2)}, u32[]{:S(2)}) collective-permute-start(bf16[16,1280]{1,0:T(8,128)(2,1)S(1)} %get-tuple-element.83), channel_id=1, source_target_pairs={{0,64},{64,128},{128,192},{192,0},{1,65},{65,129},{129,193},{193,1... | collective-permute-start | bytes 122888 | tf_op jit(solution)/shard_map/ppermute | solution.py:32
  (19 other events, 79.1 us)

commit v6 on v5

--- a/solution.py
+++ b/solution.py
@@ -43,7 +43,7 @@
 def attention_kernel(ny, per, scale, info, starts_ref, q_ref, do_ref, *refs):
     kv_refs, refs = refs[:ny], refs[ny:]
     dq_ref, refs = refs[0], refs[1:]
-    out_refs, refs = refs[:ny], refs[ny:]
+    out_ref, refs = refs[0], refs[1:]
     kv_s, kt_s, acc_s, e_s, dp_s, md_s, stat_s, dqt_s, qt_s, dot_s, p_s, ds_s, qk_s, dk_s, sem = refs
     rows = q_ref.shape[0]
     hd = kt_s.shape[1]
@@ -119,25 +119,22 @@
     delta = [stat_s[2, h] * inverse[h] for h in range(per)]
 
     def second(d, carry):
-        at = slot(d)
+        at = place - d
         for h in range(per):
             p = e_s[d, h] * (jnp.exp2((md_s[d, h] - tops[h]) * power) * inverse[h])
             p_s[:, h * rows : (h + 1) * rows] = p.astype(BF)
             ds_s[:, h * rows : (h + 1) * rows] = (p * (dp_s[d, h] - delta[h])).astype(BF)
         acc_s[at, :, hd:] += dot(p_s[...], dk_s[...])
         acc_s[at, :, :hd] += dot(ds_s[...], qk_s[...])
-        dqt_s[...] += dot(kt_s[at], ds_s[...])
+        dqt_s[...] += dot(kt_s[slot(d)], ds_s[...])
         return carry
 
     lax.fori_loop(0, used, second, 0)
 
     for h in range(per):
         dq_ref[:, h * hd : (h + 1) * hd] = (dqt_s[:, h * rows : (h + 1) * rows].T * scale).astype(BF)
-    for s in range(ny):
-        for k in range(2):
-            at = 2 * s + k
-            out_refs[s][k, :, :hd] = (acc_s[at, :, :hd] * scale).astype(BF)
-            out_refs[s][k, :, hd:] = acc_s[at, :, hd:].astype(BF)
+    out_ref[:, :, :hd] = (acc_s[:, :, :hd] * scale).astype(BF)
+    out_ref[:, :, hd:] = acc_s[:, :, hd:].astype(BF)
 
 
 def attention(q, do, kv, info, starts):
@@ -149,13 +146,16 @@
     blocks = 2 * ny
     slab = whole((rows, width))
     pair = kv[0].shape
-    outs = pl.pallas_call(
+    return pl.pallas_call(
         functools.partial(attention_kernel, ny, per, hd ** (-0.5)),
         grid=(1,),
         in_specs=[pl.BlockSpec(memory_space=pltpu.SMEM), whole((1, rows)), slab, slab]
         + [pl.BlockSpec(memory_space=pl.ANY)] * ny,
-        out_specs=[whole((rows, width))] + [whole(pair)] * ny,
-        out_shape=[jax.ShapeDtypeStruct((rows, width), BF)] + [jax.ShapeDtypeStruct(pair, BF)] * ny,
+        out_specs=[whole((rows, width)), whole((blocks, *pair[1:]))],
+        out_shape=[
+            jax.ShapeDtypeStruct((rows, width), BF),
+            jax.ShapeDtypeStruct((blocks, *pair[1:]), BF),
+        ],
         scratch_shapes=[
             pltpu.VMEM((blocks, rows, 2 * hd), BF),
             pltpu.VMEM((blocks, hd, rows), BF),
@@ -181,7 +181,6 @@
         ),
         name="attention_backward",
     )(info, starts, q, do, *kv)
-    return outs[0], outs[1:]
 
 
 def split_kernel(info, *refs):
@@ -211,73 +210,71 @@
     )(my_x[None], *([x] * nx))
 
 
-def weight_kernel(nx, z_hi, ny, info, *refs):
-    f_refs, g_refs, (out_ref, ft_s, total_s) = refs[:nx], refs[nx:-3], refs[-3:]
-    own_ref, left_ref, far_refs, right_ref = g_refs[0], g_refs[1], g_refs[2:4], g_refs[4]
+def weight_kernel(nx, z_hi, narrow, info, *refs):
+    f_refs, wide_refs, narrow_refs = refs[:nx], refs[nx : 2 * nx], refs[2 * nx : 3 * nx]
+    out_ref, ft_s, sem = refs[3 * nx :]
     rows = f_refs[0].shape[1]
-    wide = f_refs[0].shape[0] // (z_hi * 2)
-    which, my_y = info[0], info[1]
+    each = f_refs[0].shape[0] // (z_hi * 2)
     step = pl.program_id(0)
-    half = pl.num_programs(0) // 2
+
+    def fetch(s, z):
+        at = pl.multiple_of((z * 2 + info[0]) * each, each)
+        into = ft_s.at[s, pl.ds(z * each, each)]
+        return pltpu.make_async_copy(f_refs[s].at[pl.ds(at, each)], into, sem.at[s, z])
 
     @pl.when(step == 0)
     def _():
         for s in range(nx):
             for z in range(z_hi):
-                at = pl.multiple_of((z * 2 + which) * wide, wide)
-                ft_s[z * wide : (z + 1) * wide, s * rows : (s + 1) * rows] = f_refs[s][pl.ds(at, wide)]
-
-    def product(s, ref):
-        return dot(ft_s[:, s * rows : (s + 1) * rows], ref[...])
-
-    for i in range(2):
-
-        @pl.when(step // half == i)
-        def _():
-            total = product(0, own_ref) + product(1, left_ref)
-            total = total + product(2, far_refs[i]) + product(3, right_ref)
-            total_s[...] = total.astype(BF)
-
-    part = wide // ny
-    for z in range(z_hi):
-        for r in range(ny):
-            at = pl.multiple_of(z * wide + (my_y + r) % ny * part, part)
-            out_ref[r, z] = total_s[pl.ds(at, part)]
-
-
-def weight_part(features, grads, which, my_y, z_hi, ny):
-    own, left, far, right = grads
+                fetch(s, z).start()
+        for s in range(nx):
+            for z in range(z_hi):
+                fetch(s, z).wait()
+
+    def store(g_refs):
+        total = dot(ft_s[0], g_refs[0][...])
+        for s in range(1, nx):
+            total += dot(ft_s[s], g_refs[s][...])
+        total = total.astype(BF)
+        part = out_ref.shape[2]
+        for z in range(z_hi):
+            for p in range(out_ref.shape[0]):
+                at = z * each + p * part
+                out_ref[p, z] = total[at : at + part]
+
+    first_narrow = pl.num_programs(0) - narrow
+    pl.when(step < first_narrow)(lambda: store(wide_refs))
+    pl.when(step >= first_narrow)(lambda: store(narrow_refs))
+
+
+def weight_part(features, wide, narrow, which, z_hi, pieces):
     nx = len(features)
-    rows, n = own.shape
-    wide = features[0].shape[0] // (z_hi * 2)
-    cols = min(n // 2, 256)
-    half = n // 2 // cols
-    skip = half if far[1].shape[1] < n else 0
-    block = pl.BlockSpec((rows, cols), lambda g: (0, g))
-    halves = [
-        pl.BlockSpec((rows, cols), lambda g: (0, jnp.minimum(g, half - 1))),
-        pl.BlockSpec((rows, cols), lambda g: (0, jnp.maximum(g - skip, 0))),
-    ]
+    rows = wide[0].shape[0]
+    each = features[0].shape[0] // (z_hi * 2)
+    cols = 256
+    n_wide, n_narrow = wide[0].shape[1] // cols, narrow[0].shape[1] // cols
+    n = (n_wide + n_narrow) * cols
     return pl.pallas_call(
-        functools.partial(weight_kernel, nx, z_hi, ny),
-        grid=(2 * half,),
+        functools.partial(weight_kernel, nx, z_hi, n_narrow),
+        grid=(n_wide + n_narrow,),
         in_specs=[pl.BlockSpec(memory_space=pltpu.SMEM)]
-        + [whole(features[0].shape)] * nx
-        + [block, block, *halves, block],
-        out_specs=pl.BlockSpec((ny, z_hi, wide // ny, cols), lambda g: (0, 0, 0, g)),
-        out_shape=jax.ShapeDtypeStruct((ny, z_hi, wide // ny, n), BF),
+        + [pl.BlockSpec(memory_space=pl.ANY)] * nx
+        + [pl.BlockSpec((rows, cols), lambda g: (0, jnp.minimum(g, n_wide - 1)))] * nx
+        + [pl.BlockSpec((rows, cols), lambda g: (0, jnp.maximum(g - n_wide, 0)))] * nx,
+        out_specs=pl.BlockSpec((pieces, z_hi, each // pieces, cols), lambda g: (0, 0, 0, g)),
+        out_shape=jax.ShapeDtypeStruct((pieces, z_hi, each // pieces, n), BF),
         scratch_shapes=[
-            pltpu.VMEM((z_hi * wide, nx * rows), BF),
-            pltpu.VMEM((z_hi * wide, cols), BF),
+            pltpu.VMEM((nx, z_hi * each, rows), BF),
+            pltpu.SemaphoreType.DMA((nx, z_hi)),
         ],
         compiler_params=pltpu.CompilerParams(vmem_limit_bytes=24 * 2**20),
         cost_estimate=pl.CostEstimate(
-            flops=2 * z_hi * wide * nx * rows * n,
+            flops=2 * z_hi * each * nx * rows * n,
             bytes_accessed=6 * 2**20,
             transcendentals=0,
         ),
         name="weight_part",
-    )(jnp.stack([which, my_y]), *features, own, left, *far, right)
+    )(which[None], *features, *wide, *narrow)
 
 
 def local(layer_input, queries, key_head, value_head, grad_output, doc_ids):
@@ -289,13 +286,12 @@
     nx, nc, z_hi = lax.axis_size("x"), lax.axis_size("core"), lax.axis_size("zh")
     ny, zl = lax.axis_size("y"), lax.axis_size("zl")
     place = lax.axis_index(CTX)
-    my_x, my_core, my_y = lax.axis_index("x"), lax.axis_index("core"), lax.axis_index("y")
+    my_x, my_core = lax.axis_index("x"), lax.axis_index("core")
 
     kv = jnp.concatenate([k, v], axis=1)
     pair = jnp.stack([kv, shifted(kv, "zl", zl, 1)])
     before, after = shifted(pair, "y", ny, 1), shifted(pair, "y", ny, -1)
     parts = split_features(x, my_x, z_hi, nx)
-    before, after, parts = lax.optimization_barrier((before, after, parts))
     far = jnp.stack([shifted(before[0], "y", ny, 1), shifted(after[1], "y", ny, -1)])
     kv_pairs = [pair, before, far, after]
     features = [shifted(part, "x", nx, s) if s else part for s, part in enumerate(parts)]
@@ -305,53 +301,26 @@
     info = jnp.stack([place - starts[0] // rows + 1, place, starts[rows - 1]])
     starts = starts[None, :]
 
-    def term(grads):
-        theirs = weight_part(features, grads, 1 - my_core, my_y, z_hi, ny)
-        theirs = shifted(theirs, "core", nc, 1)
-        mine = weight_part(features, grads, my_core, my_y, z_hi, ny)
-        return [(mine[r].astype(F32) + theirs[r].astype(F32)).astype(BF) for r in range(ny)]
-
-    def far_y(pieces):
-        half = pieces[2].shape[0] // 2
-        ahead = shifted(pieces[2][:half], "y", ny, 1)
-        behind = shifted(pieces[2][half:], "y", ny, -1)
-        ahead = jnp.concatenate([plus(pieces[1][:half], ahead), pieces[1][half:]])
-        behind = jnp.concatenate([pieces[3][:half], plus(pieces[3][half:], behind)])
-        return pieces[0], ahead, behind
-
-    def near_y(pieces):
-        own, ahead, behind = pieces
-        total = own.astype(F32) + shifted(ahead, "y", ny, 1).astype(F32)
-        return total + shifted(behind, "y", ny, -1).astype(F32)
+    def along_x(grads):
+        return [grads] + [shifted(grads, "x", nx, s) for s in range(1, nx)]
 
     dq, dkv = attention(q, do, kv_pairs, info, starts)
     dq, dkv, features = lax.optimization_barrier((dq, dkv, features))
-    left, right = shifted(dq, "x", nx, 1), shifted(dq, "x", nx, -1)
-    total = near_y(far_y([dkv[0], dkv[3], dkv[2], dkv[1]]))
-    left, right, total = lax.optimization_barrier((left, right, total))
-    half = dq.shape[1] // 2
-    far = shifted(left[:, :half], "x", nx, 1), shifted(right[:, half:], "x", nx, -1)
-    other = shifted(total[1].astype(BF), "zl", zl, 1)
-    dkv_own = (total[0] + other.astype(F32)).astype(BF)
-
-    pieces = far_y(term((dq, left, far, right)))
-    along = [shifted(dkv_own, "x", nx, s) for s in range(1, nx)]
-    pieces, along = lax.optimization_barrier((pieces, along))
-    part = near_y(pieces).astype(BF)
-    narrow = near_y(far_y(term((dkv_own, along[0], (along[1], along[1]), along[2])))).astype(BF)
-    part = jnp.concatenate([part, narrow], axis=-1)
-    n = part.shape[-1]
-    part = part.reshape(z_hi, zl, -1, n)
-    my_zl, my_zh = lax.axis_index("zl"), lax.axis_index("zh")
-    kept = lax.dynamic_index_in_dim(part, my_zl, 1, keepdims=False)
-    given = shifted(lax.dynamic_index_in_dim(part, 1 - my_zl, 1, keepdims=False), "zl", zl, 1)
-    part = (kept.astype(F32) + given.astype(F32)).astype(BF)
-    weight = 0.0
-    for s in range(z_hi):
-        piece = lax.dynamic_index_in_dim(part, (my_zh + s) % z_hi, 0, keepdims=False)
-        weight = weight + (shifted(piece, "zh", z_hi, s) if s else piece).astype(F32)
+    wide = along_x(dq)
+    dkv = lax.all_to_all(dkv, CTX, 0, 0, tiled=True)
+    dkv_own = jnp.sum(dkv.astype(F32), axis=0).astype(BF)
+    narrow = along_x(dkv_own)
+
+    theirs = weight_part(features, wide, narrow, 1 - my_core, z_hi, ctx)
+    theirs = shifted(theirs, "core", nc, 1)
+    mine = weight_part(features, wide, narrow, my_core, z_hi, ctx)
+    n = mine.shape[-1]
+    part = plus(mine, theirs).reshape(ctx, -1, n)
+    part = lax.all_to_all(part, CTX, 0, 0, tiled=True)
+    part = jnp.sum(part.astype(F32), axis=0).astype(BF).reshape(z_hi, -1, n)
+    part = lax.all_to_all(part, "zh", 0, 0, tiled=True)
     tokens = rows * ctx * nx * nc * z_hi
-    weight = weight * (1.0 / math.sqrt(tokens))
+    weight = jnp.sum(part.astype(F32), axis=0) * (1.0 / math.sqrt(tokens))
     width = q.shape[1]
     return (
         dq[None],

time: 154 us -> 141 us (0.916)
  blocking collectives: 0 us -> 23.5 us
  waiting for transfers between devices: 54.3 us -> 35.7 us
  starting transfers between devices: 56.6 us -> 45.4 us
  local copies, waits for them, and re-layouts: 9.22 us -> 4.76 us
  other arithmetic: 8.13 us -> 5.61 us
    ppermute x34 -> x15, starting transfers between devices: 56.6 us -> 20.4 us  [shifted(): return lax.ppermute(value, axis, pairs)]
    ppermute x34 -> x15, waiting for transfers between devices: 54.3 us -> 19.3 us  [shifted(): return lax.ppermute(value, axis, pairs)]
    all_to_all x0 -> x2, starting transfers between devices: none -> 25 us  [the longest x1 16.8 us: local(): dkv = lax.all_to_all(dkv, CTX, 0, 0, tiled=True)]
    all_to_all x0 -> x1, blocking collectives: none -> 23.5 us  [local(): part = lax.all_to_all(part, CTX, 0, 0, tiled=True)]
    all_to_all x0 -> x2, waiting for transfers between devices: none -> 16.4 us  [the longest x1 8.31 us: local(): part = lax.all_to_all(part, 'zh', 0, 0, tiled=True)]
    unnamed x18 -> x8, local copies, waits for them, and re-layouts: 5.14 us -> 1.6 us
    convert_element_type x6 -> x0, other arithmetic: 2.44 us -> none  [the longest x2 1.37 us: term(): (mine[r].astype(F32) + theirs[r].astype(F32)).astype(BF)]
    reduce_sum x0 -> x3, other arithmetic: none -> 2.27 us  [the longest x1 1.37 us: local(): dkv_own = jnp.sum(dkv.astype(F32), axis=0).astype(BF)]
  transfers between devices with their start and end apart: 34 -> 17, of which waited for: 16 -> 7; matrix products, arithmetic and copies ran while one was open for 5% -> 4% of each run, Pallas kernels for 10% -> 11%
where the time goes in v6:
time: 141 us; the launch traced here: 139 us
  starting transfers between devices  45.4 us (32%)
  waiting for transfers between devices  35.7 us (25%)
  blocking collectives  23.5 us (17%)
  Pallas kernels  20.8 us (15%)
  other arithmetic  5.61 us (4%)
  local copies, waits for them, and re-layouts  4.76 us (3%)
  between operations  3.39 us (2%)
    all_to_all x1, blocking collectives, local(): part = lax.all_to_all(part, CTX, 0, 0, tiled=True)  23.5 us
    ppermute x15, starting transfers between devices, shifted(): return lax.ppermute(value, axis, pairs)  20.4 us
    ppermute x15, waiting for transfers between devices, shifted(): return lax.ppermute(value, axis, pairs)  19.3 us
    all_to_all x1, starting transfers between devices, local(): dkv = lax.all_to_all(dkv, CTX, 0, 0, tiled=True)  16.8 us
    pallas_call x2, Pallas kernels, weight_part(): pl.pallas_call(functools.partial(weight_kernel, nx, z_hi, n_narrow), grid...  11.4 us
    all_to_all x1, waiting for transfers between devices, local(): part = lax.all_to_all(part, 'zh', 0, 0, tiled=True)  8.31 us
    all_to_all x1, starting transfers between devices, local(): part = lax.all_to_all(part, 'zh', 0, 0, tiled=True)  8.17 us
    all_to_all x1, waiting for transfers between devices, local(): dkv = lax.all_to_all(dkv, CTX, 0, 0, tiled=True)  8.06 us
  transfers between devices with their start and end apart: 17, of which 7 were waited for; matrix products, arithmetic and copies ran while one was open for 4% of the time, Pallas kernels for 11%

profile of v6, /device:TPU:32, one launch (start us, length us, event | category | flops | bytes accessed | tf_op | source)
XLA Modules:
  0.0 139.1 jit_solution(4017598372352057362)
XLA Ops:
  1.5 1.9 %collective-permute-start = (bf16[256,256]{1,0:T(8,128)(2,1)S(1)}, bf16[256,256]{1,0:T(8,128)(2,1)S(1)}, u32[]{:S(2)}, u32[]{:S(2)}) collective-permute-start(bf16[256,256]{1,0:T(8,128)(2,1)S(1)} %get-tuple-element.33), channel_id=1, source_target_pairs={{0,1},{1,0},{2,3},{3,2},{4,5},{5,4},{6,7},{7,6},{8,9},{9,8},{10,11... | collective-permute-start | bytes 393224 | tf_op jit(solution)/shard_map/ppermute | solution.py:32
  3.5 3.4 %collective-permute-done = bf16[256,256]{1,0:T(8,128)(2,1)S(1)} collective-permute-done((bf16[256,256]{1,0:T(8,128)(2,1)S(1)}, bf16[256,256]{1,0:T(8,128)(2,1)S(1)}, u32[]{:S(2)}, u32[]{:S(2)}) %collective-permute-start) | collective-permute-done | bytes 131104 | tf_op jit(solution)/shard_map/ppermute | solution.py:32
  6.9 1.7 %collective-permute-start.1 = (bf16[2,256,256]{2,1,0:T(8,128)(2,1)S(1)}, bf16[2,256,256]{2,1,0:T(8,128)(2,1)S(1)}, u32[]{:S(2)}, u32[]{:S(2)}) collective-permute-start(bf16[2,256,256]{2,1,0:T(8,128)(2,1)S(1)} %pad_maximum_fusion.refs_0_), channel_id=1, source_target_pairs={{0,2},{2,4},{4,6},{6,0},{1,3},{3,5},{5,7},{7,1},{8,10},{10,12},{12... | collective-permute-start | bytes 786440 | tf_op jit(solution)/shard_map/ppermute | solution.py:32
  8.5 1.6 %copy-done = bf16[1,256,4096]{2,1,0:T(8,128)(2,1)S(1)} copy-done((bf16[1,256,4096]{2,1,0:T(8,128)(2,1)S(1)}, bf16[1,256,4096]{2,1,0:T(8,128)(2,1)}, u32[]{:S(2)}) %copy-start) | copy-done | bytes 2097176
  10.1 2.4 %split_features.1 = (bf16[1024,256]{1,0:T(8,128)(2,1)S(1)}, bf16[1024,256]{1,0:T(8,128)(2,1)}, bf16[1024,256]{1,0:T(8,128)(2,1)}, bf16[1024,256]{1,0:T(8,128)(2,1)}) custom-call(s32[1]{0:T(128)} %bitcast.16.info, bf16[256,4096]{1,0:T(8,128)(2,1)S(1)} %bitcast.30, bf16[256,4096]{1,0:T(8,128)(2,1)S(1)} %bitcast.31, bf16[256,4096]{1,0:T(8,128)(2,1)S(1)} %bitcast.32, ...), custom_call_target="tpu_custom_call" | custom-call | tf_op jit(solution)/shard_map/split_features/pallas_call | solution.py:199
  12.5 1.5 %collective-permute-start.5 = (bf16[1024,256]{1,0:T(8,128)(2,1)}, bf16[1024,256]{1,0:T(8,128)(2,1)S(1)}, u32[]{:S(2)}, u32[]{:S(2)}) collective-permute-start(bf16[1024,256]{1,0:T(8,128)(2,1)} %get-tuple-element.21), channel_id=1, source_target_pairs={{0,16},{16,32},{32,48},{48,0},{1,17},{17,33},{33,49},{49,1},{2,18}... | collective-permute-start | bytes 1572872 | tf_op jit(solution)/shard_map/ppermute | solution.py:32
  14.0 2.7 %collective-permute-start.6 = (bf16[1024,256]{1,0:T(8,128)(2,1)}, bf16[1024,256]{1,0:T(8,128)(2,1)S(1)}, u32[]{:S(2)}, u32[]{:S(2)}) collective-permute-start(bf16[1024,256]{1,0:T(8,128)(2,1)} %get-tuple-element.22), channel_id=1, source_target_pairs={{0,32},{16,48},{32,0},{48,16},{1,33},{17,49},{33,1},{49,17},{2,34}... | collective-permute-start | bytes 1572872 | tf_op jit(solution)/shard_map/ppermute | solution.py:32
  16.7 1.4 %collective-permute-start.7 = (bf16[1024,256]{1,0:T(8,128)(2,1)}, bf16[1024,256]{1,0:T(8,128)(2,1)S(1)}, u32[]{:S(2)}, u32[]{:S(2)}) collective-permute-start(bf16[1024,256]{1,0:T(8,128)(2,1)} %get-tuple-element.23), channel_id=1, source_target_pairs={{0,48},{16,0},{32,16},{48,32},{1,49},{17,1},{33,17},{49,33},{2,50}... | collective-permute-start | bytes 1572872 | tf_op jit(solution)/shard_map/ppermute | solution.py:32
  18.2 1.7 %collective-permute-start.3 = (bf16[2,256,256]{2,1,0:T(8,128)(2,1)S(1)}, bf16[2,256,256]{2,1,0:T(8,128)(2,1)S(1)}, u32[]{:S(2)}, u32[]{:S(2)}) collective-permute-start(bf16[2,256,256]{2,1,0:T(8,128)(2,1)S(1)} %pad_maximum_fusion.refs_0_), channel_id=1, source_target_pairs={{0,6},{2,0},{4,2},{6,4},{1,7},{3,1},{5,3},{7,5},{8,14},{10,8},{12,... | collective-permute-start | bytes 786440 | tf_op jit(solution)/shard_map/ppermute | solution.py:32
  20.6 3.9 %collective-permute-done.3.refs_3_ = bf16[2,256,256]{2,1,0:T(8,128)(2,1)S(1)} collective-permute-done((bf16[2,256,256]{2,1,0:T(8,128)(2,1)S(1)}, bf16[2,256,256]{2,1,0:T(8,128)(2,1)S(1)}, u32[]{:S(2)}, u32[]{:S(2)}) %collective-permute-start.3) | collective-permute-done | bytes 262176 | tf_op jit(solution)/shard_map/ppermute | solution.py:32
  25.2 2.9 %collective-permute-start.4 = (bf16[256,256]{1,0:T(8,128)(2,1)}, bf16[256,256]{1,0:T(8,128)(2,1)}, u32[]{:S(2)}, u32[]{:S(2)}) collective-permute-start(bf16[256,256]{1,0:T(8,128)(2,1)} %slice_bitcast_fusion), channel_id=1, source_target_pairs={{0,6},{2,0},{4,2},{6,4},{1,7},{3,1},{5,3},{7,5},{8,14},{10,8},{12,... | collective-permute-start | bytes 393224 | tf_op jit(solution)/shard_map/ppermute | solution.py:32
  33.0 7.1 %attention_backward.1 = (bf16[256,1024]{1,0:T(8,128)(2,1)}, bf16[8,256,256]{2,1,0:T(8,128)(2,1)}) custom-call(s32[3]{0:T(128)S(1)} %pad_add_fusion.info, s32[1,256]{1,0:T(1,128)S(1)} %bitcast.35, bf16[256,1024]{1,0:T(8,128)(2,1)S(1)} %bitcast.36, bf16[256,1024]{1,0:T(8,128)(2,1)} %bitcast.43, bf16[2,256,256]{2,1,0:T(8,128)(2,1)S(1)} %pad_maximum_fusion.refs_0_, ...), custom_call_target="tpu_custom_call" | custom-call | flops 5368709120 | bytes 4194304 | tf_op jit(solution)/shard_map/attention_backward/pallas_call | solution.py:149
  40.1 16.8 %all-to-all-start = ((bf16[8,256,256]{2,1,0:T(8,128)(2,1)}), bf16[8,256,256]{2,1,0:T(8,128)(2,1)}, u32[]{:S(2)}, u32[]{:S(2)}) async-start(bf16[8,256,256]{2,1,0:T(8,128)(2,1)} %get-tuple-element.25), calls=%async_computation | async-start | bytes 2097152 | tf_op jit(solution)/shard_map/all_to_all | solution.py:310
  57.1 1.9 %collective-permute-start.8 = (bf16[256,1024]{1,0:T(8,128)(2,1)S(1)}, bf16[256,1024]{1,0:T(8,128)(2,1)}, u32[]{:S(2)}, u32[]{:S(2)}) collective-permute-start(bf16[256,1024]{1,0:T(8,128)(2,1)S(1)} %copy-done.1), channel_id=1, source_target_pairs={{0,16},{16,32},{32,48},{48,0},{1,17},{17,33},{33,49},{49,1},{2,18}... | collective-permute-start | bytes 1572872 | tf_op jit(solution)/shard_map/ppermute | solution.py:32
  59.6 8.1 %all-to-all-done = bf16[8,256,256]{2,1,0:T(8,128)(2,1)} async-done(((bf16[8,256,256]{2,1,0:T(8,128)(2,1)}), bf16[8,256,256]{2,1,0:T(8,128)(2,1)}, u32[]{:S(2)}, u32[]{:S(2)}) %all-to-all-start) | async-done | bytes 1048608 | tf_op jit(solution)/shard_map/all_to_all | solution.py:310
  67.7 1.4 reduce_sum.43.refs_8_
  70.5 1.3 collective-permute-done.10.refs_7_
  71.8 2.0 %collective-permute-start.13 = (bf16[256,256]{1,0:T(8,128)(2,1)S(1)}, bf16[256,256]{1,0:T(8,128)(2,1)}, u32[]{:S(2)}, u32[]{:S(2)}) collective-permute-start(bf16[256,256]{1,0:T(8,128)(2,1)S(1)} %reduce_sum.43.refs_8_), channel_id=1, source_target_pairs={{0,48},{16,0},{32,16},{48,32},{1,49},{17,1},{33,17},{49,33},{2,50}... | collective-permute-start | bytes 393224 | tf_op jit(solution)/shard_map/ppermute | solution.py:32
  73.8 9.4 %collective-permute-done.8.refs_5_ = bf16[256,1024]{1,0:T(8,128)(2,1)} collective-permute-done((bf16[256,1024]{1,0:T(8,128)(2,1)S(1)}, bf16[256,1024]{1,0:T(8,128)(2,1)}, u32[]{:S(2)}, u32[]{:S(2)}) %collective-permute-start.8) | collective-permute-done | bytes 524320 | tf_op jit(solution)/shard_map/ppermute | solution.py:32
  84.5 5.7 %weight_part.3 = bf16[8,4,16,1280]{3,2,1,0:T(8,128)(2,1)S(1)} custom-call(s32[1]{0:T(128)} %bitcast.22.info, bf16[1024,256]{1,0:T(8,128)(2,1)S(1)} %get-tuple-element.26.refs_0_, bf16[1024,256]{1,0:T(8,128)(2,1)S(1)} %collective-permute-done.5.refs_1_, bf16[1024,256]{1,0:T(8,128)(2,1)S(1)} %collective-permute-done.6.refs_2_, ...), custom_call_target="tpu_custom_call" | custom-call | flops 1342177280 | bytes 6291456 | tf_op jit(solution)/shard_map/weight_part/pallas_call | solution.py:257
  90.3 5.7 %weight_part.2 = bf16[8,4,16,1280]{3,2,1,0:T(8,128)(2,1)S(1)} custom-call(s32[1]{0:T(128)} %bitcast.21.info, bf16[1024,256]{1,0:T(8,128)(2,1)S(1)} %get-tuple-element.26.refs_0_, bf16[1024,256]{1,0:T(8,128)(2,1)S(1)} %collective-permute-done.5.refs_1_, bf16[1024,256]{1,0:T(8,128)(2,1)S(1)} %collective-permute-done.6.refs_2_, ...), custom_call_target="tpu_custom_call" | custom-call | flops 1342177280 | bytes 6291456 | tf_op jit(solution)/shard_map/weight_part/pallas_call | solution.py:257
  96.4 23.5 %all_to_all.15 = bf16[8,64,1280]{2,1,0:T(8,128)(2,1)S(1)} all-to-all(bf16[8,64,1280]{2,1,0:T(8,128)(2,1)S(1)} %bitcast.37), channel_id=1, replica_groups=mesh['zh'=4,'x'=4,'core'=2,'y'=4,'zl'=2] {'y','zl'}, dimensions={0} | all-to-all | bytes 2621440 | tf_op jit(solution)/shard_map/all_to_all | solution.py:319
  120.7 8.2 %all-to-all-start.2 = ((bf16[4,16,1280]{2,1,0:T(8,128)(2,1)}), bf16[4,16,1280]{2,1,0:T(8,128)(2,1)S(1)}, u32[]{:S(2)}, u32[]{:S(2)}) async-start(bf16[4,16,1280]{2,1,0:T(8,128)(2,1)} %bitcast.24), calls=%async_computation.2 | async-start | bytes 327680 | tf_op jit(solution)/shard_map/all_to_all | solution.py:321
  129.5 8.3 %all-to-all-done.2 = bf16[4,16,1280]{2,1,0:T(8,128)(2,1)S(1)} async-done(((bf16[4,16,1280]{2,1,0:T(8,128)(2,1)}), bf16[4,16,1280]{2,1,0:T(8,128)(2,1)S(1)}, u32[]{:S(2)}, u32[]{:S(2)}) %all-to-all-start.2) | async-done | bytes 163872 | tf_op jit(solution)/shard_map/all_to_all | solution.py:321
  (40 shorter events, 11.5 us)
Async XLA Ops:
  1.5 5.3 %collective-permute-start = (bf16[256,256]{1,0:T(8,128)(2,1)S(1)}, bf16[256,256]{1,0:T(8,128)(2,1)S(1)}, u32[]{:S(2)}, u32[]{:S(2)}) collective-permute-start(bf16[256,256]{1,0:T(8,128)(2,1)S(1)} %get-tuple-element.33), channel_id=1, source_target_pairs={{0,1},{1,0},{2,3},{3,2},{4,5},{5,4},{6,7},{7,6},{8,9},{9,8},{10,11... | collective-permute-start | bytes 393224 | tf_op jit(solution)/shard_map/ppermute | solution.py:32
  6.9 13.3 %collective-permute-start.1 = (bf16[2,256,256]{2,1,0:T(8,128)(2,1)S(1)}, bf16[2,256,256]{2,1,0:T(8,128)(2,1)S(1)}, u32[]{:S(2)}, u32[]{:S(2)}) collective-permute-start(bf16[2,256,256]{2,1,0:T(8,128)(2,1)S(1)} %pad_maximum_fusion.refs_0_), channel_id=1, source_target_pairs={{0,2},{2,4},{4,6},{6,0},{1,3},{3,5},{5,7},{7,1},{8,10},{10,12},{12... | collective-permute-start | bytes 786440 | tf_op jit(solution)/shard_map/ppermute | solution.py:32
  8.5 1.6 %copy-start = (bf16[1,256,4096]{2,1,0:T(8,128)(2,1)S(1)}, bf16[1,256,4096]{2,1,0:T(8,128)(2,1)}, u32[]{:S(2)}) copy-start(bf16[1,256,4096]{2,1,0:T(8,128)(2,1)} %param.6) | copy-start | bytes 6291460
  10.1 8.0 %copy-start.3 = (s32[1,2048]{1,0:T(1,128)S(1)}, s32[1,2048]{1,0:T(1,128)}, u32[]{:S(2)}) copy-start(s32[1,2048]{1,0:T(1,128)} %param.11) | copy-start | bytes 24580
  10.1 22.9 %copy-start.2 = (bf16[1,256,1024]{2,1,0:T(8,128)(2,1)S(1)}, bf16[1,256,1024]{2,1,0:T(8,128)(2,1)}, u32[]{:S(2)}) copy-start(bf16[1,256,1024]{2,1,0:T(8,128)(2,1)} %param.7) | copy-start | bytes 1572868
  12.5 27.6 %collective-permute-start.5 = (bf16[1024,256]{1,0:T(8,128)(2,1)}, bf16[1024,256]{1,0:T(8,128)(2,1)S(1)}, u32[]{:S(2)}, u32[]{:S(2)}) collective-permute-start(bf16[1024,256]{1,0:T(8,128)(2,1)} %get-tuple-element.21), channel_id=1, source_target_pairs={{0,16},{16,32},{32,48},{48,0},{1,17},{17,33},{33,49},{49,1},{2,18}... | collective-permute-start | bytes 1572872 | tf_op jit(solution)/shard_map/ppermute | solution.py:32
  14.0 26.1 %collective-permute-start.6 = (bf16[1024,256]{1,0:T(8,128)(2,1)}, bf16[1024,256]{1,0:T(8,128)(2,1)S(1)}, u32[]{:S(2)}, u32[]{:S(2)}) collective-permute-start(bf16[1024,256]{1,0:T(8,128)(2,1)} %get-tuple-element.22), channel_id=1, source_target_pairs={{0,32},{16,48},{32,0},{48,16},{1,33},{17,49},{33,1},{49,17},{2,34}... | collective-permute-start | bytes 1572872 | tf_op jit(solution)/shard_map/ppermute | solution.py:32
  16.7 23.4 %collective-permute-start.7 = (bf16[1024,256]{1,0:T(8,128)(2,1)}, bf16[1024,256]{1,0:T(8,128)(2,1)S(1)}, u32[]{:S(2)}, u32[]{:S(2)}) collective-permute-start(bf16[1024,256]{1,0:T(8,128)(2,1)} %get-tuple-element.23), channel_id=1, source_target_pairs={{0,48},{16,0},{32,16},{48,32},{1,49},{17,1},{33,17},{49,33},{2,50}... | collective-permute-start | bytes 1572872 | tf_op jit(solution)/shard_map/ppermute | solution.py:32
  18.2 6.4 %collective-permute-start.3 = (bf16[2,256,256]{2,1,0:T(8,128)(2,1)S(1)}, bf16[2,256,256]{2,1,0:T(8,128)(2,1)S(1)}, u32[]{:S(2)}, u32[]{:S(2)}) collective-permute-start(bf16[2,256,256]{2,1,0:T(8,128)(2,1)S(1)} %pad_maximum_fusion.refs_0_), channel_id=1, source_target_pairs={{0,6},{2,0},{4,2},{6,4},{1,7},{3,1},{5,3},{7,5},{8,14},{10,8},{12,... | collective-permute-start | bytes 786440 | tf_op jit(solution)/shard_map/ppermute | solution.py:32
  20.2 11.8 %collective-permute-start.2 = (bf16[256,256]{1,0:T(8,128)(2,1)S(1)}, bf16[256,256]{1,0:T(8,128)(2,1)}, u32[]{:S(2)}, u32[]{:S(2)}) collective-permute-start(bf16[256,256]{1,0:T(8,128)(2,1)S(1)} %slice_bitcast_fusion.1), channel_id=1, source_target_pairs={{0,2},{2,4},{4,6},{6,0},{1,3},{3,5},{5,7},{7,1},{8,10},{10,12},{12... | collective-permute-start | bytes 393224 | tf_op jit(solution)/shard_map/ppermute | solution.py:32
  25.2 6.8 %collective-permute-start.4 = (bf16[256,256]{1,0:T(8,128)(2,1)}, bf16[256,256]{1,0:T(8,128)(2,1)}, u32[]{:S(2)}, u32[]{:S(2)}) collective-permute-start(bf16[256,256]{1,0:T(8,128)(2,1)} %slice_bitcast_fusion), channel_id=1, source_target_pairs={{0,6},{2,0},{4,2},{6,4},{1,7},{3,1},{5,3},{7,5},{8,14},{10,8},{12,... | collective-permute-start | bytes 393224 | tf_op jit(solution)/shard_map/ppermute | solution.py:32
  40.1 16.9 %copy-start.1 = (bf16[256,1024]{1,0:T(8,128)(2,1)S(1)}, bf16[256,1024]{1,0:T(8,128)(2,1)}, u32[]{:S(2)}) copy-start(bf16[256,1024]{1,0:T(8,128)(2,1)} %get-tuple-element.24.refs_4_) | copy-start | bytes 1572868
  40.1 27.6 %all-to-all-start = ((bf16[8,256,256]{2,1,0:T(8,128)(2,1)}), bf16[8,256,256]{2,1,0:T(8,128)(2,1)}, u32[]{:S(2)}, u32[]{:S(2)}) async-start(bf16[8,256,256]{2,1,0:T(8,128)(2,1)} %get-tuple-element.25), calls=%async_computation | async-start | bytes 2097152 | tf_op jit(solution)/shard_map/all_to_all | solution.py:310
  57.0 14.9 %collective-permute-start.10 = (bf16[256,1024]{1,0:T(8,128)(2,1)S(1)}, bf16[256,1024]{1,0:T(8,128)(2,1)S(1)}, u32[]{:S(2)}, u32[]{:S(2)}) collective-permute-start(bf16[256,1024]{1,0:T(8,128)(2,1)S(1)} %copy-done.1), channel_id=1, source_target_pairs={{0,48},{16,0},{32,16},{48,32},{1,49},{17,1},{33,17},{49,33},{2,50}... | collective-permute-start | bytes 1572872 | tf_op jit(solution)/shard_map/ppermute | solution.py:32
  57.1 26.1 %collective-permute-start.8 = (bf16[256,1024]{1,0:T(8,128)(2,1)S(1)}, bf16[256,1024]{1,0:T(8,128)(2,1)}, u32[]{:S(2)}, u32[]{:S(2)}) collective-permute-start(bf16[256,1024]{1,0:T(8,128)(2,1)S(1)} %copy-done.1), channel_id=1, source_target_pairs={{0,16},{16,32},{32,48},{48,0},{1,17},{17,33},{33,49},{49,1},{2,18}... | collective-permute-start | bytes 1572872 | tf_op jit(solution)/shard_map/ppermute | solution.py:32
  59.0 24.2 %collective-permute-start.9 = (bf16[256,1024]{1,0:T(8,128)(2,1)S(1)}, bf16[256,1024]{1,0:T(8,128)(2,1)}, u32[]{:S(2)}, u32[]{:S(2)}) collective-permute-start(bf16[256,1024]{1,0:T(8,128)(2,1)S(1)} %copy-done.1), channel_id=1, source_target_pairs={{0,32},{16,48},{32,0},{48,16},{1,33},{17,49},{33,1},{49,17},{2,34}... | collective-permute-start | bytes 1572872 | tf_op jit(solution)/shard_map/ppermute | solution.py:32
  69.1 15.4 %collective-permute-start.11 = (bf16[256,256]{1,0:T(8,128)(2,1)S(1)}, bf16[256,256]{1,0:T(8,128)(2,1)S(1)}, u32[]{:S(2)}, u32[]{:S(2)}) collective-permute-start(bf16[256,256]{1,0:T(8,128)(2,1)S(1)} %reduce_sum.43.refs_8_), channel_id=1, source_target_pairs={{0,16},{16,32},{32,48},{48,0},{1,17},{17,33},{33,49},{49,1},{2,18}... | collective-permute-start | bytes 393224 | tf_op jit(solution)/shard_map/ppermute | solution.py:32
  69.4 15.0 %collective-permute-start.12 = (bf16[256,256]{1,0:T(8,128)(2,1)S(1)}, bf16[256,256]{1,0:T(8,128)(2,1)S(1)}, u32[]{:S(2)}, u32[]{:S(2)}) collective-permute-start(bf16[256,256]{1,0:T(8,128)(2,1)S(1)} %reduce_sum.43.refs_8_), channel_id=1, source_target_pairs={{0,32},{16,48},{32,0},{48,16},{1,33},{17,49},{33,1},{49,17},{2,34}... | collective-permute-start | bytes 393224 | tf_op jit(solution)/shard_map/ppermute | solution.py:32
  71.8 12.7 %collective-permute-start.13 = (bf16[256,256]{1,0:T(8,128)(2,1)S(1)}, bf16[256,256]{1,0:T(8,128)(2,1)}, u32[]{:S(2)}, u32[]{:S(2)}) collective-permute-start(bf16[256,256]{1,0:T(8,128)(2,1)S(1)} %reduce_sum.43.refs_8_), channel_id=1, source_target_pairs={{0,48},{16,0},{32,16},{48,32},{1,49},{17,1},{33,17},{49,33},{2,50}... | collective-permute-start | bytes 393224 | tf_op jit(solution)/shard_map/ppermute | solution.py:32
  90.2 5.8 %collective-permute-start.14 = (bf16[8,4,16,1280]{3,2,1,0:T(8,128)(2,1)S(1)}, bf16[8,4,16,1280]{3,2,1,0:T(8,128)(2,1)S(1)}, u32[]{:S(2)}, u32[]{:S(2)}) collective-permute-start(bf16[8,4,16,1280]{3,2,1,0:T(8,128)(2,1)S(1)} %weight_part.3), channel_id=1, source_target_pairs={{0,8},{8,0},{1,9},{9,1},{2,10},{10,2},{3,11},{11,3},{4,12},{12,4},... | collective-permute-start | bytes 3932168 | tf_op jit(solution)/shard_map/ppermute | solution.py:32
  120.7 17.1 %all-to-all-start.2 = ((bf16[4,16,1280]{2,1,0:T(8,128)(2,1)}), bf16[4,16,1280]{2,1,0:T(8,128)(2,1)S(1)}, u32[]{:S(2)}, u32[]{:S(2)}) async-start(bf16[4,16,1280]{2,1,0:T(8,128)(2,1)} %bitcast.24), calls=%async_computation.2 | async-start | bytes 327680 | tf_op jit(solution)/shard_map/all_to_all | solution.py:321

commit v7 on v6

--- a/solution.py
+++ b/solution.py
@@ -9,6 +9,7 @@
 from jax.sharding import Mesh, PartitionSpec as P
 
 NEG = -1e30
+DOCS = 4
 AXES = ("zh", "x", "core", "y", "zl")
 SIZES = (4, 4, 2, 4, 2)
 CTX = ("y", "zl")
@@ -40,22 +41,35 @@
     return pl.BlockSpec(shape, lambda *g: (0,) * len(shape))
 
 
-def attention_kernel(ny, per, scale, info, starts_ref, q_ref, do_ref, *refs):
-    kv_refs, refs = refs[:ny], refs[ny:]
+def attention_kernel(ny, per, docs, scale, info, docs_ref, q_ref, do_ref, *refs):
+    (pair_ref, before_ref, far_refs, after_ref), refs = (refs[0], refs[1], refs[2:4], refs[4]), refs[5:]
     dq_ref, refs = refs[0], refs[1:]
     out_ref, refs = refs[0], refs[1:]
-    kv_s, kt_s, acc_s, e_s, dp_s, md_s, stat_s, dqt_s, qt_s, dot_s, p_s, ds_s, qk_s, dk_s, sem = refs
+    kv_s, kt_s, acc_s, e_s, dp_s, md_s, stat_s, dqt_s, qt_s, dot_s, p_s, ds_s, qk_s, dk_s, starts_ref, sem = refs
     rows = q_ref.shape[0]
     hd = kt_s.shape[1]
-    used, place, limit = info[0], info[1], info[2]
+    place = info[0]
+    documents = docs_ref[...]
+    mine = docs_ref[:, pl.ds(pl.multiple_of(place * rows, rows), rows)]
+    starts = jnp.zeros((1, rows), jnp.int32)
+    for t in range(docs - 1):
+        length = jnp.sum((documents == t).astype(jnp.int32))
+        starts += jnp.where(mine > t, length, 0)
+    starts_ref[...] = starts
+    limit = jnp.max(starts)
+    used = place - jnp.min(starts) // rows + 1
     power = scale * math.log2(math.e)
     farthest = place // 2 - (place - used + 1) // 2
 
-    for s in range(ny):
-
-        @pl.when(s <= farthest)
-        def _():
-            pltpu.make_async_copy(kv_refs[s], kv_s.at[pl.ds(2 * s, 2)], sem.at[s]).start()
+    copies = [
+        (0, pltpu.make_async_copy(pair_ref, kv_s.at[pl.ds(0, 2)], sem.at[0])),
+        (1, pltpu.make_async_copy(before_ref, kv_s.at[pl.ds(2, 2)], sem.at[1])),
+        (2, pltpu.make_async_copy(far_refs[0], kv_s.at[4], sem.at[2])),
+        (2, pltpu.make_async_copy(far_refs[1], kv_s.at[5], sem.at[3])),
+        (3, pltpu.make_async_copy(after_ref, kv_s.at[pl.ds(6, 2)], sem.at[4])),
+    ]
+    for s, copy in copies:
+        pl.when(s <= farthest)(copy.start)
 
     acc_s[...] = jnp.zeros_like(acc_s)
     for h in range(per):
@@ -70,11 +84,12 @@
         stat_s[2, h] = jnp.zeros((1, rows), F32)
     dqt_s[...] = jnp.zeros_like(dqt_s)
 
+    for s, copy in copies:
+        pl.when(s <= farthest)(copy.wait)
     for s in range(ny):
 
         @pl.when(s <= farthest)
         def _():
-            pltpu.make_async_copy(kv_refs[s], kv_s.at[pl.ds(2 * s, 2)], sem.at[s]).wait()
             for k in range(2):
                 kt_s[2 * s + k] = kv_s[2 * s + k, :, :hd].T
 
@@ -137,20 +152,19 @@
     out_ref[:, :, hd:] = acc_s[:, :, hd:].astype(BF)
 
 
-def attention(q, do, kv, info, starts):
+def attention(q, do, kv, docs, place, ny):
     rows = q.shape[0]
     hd = kv[0].shape[2] // 2
     width = q.shape[1]
     per = width // hd
-    ny = len(kv)
     blocks = 2 * ny
     slab = whole((rows, width))
     pair = kv[0].shape
     return pl.pallas_call(
-        functools.partial(attention_kernel, ny, per, hd ** (-0.5)),
+        functools.partial(attention_kernel, ny, per, DOCS, hd ** (-0.5)),
         grid=(1,),
-        in_specs=[pl.BlockSpec(memory_space=pltpu.SMEM), whole((1, rows)), slab, slab]
-        + [pl.BlockSpec(memory_space=pl.ANY)] * ny,
+        in_specs=[pl.BlockSpec(memory_space=pltpu.SMEM), whole(docs.shape), slab, slab]
+        + [pl.BlockSpec(memory_space=pl.ANY)] * len(kv),
         out_specs=[whole((rows, width)), whole((blocks, *pair[1:]))],
         out_shape=[
             jax.ShapeDtypeStruct((rows, width), BF),
@@ -171,7 +185,8 @@
             pltpu.VMEM((rows, per * rows), BF),
             pltpu.VMEM((per * rows, hd), BF),
             pltpu.VMEM((per * rows, hd), BF),
-            pltpu.SemaphoreType.DMA((ny,)),
+            pltpu.VMEM((1, rows), jnp.int32),
+            pltpu.SemaphoreType.DMA((len(kv),)),
         ],
         compiler_params=pltpu.CompilerParams(vmem_limit_bytes=52 * 2**20),
         cost_estimate=pl.CostEstimate(
@@ -180,7 +195,7 @@
             transcendentals=per * rows * rows * blocks,
         ),
         name="attention_backward",
-    )(info, starts, q, do, *kv)
+    )(place[None], docs, q, do, *kv)
 
 
 def split_kernel(info, *refs):
@@ -210,77 +225,61 @@
     )(my_x[None], *([x] * nx))
 
 
-def weight_kernel(nx, z_hi, narrow, info, *refs):
+def weight_kernel(nx, z_hi, n_wide, info, *refs):
     f_refs, wide_refs, narrow_refs = refs[:nx], refs[nx : 2 * nx], refs[2 * nx : 3 * nx]
-    out_ref, ft_s, sem = refs[3 * nx :]
-    rows = f_refs[0].shape[1]
+    out_ref, ft_s = refs[3 * nx :]
+    rows = wide_refs[0].shape[0]
     each = f_refs[0].shape[0] // (z_hi * 2)
-    step = pl.program_id(0)
-
-    def fetch(s, z):
-        at = pl.multiple_of((z * 2 + info[0]) * each, each)
-        into = ft_s.at[s, pl.ds(z * each, each)]
-        return pltpu.make_async_copy(f_refs[s].at[pl.ds(at, each)], into, sem.at[s, z])
-
-    @pl.when(step == 0)
-    def _():
-        for s in range(nx):
-            for z in range(z_hi):
-                fetch(s, z).start()
-        for s in range(nx):
-            for z in range(z_hi):
-                fetch(s, z).wait()
-
-    def store(g_refs):
-        total = dot(ft_s[0], g_refs[0][...])
+    cols = 256
+    part = out_ref.shape[2]
+    for s in range(nx):
+        for z in range(z_hi):
+            at = pl.multiple_of((z * 2 + info[0]) * each, each)
+            ft_s[z * each : (z + 1) * each, s * rows : (s + 1) * rows] = f_refs[s][pl.ds(at, each)]
+
+    def columns(g_refs, at, to):
+        total = dot(ft_s[:, :rows], g_refs[0][:, at : at + cols])
         for s in range(1, nx):
-            total += dot(ft_s[s], g_refs[s][...])
+            total += dot(ft_s[:, s * rows : (s + 1) * rows], g_refs[s][:, at : at + cols])
         total = total.astype(BF)
-        part = out_ref.shape[2]
         for z in range(z_hi):
             for p in range(out_ref.shape[0]):
-                at = z * each + p * part
-                out_ref[p, z] = total[at : at + part]
-
-    first_narrow = pl.num_programs(0) - narrow
-    pl.when(step < first_narrow)(lambda: store(wide_refs))
-    pl.when(step >= first_narrow)(lambda: store(narrow_refs))
+                row = z * each + p * part
+                out_ref[p, z, :, to : to + cols] = total[row : row + part]
+
+    for j in range(out_ref.shape[3] // cols):
+        if j < n_wide:
+            columns(wide_refs, j * cols, j * cols)
+        else:
+            columns(narrow_refs, (j - n_wide) * cols, j * cols)
 
 
 def weight_part(features, wide, narrow, which, z_hi, pieces):
     nx = len(features)
     rows = wide[0].shape[0]
     each = features[0].shape[0] // (z_hi * 2)
-    cols = 256
-    n_wide, n_narrow = wide[0].shape[1] // cols, narrow[0].shape[1] // cols
-    n = (n_wide + n_narrow) * cols
+    n = wide[0].shape[1] + narrow[0].shape[1]
+    operands = [*features, *wide, *narrow]
+    out_shape = (pieces, z_hi, each // pieces, n)
     return pl.pallas_call(
-        functools.partial(weight_kernel, nx, z_hi, n_narrow),
-        grid=(n_wide + n_narrow,),
+        functools.partial(weight_kernel, nx, z_hi, wide[0].shape[1] // 256),
         in_specs=[pl.BlockSpec(memory_space=pltpu.SMEM)]
-        + [pl.BlockSpec(memory_space=pl.ANY)] * nx
-        + [pl.BlockSpec((rows, cols), lambda g: (0, jnp.minimum(g, n_wide - 1)))] * nx
-        + [pl.BlockSpec((rows, cols), lambda g: (0, jnp.maximum(g - n_wide, 0)))] * nx,
-        out_specs=pl.BlockSpec((pieces, z_hi, each // pieces, cols), lambda g: (0, 0, 0, g)),
-        out_shape=jax.ShapeDtypeStruct((pieces, z_hi, each // pieces, n), BF),
-        scratch_shapes=[
-            pltpu.VMEM((nx, z_hi * each, rows), BF),
-            pltpu.SemaphoreType.DMA((nx, z_hi)),
-        ],
-        compiler_params=pltpu.CompilerParams(vmem_limit_bytes=24 * 2**20),
+        + [pl.BlockSpec(memory_space=pltpu.VMEM)] * len(operands),
+        out_specs=pl.BlockSpec(memory_space=pltpu.VMEM),
+        out_shape=jax.ShapeDtypeStruct(out_shape, BF),
+        scratch_shapes=[pltpu.VMEM((z_hi * each, nx * rows), BF)],
+        compiler_params=pltpu.CompilerParams(vmem_limit_bytes=20 * 2**20),
         cost_estimate=pl.CostEstimate(
             flops=2 * z_hi * each * nx * rows * n,
             bytes_accessed=6 * 2**20,
             transcendentals=0,
         ),
         name="weight_part",
-    )(which[None], *features, *wide, *narrow)
+    )(which[None], *operands)
 
 
 def local(layer_input, queries, key_head, value_head, grad_output, doc_ids):
-    x, q, k, v, do, docs = (
-        a[0] for a in (layer_input, queries, key_head, value_head, grad_output, doc_ids)
-    )
+    x, q, k, v, do = (a[0] for a in (layer_input, queries, key_head, value_head, grad_output))
     rows, hd = k.shape
     ctx = lax.axis_size(CTX)
     nx, nc, z_hi = lax.axis_size("x"), lax.axis_size("core"), lax.axis_size("zh")
@@ -289,22 +288,18 @@
     my_x, my_core = lax.axis_index("x"), lax.axis_index("core")
 
     kv = jnp.concatenate([k, v], axis=1)
-    pair = jnp.stack([kv, shifted(kv, "zl", zl, 1)])
+    other = shifted(kv, "zl", zl, 1)
+    parts = split_features(x, my_x, z_hi, nx)
+    other, parts = lax.optimization_barrier((other, parts))
+    pair = jnp.stack([kv, other])
     before, after = shifted(pair, "y", ny, 1), shifted(pair, "y", ny, -1)
-    parts = split_features(x, my_x, z_hi, nx)
-    far = jnp.stack([shifted(before[0], "y", ny, 1), shifted(after[1], "y", ny, -1)])
-    kv_pairs = [pair, before, far, after]
+    far = shifted(before[0], "y", ny, 1), shifted(after[1], "y", ny, -1)
     features = [shifted(part, "x", nx, s) if s else part for s, part in enumerate(parts)]
-
-    my_docs = lax.dynamic_slice_in_dim(docs, place * rows, rows)
-    starts = jnp.sum((docs[:, None] < my_docs[None, :]).astype(jnp.int32), axis=0)
-    info = jnp.stack([place - starts[0] // rows + 1, place, starts[rows - 1]])
-    starts = starts[None, :]
 
     def along_x(grads):
         return [grads] + [shifted(grads, "x", nx, s) for s in range(1, nx)]
 
-    dq, dkv = attention(q, do, kv_pairs, info, starts)
+    dq, dkv = attention(q, do, [pair, before, *far, after], doc_ids, place, ny)
     dq, dkv, features = lax.optimization_barrier((dq, dkv, features))
     wide = along_x(dq)
     dkv = lax.all_to_all(dkv, CTX, 0, 0, tiled=True)

time: 141 us -> 135 us (0.957)
  the two profiles are of different devices: /device:TPU:32 before, /device:TPU:6 now
where the time goes in v7:
time: 135 us
  waiting for transfers between devices  59.9 us (44%)
  starting transfers between devices  28.1 us (21%)
  blocking collectives  23.9 us (18%)
  Pallas kernels  13.6 us (10%)
  local copies, waits for them, and re-layouts  4.83 us (4%)
  other arithmetic  3.49 us (3%)
    ppermute x15, waiting for transfers between devices, shifted(): return lax.ppermute(value, axis, pairs)  39.2 us
    all_to_all x1, blocking collectives, local(): part = lax.all_to_all(part, CTX, 0, 0, tiled=True)  23.9 us
    ppermute x15, starting transfers between devices, shifted(): return lax.ppermute(value, axis, pairs)  16.3 us
    all_to_all x1, waiting for transfers between devices, local(): dkv = lax.all_to_all(dkv, CTX, 0, 0, tiled=True)  12.4 us
    all_to_all x1, waiting for transfers between devices, local(): part = lax.all_to_all(part, 'zh', 0, 0, tiled=True)  8.33 us
    all_to_all x1, starting transfers between devices, local(): part = lax.all_to_all(part, 'zh', 0, 0, tiled=True)  7.48 us
    pallas_call x1, Pallas kernels, attention(): pl.pallas_call(functools.partial(attention_kernel, ny, per, DOCS, hd ** (...  5.76 us
    pallas_call x2, Pallas kernels, weight_part(): pl.pallas_call(functools.partial(weight_kernel, nx, z_hi, wide[0].shape[1...  5.5 us
  transfers between devices with their start and end apart: 17, of which 10 were waited for; matrix products, arithmetic and copies ran while one was open for 2% of the time, Pallas kernels for 8%

profile of v7, /device:TPU:6, one launch (start us, length us, event | category | flops | bytes accessed | tf_op | source)
XLA Modules:
  0.0 134.6 jit_solution(5126688773924956746)
XLA Ops:
  1.5 2.0 %collective-permute-start = (bf16[256,256]{1,0:T(8,128)(2,1)S(1)}, bf16[256,256]{1,0:T(8,128)(2,1)S(1)}, u32[]{:S(2)}, u32[]{:S(2)}) collective-permute-start(bf16[256,256]{1,0:T(8,128)(2,1)S(1)} %get-tuple-element.43), channel_id=1, source_target_pairs={{0,1},{1,0},{2,3},{3,2},{4,5},{5,4},{6,7},{7,6},{8,9},{9,8},{10,11... | collective-permute-start | bytes 393224 | tf_op jit(solution)/shard_map/ppermute | solution.py:33
  3.5 1.6 %copy-done = bf16[1,256,4096]{2,1,0:T(8,128)(2,1)S(1)} copy-done((bf16[1,256,4096]{2,1,0:T(8,128)(2,1)S(1)}, bf16[1,256,4096]{2,1,0:T(8,128)(2,1)}, u32[]{:S(2)}) %copy-start) | copy-done | bytes 2097176
  5.1 2.4 %split_features.1 = (bf16[1024,256]{1,0:T(8,128)(2,1)S(1)}, bf16[1024,256]{1,0:T(8,128)(2,1)}, bf16[1024,256]{1,0:T(8,128)(2,1)}, bf16[1024,256]{1,0:T(8,128)(2,1)}) custom-call(s32[1]{0:T(128)} %bitcast.6.info, bf16[256,4096]{1,0:T(8,128)(2,1)S(1)} %bitcast.23, bf16[256,4096]{1,0:T(8,128)(2,1)S(1)} %bitcast.24, bf16[256,4096]{1,0:T(8,128)(2,1)S(1)} %bitcast.25, ...), custom_call_target="tpu_custom_call" | custom-call | tf_op jit(solution)/shard_map/split_features/pallas_call | solution.py:214
  7.5 1.7 %collective-permute-start.1 = (bf16[2,256,256]{2,1,0:T(8,128)(2,1)S(1)}, bf16[2,256,256]{2,1,0:T(8,128)(2,1)S(1)}, u32[]{:S(2)}, u32[]{:S(2)}) collective-permute-start(bf16[2,256,256]{2,1,0:T(8,128)(2,1)S(1)} %pad_maximum_fusion.refs_0_), channel_id=1, source_target_pairs={{0,2},{2,4},{4,6},{6,0},{1,3},{3,5},{5,7},{7,1},{8,10},{10,12},{12... | collective-permute-start | bytes 786440 | tf_op jit(solution)/shard_map/ppermute | solution.py:33
  9.2 1.7 %collective-permute-start.3 = (bf16[2,256,256]{2,1,0:T(8,128)(2,1)S(1)}, bf16[2,256,256]{2,1,0:T(8,128)(2,1)S(1)}, u32[]{:S(2)}, u32[]{:S(2)}) collective-permute-start(bf16[2,256,256]{2,1,0:T(8,128)(2,1)S(1)} %pad_maximum_fusion.refs_0_), channel_id=1, source_target_pairs={{0,6},{2,0},{4,2},{6,4},{1,7},{3,1},{5,3},{7,5},{8,14},{10,8},{12,... | collective-permute-start | bytes 786440 | tf_op jit(solution)/shard_map/ppermute | solution.py:33
  10.8 5.8 %collective-permute-done.1.refs_1_ = bf16[2,256,256]{2,1,0:T(8,128)(2,1)S(1)} collective-permute-done((bf16[2,256,256]{2,1,0:T(8,128)(2,1)S(1)}, bf16[2,256,256]{2,1,0:T(8,128)(2,1)S(1)}, u32[]{:S(2)}, u32[]{:S(2)}) %collective-permute-start.1) | collective-permute-done | bytes 262176 | tf_op jit(solution)/shard_map/ppermute | solution.py:33
  18.3 2.9 %collective-permute-start.4 = (bf16[256,256]{1,0:T(8,128)(2,1)}, bf16[256,256]{1,0:T(8,128)(2,1)}, u32[]{:S(2)}, u32[]{:S(2)}) collective-permute-start(bf16[256,256]{1,0:T(8,128)(2,1)} %slice_bitcast_fusion), channel_id=1, source_target_pairs={{0,6},{2,0},{4,2},{6,4},{1,7},{3,1},{5,3},{7,5},{8,14},{10,8},{12,... | collective-permute-start | bytes 393224 | tf_op jit(solution)/shard_map/ppermute | solution.py:33
  21.7 2.4 %collective-permute-start.6 = (bf16[1024,256]{1,0:T(8,128)(2,1)}, bf16[1024,256]{1,0:T(8,128)(2,1)S(1)}, u32[]{:S(2)}, u32[]{:S(2)}) collective-permute-start(bf16[1024,256]{1,0:T(8,128)(2,1)} %get-tuple-element.32), channel_id=1, source_target_pairs={{0,32},{16,48},{32,0},{48,16},{1,33},{17,49},{33,1},{49,17},{2,34}... | collective-permute-start | bytes 1572872 | tf_op jit(solution)/shard_map/ppermute | solution.py:33
  24.1 5.8 %attention_backward.1 = (bf16[256,1024]{1,0:T(8,128)(2,1)}, bf16[8,256,256]{2,1,0:T(8,128)(2,1)}) custom-call(s32[1]{0:T(128)} %bitcast.info, s32[1,2048]{1,0:T(1,128)S(1)} %copy-done.3, bf16[256,1024]{1,0:T(8,128)(2,1)S(1)} %bitcast.28, bf16[256,1024]{1,0:T(8,128)(2,1)} %bitcast.33, bf16[2,256,256]{2,1,0:T(8,128)(2,1)S(1)} %pad_maximum_fusion.refs_0_, ...), custom_call_target="tpu_custom_call" | custom-call | flops 5368709120 | bytes 4194304 | tf_op jit(solution)/shard_map/attention_backward/pallas_call | solution.py:163
  29.9 6.4 %collective-permute-done.5.refs_1_ = bf16[1024,256]{1,0:T(8,128)(2,1)S(1)} collective-permute-done((bf16[1024,256]{1,0:T(8,128)(2,1)}, bf16[1024,256]{1,0:T(8,128)(2,1)S(1)}, u32[]{:S(2)}, u32[]{:S(2)}) %collective-permute-start.5) | collective-permute-done | bytes 524320 | tf_op jit(solution)/shard_map/ppermute | solution.py:33
  36.3 2.0 %collective-permute-done.6.refs_2_ = bf16[1024,256]{1,0:T(8,128)(2,1)S(1)} collective-permute-done((bf16[1024,256]{1,0:T(8,128)(2,1)}, bf16[1024,256]{1,0:T(8,128)(2,1)S(1)}, u32[]{:S(2)}, u32[]{:S(2)}) %collective-permute-start.6) | collective-permute-done | bytes 524320 | tf_op jit(solution)/shard_map/ppermute | solution.py:33
  38.3 7.8 %collective-permute-done.7.refs_3_ = bf16[1024,256]{1,0:T(8,128)(2,1)S(1)} collective-permute-done((bf16[1024,256]{1,0:T(8,128)(2,1)}, bf16[1024,256]{1,0:T(8,128)(2,1)S(1)}, u32[]{:S(2)}, u32[]{:S(2)}) %collective-permute-start.7) | collective-permute-done | bytes 524320 | tf_op jit(solution)/shard_map/ppermute | solution.py:33
  46.1 4.2 %all-to-all-start = ((bf16[8,256,256]{2,1,0:T(8,128)(2,1)}), bf16[8,256,256]{2,1,0:T(8,128)(2,1)}, u32[]{:S(2)}, u32[]{:S(2)}) async-start(bf16[8,256,256]{2,1,0:T(8,128)(2,1)} %get-tuple-element.35), calls=%async_computation | async-start | bytes 2097152 | tf_op jit(solution)/shard_map/all_to_all | solution.py:305
  51.6 2.1 %collective-permute-start.8 = (bf16[256,1024]{1,0:T(8,128)(2,1)S(1)}, bf16[256,1024]{1,0:T(8,128)(2,1)}, u32[]{:S(2)}, u32[]{:S(2)}) collective-permute-start(bf16[256,1024]{1,0:T(8,128)(2,1)S(1)} %copy-done.1), channel_id=1, source_target_pairs={{0,16},{16,32},{32,48},{48,0},{1,17},{17,33},{33,49},{49,1},{2,18}... | collective-permute-start | bytes 1572872 | tf_op jit(solution)/shard_map/ppermute | solution.py:33
  54.3 12.4 %all-to-all-done = bf16[8,256,256]{2,1,0:T(8,128)(2,1)} async-done(((bf16[8,256,256]{2,1,0:T(8,128)(2,1)}), bf16[8,256,256]{2,1,0:T(8,128)(2,1)}, u32[]{:S(2)}, u32[]{:S(2)}) %all-to-all-start) | async-done | bytes 1048608 | tf_op jit(solution)/shard_map/all_to_all | solution.py:305
  66.6 1.4 %reduce_sum.33.refs_8_ = bf16[256,256]{1,0:T(8,128)(2,1)S(1)} reduce(bf16[8,256,256]{2,1,0:T(8,128)(2,1)} %all-to-all-done, bf16[]{:T(256)} %constant.22.clone.1), dimensions={0}, to_apply=%region_0.0 | reduce | flops 458752 | bytes 1179650 | tf_op jit(solution)/shard_map/reduce_sum | solution.py:306
  68.9 10.7 %collective-permute-done.10.refs_7_ = bf16[256,1024]{1,0:T(8,128)(2,1)S(1)} collective-permute-done((bf16[256,1024]{1,0:T(8,128)(2,1)S(1)}, bf16[256,1024]{1,0:T(8,128)(2,1)S(1)}, u32[]{:S(2)}, u32[]{:S(2)}) %collective-permute-start.10) | collective-permute-done | bytes 524320 | tf_op jit(solution)/shard_map/ppermute | solution.py:33
  79.6 2.1 %collective-permute-done.11.refs_9_ = bf16[256,256]{1,0:T(8,128)(2,1)S(1)} collective-permute-done((bf16[256,256]{1,0:T(8,128)(2,1)S(1)}, bf16[256,256]{1,0:T(8,128)(2,1)S(1)}, u32[]{:S(2)}, u32[]{:S(2)}) %collective-permute-start.11) | collective-permute-done | bytes 131104 | tf_op jit(solution)/shard_map/ppermute | solution.py:33
  81.7 4.2 %collective-permute-done.13.refs_11_ = bf16[256,256]{1,0:T(8,128)(2,1)} collective-permute-done((bf16[256,256]{1,0:T(8,128)(2,1)S(1)}, bf16[256,256]{1,0:T(8,128)(2,1)}, u32[]{:S(2)}, u32[]{:S(2)}) %collective-permute-start.13) | collective-permute-done | bytes 131104 | tf_op jit(solution)/shard_map/ppermute | solution.py:33
  85.9 2.7 %weight_part.3 = bf16[8,4,16,1280]{3,2,1,0:T(8,128)(2,1)S(1)} custom-call(s32[1]{0:T(128)} %bitcast.15.info, bf16[1024,256]{1,0:T(8,128)(2,1)S(1)} %get-tuple-element.36.refs_0_, bf16[1024,256]{1,0:T(8,128)(2,1)S(1)} %collective-permute-done.5.refs_1_, bf16[1024,256]{1,0:T(8,128)(2,1)S(1)} %collective-permute-done.6.refs_2_, ...), custom_call_target="tpu_custom_call" | custom-call | flops 1342177280 | bytes 6291456 | tf_op jit(solution)/shard_map/weight_part/pallas_call | solution.py:264
  88.7 2.8 %weight_part.2 = bf16[8,4,16,1280]{3,2,1,0:T(8,128)(2,1)S(1)} custom-call(s32[1]{0:T(128)} %bitcast.14.info, bf16[1024,256]{1,0:T(8,128)(2,1)S(1)} %get-tuple-element.36.refs_0_, bf16[1024,256]{1,0:T(8,128)(2,1)S(1)} %collective-permute-done.5.refs_1_, bf16[1024,256]{1,0:T(8,128)(2,1)S(1)} %collective-permute-done.6.refs_2_, ...), custom_call_target="tpu_custom_call" | custom-call | flops 1342177280 | bytes 6291456 | tf_op jit(solution)/shard_map/weight_part/pallas_call | solution.py:264
  92.1 23.9 %all_to_all.15 = bf16[8,64,1280]{2,1,0:T(8,128)(2,1)S(1)} all-to-all(bf16[8,64,1280]{2,1,0:T(8,128)(2,1)S(1)} %bitcast.29), channel_id=1, replica_groups=mesh['zh'=4,'x'=4,'core'=2,'y'=4,'zl'=2] {'y','zl'}, dimensions={0} | all-to-all | bytes 2621440 | tf_op jit(solution)/shard_map/all_to_all | solution.py:314
  116.9 7.5 %all-to-all-start.2 = ((bf16[4,16,1280]{2,1,0:T(8,128)(2,1)}), bf16[4,16,1280]{2,1,0:T(8,128)(2,1)S(1)}, u32[]{:S(2)}, u32[]{:S(2)}) async-start(bf16[4,16,1280]{2,1,0:T(8,128)(2,1)} %bitcast.17), calls=%async_computation.2 | async-start | bytes 327680 | tf_op jit(solution)/shard_map/all_to_all | solution.py:316
  125.0 8.3 %all-to-all-done.2 = bf16[4,16,1280]{2,1,0:T(8,128)(2,1)S(1)} async-done(((bf16[4,16,1280]{2,1,0:T(8,128)(2,1)}), bf16[4,16,1280]{2,1,0:T(8,128)(2,1)S(1)}, u32[]{:S(2)}, u32[]{:S(2)}) %all-to-all-start.2) | async-done | bytes 163872 | tf_op jit(solution)/shard_map/all_to_all | solution.py:316
  (35 shorter events, 9.2 us)
Async XLA Ops:
  1.5 6.0 %collective-permute-start = (bf16[256,256]{1,0:T(8,128)(2,1)S(1)}, bf16[256,256]{1,0:T(8,128)(2,1)S(1)}, u32[]{:S(2)}, u32[]{:S(2)}) collective-permute-start(bf16[256,256]{1,0:T(8,128)(2,1)S(1)} %get-tuple-element.43), channel_id=1, source_target_pairs={{0,1},{1,0},{2,3},{3,2},{4,5},{5,4},{6,7},{7,6},{8,9},{9,8},{10,11... | collective-permute-start | bytes 393224 | tf_op jit(solution)/shard_map/ppermute | solution.py:33
  3.5 1.6 %copy-start = (bf16[1,256,4096]{2,1,0:T(8,128)(2,1)S(1)}, bf16[1,256,4096]{2,1,0:T(8,128)(2,1)}, u32[]{:S(2)}) copy-start(bf16[1,256,4096]{2,1,0:T(8,128)(2,1)} %param.6) | copy-start | bytes 6291460
  5.1 19.0 %copy-start.2 = (bf16[1,256,1024]{2,1,0:T(8,128)(2,1)S(1)}, bf16[1,256,1024]{2,1,0:T(8,128)(2,1)}, u32[]{:S(2)}) copy-start(bf16[1,256,1024]{2,1,0:T(8,128)(2,1)} %param.7) | copy-start | bytes 1572868
  5.1 19.0 %copy-start.3 = (s32[1,2048]{1,0:T(1,128)S(1)}, s32[1,2048]{1,0:T(1,128)}, u32[]{:S(2)}) copy-start(s32[1,2048]{1,0:T(1,128)} %docs_ref.1) | copy-start | bytes 24580
  7.5 9.1 %collective-permute-start.1 = (bf16[2,256,256]{2,1,0:T(8,128)(2,1)S(1)}, bf16[2,256,256]{2,1,0:T(8,128)(2,1)S(1)}, u32[]{:S(2)}, u32[]{:S(2)}) collective-permute-start(bf16[2,256,256]{2,1,0:T(8,128)(2,1)S(1)} %pad_maximum_fusion.refs_0_), channel_id=1, source_target_pairs={{0,2},{2,4},{4,6},{6,0},{1,3},{3,5},{5,7},{7,1},{8,10},{10,12},{12... | collective-permute-start | bytes 786440 | tf_op jit(solution)/shard_map/ppermute | solution.py:33
  9.2 8.4 %collective-permute-start.3 = (bf16[2,256,256]{2,1,0:T(8,128)(2,1)S(1)}, bf16[2,256,256]{2,1,0:T(8,128)(2,1)S(1)}, u32[]{:S(2)}, u32[]{:S(2)}) collective-permute-start(bf16[2,256,256]{2,1,0:T(8,128)(2,1)S(1)} %pad_maximum_fusion.refs_0_), channel_id=1, source_target_pairs={{0,6},{2,0},{4,2},{6,4},{1,7},{3,1},{5,3},{7,5},{8,14},{10,8},{12,... | collective-permute-start | bytes 786440 | tf_op jit(solution)/shard_map/ppermute | solution.py:33
  17.3 6.8 %collective-permute-start.2 = (bf16[256,256]{1,0:T(8,128)(2,1)}, bf16[256,256]{1,0:T(8,128)(2,1)S(1)}, u32[]{:S(2)}, u32[]{:S(2)}) collective-permute-start(bf16[256,256]{1,0:T(8,128)(2,1)} %slice_bitcast_fusion.1), channel_id=1, source_target_pairs={{0,2},{2,4},{4,6},{6,0},{1,3},{3,5},{5,7},{7,1},{8,10},{10,12},{12... | collective-permute-start | bytes 393224 | tf_op jit(solution)/shard_map/ppermute | solution.py:33
  18.3 5.8 %collective-permute-start.4 = (bf16[256,256]{1,0:T(8,128)(2,1)}, bf16[256,256]{1,0:T(8,128)(2,1)}, u32[]{:S(2)}, u32[]{:S(2)}) collective-permute-start(bf16[256,256]{1,0:T(8,128)(2,1)} %slice_bitcast_fusion), channel_id=1, source_target_pairs={{0,6},{2,0},{4,2},{6,4},{1,7},{3,1},{5,3},{7,5},{8,14},{10,8},{12,... | collective-permute-start | bytes 393224 | tf_op jit(solution)/shard_map/ppermute | solution.py:33
  21.2 15.1 %collective-permute-start.5 = (bf16[1024,256]{1,0:T(8,128)(2,1)}, bf16[1024,256]{1,0:T(8,128)(2,1)S(1)}, u32[]{:S(2)}, u32[]{:S(2)}) collective-permute-start(bf16[1024,256]{1,0:T(8,128)(2,1)} %get-tuple-element.31), channel_id=1, source_target_pairs={{0,16},{16,32},{32,48},{48,0},{1,17},{17,33},{33,49},{49,1},{2,18}... | collective-permute-start | bytes 1572872 | tf_op jit(solution)/shard_map/ppermute | solution.py:33
  21.7 16.6 %collective-permute-start.6 = (bf16[1024,256]{1,0:T(8,128)(2,1)}, bf16[1024,256]{1,0:T(8,128)(2,1)S(1)}, u32[]{:S(2)}, u32[]{:S(2)}) collective-permute-start(bf16[1024,256]{1,0:T(8,128)(2,1)} %get-tuple-element.32), channel_id=1, source_target_pairs={{0,32},{16,48},{32,0},{48,16},{1,33},{17,49},{33,1},{49,17},{2,34}... | collective-permute-start | bytes 1572872 | tf_op jit(solution)/shard_map/ppermute | solution.py:33
  24.1 22.0 %collective-permute-start.7 = (bf16[1024,256]{1,0:T(8,128)(2,1)}, bf16[1024,256]{1,0:T(8,128)(2,1)S(1)}, u32[]{:S(2)}, u32[]{:S(2)}) collective-permute-start(bf16[1024,256]{1,0:T(8,128)(2,1)} %get-tuple-element.33), channel_id=1, source_target_pairs={{0,48},{16,0},{32,16},{48,32},{1,49},{17,1},{33,17},{49,33},{2,50}... | collective-permute-start | bytes 1572872 | tf_op jit(solution)/shard_map/ppermute | solution.py:33
  29.9 20.5 %copy-start.1 = (bf16[256,1024]{1,0:T(8,128)(2,1)S(1)}, bf16[256,1024]{1,0:T(8,128)(2,1)}, u32[]{:S(2)}) copy-start(bf16[256,1024]{1,0:T(8,128)(2,1)} %get-tuple-element.34.refs_4_) | copy-start | bytes 1572868
  46.1 20.5 %all-to-all-start = ((bf16[8,256,256]{2,1,0:T(8,128)(2,1)}), bf16[8,256,256]{2,1,0:T(8,128)(2,1)}, u32[]{:S(2)}, u32[]{:S(2)}) async-start(bf16[8,256,256]{2,1,0:T(8,128)(2,1)} %get-tuple-element.35), calls=%async_computation | async-start | bytes 2097152 | tf_op jit(solution)/shard_map/all_to_all | solution.py:305
  50.4 29.2 %collective-permute-start.10 = (bf16[256,1024]{1,0:T(8,128)(2,1)S(1)}, bf16[256,1024]{1,0:T(8,128)(2,1)S(1)}, u32[]{:S(2)}, u32[]{:S(2)}) collective-permute-start(bf16[256,1024]{1,0:T(8,128)(2,1)S(1)} %copy-done.1), channel_id=1, source_target_pairs={{0,48},{16,0},{32,16},{48,32},{1,49},{17,1},{33,17},{49,33},{2,50}... | collective-permute-start | bytes 1572872 | tf_op jit(solution)/shard_map/ppermute | solution.py:33
  51.6 27.9 %collective-permute-start.8 = (bf16[256,1024]{1,0:T(8,128)(2,1)S(1)}, bf16[256,1024]{1,0:T(8,128)(2,1)}, u32[]{:S(2)}, u32[]{:S(2)}) collective-permute-start(bf16[256,1024]{1,0:T(8,128)(2,1)S(1)} %copy-done.1), channel_id=1, source_target_pairs={{0,16},{16,32},{32,48},{48,0},{1,17},{17,33},{33,49},{49,1},{2,18}... | collective-permute-start | bytes 1572872 | tf_op jit(solution)/shard_map/ppermute | solution.py:33
  53.7 25.9 %collective-permute-start.9 = (bf16[256,1024]{1,0:T(8,128)(2,1)S(1)}, bf16[256,1024]{1,0:T(8,128)(2,1)}, u32[]{:S(2)}, u32[]{:S(2)}) collective-permute-start(bf16[256,1024]{1,0:T(8,128)(2,1)S(1)} %copy-done.1), channel_id=1, source_target_pairs={{0,32},{16,48},{32,0},{48,16},{1,33},{17,49},{33,1},{49,17},{2,34}... | collective-permute-start | bytes 1572872 | tf_op jit(solution)/shard_map/ppermute | solution.py:33
  68.0 13.7 %collective-permute-start.11 = (bf16[256,256]{1,0:T(8,128)(2,1)S(1)}, bf16[256,256]{1,0:T(8,128)(2,1)S(1)}, u32[]{:S(2)}, u32[]{:S(2)}) collective-permute-start(bf16[256,256]{1,0:T(8,128)(2,1)S(1)} %reduce_sum.33.refs_8_), channel_id=1, source_target_pairs={{0,16},{16,32},{32,48},{48,0},{1,17},{17,33},{33,49},{49,1},{2,18}... | collective-permute-start | bytes 393224 | tf_op jit(solution)/shard_map/ppermute | solution.py:33
  68.1 13.6 %collective-permute-start.12 = (bf16[256,256]{1,0:T(8,128)(2,1)S(1)}, bf16[256,256]{1,0:T(8,128)(2,1)S(1)}, u32[]{:S(2)}, u32[]{:S(2)}) collective-permute-start(bf16[256,256]{1,0:T(8,128)(2,1)S(1)} %reduce_sum.33.refs_8_), channel_id=1, source_target_pairs={{0,32},{16,48},{32,0},{48,16},{1,33},{17,49},{33,1},{49,17},{2,34}... | collective-permute-start | bytes 393224 | tf_op jit(solution)/shard_map/ppermute | solution.py:33
  79.6 6.3 %collective-permute-start.13 = (bf16[256,256]{1,0:T(8,128)(2,1)S(1)}, bf16[256,256]{1,0:T(8,128)(2,1)}, u32[]{:S(2)}, u32[]{:S(2)}) collective-permute-start(bf16[256,256]{1,0:T(8,128)(2,1)S(1)} %reduce_sum.33.refs_8_), channel_id=1, source_target_pairs={{0,48},{16,0},{32,16},{48,32},{1,49},{17,1},{33,17},{49,33},{2,50}... | collective-permute-start | bytes 393224 | tf_op jit(solution)/shard_map/ppermute | solution.py:33
  88.6 3.1 %collective-permute-start.14 = (bf16[8,4,16,1280]{3,2,1,0:T(8,128)(2,1)S(1)}, bf16[8,4,16,1280]{3,2,1,0:T(8,128)(2,1)S(1)}, u32[]{:S(2)}, u32[]{:S(2)}) collective-permute-start(bf16[8,4,16,1280]{3,2,1,0:T(8,128)(2,1)S(1)} %weight_part.3), channel_id=1, source_target_pairs={{0,8},{8,0},{1,9},{9,1},{2,10},{10,2},{3,11},{11,3},{4,12},{12,4},... | collective-permute-start | bytes 3932168 | tf_op jit(solution)/shard_map/ppermute | solution.py:33
  116.9 16.5 %all-to-all-start.2 = ((bf16[4,16,1280]{2,1,0:T(8,128)(2,1)}), bf16[4,16,1280]{2,1,0:T(8,128)(2,1)S(1)}, u32[]{:S(2)}, u32[]{:S(2)}) async-start(bf16[4,16,1280]{2,1,0:T(8,128)(2,1)} %bitcast.17), calls=%async_computation.2 | async-start | bytes 327680 | tf_op jit(solution)/shard_map/all_to_all | solution.py:316

commit v8 on v7

--- a/solution.py
+++ b/solution.py
@@ -45,21 +45,12 @@
     (pair_ref, before_ref, far_refs, after_ref), refs = (refs[0], refs[1], refs[2:4], refs[4]), refs[5:]
     dq_ref, refs = refs[0], refs[1:]
     out_ref, refs = refs[0], refs[1:]
-    kv_s, kt_s, acc_s, e_s, dp_s, md_s, stat_s, dqt_s, qt_s, dot_s, p_s, ds_s, qk_s, dk_s, starts_ref, sem = refs
+    kv_s, kt_s, e_s, dp_s, md_s, stat_s, dqt_s, qt_s, dot_s, p_s, ds_s, qk_s, dk_s, starts_ref, sem = refs
     rows = q_ref.shape[0]
     hd = kt_s.shape[1]
     place = info[0]
-    documents = docs_ref[...]
-    mine = docs_ref[:, pl.ds(pl.multiple_of(place * rows, rows), rows)]
-    starts = jnp.zeros((1, rows), jnp.int32)
-    for t in range(docs - 1):
-        length = jnp.sum((documents == t).astype(jnp.int32))
-        starts += jnp.where(mine > t, length, 0)
-    starts_ref[...] = starts
-    limit = jnp.max(starts)
-    used = place - jnp.min(starts) // rows + 1
     power = scale * math.log2(math.e)
-    farthest = place // 2 - (place - used + 1) // 2
+    farthest = place // 2
 
     copies = [
         (0, pltpu.make_async_copy(pair_ref, kv_s.at[pl.ds(0, 2)], sem.at[0])),
@@ -71,7 +62,6 @@
     for s, copy in copies:
         pl.when(s <= farthest)(copy.start)
 
-    acc_s[...] = jnp.zeros_like(acc_s)
     for h in range(per):
         cols = slice(h * hd, (h + 1) * hd)
         span = slice(h * rows, (h + 1) * rows)
@@ -84,14 +74,24 @@
         stat_s[2, h] = jnp.zeros((1, rows), F32)
     dqt_s[...] = jnp.zeros_like(dqt_s)
 
+    documents = docs_ref[...]
+    mine = docs_ref[:, pl.ds(pl.multiple_of(place * rows, rows), rows)]
+    starts = jnp.zeros((1, rows), jnp.int32)
+    for t in range(docs - 1):
+        length = jnp.sum((documents == t).astype(jnp.int32))
+        starts += jnp.where(mine > t, length, 0)
+    starts_ref[...] = starts
+    limit = jnp.max(starts)
+    used = place - jnp.min(starts) // rows + 1
     for s, copy in copies:
         pl.when(s <= farthest)(copy.wait)
-    for s in range(ny):
-
-        @pl.when(s <= farthest)
-        def _():
-            for k in range(2):
-                kt_s[2 * s + k] = kv_s[2 * s + k, :, :hd].T
+
+    def clear(block, carry):
+        out_ref[block] = jnp.zeros(out_ref.shape[1:], BF)
+        return carry
+
+    lax.fori_loop(0, place - used + 1, clear, 0)
+    lax.fori_loop(place + 1, out_ref.shape[0], clear, 0)
 
     def slot(d):
         block = place - d
@@ -101,6 +101,7 @@
         at = slot(d)
         kd = kv_s[at, :, :hd]
         vd = kv_s[at, :, hd:]
+        kt_s[at] = kd.T
         if masked:
             kp = lax.broadcasted_iota(jnp.int32, (rows, rows), 0) + (place - d) * rows
             qp = lax.broadcasted_iota(jnp.int32, (rows, rows), 1) + place * rows
@@ -134,13 +135,12 @@
     delta = [stat_s[2, h] * inverse[h] for h in range(per)]
 
     def second(d, carry):
-        at = place - d
         for h in range(per):
             p = e_s[d, h] * (jnp.exp2((md_s[d, h] - tops[h]) * power) * inverse[h])
             p_s[:, h * rows : (h + 1) * rows] = p.astype(BF)
             ds_s[:, h * rows : (h + 1) * rows] = (p * (dp_s[d, h] - delta[h])).astype(BF)
-        acc_s[at, :, hd:] += dot(p_s[...], dk_s[...])
-        acc_s[at, :, :hd] += dot(ds_s[...], qk_s[...])
+        out_ref[place - d, :, hd:] = dot(p_s[...], dk_s[...]).astype(BF)
+        out_ref[place - d, :, :hd] = (dot(ds_s[...], qk_s[...]) * scale).astype(BF)
         dqt_s[...] += dot(kt_s[slot(d)], ds_s[...])
         return carry
 
@@ -148,8 +148,6 @@
 
     for h in range(per):
         dq_ref[:, h * hd : (h + 1) * hd] = (dqt_s[:, h * rows : (h + 1) * rows].T * scale).astype(BF)
-    out_ref[:, :, :hd] = (acc_s[:, :, :hd] * scale).astype(BF)
-    out_ref[:, :, hd:] = acc_s[:, :, hd:].astype(BF)
 
 
 def attention(q, do, kv, docs, place, ny):
@@ -173,7 +171,6 @@
         scratch_shapes=[
             pltpu.VMEM((blocks, rows, 2 * hd), BF),
             pltpu.VMEM((blocks, hd, rows), BF),
-            pltpu.VMEM((blocks, rows, 2 * hd), F32),
             pltpu.VMEM((blocks, per, rows, rows), F32),
             pltpu.VMEM((blocks, per, rows, rows), F32),
             pltpu.VMEM((blocks, per, 1, rows), F32),
@@ -225,10 +222,10 @@
     )(my_x[None], *([x] * nx))
 
 
-def weight_kernel(nx, z_hi, n_wide, info, *refs):
-    f_refs, wide_refs, narrow_refs = refs[:nx], refs[nx : 2 * nx], refs[2 * nx : 3 * nx]
-    out_ref, ft_s = refs[3 * nx :]
-    rows = wide_refs[0].shape[0]
+def weight_kernel(nx, z_hi, info, *refs):
+    f_refs, wide_refs, narrow_refs = refs[:nx], refs[nx : 2 * nx + 1], refs[2 * nx + 1 : 3 * nx + 1]
+    out_ref, ft_s = refs[3 * nx + 1 :]
+    rows, width = wide_refs[0].shape
     each = f_refs[0].shape[0] // (z_hi * 2)
     cols = 256
     part = out_ref.shape[2]
@@ -237,21 +234,23 @@
             at = pl.multiple_of((z * 2 + info[0]) * each, each)
             ft_s[z * each : (z + 1) * each, s * rows : (s + 1) * rows] = f_refs[s][pl.ds(at, each)]
 
-    def columns(g_refs, at, to):
-        total = dot(ft_s[:, :rows], g_refs[0][:, at : at + cols])
+    def columns(blocks, to):
+        total = dot(ft_s[:, :rows], blocks[0])
         for s in range(1, nx):
-            total += dot(ft_s[:, s * rows : (s + 1) * rows], g_refs[s][:, at : at + cols])
+            total += dot(ft_s[:, s * rows : (s + 1) * rows], blocks[s])
         total = total.astype(BF)
         for z in range(z_hi):
             for p in range(out_ref.shape[0]):
                 row = z * each + p * part
                 out_ref[p, z, :, to : to + cols] = total[row : row + part]
 
-    for j in range(out_ref.shape[3] // cols):
-        if j < n_wide:
-            columns(wide_refs, j * cols, j * cols)
-        else:
-            columns(narrow_refs, (j - n_wide) * cols, j * cols)
+    for at in range(0, width, cols):
+        own, left, far_first, far_second, right = wide_refs
+        split = far_first.shape[1]
+        far = far_first[:, at : at + cols] if at < split else far_second[:, at - split : at - split + cols]
+        columns([own[:, at : at + cols], left[:, at : at + cols], far, right[:, at : at + cols]], at)
+    for at in range(0, narrow_refs[0].shape[1], cols):
+        columns([ref[:, at : at + cols] for ref in narrow_refs], width + at)
 
 
 def weight_part(features, wide, narrow, which, z_hi, pieces):
@@ -262,7 +261,7 @@
     operands = [*features, *wide, *narrow]
     out_shape = (pieces, z_hi, each // pieces, n)
     return pl.pallas_call(
-        functools.partial(weight_kernel, nx, z_hi, wide[0].shape[1] // 256),
+        functools.partial(weight_kernel, nx, z_hi),
         in_specs=[pl.BlockSpec(memory_space=pltpu.SMEM)]
         + [pl.BlockSpec(memory_space=pltpu.VMEM)] * len(operands),
         out_specs=pl.BlockSpec(memory_space=pltpu.VMEM),
@@ -296,15 +295,15 @@
     far = shifted(before[0], "y", ny, 1), shifted(after[1], "y", ny, -1)
     features = [shifted(part, "x", nx, s) if s else part for s, part in enumerate(parts)]
 
-    def along_x(grads):
-        return [grads] + [shifted(grads, "x", nx, s) for s in range(1, nx)]
-
     dq, dkv = attention(q, do, [pair, before, *far, after], doc_ids, place, ny)
     dq, dkv, features = lax.optimization_barrier((dq, dkv, features))
-    wide = along_x(dq)
+    left, right = shifted(dq, "x", nx, 1), shifted(dq, "x", nx, -1)
+    half = dq.shape[1] // 2
+    far = shifted(left[:, :half], "x", nx, 1), shifted(right[:, half:], "x", nx, -1)
+    wide = [dq, left, *far, right]
     dkv = lax.all_to_all(dkv, CTX, 0, 0, tiled=True)
     dkv_own = jnp.sum(dkv.astype(F32), axis=0).astype(BF)
-    narrow = along_x(dkv_own)
+    narrow = [dkv_own] + [shifted(dkv_own, "x", nx, s) for s in range(1, nx)]
 
     theirs = weight_part(features, wide, narrow, 1 - my_core, z_hi, ctx)
     theirs = shifted(theirs, "core", nc, 1)

time: 135 us -> 132 us (0.978)
  the two profiles are of different devices: /device:TPU:6 before, /device:TPU:32 now
where the time goes in v8:
time: 132 us
  waiting for transfers between devices  43.6 us (33%)
  starting transfers between devices  38.5 us (29%)
  blocking collectives  23.1 us (18%)
  Pallas kernels  14.4 us (11%)
  local copies, waits for them, and re-layouts  7.81 us (6%)
  other arithmetic  3.49 us (3%)
    ppermute x16, waiting for transfers between devices, shifted(): return lax.ppermute(value, axis, pairs)  35.5 us
    ppermute x16, starting transfers between devices, shifted(): return lax.ppermute(value, axis, pairs)  24.9 us
    all_to_all x1, blocking collectives, local(): part = lax.all_to_all(part, CTX, 0, 0, tiled=True)  23.1 us
    all_to_all x1, waiting for transfers between devices, local(): part = lax.all_to_all(part, 'zh', 0, 0, tiled=True)  8.08 us
    all_to_all x1, starting transfers between devices, local(): part = lax.all_to_all(part, 'zh', 0, 0, tiled=True)  7.5 us
    pallas_call x1, Pallas kernels, attention(): pl.pallas_call(functools.partial(attention_kernel, ny, per, DOCS, hd ** (...  6.7 us
    all_to_all x1, starting transfers between devices, local(): dkv = lax.all_to_all(dkv, CTX, 0, 0, tiled=True)  6.09 us
    pallas_call x2, Pallas kernels, weight_part(): pl.pallas_call(functools.partial(weight_kernel, nx, z_hi), in_specs=[pl.B...  5.33 us
  transfers between devices with their start and end apart: 18, of which 8 were waited for; matrix products, arithmetic and copies ran while one was open for 3% of the time, Pallas kernels for 9%

profile of v8, /device:TPU:32, one launch (start us, length us, event | category | flops | bytes accessed | tf_op | source)
XLA Modules:
  0.0 131.7 jit_solution(14269203341928558049)
XLA Ops:
  1.5 1.9 %collective-permute-start = (bf16[256,256]{1,0:T(8,128)(2,1)S(1)}, bf16[256,256]{1,0:T(8,128)(2,1)S(1)}, u32[]{:S(2)}, u32[]{:S(2)}) collective-permute-start(bf16[256,256]{1,0:T(8,128)(2,1)S(1)} %get-tuple-element.43), channel_id=1, source_target_pairs={{0,1},{1,0},{2,3},{3,2},{4,5},{5,4},{6,7},{7,6},{8,9},{9,8},{10,11... | collective-permute-start | bytes 393224 | tf_op jit(solution)/shard_map/ppermute | solution.py:33
  3.5 1.6 %copy-done = bf16[1,256,4096]{2,1,0:T(8,128)(2,1)S(1)} copy-done((bf16[1,256,4096]{2,1,0:T(8,128)(2,1)S(1)}, bf16[1,256,4096]{2,1,0:T(8,128)(2,1)}, u32[]{:S(2)}) %copy-start) | copy-done | bytes 2097176
  5.1 2.4 %split_features.1 = (bf16[1024,256]{1,0:T(8,128)(2,1)S(1)}, bf16[1024,256]{1,0:T(8,128)(2,1)}, bf16[1024,256]{1,0:T(8,128)(2,1)}, bf16[1024,256]{1,0:T(8,128)(2,1)}) custom-call(s32[1]{0:T(128)} %bitcast.6.info, bf16[256,4096]{1,0:T(8,128)(2,1)S(1)} %bitcast.23, bf16[256,4096]{1,0:T(8,128)(2,1)S(1)} %bitcast.24, bf16[256,4096]{1,0:T(8,128)(2,1)S(1)} %bitcast.25, ...), custom_call_target="tpu_custom_call" | custom-call | tf_op jit(solution)/shard_map/split_features/pallas_call | solution.py:211
  8.5 2.2 %collective-permute-start.3 = (bf16[2,256,256]{2,1,0:T(8,128)(2,1)S(1)}, bf16[2,256,256]{2,1,0:T(8,128)(2,1)S(1)}, u32[]{:S(2)}, u32[]{:S(2)}) collective-permute-start(bf16[2,256,256]{2,1,0:T(8,128)(2,1)S(1)} %pad_maximum_fusion.refs_0_), channel_id=1, source_target_pairs={{0,6},{2,0},{4,2},{6,4},{1,7},{3,1},{5,3},{7,5},{8,14},{10,8},{12,... | collective-permute-start | bytes 786440 | tf_op jit(solution)/shard_map/ppermute | solution.py:33
  10.8 4.6 %collective-permute-done.1.refs_1_ = bf16[2,256,256]{2,1,0:T(8,128)(2,1)S(1)} collective-permute-done((bf16[2,256,256]{2,1,0:T(8,128)(2,1)S(1)}, bf16[2,256,256]{2,1,0:T(8,128)(2,1)S(1)}, u32[]{:S(2)}, u32[]{:S(2)}) %collective-permute-start.1) | collective-permute-done | bytes 262176 | tf_op jit(solution)/shard_map/ppermute | solution.py:33
  15.8 3.0 %collective-permute-start.4 = (bf16[256,256]{1,0:T(8,128)(2,1)S(1)}, bf16[256,256]{1,0:T(8,128)(2,1)S(1)}, u32[]{:S(2)}, u32[]{:S(2)}) collective-permute-start(bf16[256,256]{1,0:T(8,128)(2,1)S(1)} %slice_bitcast_fusion), channel_id=1, source_target_pairs={{0,6},{2,0},{4,2},{6,4},{1,7},{3,1},{5,3},{7,5},{8,14},{10,8},{12,... | collective-permute-start | bytes 393224 | tf_op jit(solution)/shard_map/ppermute | solution.py:33
  18.8 1.5 %collective-permute-start.5 = (bf16[1024,256]{1,0:T(8,128)(2,1)}, bf16[1024,256]{1,0:T(8,128)(2,1)S(1)}, u32[]{:S(2)}, u32[]{:S(2)}) collective-permute-start(bf16[1024,256]{1,0:T(8,128)(2,1)} %get-tuple-element.31), channel_id=1, source_target_pairs={{0,16},{16,32},{32,48},{48,0},{1,17},{17,33},{33,49},{49,1},{2,18}... | collective-permute-start | bytes 1572872 | tf_op jit(solution)/shard_map/ppermute | solution.py:33
  20.3 2.7 %collective-permute-start.6 = (bf16[1024,256]{1,0:T(8,128)(2,1)}, bf16[1024,256]{1,0:T(8,128)(2,1)S(1)}, u32[]{:S(2)}, u32[]{:S(2)}) collective-permute-start(bf16[1024,256]{1,0:T(8,128)(2,1)} %get-tuple-element.32), channel_id=1, source_target_pairs={{0,32},{16,48},{32,0},{48,16},{1,33},{17,49},{33,1},{49,17},{2,34}... | collective-permute-start | bytes 1572872 | tf_op jit(solution)/shard_map/ppermute | solution.py:33
  23.0 1.4 %collective-permute-start.7 = (bf16[1024,256]{1,0:T(8,128)(2,1)}, bf16[1024,256]{1,0:T(8,128)(2,1)S(1)}, u32[]{:S(2)}, u32[]{:S(2)}) collective-permute-start(bf16[1024,256]{1,0:T(8,128)(2,1)} %get-tuple-element.33), channel_id=1, source_target_pairs={{0,48},{16,0},{32,16},{48,32},{1,49},{17,1},{33,17},{49,33},{2,50}... | collective-permute-start | bytes 1572872 | tf_op jit(solution)/shard_map/ppermute | solution.py:33
  25.5 6.7 %attention_backward.1 = (bf16[256,1024]{1,0:T(8,128)(2,1)}, bf16[8,256,256]{2,1,0:T(8,128)(2,1)}) custom-call(s32[1]{0:T(128)} %bitcast.info, s32[1,2048]{1,0:T(1,128)S(1)} %copy-done.6, bf16[256,1024]{1,0:T(8,128)(2,1)S(1)} %bitcast.28, bf16[256,1024]{1,0:T(8,128)(2,1)} %bitcast.33, bf16[2,256,256]{2,1,0:T(8,128)(2,1)S(1)} %pad_maximum_fusion.refs_0_, ...), custom_call_target="tpu_custom_call" | custom-call | flops 5368709120 | bytes 4194304 | tf_op jit(solution)/shard_map/attention_backward/pallas_call | solution.py:161
  32.3 1.5 %collective-permute-done.5.refs_1_ = bf16[1024,256]{1,0:T(8,128)(2,1)S(1)} collective-permute-done((bf16[1024,256]{1,0:T(8,128)(2,1)}, bf16[1024,256]{1,0:T(8,128)(2,1)S(1)}, u32[]{:S(2)}, u32[]{:S(2)}) %collective-permute-start.5) | collective-permute-done | bytes 524320 | tf_op jit(solution)/shard_map/ppermute | solution.py:33
  33.7 10.1 %collective-permute-done.6.refs_2_ = bf16[1024,256]{1,0:T(8,128)(2,1)S(1)} collective-permute-done((bf16[1024,256]{1,0:T(8,128)(2,1)}, bf16[1024,256]{1,0:T(8,128)(2,1)S(1)}, u32[]{:S(2)}, u32[]{:S(2)}) %collective-permute-start.6) | collective-permute-done | bytes 524320 | tf_op jit(solution)/shard_map/ppermute | solution.py:33
  44.6 6.1 %all-to-all-start = ((bf16[8,256,256]{2,1,0:T(8,128)(2,1)}), bf16[8,256,256]{2,1,0:T(8,128)(2,1)}, u32[]{:S(2)}, u32[]{:S(2)}) async-start(bf16[8,256,256]{2,1,0:T(8,128)(2,1)} %get-tuple-element.35), calls=%async_computation | async-start | bytes 2097152 | tf_op jit(solution)/shard_map/all_to_all | solution.py:304
  50.7 2.1 %collective-permute-start.10 = (bf16[256,1024]{1,0:T(8,128)(2,1)S(1)}, bf16[256,1024]{1,0:T(8,128)(2,1)S(1)}, u32[]{:S(2)}, u32[]{:S(2)}) collective-permute-start(bf16[256,1024]{1,0:T(8,128)(2,1)S(1)} %copy-done.1), channel_id=1, source_target_pairs={{0,48},{16,0},{32,16},{48,32},{1,49},{17,1},{33,17},{49,33},{2,50}... | collective-permute-start | bytes 1572872 | tf_op jit(solution)/shard_map/ppermute | solution.py:33
  52.8 11.1 %collective-permute-done.10.refs_8_ = bf16[256,1024]{1,0:T(8,128)(2,1)S(1)} collective-permute-done((bf16[256,1024]{1,0:T(8,128)(2,1)S(1)}, bf16[256,1024]{1,0:T(8,128)(2,1)S(1)}, u32[]{:S(2)}, u32[]{:S(2)}) %collective-permute-start.10) | collective-permute-done | bytes 524320 | tf_op jit(solution)/shard_map/ppermute | solution.py:33
  64.6 3.7 %collective-permute-start.11 = (bf16[256,512]{1,0:T(8,128)(2,1)}, bf16[256,512]{1,0:T(8,128)(2,1)S(1)}, u32[]{:S(2)}, u32[]{:S(2)}) collective-permute-start(bf16[256,512]{1,0:T(8,128)(2,1)} %slice.41), channel_id=1, source_target_pairs={{0,48},{16,0},{32,16},{48,32},{1,49},{17,1},{33,17},{49,33},{2,50}... | collective-permute-start | bytes 786440 | tf_op jit(solution)/shard_map/ppermute | solution.py:33
  70.5 4.7 %collective-permute-start.13 = (bf16[256,256]{1,0:T(8,128)(2,1)S(1)}, bf16[256,256]{1,0:T(8,128)(2,1)}, u32[]{:S(2)}, u32[]{:S(2)}) collective-permute-start(bf16[256,256]{1,0:T(8,128)(2,1)S(1)} %reduce_sum.33.refs_9_), channel_id=1, source_target_pairs={{0,32},{16,48},{32,0},{48,16},{1,33},{17,49},{33,1},{49,17},{2,34}... | collective-permute-start | bytes 393224 | tf_op jit(solution)/shard_map/ppermute | solution.py:33
  75.1 5.1 %collective-permute-done.9.refs_6_ = bf16[256,512]{1,0:T(8,128)(2,1)} collective-permute-done((bf16[256,512]{1,0:T(8,128)(2,1)}, bf16[256,512]{1,0:T(8,128)(2,1)}, u32[]{:S(2)}, u32[]{:S(2)}) %collective-permute-start.9) | collective-permute-done | bytes 262176 | tf_op jit(solution)/shard_map/ppermute | solution.py:33
  80.2 2.8 %collective-permute-done.12.refs_10_ = bf16[256,256]{1,0:T(8,128)(2,1)} collective-permute-done((bf16[256,256]{1,0:T(8,128)(2,1)S(1)}, bf16[256,256]{1,0:T(8,128)(2,1)}, u32[]{:S(2)}, u32[]{:S(2)}) %collective-permute-start.12) | collective-permute-done | bytes 131104 | tf_op jit(solution)/shard_map/ppermute | solution.py:33
  84.1 2.7 %weight_part.3 = bf16[8,4,16,1280]{3,2,1,0:T(8,128)(2,1)S(1)} custom-call(s32[1]{0:T(128)} %bitcast.15.info, bf16[1024,256]{1,0:T(8,128)(2,1)S(1)} %get-tuple-element.36.refs_0_, bf16[1024,256]{1,0:T(8,128)(2,1)S(1)} %collective-permute-done.5.refs_1_, bf16[1024,256]{1,0:T(8,128)(2,1)S(1)} %collective-permute-done.6.refs_2_, ...), custom_call_target="tpu_custom_call" | custom-call | flops 1342177280 | bytes 6291456 | tf_op jit(solution)/shard_map/weight_part/pallas_call | solution.py:263
  86.9 2.6 %weight_part.2 = bf16[8,4,16,1280]{3,2,1,0:T(8,128)(2,1)S(1)} custom-call(s32[1]{0:T(128)} %bitcast.14.info, bf16[1024,256]{1,0:T(8,128)(2,1)S(1)} %get-tuple-element.36.refs_0_, bf16[1024,256]{1,0:T(8,128)(2,1)S(1)} %collective-permute-done.5.refs_1_, bf16[1024,256]{1,0:T(8,128)(2,1)S(1)} %collective-permute-done.6.refs_2_, ...), custom_call_target="tpu_custom_call" | custom-call | flops 1342177280 | bytes 6291456 | tf_op jit(solution)/shard_map/weight_part/pallas_call | solution.py:263
  90.2 23.1 %all_to_all.15 = bf16[8,64,1280]{2,1,0:T(8,128)(2,1)S(1)} all-to-all(bf16[8,64,1280]{2,1,0:T(8,128)(2,1)S(1)} %bitcast.29), channel_id=1, replica_groups=mesh['zh'=4,'x'=4,'core'=2,'y'=4,'zl'=2] {'y','zl'}, dimensions={0} | all-to-all | bytes 2621440 | tf_op jit(solution)/shard_map/all_to_all | solution.py:313
  114.1 7.5 %all-to-all-start.2 = ((bf16[4,16,1280]{2,1,0:T(8,128)(2,1)}), bf16[4,16,1280]{2,1,0:T(8,128)(2,1)S(1)}, u32[]{:S(2)}, u32[]{:S(2)}) async-start(bf16[4,16,1280]{2,1,0:T(8,128)(2,1)} %bitcast.17), calls=%async_computation.2 | async-start | bytes 327680 | tf_op jit(solution)/shard_map/all_to_all | solution.py:315
  122.3 8.1 %all-to-all-done.2 = bf16[4,16,1280]{2,1,0:T(8,128)(2,1)S(1)} async-done(((bf16[4,16,1280]{2,1,0:T(8,128)(2,1)}), bf16[4,16,1280]{2,1,0:T(8,128)(2,1)S(1)}, u32[]{:S(2)}, u32[]{:S(2)}) %all-to-all-start.2) | async-done | bytes 163872 | tf_op jit(solution)/shard_map/all_to_all | solution.py:315
  (45 shorter events, 11.7 us)
Async XLA Ops:
  1.5 5.9 %collective-permute-start = (bf16[256,256]{1,0:T(8,128)(2,1)S(1)}, bf16[256,256]{1,0:T(8,128)(2,1)S(1)}, u32[]{:S(2)}, u32[]{:S(2)}) collective-permute-start(bf16[256,256]{1,0:T(8,128)(2,1)S(1)} %get-tuple-element.43), channel_id=1, source_target_pairs={{0,1},{1,0},{2,3},{3,2},{4,5},{5,4},{6,7},{7,6},{8,9},{9,8},{10,11... | collective-permute-start | bytes 393224 | tf_op jit(solution)/shard_map/ppermute | solution.py:33
  3.5 1.6 %copy-start = (bf16[1,256,4096]{2,1,0:T(8,128)(2,1)S(1)}, bf16[1,256,4096]{2,1,0:T(8,128)(2,1)}, u32[]{:S(2)}) copy-start(bf16[1,256,4096]{2,1,0:T(8,128)(2,1)} %param.6) | copy-start | bytes 6291460
  5.0 19.4 %copy-start.6 = (s32[1,2048]{1,0:T(1,128)S(1)}, s32[1,2048]{1,0:T(1,128)}, u32[]{:S(2)}) copy-start(s32[1,2048]{1,0:T(1,128)} %docs_ref.1) | copy-start | bytes 24580
  7.5 7.9 %collective-permute-start.1 = (bf16[2,256,256]{2,1,0:T(8,128)(2,1)S(1)}, bf16[2,256,256]{2,1,0:T(8,128)(2,1)S(1)}, u32[]{:S(2)}, u32[]{:S(2)}) collective-permute-start(bf16[2,256,256]{2,1,0:T(8,128)(2,1)S(1)} %pad_maximum_fusion.refs_0_), channel_id=1, source_target_pairs={{0,2},{2,4},{4,6},{6,0},{1,3},{3,5},{5,7},{7,1},{8,10},{10,12},{12... | collective-permute-start | bytes 786440 | tf_op jit(solution)/shard_map/ppermute | solution.py:33
  8.5 7.3 %collective-permute-start.3 = (bf16[2,256,256]{2,1,0:T(8,128)(2,1)S(1)}, bf16[2,256,256]{2,1,0:T(8,128)(2,1)S(1)}, u32[]{:S(2)}, u32[]{:S(2)}) collective-permute-start(bf16[2,256,256]{2,1,0:T(8,128)(2,1)S(1)} %pad_maximum_fusion.refs_0_), channel_id=1, source_target_pairs={{0,6},{2,0},{4,2},{6,4},{1,7},{3,1},{5,3},{7,5},{8,14},{10,8},{12,... | collective-permute-start | bytes 786440 | tf_op jit(solution)/shard_map/ppermute | solution.py:33
  15.4 9.1 %collective-permute-start.2 = (bf16[256,256]{1,0:T(8,128)(2,1)S(1)}, bf16[256,256]{1,0:T(8,128)(2,1)S(1)}, u32[]{:S(2)}, u32[]{:S(2)}) collective-permute-start(bf16[256,256]{1,0:T(8,128)(2,1)S(1)} %slice_bitcast_fusion.1), channel_id=1, source_target_pairs={{0,2},{2,4},{4,6},{6,0},{1,3},{3,5},{5,7},{7,1},{8,10},{10,12},{12... | collective-permute-start | bytes 393224 | tf_op jit(solution)/shard_map/ppermute | solution.py:33
  15.8 8.7 %collective-permute-start.4 = (bf16[256,256]{1,0:T(8,128)(2,1)S(1)}, bf16[256,256]{1,0:T(8,128)(2,1)S(1)}, u32[]{:S(2)}, u32[]{:S(2)}) collective-permute-start(bf16[256,256]{1,0:T(8,128)(2,1)S(1)} %slice_bitcast_fusion), channel_id=1, source_target_pairs={{0,6},{2,0},{4,2},{6,4},{1,7},{3,1},{5,3},{7,5},{8,14},{10,8},{12,... | collective-permute-start | bytes 393224 | tf_op jit(solution)/shard_map/ppermute | solution.py:33
  18.8 14.9 %collective-permute-start.5 = (bf16[1024,256]{1,0:T(8,128)(2,1)}, bf16[1024,256]{1,0:T(8,128)(2,1)S(1)}, u32[]{:S(2)}, u32[]{:S(2)}) collective-permute-start(bf16[1024,256]{1,0:T(8,128)(2,1)} %get-tuple-element.31), channel_id=1, source_target_pairs={{0,16},{16,32},{32,48},{48,0},{1,17},{17,33},{33,49},{49,1},{2,18}... | collective-permute-start | bytes 1572872 | tf_op jit(solution)/shard_map/ppermute | solution.py:33
  20.3 23.5 %collective-permute-start.6 = (bf16[1024,256]{1,0:T(8,128)(2,1)}, bf16[1024,256]{1,0:T(8,128)(2,1)S(1)}, u32[]{:S(2)}, u32[]{:S(2)}) collective-permute-start(bf16[1024,256]{1,0:T(8,128)(2,1)} %get-tuple-element.32), channel_id=1, source_target_pairs={{0,32},{16,48},{32,0},{48,16},{1,33},{17,49},{33,1},{49,17},{2,34}... | collective-permute-start | bytes 1572872 | tf_op jit(solution)/shard_map/ppermute | solution.py:33
  23.0 20.8 %collective-permute-start.7 = (bf16[1024,256]{1,0:T(8,128)(2,1)}, bf16[1024,256]{1,0:T(8,128)(2,1)S(1)}, u32[]{:S(2)}, u32[]{:S(2)}) collective-permute-start(bf16[1024,256]{1,0:T(8,128)(2,1)} %get-tuple-element.33), channel_id=1, source_target_pairs={{0,48},{16,0},{32,16},{48,32},{1,49},{17,1},{33,17},{49,33},{2,50}... | collective-permute-start | bytes 1572872 | tf_op jit(solution)/shard_map/ppermute | solution.py:33
  24.5 1.0 copy-start.5
  32.2 18.5 %copy-start.1 = (bf16[256,1024]{1,0:T(8,128)(2,1)S(1)}, bf16[256,1024]{1,0:T(8,128)(2,1)}, u32[]{:S(2)}) copy-start(bf16[256,1024]{1,0:T(8,128)(2,1)} %get-tuple-element.34.refs_4_) | copy-start | bytes 1572868
  44.6 24.4 %all-to-all-start = ((bf16[8,256,256]{2,1,0:T(8,128)(2,1)}), bf16[8,256,256]{2,1,0:T(8,128)(2,1)}, u32[]{:S(2)}, u32[]{:S(2)}) async-start(bf16[8,256,256]{2,1,0:T(8,128)(2,1)} %get-tuple-element.35), calls=%async_computation | async-start | bytes 2097152 | tf_op jit(solution)/shard_map/all_to_all | solution.py:304
  50.7 13.2 %collective-permute-start.10 = (bf16[256,1024]{1,0:T(8,128)(2,1)S(1)}, bf16[256,1024]{1,0:T(8,128)(2,1)S(1)}, u32[]{:S(2)}, u32[]{:S(2)}) collective-permute-start(bf16[256,1024]{1,0:T(8,128)(2,1)S(1)} %copy-done.1), channel_id=1, source_target_pairs={{0,48},{16,0},{32,16},{48,32},{1,49},{17,1},{33,17},{49,33},{2,50}... | collective-permute-start | bytes 1572872 | tf_op jit(solution)/shard_map/ppermute | solution.py:33
  52.8 15.5 %collective-permute-start.8 = (bf16[256,1024]{1,0:T(8,128)(2,1)S(1)}, bf16[256,1024]{1,0:T(8,128)(2,1)S(1)}, u32[]{:S(2)}, u32[]{:S(2)}) collective-permute-start(bf16[256,1024]{1,0:T(8,128)(2,1)S(1)} %copy-done.1), channel_id=1, source_target_pairs={{0,16},{16,32},{32,48},{48,0},{1,17},{17,33},{33,49},{49,1},{2,18}... | collective-permute-start | bytes 1572872 | tf_op jit(solution)/shard_map/ppermute | solution.py:33
  64.6 10.6 %collective-permute-start.11 = (bf16[256,512]{1,0:T(8,128)(2,1)}, bf16[256,512]{1,0:T(8,128)(2,1)S(1)}, u32[]{:S(2)}, u32[]{:S(2)}) collective-permute-start(bf16[256,512]{1,0:T(8,128)(2,1)} %slice.41), channel_id=1, source_target_pairs={{0,48},{16,0},{32,16},{48,32},{1,49},{17,1},{33,17},{49,33},{2,50}... | collective-permute-start | bytes 786440 | tf_op jit(solution)/shard_map/ppermute | solution.py:33
  69.0 11.2 %collective-permute-start.9 = (bf16[256,512]{1,0:T(8,128)(2,1)}, bf16[256,512]{1,0:T(8,128)(2,1)}, u32[]{:S(2)}, u32[]{:S(2)}) collective-permute-start(bf16[256,512]{1,0:T(8,128)(2,1)} %slice.40), channel_id=1, source_target_pairs={{0,16},{16,32},{32,48},{48,0},{1,17},{17,33},{33,49},{49,1},{2,18}... | collective-permute-start | bytes 786440 | tf_op jit(solution)/shard_map/ppermute | solution.py:33
  70.4 12.6 %collective-permute-start.12 = (bf16[256,256]{1,0:T(8,128)(2,1)S(1)}, bf16[256,256]{1,0:T(8,128)(2,1)}, u32[]{:S(2)}, u32[]{:S(2)}) collective-permute-start(bf16[256,256]{1,0:T(8,128)(2,1)S(1)} %reduce_sum.33.refs_9_), channel_id=1, source_target_pairs={{0,16},{16,32},{32,48},{48,0},{1,17},{17,33},{33,49},{49,1},{2,18}... | collective-permute-start | bytes 393224 | tf_op jit(solution)/shard_map/ppermute | solution.py:33
  70.5 12.6 %collective-permute-start.13 = (bf16[256,256]{1,0:T(8,128)(2,1)S(1)}, bf16[256,256]{1,0:T(8,128)(2,1)}, u32[]{:S(2)}, u32[]{:S(2)}) collective-permute-start(bf16[256,256]{1,0:T(8,128)(2,1)S(1)} %reduce_sum.33.refs_9_), channel_id=1, source_target_pairs={{0,32},{16,48},{32,0},{48,16},{1,33},{17,49},{33,1},{49,17},{2,34}... | collective-permute-start | bytes 393224 | tf_op jit(solution)/shard_map/ppermute | solution.py:33
  75.1 7.9 %collective-permute-start.14 = (bf16[256,256]{1,0:T(8,128)(2,1)S(1)}, bf16[256,256]{1,0:T(8,128)(2,1)}, u32[]{:S(2)}, u32[]{:S(2)}) collective-permute-start(bf16[256,256]{1,0:T(8,128)(2,1)S(1)} %reduce_sum.33.refs_9_), channel_id=1, source_target_pairs={{0,48},{16,0},{32,16},{48,32},{1,49},{17,1},{33,17},{49,33},{2,50}... | collective-permute-start | bytes 393224 | tf_op jit(solution)/shard_map/ppermute | solution.py:33
  83.0 1.0 copy-start.3
  84.1 2.8 %copy-start.4 = (bf16[1024,256]{1,0:T(8,128)(2,1)S(1)}, bf16[1024,256]{1,0:T(8,128)(2,1)}, u32[]{:S(2)}) copy-start(bf16[1024,256]{1,0:T(8,128)(2,1)} %copy-done.2) | copy-start | bytes 1572868
  86.8 3.1 %collective-permute-start.15 = (bf16[8,4,16,1280]{3,2,1,0:T(8,128)(2,1)S(1)}, bf16[8,4,16,1280]{3,2,1,0:T(8,128)(2,1)S(1)}, u32[]{:S(2)}, u32[]{:S(2)}) collective-permute-start(bf16[8,4,16,1280]{3,2,1,0:T(8,128)(2,1)S(1)} %weight_part.3), channel_id=1, source_target_pairs={{0,8},{8,0},{1,9},{9,1},{2,10},{10,2},{3,11},{11,3},{4,12},{12,4},... | collective-permute-start | bytes 3932168 | tf_op jit(solution)/shard_map/ppermute | solution.py:33
  114.1 16.2 %all-to-all-start.2 = ((bf16[4,16,1280]{2,1,0:T(8,128)(2,1)}), bf16[4,16,1280]{2,1,0:T(8,128)(2,1)S(1)}, u32[]{:S(2)}, u32[]{:S(2)}) async-start(bf16[4,16,1280]{2,1,0:T(8,128)(2,1)} %bitcast.17), calls=%async_computation.2 | async-start | bytes 327680 | tf_op jit(solution)/shard_map/all_to_all | solution.py:315
  (1 other events, 0.8 us)

commit v9 on v8

--- a/solution.py
+++ b/solution.py
@@ -44,8 +44,8 @@
 def attention_kernel(ny, per, docs, scale, info, docs_ref, q_ref, do_ref, *refs):
     (pair_ref, before_ref, far_refs, after_ref), refs = (refs[0], refs[1], refs[2:4], refs[4]), refs[5:]
     dq_ref, refs = refs[0], refs[1:]
-    out_ref, refs = refs[0], refs[1:]
-    kv_s, kt_s, e_s, dp_s, md_s, stat_s, dqt_s, qt_s, dot_s, p_s, ds_s, qk_s, dk_s, starts_ref, sem = refs
+    out_refs, refs = refs[: 2 * ny], refs[2 * ny :]
+    kv_s, kt_s, e_s, dp_s, md_s, stat_s, dqt_s, qt_s, dot_s, p_s, ds_s, qk_s, dk_s, starts_ref, out_s, sem, out_sem = refs
     rows = q_ref.shape[0]
     hd = kt_s.shape[1]
     place = info[0]
@@ -86,12 +86,9 @@
     for s, copy in copies:
         pl.when(s <= farthest)(copy.wait)
 
-    def clear(block, carry):
-        out_ref[block] = jnp.zeros(out_ref.shape[1:], BF)
-        return carry
-
-    lax.fori_loop(0, place - used + 1, clear, 0)
-    lax.fori_loop(place + 1, out_ref.shape[0], clear, 0)
+    results = [
+        pltpu.make_async_copy(out_s.at[d], out_refs[d], out_sem.at[d]) for d in range(2 * ny)
+    ]
 
     def slot(d):
         block = place - d
@@ -139,15 +136,26 @@
             p = e_s[d, h] * (jnp.exp2((md_s[d, h] - tops[h]) * power) * inverse[h])
             p_s[:, h * rows : (h + 1) * rows] = p.astype(BF)
             ds_s[:, h * rows : (h + 1) * rows] = (p * (dp_s[d, h] - delta[h])).astype(BF)
-        out_ref[place - d, :, hd:] = dot(p_s[...], dk_s[...]).astype(BF)
-        out_ref[place - d, :, :hd] = (dot(ds_s[...], qk_s[...]) * scale).astype(BF)
+        out_s[d, :, hd:] = dot(p_s[...], dk_s[...]).astype(BF)
+        out_s[d, :, :hd] = (dot(ds_s[...], qk_s[...]) * scale).astype(BF)
+        for i, copy in enumerate(results):
+            pl.when(d == i)(copy.start)
         dqt_s[...] += dot(kt_s[slot(d)], ds_s[...])
         return carry
 
     lax.fori_loop(0, used, second, 0)
 
+    for d, copy in enumerate(results):
+
+        @pl.when(d >= used)
+        def _():
+            out_s[d] = jnp.zeros(out_s.shape[1:], BF)
+            copy.start()
+
     for h in range(per):
         dq_ref[:, h * hd : (h + 1) * hd] = (dqt_s[:, h * rows : (h + 1) * rows].T * scale).astype(BF)
+    for copy in results:
+        copy.wait()
 
 
 def attention(q, do, kv, docs, place, ny):
@@ -163,11 +171,9 @@
         grid=(1,),
         in_specs=[pl.BlockSpec(memory_space=pltpu.SMEM), whole(docs.shape), slab, slab]
         + [pl.BlockSpec(memory_space=pl.ANY)] * len(kv),
-        out_specs=[whole((rows, width)), whole((blocks, *pair[1:]))],
-        out_shape=[
-            jax.ShapeDtypeStruct((rows, width), BF),
-            jax.ShapeDtypeStruct((blocks, *pair[1:]), BF),
-        ],
+        out_specs=[whole((rows, width))] + [pl.BlockSpec(memory_space=pl.ANY)] * blocks,
+        out_shape=[jax.ShapeDtypeStruct((rows, width), BF)]
+        + [jax.ShapeDtypeStruct(pair[1:], BF)] * blocks,
         scratch_shapes=[
             pltpu.VMEM((blocks, rows, 2 * hd), BF),
             pltpu.VMEM((blocks, hd, rows), BF),
@@ -183,7 +189,9 @@
             pltpu.VMEM((per * rows, hd), BF),
             pltpu.VMEM((per * rows, hd), BF),
             pltpu.VMEM((1, rows), jnp.int32),
+            pltpu.VMEM((blocks, rows, 2 * hd), BF),
             pltpu.SemaphoreType.DMA((len(kv),)),
+            pltpu.SemaphoreType.DMA((blocks,)),
         ],
         compiler_params=pltpu.CompilerParams(vmem_limit_bytes=52 * 2**20),
         cost_estimate=pl.CostEstimate(
@@ -295,14 +303,16 @@
     far = shifted(before[0], "y", ny, 1), shifted(after[1], "y", ny, -1)
     features = [shifted(part, "x", nx, s) if s else part for s, part in enumerate(parts)]
 
-    dq, dkv = attention(q, do, [pair, before, *far, after], doc_ids, place, ny)
+    dq, *dkv = attention(q, do, [pair, before, *far, after], doc_ids, place, ny)
     dq, dkv, features = lax.optimization_barrier((dq, dkv, features))
     left, right = shifted(dq, "x", nx, 1), shifted(dq, "x", nx, -1)
     half = dq.shape[1] // 2
     far = shifted(left[:, :half], "x", nx, 1), shifted(right[:, half:], "x", nx, -1)
     wide = [dq, left, *far, right]
-    dkv = lax.all_to_all(dkv, CTX, 0, 0, tiled=True)
-    dkv_own = jnp.sum(dkv.astype(F32), axis=0).astype(BF)
+    total = dkv[0].astype(F32)
+    for d in range(1, ctx):
+        total = total + shifted(dkv[d], CTX, ctx, -d, False).astype(F32)
+    dkv_own = total.astype(BF)
     narrow = [dkv_own] + [shifted(dkv_own, "x", nx, s) for s in range(1, nx)]
 
     theirs = weight_part(features, wide, narrow, 1 - my_core, z_hi, ctx)

time: 132 us -> 135 us (1.023)
  starting transfers between devices: 38.5 us -> 43.7 us
  waiting for transfers between devices: 43.6 us -> 39.5 us
  Pallas kernels: 14.4 us -> 16.6 us
    ppermute x16 -> x23, starting transfers between devices: 24.9 us -> 35.2 us  [shifted(): return lax.ppermute(value, axis, pairs)]
    all_to_all x1 -> x0, starting transfers between devices: 6.09 us -> none  [local(): dkv = lax.all_to_all(dkv, CTX, 0, 0, tiled=True)]
    ppermute x16 -> x23, waiting for transfers between devices: 35.5 us -> 31.5 us  [shifted(): return lax.ppermute(value, axis, pairs)]
    pallas_call x1, Pallas kernels: 6.7 us -> 8.84 us  [attention(): pl.pallas_call(functools.partial(attention_kernel, ny, per, DOCS, hd ** (...]
    reduce_sum x1 -> x0, other arithmetic: 1.37 us -> none  [local(): dkv_own = jnp.sum(dkv.astype(F32), axis=0).astype(BF)]
  transfers between devices with their start and end apart: 18 -> 24, of which waited for: 8 -> 10; matrix products, arithmetic and copies ran while one was open for 3% -> 2% of each run, Pallas kernels for 9% -> 10%
where the time goes in v9:
time: 135 us; the launch traced here: 133 us
  starting transfers between devices  43.7 us (32%)
  waiting for transfers between devices  39.5 us (29%)
  blocking collectives  23.6 us (17%)
  Pallas kernels  16.6 us (12%)
  local copies, waits for them, and re-layouts  6.83 us (5%)
  other arithmetic  2.3 us (2%)
    ppermute x23, starting transfers between devices, shifted(): return lax.ppermute(value, axis, pairs)  35.2 us
    ppermute x23, waiting for transfers between devices, shifted(): return lax.ppermute(value, axis, pairs)  31.5 us
    all_to_all x1, blocking collectives, local(): part = lax.all_to_all(part, CTX, 0, 0, tiled=True)  23.6 us
    pallas_call x1, Pallas kernels, attention(): pl.pallas_call(functools.partial(attention_kernel, ny, per, DOCS, hd ** (...  8.84 us
    all_to_all x1, starting transfers between devices, local(): part = lax.all_to_all(part, 'zh', 0, 0, tiled=True)  8.43 us
    all_to_all x1, waiting for transfers between devices, local(): part = lax.all_to_all(part, 'zh', 0, 0, tiled=True)  8.08 us
    pallas_call x2, Pallas kernels, weight_part(): pl.pallas_call(functools.partial(weight_kernel, nx, z_hi), in_specs=[pl.B...  5.34 us
    unnamed x14, local copies, waits for them, and re-layouts  3.45 us
  transfers between devices with their start and end apart: 24, of which 10 were waited for; matrix products, arithmetic and copies ran while one was open for 2% of the time, Pallas kernels for 10%

profile of v9, /device:TPU:32, one launch (start us, length us, event | category | flops | bytes accessed | tf_op | source)
XLA Modules:
  0.0 133.3 jit_solution(17214708269882403782)
XLA Ops:
  1.5 1.9 %collective-permute-start = (bf16[256,256]{1,0:T(8,128)(2,1)S(1)}, bf16[256,256]{1,0:T(8,128)(2,1)S(1)}, u32[]{:S(2)}, u32[]{:S(2)}) collective-permute-start(bf16[256,256]{1,0:T(8,128)(2,1)S(1)} %get-tuple-element.71), channel_id=1, source_target_pairs={{0,1},{1,0},{2,3},{3,2},{4,5},{5,4},{6,7},{7,6},{8,9},{9,8},{10,11... | collective-permute-start | bytes 393224 | tf_op jit(solution)/shard_map/ppermute | solution.py:33
  3.5 1.6 %copy-done = bf16[1,256,4096]{2,1,0:T(8,128)(2,1)S(1)} copy-done((bf16[1,256,4096]{2,1,0:T(8,128)(2,1)S(1)}, bf16[1,256,4096]{2,1,0:T(8,128)(2,1)}, u32[]{:S(2)}) %copy-start) | copy-done | bytes 2097176
  5.1 2.4 %split_features.1 = (bf16[1024,256]{1,0:T(8,128)(2,1)S(1)}, bf16[1024,256]{1,0:T(8,128)(2,1)}, bf16[1024,256]{1,0:T(8,128)(2,1)}, bf16[1024,256]{1,0:T(8,128)(2,1)}) custom-call(s32[1]{0:T(128)} %bitcast.6.info, bf16[256,4096]{1,0:T(8,128)(2,1)S(1)} %bitcast.23, bf16[256,4096]{1,0:T(8,128)(2,1)S(1)} %bitcast.24, bf16[256,4096]{1,0:T(8,128)(2,1)S(1)} %bitcast.25, ...), custom_call_target="tpu_custom_call" | custom-call | tf_op jit(solution)/shard_map/split_features/pallas_call | solution.py:219
  8.5 2.2 %collective-permute-start.3 = (bf16[2,256,256]{2,1,0:T(8,128)(2,1)S(1)}, bf16[2,256,256]{2,1,0:T(8,128)(2,1)S(1)}, u32[]{:S(2)}, u32[]{:S(2)}) collective-permute-start(bf16[2,256,256]{2,1,0:T(8,128)(2,1)S(1)} %pad_maximum_fusion.refs_0_), channel_id=1, source_target_pairs={{0,6},{2,0},{4,2},{6,4},{1,7},{3,1},{5,3},{7,5},{8,14},{10,8},{12,... | collective-permute-start | bytes 786440 | tf_op jit(solution)/shard_map/ppermute | solution.py:33
  10.8 4.6 %collective-permute-done.1.refs_1_ = bf16[2,256,256]{2,1,0:T(8,128)(2,1)S(1)} collective-permute-done((bf16[2,256,256]{2,1,0:T(8,128)(2,1)S(1)}, bf16[2,256,256]{2,1,0:T(8,128)(2,1)S(1)}, u32[]{:S(2)}, u32[]{:S(2)}) %collective-permute-start.1) | collective-permute-done | bytes 262176 | tf_op jit(solution)/shard_map/ppermute | solution.py:33
  15.8 3.0 %collective-permute-start.4 = (bf16[256,256]{1,0:T(8,128)(2,1)S(1)}, bf16[256,256]{1,0:T(8,128)(2,1)S(1)}, u32[]{:S(2)}, u32[]{:S(2)}) collective-permute-start(bf16[256,256]{1,0:T(8,128)(2,1)S(1)} %slice_bitcast_fusion), channel_id=1, source_target_pairs={{0,6},{2,0},{4,2},{6,4},{1,7},{3,1},{5,3},{7,5},{8,14},{10,8},{12,... | collective-permute-start | bytes 393224 | tf_op jit(solution)/shard_map/ppermute | solution.py:33
  18.8 1.5 %collective-permute-start.5 = (bf16[1024,256]{1,0:T(8,128)(2,1)}, bf16[1024,256]{1,0:T(8,128)(2,1)S(1)}, u32[]{:S(2)}, u32[]{:S(2)}) collective-permute-start(bf16[1024,256]{1,0:T(8,128)(2,1)} %get-tuple-element.52), channel_id=1, source_target_pairs={{0,16},{16,32},{32,48},{48,0},{1,17},{17,33},{33,49},{49,1},{2,18}... | collective-permute-start | bytes 1572872 | tf_op jit(solution)/shard_map/ppermute | solution.py:33
  20.3 2.7 %collective-permute-start.6 = (bf16[1024,256]{1,0:T(8,128)(2,1)}, bf16[1024,256]{1,0:T(8,128)(2,1)S(1)}, u32[]{:S(2)}, u32[]{:S(2)}) collective-permute-start(bf16[1024,256]{1,0:T(8,128)(2,1)} %get-tuple-element.53), channel_id=1, source_target_pairs={{0,32},{16,48},{32,0},{48,16},{1,33},{17,49},{33,1},{49,17},{2,34}... | collective-permute-start | bytes 1572872 | tf_op jit(solution)/shard_map/ppermute | solution.py:33
  23.1 1.4 %collective-permute-start.7 = (bf16[1024,256]{1,0:T(8,128)(2,1)}, bf16[1024,256]{1,0:T(8,128)(2,1)S(1)}, u32[]{:S(2)}, u32[]{:S(2)}) collective-permute-start(bf16[1024,256]{1,0:T(8,128)(2,1)} %get-tuple-element.54), channel_id=1, source_target_pairs={{0,48},{16,0},{32,16},{48,32},{1,49},{17,1},{33,17},{49,33},{2,50}... | collective-permute-start | bytes 1572872 | tf_op jit(solution)/shard_map/ppermute | solution.py:33
  24.5 8.8 %attention_backward.1 = (bf16[256,1024]{1,0:T(8,128)(2,1)}, bf16[256,256]{1,0:T(8,128)(2,1)S(1)}, bf16[256,256]{1,0:T(8,128)(2,1)S(1)}, bf16[256,256]{1,0:T(8,12...) custom-call(s32[1]{0:T(128)} %bitcast.info, ...), custom_call_target="tpu_custom_call" | custom-call | flops 5368709120 | bytes 4194304 | tf_op jit(solution)/shard_map/attention_backward/pallas_call | solution.py:169
  33.7 10.1 %collective-permute-done.6.refs_2_ = bf16[1024,256]{1,0:T(8,128)(2,1)S(1)} collective-permute-done((bf16[1024,256]{1,0:T(8,128)(2,1)}, bf16[1024,256]{1,0:T(8,128)(2,1)S(1)}, u32[]{:S(2)}, u32[]{:S(2)}) %collective-permute-start.6) | collective-permute-done | bytes 524320 | tf_op jit(solution)/shard_map/ppermute | solution.py:33
  45.8 2.1 %collective-permute-start.17 = (bf16[256,1024]{1,0:T(8,128)(2,1)}, bf16[256,1024]{1,0:T(8,128)(2,1)S(1)}, u32[]{:S(2)}, u32[]{:S(2)}) collective-permute-start(bf16[256,1024]{1,0:T(8,128)(2,1)} %get-tuple-element.55.refs_4_), channel_id=1, source_target_pairs={{0,48},{16,0},{32,16},{48,32},{1,49},{17,1},{33,17},{49,33},{2,50}... | collective-permute-start | bytes 1572872 | tf_op jit(solution)/shard_map/ppermute | solution.py:33
  51.8 6.9 %collective-permute-done.10 = bf16[256,256]{1,0:T(8,128)(2,1)S(1)} collective-permute-done((bf16[256,256]{1,0:T(8,128)(2,1)S(1)}, bf16[256,256]{1,0:T(8,128)(2,1)S(1)}, u32[]{:S(2)}, u32[]{:S(2)}) %collective-permute-start.10) | collective-permute-done | bytes 131104 | tf_op jit(solution)/shard_map/ppermute | solution.py:33
  59.9 1.9 %collective-permute-done.11 = bf16[256,256]{1,0:T(8,128)(2,1)S(1)} collective-permute-done((bf16[256,256]{1,0:T(8,128)(2,1)S(1)}, bf16[256,256]{1,0:T(8,128)(2,1)S(1)}, u32[]{:S(2)}, u32[]{:S(2)}) %collective-permute-start.11) | collective-permute-done | bytes 131104 | tf_op jit(solution)/shard_map/ppermute | solution.py:33
  62.5 3.1 %collective-permute-start.8 = (bf16[256,256]{1,0:T(8,128)(2,1)S(1)}, bf16[256,256]{1,0:T(8,128)(2,1)S(1)}, u32[]{:S(2)}, u32[]{:S(2)}) collective-permute-start(bf16[256,256]{1,0:T(8,128)(2,1)S(1)} %get-tuple-element.57), channel_id=1, source_target_pairs={{1,0},{2,1},{3,2},{4,3},{5,4},{6,5},{7,6},{9,8},{10,9},{11,10},{12... | collective-permute-start | bytes 393224 | tf_op jit(solution)/shard_map/ppermute | solution.py:33
  68.4 3.2 %collective-permute-start.18 = (bf16[256,512]{1,0:T(8,128)(2,1)}, bf16[256,512]{1,0:T(8,128)(2,1)}, u32[]{:S(2)}, u32[]{:S(2)}) collective-permute-start(bf16[256,512]{1,0:T(8,128)(2,1)} %slice.41), channel_id=1, source_target_pairs={{0,48},{16,0},{32,16},{48,32},{1,49},{17,1},{33,17},{49,33},{2,50}... | collective-permute-start | bytes 786440 | tf_op jit(solution)/shard_map/ppermute | solution.py:33
  72.7 4.1 %collective-permute-start.20 = (bf16[256,256]{1,0:T(8,128)(2,1)S(1)}, bf16[256,256]{1,0:T(8,128)(2,1)}, u32[]{:S(2)}, u32[]{:S(2)}) collective-permute-start(bf16[256,256]{1,0:T(8,128)(2,1)S(1)} %add_convert_fusion.1.refs_9_), channel_id=1, source_target_pairs={{0,32},{16,48},{32,0},{48,16},{1,33},{17,49},{33,1},{49,17},{2,34}... | collective-permute-start | bytes 393224 | tf_op jit(solution)/shard_map/ppermute | solution.py:33
  76.9 2.3 %collective-permute-done.19.refs_10_ = bf16[256,256]{1,0:T(8,128)(2,1)} collective-permute-done((bf16[256,256]{1,0:T(8,128)(2,1)S(1)}, bf16[256,256]{1,0:T(8,128)(2,1)}, u32[]{:S(2)}, u32[]{:S(2)}) %collective-permute-start.19) | collective-permute-done | bytes 131104 | tf_op jit(solution)/shard_map/ppermute | solution.py:33
  79.2 4.0 %collective-permute-done.20.refs_11_ = bf16[256,256]{1,0:T(8,128)(2,1)} collective-permute-done((bf16[256,256]{1,0:T(8,128)(2,1)S(1)}, bf16[256,256]{1,0:T(8,128)(2,1)}, u32[]{:S(2)}, u32[]{:S(2)}) %collective-permute-start.20) | collective-permute-done | bytes 131104 | tf_op jit(solution)/shard_map/ppermute | solution.py:33
  84.2 2.7 %weight_part.3 = bf16[8,4,16,1280]{3,2,1,0:T(8,128)(2,1)S(1)} custom-call(s32[1]{0:T(128)} %bitcast.15.info, bf16[1024,256]{1,0:T(8,128)(2,1)S(1)} %get-tuple-element.64.refs_0_, bf16[1024,256]{1,0:T(8,128)(2,1)S(1)} %collective-permute-done.5.refs_1_, bf16[1024,256]{1,0:T(8,128)(2,1)S(1)} %collective-permute-done.6.refs_2_, ...), custom_call_target="tpu_custom_call" | custom-call | flops 1342177280 | bytes 6291456 | tf_op jit(solution)/shard_map/weight_part/pallas_call | solution.py:271
  87.1 2.6 %weight_part.2 = bf16[8,4,16,1280]{3,2,1,0:T(8,128)(2,1)S(1)} custom-call(s32[1]{0:T(128)} %bitcast.14.info, bf16[1024,256]{1,0:T(8,128)(2,1)S(1)} %get-tuple-element.64.refs_0_, bf16[1024,256]{1,0:T(8,128)(2,1)S(1)} %collective-permute-done.5.refs_1_, bf16[1024,256]{1,0:T(8,128)(2,1)S(1)} %collective-permute-done.6.refs_2_, ...), custom_call_target="tpu_custom_call" | custom-call | flops 1342177280 | bytes 6291456 | tf_op jit(solution)/shard_map/weight_part/pallas_call | solution.py:271
  90.4 23.6 %all_to_all.10 = bf16[8,64,1280]{2,1,0:T(8,128)(2,1)S(1)} all-to-all(bf16[8,64,1280]{2,1,0:T(8,128)(2,1)S(1)} %bitcast.28), channel_id=1, replica_groups=mesh['zh'=4,'x'=4,'core'=2,'y'=4,'zl'=2] {'y','zl'}, dimensions={0} | all-to-all | bytes 2621440 | tf_op jit(solution)/shard_map/all_to_all | solution.py:323
  114.9 8.4 %all-to-all-start.1 = ((bf16[4,16,1280]{2,1,0:T(8,128)(2,1)}), bf16[4,16,1280]{2,1,0:T(8,128)(2,1)S(1)}, u32[]{:S(2)}, u32[]{:S(2)}) async-start(bf16[4,16,1280]{2,1,0:T(8,128)(2,1)} %bitcast.17), calls=%async_computation.1 | async-start | bytes 327680 | tf_op jit(solution)/shard_map/all_to_all | solution.py:325
  124.0 8.1 %all-to-all-done.1 = bf16[4,16,1280]{2,1,0:T(8,128)(2,1)S(1)} async-done(((bf16[4,16,1280]{2,1,0:T(8,128)(2,1)}), bf16[4,16,1280]{2,1,0:T(8,128)(2,1)S(1)}, u32[]{:S(2)}, u32[]{:S(2)}) %all-to-all-start.1) | async-done | bytes 163872 | tf_op jit(solution)/shard_map/all_to_all | solution.py:325
  (57 shorter events, 19.0 us)
Async XLA Ops:
  1.5 5.9 %collective-permute-start = (bf16[256,256]{1,0:T(8,128)(2,1)S(1)}, bf16[256,256]{1,0:T(8,128)(2,1)S(1)}, u32[]{:S(2)}, u32[]{:S(2)}) collective-permute-start(bf16[256,256]{1,0:T(8,128)(2,1)S(1)} %get-tuple-element.71), channel_id=1, source_target_pairs={{0,1},{1,0},{2,3},{3,2},{4,5},{5,4},{6,7},{7,6},{8,9},{9,8},{10,11... | collective-permute-start | bytes 393224 | tf_op jit(solution)/shard_map/ppermute | solution.py:33
  7.5 7.9 %collective-permute-start.1 = (bf16[2,256,256]{2,1,0:T(8,128)(2,1)S(1)}, bf16[2,256,256]{2,1,0:T(8,128)(2,1)S(1)}, u32[]{:S(2)}, u32[]{:S(2)}) collective-permute-start(bf16[2,256,256]{2,1,0:T(8,128)(2,1)S(1)} %pad_maximum_fusion.refs_0_), channel_id=1, source_target_pairs={{0,2},{2,4},{4,6},{6,0},{1,3},{3,5},{5,7},{7,1},{8,10},{10,12},{12... | collective-permute-start | bytes 786440 | tf_op jit(solution)/shard_map/ppermute | solution.py:33
  8.5 7.3 %collective-permute-start.3 = (bf16[2,256,256]{2,1,0:T(8,128)(2,1)S(1)}, bf16[2,256,256]{2,1,0:T(8,128)(2,1)S(1)}, u32[]{:S(2)}, u32[]{:S(2)}) collective-permute-start(bf16[2,256,256]{2,1,0:T(8,128)(2,1)S(1)} %pad_maximum_fusion.refs_0_), channel_id=1, source_target_pairs={{0,6},{2,0},{4,2},{6,4},{1,7},{3,1},{5,3},{7,5},{8,14},{10,8},{12,... | collective-permute-start | bytes 786440 | tf_op jit(solution)/shard_map/ppermute | solution.py:33
  15.4 9.1 %collective-permute-start.2 = (bf16[256,256]{1,0:T(8,128)(2,1)S(1)}, bf16[256,256]{1,0:T(8,128)(2,1)S(1)}, u32[]{:S(2)}, u32[]{:S(2)}) collective-permute-start(bf16[256,256]{1,0:T(8,128)(2,1)S(1)} %slice_bitcast_fusion.1), channel_id=1, source_target_pairs={{0,2},{2,4},{4,6},{6,0},{1,3},{3,5},{5,7},{7,1},{8,10},{10,12},{12... | collective-permute-start | bytes 393224 | tf_op jit(solution)/shard_map/ppermute | solution.py:33
  15.8 8.7 %collective-permute-start.4 = (bf16[256,256]{1,0:T(8,128)(2,1)S(1)}, bf16[256,256]{1,0:T(8,128)(2,1)S(1)}, u32[]{:S(2)}, u32[]{:S(2)}) collective-permute-start(bf16[256,256]{1,0:T(8,128)(2,1)S(1)} %slice_bitcast_fusion), channel_id=1, source_target_pairs={{0,6},{2,0},{4,2},{6,4},{1,7},{3,1},{5,3},{7,5},{8,14},{10,8},{12,... | collective-permute-start | bytes 393224 | tf_op jit(solution)/shard_map/ppermute | solution.py:33
  18.8 14.9 %collective-permute-start.5 = (bf16[1024,256]{1,0:T(8,128)(2,1)}, bf16[1024,256]{1,0:T(8,128)(2,1)S(1)}, u32[]{:S(2)}, u32[]{:S(2)}) collective-permute-start(bf16[1024,256]{1,0:T(8,128)(2,1)} %get-tuple-element.52), channel_id=1, source_target_pairs={{0,16},{16,32},{32,48},{48,0},{1,17},{17,33},{33,49},{49,1},{2,18}... | collective-permute-start | bytes 1572872 | tf_op jit(solution)/shard_map/ppermute | solution.py:33
  20.3 23.5 %collective-permute-start.6 = (bf16[1024,256]{1,0:T(8,128)(2,1)}, bf16[1024,256]{1,0:T(8,128)(2,1)S(1)}, u32[]{:S(2)}, u32[]{:S(2)}) collective-permute-start(bf16[1024,256]{1,0:T(8,128)(2,1)} %get-tuple-element.53), channel_id=1, source_target_pairs={{0,32},{16,48},{32,0},{48,16},{1,33},{17,49},{33,1},{49,17},{2,34}... | collective-permute-start | bytes 1572872 | tf_op jit(solution)/shard_map/ppermute | solution.py:33
  23.1 20.8 %collective-permute-start.7 = (bf16[1024,256]{1,0:T(8,128)(2,1)}, bf16[1024,256]{1,0:T(8,128)(2,1)S(1)}, u32[]{:S(2)}, u32[]{:S(2)}) collective-permute-start(bf16[1024,256]{1,0:T(8,128)(2,1)} %get-tuple-element.54), channel_id=1, source_target_pairs={{0,48},{16,0},{32,16},{48,32},{1,49},{17,1},{33,17},{49,33},{2,50}... | collective-permute-start | bytes 1572872 | tf_op jit(solution)/shard_map/ppermute | solution.py:33
  44.7 17.9 %collective-permute-start.15 = (bf16[256,1024]{1,0:T(8,128)(2,1)}, bf16[256,1024]{1,0:T(8,128)(2,1)S(1)}, u32[]{:S(2)}, u32[]{:S(2)}) collective-permute-start(bf16[256,1024]{1,0:T(8,128)(2,1)} %get-tuple-element.55.refs_4_), channel_id=1, source_target_pairs={{0,16},{16,32},{32,48},{48,0},{1,17},{17,33},{33,49},{49,1},{2,18}... | collective-permute-start | bytes 1572872 | tf_op jit(solution)/shard_map/ppermute | solution.py:33
  45.8 19.8 %collective-permute-start.17 = (bf16[256,1024]{1,0:T(8,128)(2,1)}, bf16[256,1024]{1,0:T(8,128)(2,1)S(1)}, u32[]{:S(2)}, u32[]{:S(2)}) collective-permute-start(bf16[256,1024]{1,0:T(8,128)(2,1)} %get-tuple-element.55.refs_4_), channel_id=1, source_target_pairs={{0,48},{16,0},{32,16},{48,32},{1,49},{17,1},{33,17},{49,33},{2,50}... | collective-permute-start | bytes 1572872 | tf_op jit(solution)/shard_map/ppermute | solution.py:33
  47.9 10.8 %collective-permute-start.10 = (bf16[256,256]{1,0:T(8,128)(2,1)S(1)}, bf16[256,256]{1,0:T(8,128)(2,1)S(1)}, u32[]{:S(2)}, u32[]{:S(2)}) collective-permute-start(bf16[256,256]{1,0:T(8,128)(2,1)S(1)} %get-tuple-element.59), channel_id=1, source_target_pairs={{3,0},{4,1},{5,2},{6,3},{7,4},{11,8},{12,9},{13,10},{14,11},{15,12... | collective-permute-start | bytes 393224 | tf_op jit(solution)/shard_map/ppermute | solution.py:33
  49.2 12.7 %collective-permute-start.11 = (bf16[256,256]{1,0:T(8,128)(2,1)S(1)}, bf16[256,256]{1,0:T(8,128)(2,1)S(1)}, u32[]{:S(2)}, u32[]{:S(2)}) collective-permute-start(bf16[256,256]{1,0:T(8,128)(2,1)S(1)} %get-tuple-element.60), channel_id=1, source_target_pairs={{4,0},{5,1},{6,2},{7,3},{12,8},{13,9},{14,10},{15,11},{20,16},{21,... | collective-permute-start | bytes 393224 | tf_op jit(solution)/shard_map/ppermute | solution.py:33
  50.5 17.9 %collective-permute-start.12 = (bf16[256,256]{1,0:T(8,128)(2,1)S(1)}, bf16[256,256]{1,0:T(8,128)(2,1)S(1)}, u32[]{:S(2)}, u32[]{:S(2)}) collective-permute-start(bf16[256,256]{1,0:T(8,128)(2,1)S(1)} %get-tuple-element.61), channel_id=1, source_target_pairs={{5,0},{6,1},{7,2},{13,8},{14,9},{15,10},{21,16},{22,17},{23,18},{2... | collective-permute-start | bytes 393224 | tf_op jit(solution)/shard_map/ppermute | solution.py:33
  58.6 9.7 %collective-permute-start.13 = (bf16[256,256]{1,0:T(8,128)(2,1)S(1)}, bf16[256,256]{1,0:T(8,128)(2,1)S(1)}, u32[]{:S(2)}, u32[]{:S(2)}) collective-permute-start(bf16[256,256]{1,0:T(8,128)(2,1)S(1)} %get-tuple-element.62), channel_id=1, source_target_pairs={{6,0},{7,1},{14,8},{15,9},{22,16},{23,17},{30,24},{31,25},{38,32},... | collective-permute-start | bytes 393224 | tf_op jit(solution)/shard_map/ppermute | solution.py:33
  61.9 9.8 %collective-permute-start.14 = (bf16[256,256]{1,0:T(8,128)(2,1)S(1)}, bf16[256,256]{1,0:T(8,128)(2,1)S(1)}, u32[]{:S(2)}, u32[]{:S(2)}) collective-permute-start(bf16[256,256]{1,0:T(8,128)(2,1)S(1)} %get-tuple-element.63), channel_id=1, source_target_pairs={{7,0},{15,8},{23,16},{31,24},{39,32},{47,40},{55,48},{63,56},{71,6... | collective-permute-start | bytes 393224 | tf_op jit(solution)/shard_map/ppermute | solution.py:33
  62.5 9.1 %collective-permute-start.8 = (bf16[256,256]{1,0:T(8,128)(2,1)S(1)}, bf16[256,256]{1,0:T(8,128)(2,1)S(1)}, u32[]{:S(2)}, u32[]{:S(2)}) collective-permute-start(bf16[256,256]{1,0:T(8,128)(2,1)S(1)} %get-tuple-element.57), channel_id=1, source_target_pairs={{1,0},{2,1},{3,2},{4,3},{5,4},{6,5},{7,6},{9,8},{10,9},{11,10},{12... | collective-permute-start | bytes 393224 | tf_op jit(solution)/shard_map/ppermute | solution.py:33
  65.6 6.9 %collective-permute-start.9 = (bf16[256,256]{1,0:T(8,128)(2,1)S(1)}, bf16[256,256]{1,0:T(8,128)(2,1)S(1)}, u32[]{:S(2)}, u32[]{:S(2)}) collective-permute-start(bf16[256,256]{1,0:T(8,128)(2,1)S(1)} %get-tuple-element.58), channel_id=1, source_target_pairs={{2,0},{3,1},{4,2},{5,3},{6,4},{7,5},{10,8},{11,9},{12,10},{13,11},... | collective-permute-start | bytes 393224 | tf_op jit(solution)/shard_map/ppermute | solution.py:33
  68.4 14.8 %collective-permute-start.16 = (bf16[256,512]{1,0:T(8,128)(2,1)}, bf16[256,512]{1,0:T(8,128)(2,1)S(1)}, u32[]{:S(2)}, u32[]{:S(2)}) collective-permute-start(bf16[256,512]{1,0:T(8,128)(2,1)} %slice.40), channel_id=1, source_target_pairs={{0,16},{16,32},{32,48},{48,0},{1,17},{17,33},{33,49},{49,1},{2,18}... | collective-permute-start | bytes 786440 | tf_op jit(solution)/shard_map/ppermute | solution.py:33
  68.4 14.8 %collective-permute-start.18 = (bf16[256,512]{1,0:T(8,128)(2,1)}, bf16[256,512]{1,0:T(8,128)(2,1)}, u32[]{:S(2)}, u32[]{:S(2)}) collective-permute-start(bf16[256,512]{1,0:T(8,128)(2,1)} %slice.41), channel_id=1, source_target_pairs={{0,48},{16,0},{32,16},{48,32},{1,49},{17,1},{33,17},{49,33},{2,50}... | collective-permute-start | bytes 786440 | tf_op jit(solution)/shard_map/ppermute | solution.py:33
  72.6 6.6 %collective-permute-start.19 = (bf16[256,256]{1,0:T(8,128)(2,1)S(1)}, bf16[256,256]{1,0:T(8,128)(2,1)}, u32[]{:S(2)}, u32[]{:S(2)}) collective-permute-start(bf16[256,256]{1,0:T(8,128)(2,1)S(1)} %add_convert_fusion.1.refs_9_), channel_id=1, source_target_pairs={{0,16},{16,32},{32,48},{48,0},{1,17},{17,33},{33,49},{49,1},{2,18}... | collective-permute-start | bytes 393224 | tf_op jit(solution)/shard_map/ppermute | solution.py:33
  72.7 10.4 %collective-permute-start.20 = (bf16[256,256]{1,0:T(8,128)(2,1)S(1)}, bf16[256,256]{1,0:T(8,128)(2,1)}, u32[]{:S(2)}, u32[]{:S(2)}) collective-permute-start(bf16[256,256]{1,0:T(8,128)(2,1)S(1)} %add_convert_fusion.1.refs_9_), channel_id=1, source_target_pairs={{0,32},{16,48},{32,0},{48,16},{1,33},{17,49},{33,1},{49,17},{2,34}... | collective-permute-start | bytes 393224 | tf_op jit(solution)/shard_map/ppermute | solution.py:33
  76.9 6.3 %collective-permute-start.21 = (bf16[256,256]{1,0:T(8,128)(2,1)S(1)}, bf16[256,256]{1,0:T(8,128)(2,1)}, u32[]{:S(2)}, u32[]{:S(2)}) collective-permute-start(bf16[256,256]{1,0:T(8,128)(2,1)S(1)} %add_convert_fusion.1.refs_9_), channel_id=1, source_target_pairs={{0,48},{16,0},{32,16},{48,32},{1,49},{17,1},{33,17},{49,33},{2,50}... | collective-permute-start | bytes 393224 | tf_op jit(solution)/shard_map/ppermute | solution.py:33
  86.9 3.1 %collective-permute-start.22 = (bf16[8,4,16,1280]{3,2,1,0:T(8,128)(2,1)S(1)}, bf16[8,4,16,1280]{3,2,1,0:T(8,128)(2,1)S(1)}, u32[]{:S(2)}, u32[]{:S(2)}) collective-permute-start(bf16[8,4,16,1280]{3,2,1,0:T(8,128)(2,1)S(1)} %weight_part.3), channel_id=1, source_target_pairs={{0,8},{8,0},{1,9},{9,1},{2,10},{10,2},{3,11},{11,3},{4,12},{12,4},... | collective-permute-start | bytes 3932168 | tf_op jit(solution)/shard_map/ppermute | solution.py:33
  114.9 17.2 %all-to-all-start.1 = ((bf16[4,16,1280]{2,1,0:T(8,128)(2,1)}), bf16[4,16,1280]{2,1,0:T(8,128)(2,1)S(1)}, u32[]{:S(2)}, u32[]{:S(2)}) async-start(bf16[4,16,1280]{2,1,0:T(8,128)(2,1)} %bitcast.17), calls=%async_computation.1 | async-start | bytes 327680 | tf_op jit(solution)/shard_map/all_to_all | solution.py:325
  (7 other events, 84.2 us)

commit v10 on v8

--- a/solution.py
+++ b/solution.py
@@ -41,11 +41,11 @@
     return pl.BlockSpec(shape, lambda *g: (0,) * len(shape))
 
 
-def attention_kernel(ny, per, docs, scale, info, docs_ref, q_ref, do_ref, *refs):
+def attention_kernel(ny, per, docs, scale, info, docs_ref, q_hbm, do_hbm, *refs):
     (pair_ref, before_ref, far_refs, after_ref), refs = (refs[0], refs[1], refs[2:4], refs[4]), refs[5:]
     dq_ref, refs = refs[0], refs[1:]
     out_ref, refs = refs[0], refs[1:]
-    kv_s, kt_s, e_s, dp_s, md_s, stat_s, dqt_s, qt_s, dot_s, p_s, ds_s, qk_s, dk_s, starts_ref, sem = refs
+    kv_s, kt_s, e_s, dp_s, md_s, stat_s, dqt_s, qt_s, dot_s, p_s, ds_s, qk_s, dk_s, starts_ref, q_ref, do_ref, sem, q_sem = refs
     rows = q_ref.shape[0]
     hd = kt_s.shape[1]
     place = info[0]
@@ -59,8 +59,16 @@
         (2, pltpu.make_async_copy(far_refs[1], kv_s.at[5], sem.at[3])),
         (3, pltpu.make_async_copy(after_ref, kv_s.at[pl.ds(6, 2)], sem.at[4])),
     ]
+    loads = [
+        pltpu.make_async_copy(q_hbm, q_ref, q_sem.at[0]),
+        pltpu.make_async_copy(do_hbm, do_ref, q_sem.at[1]),
+    ]
+    for copy in loads:
+        copy.start()
     for s, copy in copies:
         pl.when(s <= farthest)(copy.start)
+    for copy in loads:
+        copy.wait()
 
     for h in range(per):
         cols = slice(h * hd, (h + 1) * hd)
@@ -156,7 +164,7 @@
     width = q.shape[1]
     per = width // hd
     blocks = 2 * ny
-    slab = whole((rows, width))
+    slab = pl.BlockSpec(memory_space=pltpu.HBM)
     pair = kv[0].shape
     return pl.pallas_call(
         functools.partial(attention_kernel, ny, per, DOCS, hd ** (-0.5)),
@@ -183,7 +191,10 @@
             pltpu.VMEM((per * rows, hd), BF),
             pltpu.VMEM((per * rows, hd), BF),
             pltpu.VMEM((1, rows), jnp.int32),
+            pltpu.VMEM((rows, width), BF),
+            pltpu.VMEM((rows, width), BF),
             pltpu.SemaphoreType.DMA((len(kv),)),
+            pltpu.SemaphoreType.DMA((2,)),
         ],
         compiler_params=pltpu.CompilerParams(vmem_limit_bytes=52 * 2**20),
         cost_estimate=pl.CostEstimate(
@@ -298,12 +309,13 @@
     dq, dkv = attention(q, do, [pair, before, *far, after], doc_ids, place, ny)
     dq, dkv, features = lax.optimization_barrier((dq, dkv, features))
     left, right = shifted(dq, "x", nx, 1), shifted(dq, "x", nx, -1)
+    dkv = lax.all_to_all(dkv, CTX, 0, 0, tiled=True)
+    dkv_own = jnp.sum(dkv.astype(F32), axis=0).astype(BF)
+    narrow = [dkv_own] + [shifted(dkv_own, "x", nx, s) for s in range(1, nx)]
+    left, right, dkv_own = lax.optimization_barrier((left, right, dkv_own))
     half = dq.shape[1] // 2
     far = shifted(left[:, :half], "x", nx, 1), shifted(right[:, half:], "x", nx, -1)
     wide = [dq, left, *far, right]
-    dkv = lax.all_to_all(dkv, CTX, 0, 0, tiled=True)
-    dkv_own = jnp.sum(dkv.astype(F32), axis=0).astype(BF)
-    narrow = [dkv_own] + [shifted(dkv_own, "x", nx, s) for s in range(1, nx)]
 
     theirs = weight_part(features, wide, narrow, 1 - my_core, z_hi, ctx)
     theirs = shifted(theirs, "core", nc, 1)

time: 132 us -> 132 us (level)
    ppermute x16, waiting for transfers between devices: 35.5 us -> 24.5 us  [shifted(): return lax.ppermute(value, axis, pairs)]
    all_to_all x1, waiting for transfers between devices: 0.01 us -> 10.4 us  [local(): dkv = lax.all_to_all(dkv, CTX, 0, 0, tiled=True)]
  transfers between devices with their start and end apart: 18 -> 18, of which waited for: 8 -> 8; matrix products, arithmetic and copies ran while one was open for 3% -> 2% of each run, Pallas kernels for 9% -> 9%
where the time goes in v10:
time: 132 us; the launch traced here: 131 us
  waiting for transfers between devices  43 us (33%)
  starting transfers between devices  38.9 us (29%)
  blocking collectives  22.2 us (17%)
  Pallas kernels  14.4 us (11%)
  local copies, waits for them, and re-layouts  7.8 us (6%)
  other arithmetic  3.49 us (3%)
    ppermute x16, starting transfers between devices, shifted(): return lax.ppermute(value, axis, pairs)  25.3 us
    ppermute x16, waiting for transfers between devices, shifted(): return lax.ppermute(value, axis, pairs)  24.5 us
    all_to_all x1, blocking collectives, local(): part = lax.all_to_all(part, CTX, 0, 0, tiled=True)  22.2 us
    all_to_all x1, waiting for transfers between devices, local(): dkv = lax.all_to_all(dkv, CTX, 0, 0, tiled=True)  10.4 us
    all_to_all x1, waiting for transfers between devices, local(): part = lax.all_to_all(part, 'zh', 0, 0, tiled=True)  8.08 us
    all_to_all x1, starting transfers between devices, local(): part = lax.all_to_all(part, 'zh', 0, 0, tiled=True)  7.5 us
    pallas_call x1, Pallas kernels, attention(): pl.pallas_call(functools.partial(attention_kernel, ny, per, DOCS, hd ** (...  6.73 us
    all_to_all x1, starting transfers between devices, local(): dkv = lax.all_to_all(dkv, CTX, 0, 0, tiled=True)  6.09 us
  transfers between devices with their start and end apart: 18, of which 8 were waited for; matrix products, arithmetic and copies ran while one was open for 2% of the time, Pallas kernels for 9%

profile of v10, /device:TPU:32, one launch (start us, length us, event | category | flops | bytes accessed | tf_op | source)
XLA Modules:
  0.0 130.5 jit_solution(11080261733757460572)
XLA Ops:
  1.5 1.9 %collective-permute-start = (bf16[256,256]{1,0:T(8,128)(2,1)S(1)}, bf16[256,256]{1,0:T(8,128)(2,1)S(1)}, u32[]{:S(2)}, u32[]{:S(2)}) collective-permute-start(bf16[256,256]{1,0:T(8,128)(2,1)S(1)} %get-tuple-element.49), channel_id=1, source_target_pairs={{0,1},{1,0},{2,3},{3,2},{4,5},{5,4},{6,7},{7,6},{8,9},{9,8},{10,11... | collective-permute-start | bytes 393224 | tf_op jit(solution)/shard_map/ppermute | solution.py:33
  3.5 1.6 %copy-done = bf16[1,256,4096]{2,1,0:T(8,128)(2,1)S(1)} copy-done((bf16[1,256,4096]{2,1,0:T(8,128)(2,1)S(1)}, bf16[1,256,4096]{2,1,0:T(8,128)(2,1)}, u32[]{:S(2)}) %copy-start) | copy-done | bytes 2097176
  5.1 2.4 %split_features.1 = (bf16[1024,256]{1,0:T(8,128)(2,1)S(1)}, bf16[1024,256]{1,0:T(8,128)(2,1)}, bf16[1024,256]{1,0:T(8,128)(2,1)}, bf16[1024,256]{1,0:T(8,128)(2,1)}) custom-call(s32[1]{0:T(128)} %bitcast.6.info, bf16[256,4096]{1,0:T(8,128)(2,1)S(1)} %bitcast.23, bf16[256,4096]{1,0:T(8,128)(2,1)S(1)} %bitcast.24, bf16[256,4096]{1,0:T(8,128)(2,1)S(1)} %bitcast.25, ...), custom_call_target="tpu_custom_call" | custom-call | tf_op jit(solution)/shard_map/split_features/pallas_call | solution.py:222
  8.5 2.2 %collective-permute-start.3 = (bf16[2,256,256]{2,1,0:T(8,128)(2,1)S(1)}, bf16[2,256,256]{2,1,0:T(8,128)(2,1)S(1)}, u32[]{:S(2)}, u32[]{:S(2)}) collective-permute-start(bf16[2,256,256]{2,1,0:T(8,128)(2,1)S(1)} %pad_maximum_fusion.refs_0_), channel_id=1, source_target_pairs={{0,6},{2,0},{4,2},{6,4},{1,7},{3,1},{5,3},{7,5},{8,14},{10,8},{12,... | collective-permute-start | bytes 786440 | tf_op jit(solution)/shard_map/ppermute | solution.py:33
  10.8 4.6 %collective-permute-done.1.refs_1_ = bf16[2,256,256]{2,1,0:T(8,128)(2,1)S(1)} collective-permute-done((bf16[2,256,256]{2,1,0:T(8,128)(2,1)S(1)}, bf16[2,256,256]{2,1,0:T(8,128)(2,1)S(1)}, u32[]{:S(2)}, u32[]{:S(2)}) %collective-permute-start.1) | collective-permute-done | bytes 262176 | tf_op jit(solution)/shard_map/ppermute | solution.py:33
  15.8 3.0 %collective-permute-start.4 = (bf16[256,256]{1,0:T(8,128)(2,1)S(1)}, bf16[256,256]{1,0:T(8,128)(2,1)S(1)}, u32[]{:S(2)}, u32[]{:S(2)}) collective-permute-start(bf16[256,256]{1,0:T(8,128)(2,1)S(1)} %slice_bitcast_fusion), channel_id=1, source_target_pairs={{0,6},{2,0},{4,2},{6,4},{1,7},{3,1},{5,3},{7,5},{8,14},{10,8},{12,... | collective-permute-start | bytes 393224 | tf_op jit(solution)/shard_map/ppermute | solution.py:33
  18.8 1.5 %collective-permute-start.5 = (bf16[1024,256]{1,0:T(8,128)(2,1)}, bf16[1024,256]{1,0:T(8,128)(2,1)S(1)}, u32[]{:S(2)}, u32[]{:S(2)}) collective-permute-start(bf16[1024,256]{1,0:T(8,128)(2,1)} %get-tuple-element.34), channel_id=1, source_target_pairs={{0,16},{16,32},{32,48},{48,0},{1,17},{17,33},{33,49},{49,1},{2,18}... | collective-permute-start | bytes 1572872 | tf_op jit(solution)/shard_map/ppermute | solution.py:33
  20.3 2.7 %collective-permute-start.6 = (bf16[1024,256]{1,0:T(8,128)(2,1)}, bf16[1024,256]{1,0:T(8,128)(2,1)S(1)}, u32[]{:S(2)}, u32[]{:S(2)}) collective-permute-start(bf16[1024,256]{1,0:T(8,128)(2,1)} %get-tuple-element.35), channel_id=1, source_target_pairs={{0,32},{16,48},{32,0},{48,16},{1,33},{17,49},{33,1},{49,17},{2,34}... | collective-permute-start | bytes 1572872 | tf_op jit(solution)/shard_map/ppermute | solution.py:33
  25.5 6.7 %attention_backward.1 = (bf16[256,1024]{1,0:T(8,128)(2,1)}, bf16[8,256,256]{2,1,0:T(8,128)(2,1)}) custom-call(s32[1]{0:T(128)} %bitcast.info, s32[1,2048]{1,0:T(1,128)S(1)} %copy-done.6, bf16[256,1024]{1,0:T(8,128)(2,1)S(1)} %bitcast.28, bf16[256,1024]{1,0:T(8,128)(2,1)} %bitcast.33, bf16[2,256,256]{2,1,0:T(8,128)(2,1)S(1)} %pad_maximum_fusion.refs_0_, ...), custom_call_target="tpu_custom_call" | custom-call | flops 5368709120 | bytes 4194304 | tf_op jit(solution)/shard_map/attention_backward/pallas_call | solution.py:169
  32.3 1.4 %collective-permute-done.5.refs_1_ = bf16[1024,256]{1,0:T(8,128)(2,1)S(1)} collective-permute-done((bf16[1024,256]{1,0:T(8,128)(2,1)}, bf16[1024,256]{1,0:T(8,128)(2,1)S(1)}, u32[]{:S(2)}, u32[]{:S(2)}) %collective-permute-start.5) | collective-permute-done | bytes 524320 | tf_op jit(solution)/shard_map/ppermute | solution.py:33
  33.7 10.1 %collective-permute-done.6.refs_2_ = bf16[1024,256]{1,0:T(8,128)(2,1)S(1)} collective-permute-done((bf16[1024,256]{1,0:T(8,128)(2,1)}, bf16[1024,256]{1,0:T(8,128)(2,1)S(1)}, u32[]{:S(2)}, u32[]{:S(2)}) %collective-permute-start.6) | collective-permute-done | bytes 524320 | tf_op jit(solution)/shard_map/ppermute | solution.py:33
  44.6 6.1 %all-to-all-start = ((bf16[8,256,256]{2,1,0:T(8,128)(2,1)}), bf16[8,256,256]{2,1,0:T(8,128)(2,1)}, u32[]{:S(2)}, u32[]{:S(2)}) async-start(bf16[8,256,256]{2,1,0:T(8,128)(2,1)} %get-tuple-element.38), calls=%async_computation | async-start | bytes 2097152 | tf_op jit(solution)/shard_map/all_to_all | solution.py:312
  51.9 2.1 %collective-permute-start.9 = (bf16[256,1024]{1,0:T(8,128)(2,1)S(1)}, bf16[256,1024]{1,0:T(8,128)(2,1)S(1)}, u32[]{:S(2)}, u32[]{:S(2)}) collective-permute-start(bf16[256,1024]{1,0:T(8,128)(2,1)S(1)} %copy-done.1), channel_id=1, source_target_pairs={{0,48},{16,0},{32,16},{48,32},{1,49},{17,1},{33,17},{49,33},{2,50}... | collective-permute-start | bytes 1572872 | tf_op jit(solution)/shard_map/ppermute | solution.py:33
  54.0 10.4 %all-to-all-done = bf16[8,256,256]{2,1,0:T(8,128)(2,1)} async-done(((bf16[8,256,256]{2,1,0:T(8,128)(2,1)}), bf16[8,256,256]{2,1,0:T(8,128)(2,1)}, u32[]{:S(2)}, u32[]{:S(2)}) %all-to-all-start) | async-done | bytes 1048608 | tf_op jit(solution)/shard_map/all_to_all | solution.py:312
  66.4 1.7 %collective-permute-start.10 = (bf16[256,512]{1,0:T(8,128)(2,1)}, bf16[256,512]{1,0:T(8,128)(2,1)S(1)}, u32[]{:S(2)}, u32[]{:S(2)}) collective-permute-start(bf16[256,512]{1,0:T(8,128)(2,1)} %slice.31), channel_id=1, source_target_pairs={{0,16},{16,32},{32,48},{48,0},{1,17},{17,33},{33,49},{49,1},{2,18}... | collective-permute-start | bytes 786440 | tf_op jit(solution)/shard_map/ppermute | solution.py:33
  68.9 1.9 %collective-permute-start.11 = (bf16[256,512]{1,0:T(8,128)(2,1)}, bf16[256,512]{1,0:T(8,128)(2,1)}, u32[]{:S(2)}, u32[]{:S(2)}) collective-permute-start(bf16[256,512]{1,0:T(8,128)(2,1)} %slice.32), channel_id=1, source_target_pairs={{0,48},{16,0},{32,16},{48,32},{1,49},{17,1},{33,17},{49,33},{2,50}... | collective-permute-start | bytes 786440 | tf_op jit(solution)/shard_map/ppermute | solution.py:33
  70.9 3.3 %collective-permute-start.13 = (bf16[256,256]{1,0:T(8,128)(2,1)S(1)}, bf16[256,256]{1,0:T(8,128)(2,1)}, u32[]{:S(2)}, u32[]{:S(2)}) collective-permute-start(bf16[256,256]{1,0:T(8,128)(2,1)S(1)} %reduce_sum.33.refs_9_), channel_id=1, source_target_pairs={{0,32},{16,48},{32,0},{48,16},{1,33},{17,49},{33,1},{49,17},{2,34}... | collective-permute-start | bytes 393224 | tf_op jit(solution)/shard_map/ppermute | solution.py:33
  74.8 4.6 %collective-permute-done.12.refs_10_ = bf16[256,256]{1,0:T(8,128)(2,1)} collective-permute-done((bf16[256,256]{1,0:T(8,128)(2,1)S(1)}, bf16[256,256]{1,0:T(8,128)(2,1)}, u32[]{:S(2)}, u32[]{:S(2)}) %collective-permute-start.12) | collective-permute-done | bytes 131104 | tf_op jit(solution)/shard_map/ppermute | solution.py:33
  79.5 3.3 %collective-permute-done.13.refs_11_ = bf16[256,256]{1,0:T(8,128)(2,1)} collective-permute-done((bf16[256,256]{1,0:T(8,128)(2,1)S(1)}, bf16[256,256]{1,0:T(8,128)(2,1)}, u32[]{:S(2)}, u32[]{:S(2)}) %collective-permute-start.13) | collective-permute-done | bytes 131104 | tf_op jit(solution)/shard_map/ppermute | solution.py:33
  83.8 2.7 %weight_part.3 = bf16[8,4,16,1280]{3,2,1,0:T(8,128)(2,1)S(1)} custom-call(s32[1]{0:T(128)} %bitcast.15.info, bf16[1024,256]{1,0:T(8,128)(2,1)S(1)} %get-tuple-element.40.refs_0_, bf16[1024,256]{1,0:T(8,128)(2,1)S(1)} %collective-permute-done.5.refs_1_, bf16[1024,256]{1,0:T(8,128)(2,1)S(1)} %collective-permute-done.6.refs_2_, ...), custom_call_target="tpu_custom_call" | custom-call | flops 1342177280 | bytes 6291456 | tf_op jit(solution)/shard_map/weight_part/pallas_call | solution.py:274
  86.6 2.6 %weight_part.2 = bf16[8,4,16,1280]{3,2,1,0:T(8,128)(2,1)S(1)} custom-call(s32[1]{0:T(128)} %bitcast.14.info, bf16[1024,256]{1,0:T(8,128)(2,1)S(1)} %get-tuple-element.40.refs_0_, bf16[1024,256]{1,0:T(8,128)(2,1)S(1)} %collective-permute-done.5.refs_1_, bf16[1024,256]{1,0:T(8,128)(2,1)S(1)} %collective-permute-done.6.refs_2_, ...), custom_call_target="tpu_custom_call" | custom-call | flops 1342177280 | bytes 6291456 | tf_op jit(solution)/shard_map/weight_part/pallas_call | solution.py:274
  90.0 22.2 %all_to_all.15 = bf16[8,64,1280]{2,1,0:T(8,128)(2,1)S(1)} all-to-all(bf16[8,64,1280]{2,1,0:T(8,128)(2,1)S(1)} %bitcast.29), channel_id=1, replica_groups=mesh['zh'=4,'x'=4,'core'=2,'y'=4,'zl'=2] {'y','zl'}, dimensions={0} | all-to-all | bytes 2621440 | tf_op jit(solution)/shard_map/all_to_all | solution.py:325
  113.0 7.5 %all-to-all-start.2 = ((bf16[4,16,1280]{2,1,0:T(8,128)(2,1)}), bf16[4,16,1280]{2,1,0:T(8,128)(2,1)S(1)}, u32[]{:S(2)}, u32[]{:S(2)}) async-start(bf16[4,16,1280]{2,1,0:T(8,128)(2,1)} %bitcast.17), calls=%async_computation.2 | async-start | bytes 327680 | tf_op jit(solution)/shard_map/all_to_all | solution.py:327
  121.2 8.1 %all-to-all-done.2 = bf16[4,16,1280]{2,1,0:T(8,128)(2,1)S(1)} async-done(((bf16[4,16,1280]{2,1,0:T(8,128)(2,1)}), bf16[4,16,1280]{2,1,0:T(8,128)(2,1)S(1)}, u32[]{:S(2)}, u32[]{:S(2)}) %all-to-all-start.2) | async-done | bytes 163872 | tf_op jit(solution)/shard_map/all_to_all | solution.py:327
  (45 shorter events, 15.0 us)
Async XLA Ops:
  1.5 5.9 %collective-permute-start = (bf16[256,256]{1,0:T(8,128)(2,1)S(1)}, bf16[256,256]{1,0:T(8,128)(2,1)S(1)}, u32[]{:S(2)}, u32[]{:S(2)}) collective-permute-start(bf16[256,256]{1,0:T(8,128)(2,1)S(1)} %get-tuple-element.49), channel_id=1, source_target_pairs={{0,1},{1,0},{2,3},{3,2},{4,5},{5,4},{6,7},{7,6},{8,9},{9,8},{10,11... | collective-permute-start | bytes 393224 | tf_op jit(solution)/shard_map/ppermute | solution.py:33
  3.5 1.6 %copy-start = (bf16[1,256,4096]{2,1,0:T(8,128)(2,1)S(1)}, bf16[1,256,4096]{2,1,0:T(8,128)(2,1)}, u32[]{:S(2)}) copy-start(bf16[1,256,4096]{2,1,0:T(8,128)(2,1)} %param.6) | copy-start | bytes 6291460
  5.0 19.4 %copy-start.6 = (s32[1,2048]{1,0:T(1,128)S(1)}, s32[1,2048]{1,0:T(1,128)}, u32[]{:S(2)}) copy-start(s32[1,2048]{1,0:T(1,128)} %docs_ref.1) | copy-start | bytes 24580
  7.5 7.9 %collective-permute-start.1 = (bf16[2,256,256]{2,1,0:T(8,128)(2,1)S(1)}, bf16[2,256,256]{2,1,0:T(8,128)(2,1)S(1)}, u32[]{:S(2)}, u32[]{:S(2)}) collective-permute-start(bf16[2,256,256]{2,1,0:T(8,128)(2,1)S(1)} %pad_maximum_fusion.refs_0_), channel_id=1, source_target_pairs={{0,2},{2,4},{4,6},{6,0},{1,3},{3,5},{5,7},{7,1},{8,10},{10,12},{12... | collective-permute-start | bytes 786440 | tf_op jit(solution)/shard_map/ppermute | solution.py:33
  8.5 7.3 %collective-permute-start.3 = (bf16[2,256,256]{2,1,0:T(8,128)(2,1)S(1)}, bf16[2,256,256]{2,1,0:T(8,128)(2,1)S(1)}, u32[]{:S(2)}, u32[]{:S(2)}) collective-permute-start(bf16[2,256,256]{2,1,0:T(8,128)(2,1)S(1)} %pad_maximum_fusion.refs_0_), channel_id=1, source_target_pairs={{0,6},{2,0},{4,2},{6,4},{1,7},{3,1},{5,3},{7,5},{8,14},{10,8},{12,... | collective-permute-start | bytes 786440 | tf_op jit(solution)/shard_map/ppermute | solution.py:33
  15.4 9.1 %collective-permute-start.2 = (bf16[256,256]{1,0:T(8,128)(2,1)S(1)}, bf16[256,256]{1,0:T(8,128)(2,1)S(1)}, u32[]{:S(2)}, u32[]{:S(2)}) collective-permute-start(bf16[256,256]{1,0:T(8,128)(2,1)S(1)} %slice_bitcast_fusion.1), channel_id=1, source_target_pairs={{0,2},{2,4},{4,6},{6,0},{1,3},{3,5},{5,7},{7,1},{8,10},{10,12},{12... | collective-permute-start | bytes 393224 | tf_op jit(solution)/shard_map/ppermute | solution.py:33
  15.8 8.7 %collective-permute-start.4 = (bf16[256,256]{1,0:T(8,128)(2,1)S(1)}, bf16[256,256]{1,0:T(8,128)(2,1)S(1)}, u32[]{:S(2)}, u32[]{:S(2)}) collective-permute-start(bf16[256,256]{1,0:T(8,128)(2,1)S(1)} %slice_bitcast_fusion), channel_id=1, source_target_pairs={{0,6},{2,0},{4,2},{6,4},{1,7},{3,1},{5,3},{7,5},{8,14},{10,8},{12,... | collective-permute-start | bytes 393224 | tf_op jit(solution)/shard_map/ppermute | solution.py:33
  18.8 14.9 %collective-permute-start.5 = (bf16[1024,256]{1,0:T(8,128)(2,1)}, bf16[1024,256]{1,0:T(8,128)(2,1)S(1)}, u32[]{:S(2)}, u32[]{:S(2)}) collective-permute-start(bf16[1024,256]{1,0:T(8,128)(2,1)} %get-tuple-element.34), channel_id=1, source_target_pairs={{0,16},{16,32},{32,48},{48,0},{1,17},{17,33},{33,49},{49,1},{2,18}... | collective-permute-start | bytes 1572872 | tf_op jit(solution)/shard_map/ppermute | solution.py:33
  20.3 23.5 %collective-permute-start.6 = (bf16[1024,256]{1,0:T(8,128)(2,1)}, bf16[1024,256]{1,0:T(8,128)(2,1)S(1)}, u32[]{:S(2)}, u32[]{:S(2)}) collective-permute-start(bf16[1024,256]{1,0:T(8,128)(2,1)} %get-tuple-element.35), channel_id=1, source_target_pairs={{0,32},{16,48},{32,0},{48,16},{1,33},{17,49},{33,1},{49,17},{2,34}... | collective-permute-start | bytes 1572872 | tf_op jit(solution)/shard_map/ppermute | solution.py:33
  23.0 20.8 %collective-permute-start.7 = (bf16[1024,256]{1,0:T(8,128)(2,1)}, bf16[1024,256]{1,0:T(8,128)(2,1)S(1)}, u32[]{:S(2)}, u32[]{:S(2)}) collective-permute-start(bf16[1024,256]{1,0:T(8,128)(2,1)} %get-tuple-element.36), channel_id=1, source_target_pairs={{0,48},{16,0},{32,16},{48,32},{1,49},{17,1},{33,17},{49,33},{2,50}... | collective-permute-start | bytes 1572872 | tf_op jit(solution)/shard_map/ppermute | solution.py:33
  24.5 1.0 copy-start.5
  32.3 18.4 %copy-start.1 = (bf16[256,1024]{1,0:T(8,128)(2,1)S(1)}, bf16[256,1024]{1,0:T(8,128)(2,1)}, u32[]{:S(2)}) copy-start(bf16[256,1024]{1,0:T(8,128)(2,1)} %get-tuple-element.37.refs_4_) | copy-start | bytes 1572868
  44.6 19.7 %all-to-all-start = ((bf16[8,256,256]{2,1,0:T(8,128)(2,1)}), bf16[8,256,256]{2,1,0:T(8,128)(2,1)}, u32[]{:S(2)}, u32[]{:S(2)}) async-start(bf16[8,256,256]{2,1,0:T(8,128)(2,1)} %get-tuple-element.38), calls=%async_computation | async-start | bytes 2097152 | tf_op jit(solution)/shard_map/all_to_all | solution.py:312
  50.7 15.0 %collective-permute-start.8 = (bf16[256,1024]{1,0:T(8,128)(2,1)S(1)}, bf16[256,1024]{1,0:T(8,128)(2,1)S(1)}, u32[]{:S(2)}, u32[]{:S(2)}) collective-permute-start(bf16[256,1024]{1,0:T(8,128)(2,1)S(1)} %copy-done.1), channel_id=1, source_target_pairs={{0,16},{16,32},{32,48},{48,0},{1,17},{17,33},{33,49},{49,1},{2,18}... | collective-permute-start | bytes 1572872 | tf_op jit(solution)/shard_map/ppermute | solution.py:33
  51.9 13.9 %collective-permute-start.9 = (bf16[256,1024]{1,0:T(8,128)(2,1)S(1)}, bf16[256,1024]{1,0:T(8,128)(2,1)S(1)}, u32[]{:S(2)}, u32[]{:S(2)}) collective-permute-start(bf16[256,1024]{1,0:T(8,128)(2,1)S(1)} %copy-done.1), channel_id=1, source_target_pairs={{0,48},{16,0},{32,16},{48,32},{1,49},{17,1},{33,17},{49,33},{2,50}... | collective-permute-start | bytes 1572872 | tf_op jit(solution)/shard_map/ppermute | solution.py:33
  66.4 16.3 %collective-permute-start.10 = (bf16[256,512]{1,0:T(8,128)(2,1)}, bf16[256,512]{1,0:T(8,128)(2,1)S(1)}, u32[]{:S(2)}, u32[]{:S(2)}) collective-permute-start(bf16[256,512]{1,0:T(8,128)(2,1)} %slice.31), channel_id=1, source_target_pairs={{0,16},{16,32},{32,48},{48,0},{1,17},{17,33},{33,49},{49,1},{2,18}... | collective-permute-start | bytes 786440 | tf_op jit(solution)/shard_map/ppermute | solution.py:33
  68.9 13.9 %collective-permute-start.11 = (bf16[256,512]{1,0:T(8,128)(2,1)}, bf16[256,512]{1,0:T(8,128)(2,1)}, u32[]{:S(2)}, u32[]{:S(2)}) collective-permute-start(bf16[256,512]{1,0:T(8,128)(2,1)} %slice.32), channel_id=1, source_target_pairs={{0,48},{16,0},{32,16},{48,32},{1,49},{17,1},{33,17},{49,33},{2,50}... | collective-permute-start | bytes 786440 | tf_op jit(solution)/shard_map/ppermute | solution.py:33
  70.7 8.7 %collective-permute-start.12 = (bf16[256,256]{1,0:T(8,128)(2,1)S(1)}, bf16[256,256]{1,0:T(8,128)(2,1)}, u32[]{:S(2)}, u32[]{:S(2)}) collective-permute-start(bf16[256,256]{1,0:T(8,128)(2,1)S(1)} %reduce_sum.33.refs_9_), channel_id=1, source_target_pairs={{0,16},{16,32},{32,48},{48,0},{1,17},{17,33},{33,49},{49,1},{2,18}... | collective-permute-start | bytes 393224 | tf_op jit(solution)/shard_map/ppermute | solution.py:33
  70.9 11.9 %collective-permute-start.13 = (bf16[256,256]{1,0:T(8,128)(2,1)S(1)}, bf16[256,256]{1,0:T(8,128)(2,1)}, u32[]{:S(2)}, u32[]{:S(2)}) collective-permute-start(bf16[256,256]{1,0:T(8,128)(2,1)S(1)} %reduce_sum.33.refs_9_), channel_id=1, source_target_pairs={{0,32},{16,48},{32,0},{48,16},{1,33},{17,49},{33,1},{49,17},{2,34}... | collective-permute-start | bytes 393224 | tf_op jit(solution)/shard_map/ppermute | solution.py:33
  74.2 8.6 %collective-permute-start.14 = (bf16[256,256]{1,0:T(8,128)(2,1)S(1)}, bf16[256,256]{1,0:T(8,128)(2,1)}, u32[]{:S(2)}, u32[]{:S(2)}) collective-permute-start(bf16[256,256]{1,0:T(8,128)(2,1)S(1)} %reduce_sum.33.refs_9_), channel_id=1, source_target_pairs={{0,48},{16,0},{32,16},{48,32},{1,49},{17,1},{33,17},{49,33},{2,50}... | collective-permute-start | bytes 393224 | tf_op jit(solution)/shard_map/ppermute | solution.py:33
  82.8 1.0 copy-start.3
  83.8 2.8 %copy-start.4 = (bf16[1024,256]{1,0:T(8,128)(2,1)S(1)}, bf16[1024,256]{1,0:T(8,128)(2,1)}, u32[]{:S(2)}) copy-start(bf16[1024,256]{1,0:T(8,128)(2,1)} %copy-done.2) | copy-start | bytes 1572868
  86.5 3.1 %collective-permute-start.15 = (bf16[8,4,16,1280]{3,2,1,0:T(8,128)(2,1)S(1)}, bf16[8,4,16,1280]{3,2,1,0:T(8,128)(2,1)S(1)}, u32[]{:S(2)}, u32[]{:S(2)}) collective-permute-start(bf16[8,4,16,1280]{3,2,1,0:T(8,128)(2,1)S(1)} %weight_part.3), channel_id=1, source_target_pairs={{0,8},{8,0},{1,9},{9,1},{2,10},{10,2},{3,11},{11,3},{4,12},{12,4},... | collective-permute-start | bytes 3932168 | tf_op jit(solution)/shard_map/ppermute | solution.py:33
  113.0 16.2 %all-to-all-start.2 = ((bf16[4,16,1280]{2,1,0:T(8,128)(2,1)}), bf16[4,16,1280]{2,1,0:T(8,128)(2,1)S(1)}, u32[]{:S(2)}, u32[]{:S(2)}) async-start(bf16[4,16,1280]{2,1,0:T(8,128)(2,1)} %bitcast.17), calls=%async_computation.2 | async-start | bytes 327680 | tf_op jit(solution)/shard_map/all_to_all | solution.py:327
  (1 other events, 0.8 us)

commit v11 on v10

--- a/solution.py
+++ b/solution.py
@@ -198,9 +198,9 @@
         ],
         compiler_params=pltpu.CompilerParams(vmem_limit_bytes=52 * 2**20),
         cost_estimate=pl.CostEstimate(
-            flops=10 * per * rows * rows * blocks * hd,
+            flops=4 * per * rows * rows * blocks * hd,
             bytes_accessed=4 * 2**20,
-            transcendentals=per * rows * rows * blocks,
+            transcendentals=0,
         ),
         name="attention_backward",
     )(place[None], docs, q, do, *kv)

time: 132 us -> 125 us (0.947)
  waiting for transfers between devices: 43 us -> 30.3 us
  starting transfers between devices: 38.9 us -> 44.6 us
    ppermute x16, waiting for transfers between devices: 24.5 us -> 14.1 us  [shifted(): return lax.ppermute(value, axis, pairs)]
    all_to_all x1, starting transfers between devices: 6.09 us -> 10.8 us  [local(): dkv = lax.all_to_all(dkv, CTX, 0, 0, tiled=True)]
    all_to_all x1, waiting for transfers between devices: 10.4 us -> 8.15 us  [local(): dkv = lax.all_to_all(dkv, CTX, 0, 0, tiled=True)]
    all_to_all x1, starting transfers between devices: 7.5 us -> 9.49 us  [local(): part = lax.all_to_all(part, 'zh', 0, 0, tiled=True)]
  transfers between devices with their start and end apart: 18 -> 18, of which waited for: 8 -> 7; matrix products, arithmetic and copies ran while one was open for 2% -> 2% of each run, Pallas kernels for 9% -> 9%
where the time goes in v11:
time: 125 us; the launch traced here: 123 us
  starting transfers between devices  44.6 us (36%)
  waiting for transfers between devices  30.3 us (24%)
  blocking collectives  21.9 us (18%)
  Pallas kernels  14.3 us (11%)
  local copies, waits for them, and re-layouts  7.81 us (6%)
  other arithmetic  3.48 us (3%)
    ppermute x16, starting transfers between devices, shifted(): return lax.ppermute(value, axis, pairs)  24.4 us
    all_to_all x1, blocking collectives, local(): part = lax.all_to_all(part, CTX, 0, 0, tiled=True)  21.9 us
    ppermute x16, waiting for transfers between devices, shifted(): return lax.ppermute(value, axis, pairs)  14.1 us
    all_to_all x1, starting transfers between devices, local(): dkv = lax.all_to_all(dkv, CTX, 0, 0, tiled=True)  10.8 us
    all_to_all x1, starting transfers between devices, local(): part = lax.all_to_all(part, 'zh', 0, 0, tiled=True)  9.49 us
    all_to_all x1, waiting for transfers between devices, local(): dkv = lax.all_to_all(dkv, CTX, 0, 0, tiled=True)  8.15 us
    all_to_all x1, waiting for transfers between devices, local(): part = lax.all_to_all(part, 'zh', 0, 0, tiled=True)  8.08 us
    pallas_call x1, Pallas kernels, attention(): pl.pallas_call(functools.partial(attention_kernel, ny, per, DOCS, hd ** (...  6.62 us
  transfers between devices with their start and end apart: 18, of which 7 were waited for; matrix products, arithmetic and copies ran while one was open for 2% of the time, Pallas kernels for 9%

profile of v11, /device:TPU:32, one launch (start us, length us, event | category | flops | bytes accessed | tf_op | source)
XLA Modules:
  0.0 123.2 jit_solution(11324921386784209297)
XLA Ops:
  1.5 1.9 %collective-permute-start = (bf16[256,256]{1,0:T(8,128)(2,1)S(1)}, bf16[256,256]{1,0:T(8,128)(2,1)S(1)}, u32[]{:S(2)}, u32[]{:S(2)}) collective-permute-start(bf16[256,256]{1,0:T(8,128)(2,1)S(1)} %get-tuple-element.49), channel_id=1, source_target_pairs={{0,1},{1,0},{2,3},{3,2},{4,5},{5,4},{6,7},{7,6},{8,9},{9,8},{10,11... | collective-permute-start | bytes 393224 | tf_op jit(solution)/shard_map/ppermute | solution.py:33
  3.5 1.6 %copy-done = bf16[1,256,4096]{2,1,0:T(8,128)(2,1)S(1)} copy-done((bf16[1,256,4096]{2,1,0:T(8,128)(2,1)S(1)}, bf16[1,256,4096]{2,1,0:T(8,128)(2,1)}, u32[]{:S(2)}) %copy-start) | copy-done | bytes 2097176
  5.1 2.4 %split_features.1 = (bf16[1024,256]{1,0:T(8,128)(2,1)S(1)}, bf16[1024,256]{1,0:T(8,128)(2,1)}, bf16[1024,256]{1,0:T(8,128)(2,1)}, bf16[1024,256]{1,0:T(8,128)(2,1)}) custom-call(s32[1]{0:T(128)} %bitcast.6.info, bf16[256,4096]{1,0:T(8,128)(2,1)S(1)} %bitcast.23, bf16[256,4096]{1,0:T(8,128)(2,1)S(1)} %bitcast.24, bf16[256,4096]{1,0:T(8,128)(2,1)S(1)} %bitcast.25, ...), custom_call_target="tpu_custom_call" | custom-call | tf_op jit(solution)/shard_map/split_features/pallas_call | solution.py:222
  7.5 1.1 collective-permute-start.1
  8.5 2.2 %collective-permute-start.3 = (bf16[2,256,256]{2,1,0:T(8,128)(2,1)S(1)}, bf16[2,256,256]{2,1,0:T(8,128)(2,1)S(1)}, u32[]{:S(2)}, u32[]{:S(2)}) collective-permute-start(bf16[2,256,256]{2,1,0:T(8,128)(2,1)S(1)} %pad_maximum_fusion.refs_0_), channel_id=1, source_target_pairs={{0,6},{2,0},{4,2},{6,4},{1,7},{3,1},{5,3},{7,5},{8,14},{10,8},{12,... | collective-permute-start | bytes 786440 | tf_op jit(solution)/shard_map/ppermute | solution.py:33
  11.7 2.7 %collective-permute-start.6 = (bf16[1024,256]{1,0:T(8,128)(2,1)}, bf16[1024,256]{1,0:T(8,128)(2,1)S(1)}, u32[]{:S(2)}, u32[]{:S(2)}) collective-permute-start(bf16[1024,256]{1,0:T(8,128)(2,1)} %get-tuple-element.35), channel_id=1, source_target_pairs={{0,32},{16,48},{32,0},{48,16},{1,33},{17,49},{33,1},{49,17},{2,34}... | collective-permute-start | bytes 1572872 | tf_op jit(solution)/shard_map/ppermute | solution.py:33
  14.4 1.4 %collective-permute-start.7 = (bf16[1024,256]{1,0:T(8,128)(2,1)}, bf16[1024,256]{1,0:T(8,128)(2,1)S(1)}, u32[]{:S(2)}, u32[]{:S(2)}) collective-permute-start(bf16[1024,256]{1,0:T(8,128)(2,1)} %get-tuple-element.36), channel_id=1, source_target_pairs={{0,48},{16,0},{32,16},{48,32},{1,49},{17,1},{33,17},{49,33},{2,50}... | collective-permute-start | bytes 1572872 | tf_op jit(solution)/shard_map/ppermute | solution.py:33
  16.3 2.9 %collective-permute-start.4 = (bf16[256,256]{1,0:T(8,128)(2,1)S(1)}, bf16[256,256]{1,0:T(8,128)(2,1)S(1)}, u32[]{:S(2)}, u32[]{:S(2)}) collective-permute-start(bf16[256,256]{1,0:T(8,128)(2,1)S(1)} %slice_bitcast_fusion), channel_id=1, source_target_pairs={{0,6},{2,0},{4,2},{6,4},{1,7},{3,1},{5,3},{7,5},{8,14},{10,8},{12,... | collective-permute-start | bytes 393224 | tf_op jit(solution)/shard_map/ppermute | solution.py:33
  19.3 2.8 %collective-permute-done.2.refs_2_ = bf16[256,256]{1,0:T(8,128)(2,1)S(1)} collective-permute-done((bf16[256,256]{1,0:T(8,128)(2,1)S(1)}, bf16[256,256]{1,0:T(8,128)(2,1)S(1)}, u32[]{:S(2)}, u32[]{:S(2)}) %collective-permute-start.2) | collective-permute-done | bytes 131104 | tf_op jit(solution)/shard_map/ppermute | solution.py:33
  23.2 6.6 %attention_backward.1 = (bf16[256,1024]{1,0:T(8,128)(2,1)}, bf16[8,256,256]{2,1,0:T(8,128)(2,1)}) custom-call(s32[1]{0:T(128)} %bitcast.info, s32[1,2048]{1,0:T(1,128)S(1)} %copy-done.6, bf16[256,1024]{1,0:T(8,128)(2,1)S(1)} %bitcast.28, bf16[256,1024]{1,0:T(8,128)(2,1)} %bitcast.33, bf16[2,256,256]{2,1,0:T(8,128)(2,1)S(1)} %pad_maximum_fusion.refs_0_, ...), custom_call_target="tpu_custom_call" | custom-call | flops 2147483648 | bytes 4194304 | tf_op jit(solution)/shard_map/attention_backward/pallas_call | solution.py:169
  29.8 6.4 %collective-permute-done.6.refs_2_ = bf16[1024,256]{1,0:T(8,128)(2,1)S(1)} collective-permute-done((bf16[1024,256]{1,0:T(8,128)(2,1)}, bf16[1024,256]{1,0:T(8,128)(2,1)S(1)}, u32[]{:S(2)}, u32[]{:S(2)}) %collective-permute-start.6) | collective-permute-done | bytes 524320 | tf_op jit(solution)/shard_map/ppermute | solution.py:33
  37.0 10.8 %all-to-all-start = ((bf16[8,256,256]{2,1,0:T(8,128)(2,1)}), bf16[8,256,256]{2,1,0:T(8,128)(2,1)}, u32[]{:S(2)}, u32[]{:S(2)}) async-start(bf16[8,256,256]{2,1,0:T(8,128)(2,1)} %get-tuple-element.38), calls=%async_computation | async-start | bytes 2097152 | tf_op jit(solution)/shard_map/all_to_all | solution.py:312
  48.8 2.2 %collective-permute-start.9 = (bf16[256,1024]{1,0:T(8,128)(2,1)S(1)}, bf16[256,1024]{1,0:T(8,128)(2,1)S(1)}, u32[]{:S(2)}, u32[]{:S(2)}) collective-permute-start(bf16[256,1024]{1,0:T(8,128)(2,1)S(1)} %copy-done.1), channel_id=1, source_target_pairs={{0,48},{16,0},{32,16},{48,32},{1,49},{17,1},{33,17},{49,33},{2,50}... | collective-permute-start | bytes 1572872 | tf_op jit(solution)/shard_map/ppermute | solution.py:33
  51.0 8.2 %all-to-all-done = bf16[8,256,256]{2,1,0:T(8,128)(2,1)} async-done(((bf16[8,256,256]{2,1,0:T(8,128)(2,1)}), bf16[8,256,256]{2,1,0:T(8,128)(2,1)}, u32[]{:S(2)}, u32[]{:S(2)}) %all-to-all-start) | async-done | bytes 1048608 | tf_op jit(solution)/shard_map/all_to_all | solution.py:312
  59.2 1.4 %reduce_sum.33.refs_9_ = bf16[256,256]{1,0:T(8,128)(2,1)S(1)} reduce(bf16[8,256,256]{2,1,0:T(8,128)(2,1)} %all-to-all-done, bf16[]{:T(256)} %constant.22.clone.1), dimensions={0}, to_apply=%region_0.0 | reduce | flops 458752 | bytes 1179650 | tf_op jit(solution)/shard_map/reduce_sum | solution.py:313
  62.6 2.6 %collective-permute-start.11 = (bf16[256,512]{1,0:T(8,128)(2,1)}, bf16[256,512]{1,0:T(8,128)(2,1)}, u32[]{:S(2)}, u32[]{:S(2)}) collective-permute-start(bf16[256,512]{1,0:T(8,128)(2,1)} %slice.32), channel_id=1, source_target_pairs={{0,48},{16,0},{32,16},{48,32},{1,49},{17,1},{33,17},{49,33},{2,50}... | collective-permute-start | bytes 786440 | tf_op jit(solution)/shard_map/ppermute | solution.py:33
  65.2 2.3 %collective-permute-start.13 = (bf16[256,256]{1,0:T(8,128)(2,1)S(1)}, bf16[256,256]{1,0:T(8,128)(2,1)}, u32[]{:S(2)}, u32[]{:S(2)}) collective-permute-start(bf16[256,256]{1,0:T(8,128)(2,1)S(1)} %reduce_sum.33.refs_9_), channel_id=1, source_target_pairs={{0,32},{16,48},{32,0},{48,16},{1,33},{17,49},{33,1},{49,17},{2,34}... | collective-permute-start | bytes 393224 | tf_op jit(solution)/shard_map/ppermute | solution.py:33
  67.5 1.8 %collective-permute-start.14 = (bf16[256,256]{1,0:T(8,128)(2,1)S(1)}, bf16[256,256]{1,0:T(8,128)(2,1)}, u32[]{:S(2)}, u32[]{:S(2)}) collective-permute-start(bf16[256,256]{1,0:T(8,128)(2,1)S(1)} %reduce_sum.33.refs_9_), channel_id=1, source_target_pairs={{0,48},{16,0},{32,16},{48,32},{1,49},{17,1},{33,17},{49,33},{2,50}... | collective-permute-start | bytes 393224 | tf_op jit(solution)/shard_map/ppermute | solution.py:33
  69.3 3.6 %collective-permute-done.12.refs_10_ = bf16[256,256]{1,0:T(8,128)(2,1)} collective-permute-done((bf16[256,256]{1,0:T(8,128)(2,1)S(1)}, bf16[256,256]{1,0:T(8,128)(2,1)}, u32[]{:S(2)}, u32[]{:S(2)}) %collective-permute-start.12) | collective-permute-done | bytes 131104 | tf_op jit(solution)/shard_map/ppermute | solution.py:33
  74.8 2.7 %weight_part.3 = bf16[8,4,16,1280]{3,2,1,0:T(8,128)(2,1)S(1)} custom-call(s32[1]{0:T(128)} %bitcast.15.info, bf16[1024,256]{1,0:T(8,128)(2,1)S(1)} %get-tuple-element.40.refs_0_, bf16[1024,256]{1,0:T(8,128)(2,1)S(1)} %collective-permute-done.5.refs_1_, bf16[1024,256]{1,0:T(8,128)(2,1)S(1)} %collective-permute-done.6.refs_2_, ...), custom_call_target="tpu_custom_call" | custom-call | flops 1342177280 | bytes 6291456 | tf_op jit(solution)/shard_map/weight_part/pallas_call | solution.py:274
  77.6 2.6 %weight_part.2 = bf16[8,4,16,1280]{3,2,1,0:T(8,128)(2,1)S(1)} custom-call(s32[1]{0:T(128)} %bitcast.14.info, bf16[1024,256]{1,0:T(8,128)(2,1)S(1)} %get-tuple-element.40.refs_0_, bf16[1024,256]{1,0:T(8,128)(2,1)S(1)} %collective-permute-done.5.refs_1_, bf16[1024,256]{1,0:T(8,128)(2,1)S(1)} %collective-permute-done.6.refs_2_, ...), custom_call_target="tpu_custom_call" | custom-call | flops 1342177280 | bytes 6291456 | tf_op jit(solution)/shard_map/weight_part/pallas_call | solution.py:274
  81.0 21.9 %all_to_all.15 = bf16[8,64,1280]{2,1,0:T(8,128)(2,1)S(1)} all-to-all(bf16[8,64,1280]{2,1,0:T(8,128)(2,1)S(1)} %bitcast.29), channel_id=1, replica_groups=mesh['zh'=4,'x'=4,'core'=2,'y'=4,'zl'=2] {'y','zl'}, dimensions={0} | all-to-all | bytes 2621440 | tf_op jit(solution)/shard_map/all_to_all | solution.py:325
  103.7 9.5 %all-to-all-start.2 = ((bf16[4,16,1280]{2,1,0:T(8,128)(2,1)}), bf16[4,16,1280]{2,1,0:T(8,128)(2,1)S(1)}, u32[]{:S(2)}, u32[]{:S(2)}) async-start(bf16[4,16,1280]{2,1,0:T(8,128)(2,1)} %bitcast.17), calls=%async_computation.2 | async-start | bytes 327680 | tf_op jit(solution)/shard_map/all_to_all | solution.py:327
  113.9 8.1 %all-to-all-done.2 = bf16[4,16,1280]{2,1,0:T(8,128)(2,1)S(1)} async-done(((bf16[4,16,1280]{2,1,0:T(8,128)(2,1)}), bf16[4,16,1280]{2,1,0:T(8,128)(2,1)S(1)}, u32[]{:S(2)}, u32[]{:S(2)}) %all-to-all-start.2) | async-done | bytes 163872 | tf_op jit(solution)/shard_map/all_to_all | solution.py:327
  (45 shorter events, 12.7 us)
Async XLA Ops:
  1.5 5.9 %collective-permute-start = (bf16[256,256]{1,0:T(8,128)(2,1)S(1)}, bf16[256,256]{1,0:T(8,128)(2,1)S(1)}, u32[]{:S(2)}, u32[]{:S(2)}) collective-permute-start(bf16[256,256]{1,0:T(8,128)(2,1)S(1)} %get-tuple-element.49), channel_id=1, source_target_pairs={{0,1},{1,0},{2,3},{3,2},{4,5},{5,4},{6,7},{7,6},{8,9},{9,8},{10,11... | collective-permute-start | bytes 393224 | tf_op jit(solution)/shard_map/ppermute | solution.py:33
  3.5 1.6 %copy-start = (bf16[1,256,4096]{2,1,0:T(8,128)(2,1)S(1)}, bf16[1,256,4096]{2,1,0:T(8,128)(2,1)}, u32[]{:S(2)}) copy-start(bf16[1,256,4096]{2,1,0:T(8,128)(2,1)} %param.6) | copy-start | bytes 6291460
  5.0 17.1 %copy-start.6 = (s32[1,2048]{1,0:T(1,128)S(1)}, s32[1,2048]{1,0:T(1,128)}, u32[]{:S(2)}) copy-start(s32[1,2048]{1,0:T(1,128)} %docs_ref.1) | copy-start | bytes 24580
  7.5 8.4 %collective-permute-start.1 = (bf16[2,256,256]{2,1,0:T(8,128)(2,1)S(1)}, bf16[2,256,256]{2,1,0:T(8,128)(2,1)S(1)}, u32[]{:S(2)}, u32[]{:S(2)}) collective-permute-start(bf16[2,256,256]{2,1,0:T(8,128)(2,1)S(1)} %pad_maximum_fusion.refs_0_), channel_id=1, source_target_pairs={{0,2},{2,4},{4,6},{6,0},{1,3},{3,5},{5,7},{7,1},{8,10},{10,12},{12... | collective-permute-start | bytes 786440 | tf_op jit(solution)/shard_map/ppermute | solution.py:33
  8.5 7.8 %collective-permute-start.3 = (bf16[2,256,256]{2,1,0:T(8,128)(2,1)S(1)}, bf16[2,256,256]{2,1,0:T(8,128)(2,1)S(1)}, u32[]{:S(2)}, u32[]{:S(2)}) collective-permute-start(bf16[2,256,256]{2,1,0:T(8,128)(2,1)S(1)} %pad_maximum_fusion.refs_0_), channel_id=1, source_target_pairs={{0,6},{2,0},{4,2},{6,4},{1,7},{3,1},{5,3},{7,5},{8,14},{10,8},{12,... | collective-permute-start | bytes 786440 | tf_op jit(solution)/shard_map/ppermute | solution.py:33
  10.8 19.0 %collective-permute-start.5 = (bf16[1024,256]{1,0:T(8,128)(2,1)}, bf16[1024,256]{1,0:T(8,128)(2,1)S(1)}, u32[]{:S(2)}, u32[]{:S(2)}) collective-permute-start(bf16[1024,256]{1,0:T(8,128)(2,1)} %get-tuple-element.34), channel_id=1, source_target_pairs={{0,16},{16,32},{32,48},{48,0},{1,17},{17,33},{33,49},{49,1},{2,18}... | collective-permute-start | bytes 1572872 | tf_op jit(solution)/shard_map/ppermute | solution.py:33
  11.7 24.5 %collective-permute-start.6 = (bf16[1024,256]{1,0:T(8,128)(2,1)}, bf16[1024,256]{1,0:T(8,128)(2,1)S(1)}, u32[]{:S(2)}, u32[]{:S(2)}) collective-permute-start(bf16[1024,256]{1,0:T(8,128)(2,1)} %get-tuple-element.35), channel_id=1, source_target_pairs={{0,32},{16,48},{32,0},{48,16},{1,33},{17,49},{33,1},{49,17},{2,34}... | collective-permute-start | bytes 1572872 | tf_op jit(solution)/shard_map/ppermute | solution.py:33
  14.4 21.8 %collective-permute-start.7 = (bf16[1024,256]{1,0:T(8,128)(2,1)}, bf16[1024,256]{1,0:T(8,128)(2,1)S(1)}, u32[]{:S(2)}, u32[]{:S(2)}) collective-permute-start(bf16[1024,256]{1,0:T(8,128)(2,1)} %get-tuple-element.36), channel_id=1, source_target_pairs={{0,48},{16,0},{32,16},{48,32},{1,49},{17,1},{33,17},{49,33},{2,50}... | collective-permute-start | bytes 1572872 | tf_op jit(solution)/shard_map/ppermute | solution.py:33
  15.9 6.3 %collective-permute-start.2 = (bf16[256,256]{1,0:T(8,128)(2,1)S(1)}, bf16[256,256]{1,0:T(8,128)(2,1)S(1)}, u32[]{:S(2)}, u32[]{:S(2)}) collective-permute-start(bf16[256,256]{1,0:T(8,128)(2,1)S(1)} %slice_bitcast_fusion.1), channel_id=1, source_target_pairs={{0,2},{2,4},{4,6},{6,0},{1,3},{3,5},{5,7},{7,1},{8,10},{10,12},{12... | collective-permute-start | bytes 393224 | tf_op jit(solution)/shard_map/ppermute | solution.py:33
  16.3 5.8 %collective-permute-start.4 = (bf16[256,256]{1,0:T(8,128)(2,1)S(1)}, bf16[256,256]{1,0:T(8,128)(2,1)S(1)}, u32[]{:S(2)}, u32[]{:S(2)}) collective-permute-start(bf16[256,256]{1,0:T(8,128)(2,1)S(1)} %slice_bitcast_fusion), channel_id=1, source_target_pairs={{0,6},{2,0},{4,2},{6,4},{1,7},{3,1},{5,3},{7,5},{8,14},{10,8},{12,... | collective-permute-start | bytes 393224 | tf_op jit(solution)/shard_map/ppermute | solution.py:33
  22.1 1.0 copy-start.5
  29.8 18.0 %copy-start.1 = (bf16[256,1024]{1,0:T(8,128)(2,1)S(1)}, bf16[256,1024]{1,0:T(8,128)(2,1)}, u32[]{:S(2)}) copy-start(bf16[256,1024]{1,0:T(8,128)(2,1)} %get-tuple-element.37.refs_4_) | copy-start | bytes 1572868
  37.0 22.2 %all-to-all-start = ((bf16[8,256,256]{2,1,0:T(8,128)(2,1)}), bf16[8,256,256]{2,1,0:T(8,128)(2,1)}, u32[]{:S(2)}, u32[]{:S(2)}) async-start(bf16[8,256,256]{2,1,0:T(8,128)(2,1)} %get-tuple-element.38), calls=%async_computation | async-start | bytes 2097152 | tf_op jit(solution)/shard_map/all_to_all | solution.py:312
  47.8 12.8 %collective-permute-start.8 = (bf16[256,1024]{1,0:T(8,128)(2,1)S(1)}, bf16[256,1024]{1,0:T(8,128)(2,1)S(1)}, u32[]{:S(2)}, u32[]{:S(2)}) collective-permute-start(bf16[256,1024]{1,0:T(8,128)(2,1)S(1)} %copy-done.1), channel_id=1, source_target_pairs={{0,16},{16,32},{32,48},{48,0},{1,17},{17,33},{33,49},{49,1},{2,18}... | collective-permute-start | bytes 1572872 | tf_op jit(solution)/shard_map/ppermute | solution.py:33
  48.8 11.7 %collective-permute-start.9 = (bf16[256,1024]{1,0:T(8,128)(2,1)S(1)}, bf16[256,1024]{1,0:T(8,128)(2,1)S(1)}, u32[]{:S(2)}, u32[]{:S(2)}) collective-permute-start(bf16[256,1024]{1,0:T(8,128)(2,1)S(1)} %copy-done.1), channel_id=1, source_target_pairs={{0,48},{16,0},{32,16},{48,32},{1,49},{17,1},{33,17},{49,33},{2,50}... | collective-permute-start | bytes 1572872 | tf_op jit(solution)/shard_map/ppermute | solution.py:33
  61.3 12.5 %collective-permute-start.10 = (bf16[256,512]{1,0:T(8,128)(2,1)}, bf16[256,512]{1,0:T(8,128)(2,1)S(1)}, u32[]{:S(2)}, u32[]{:S(2)}) collective-permute-start(bf16[256,512]{1,0:T(8,128)(2,1)} %slice.31), channel_id=1, source_target_pairs={{0,16},{16,32},{32,48},{48,0},{1,17},{17,33},{33,49},{49,1},{2,18}... | collective-permute-start | bytes 786440 | tf_op jit(solution)/shard_map/ppermute | solution.py:33
  62.6 11.2 %collective-permute-start.11 = (bf16[256,512]{1,0:T(8,128)(2,1)}, bf16[256,512]{1,0:T(8,128)(2,1)}, u32[]{:S(2)}, u32[]{:S(2)}) collective-permute-start(bf16[256,512]{1,0:T(8,128)(2,1)} %slice.32), channel_id=1, source_target_pairs={{0,48},{16,0},{32,16},{48,32},{1,49},{17,1},{33,17},{49,33},{2,50}... | collective-permute-start | bytes 786440 | tf_op jit(solution)/shard_map/ppermute | solution.py:33
  65.2 7.7 %collective-permute-start.12 = (bf16[256,256]{1,0:T(8,128)(2,1)S(1)}, bf16[256,256]{1,0:T(8,128)(2,1)}, u32[]{:S(2)}, u32[]{:S(2)}) collective-permute-start(bf16[256,256]{1,0:T(8,128)(2,1)S(1)} %reduce_sum.33.refs_9_), channel_id=1, source_target_pairs={{0,16},{16,32},{32,48},{48,0},{1,17},{17,33},{33,49},{49,1},{2,18}... | collective-permute-start | bytes 393224 | tf_op jit(solution)/shard_map/ppermute | solution.py:33
  65.2 7.7 %collective-permute-start.13 = (bf16[256,256]{1,0:T(8,128)(2,1)S(1)}, bf16[256,256]{1,0:T(8,128)(2,1)}, u32[]{:S(2)}, u32[]{:S(2)}) collective-permute-start(bf16[256,256]{1,0:T(8,128)(2,1)S(1)} %reduce_sum.33.refs_9_), channel_id=1, source_target_pairs={{0,32},{16,48},{32,0},{48,16},{1,33},{17,49},{33,1},{49,17},{2,34}... | collective-permute-start | bytes 393224 | tf_op jit(solution)/shard_map/ppermute | solution.py:33
  67.5 6.2 %collective-permute-start.14 = (bf16[256,256]{1,0:T(8,128)(2,1)S(1)}, bf16[256,256]{1,0:T(8,128)(2,1)}, u32[]{:S(2)}, u32[]{:S(2)}) collective-permute-start(bf16[256,256]{1,0:T(8,128)(2,1)S(1)} %reduce_sum.33.refs_9_), channel_id=1, source_target_pairs={{0,48},{16,0},{32,16},{48,32},{1,49},{17,1},{33,17},{49,33},{2,50}... | collective-permute-start | bytes 393224 | tf_op jit(solution)/shard_map/ppermute | solution.py:33
  73.8 1.0 copy-start.3
  74.8 2.8 %copy-start.4 = (bf16[1024,256]{1,0:T(8,128)(2,1)S(1)}, bf16[1024,256]{1,0:T(8,128)(2,1)}, u32[]{:S(2)}) copy-start(bf16[1024,256]{1,0:T(8,128)(2,1)} %copy-done.2) | copy-start | bytes 1572868
  77.5 3.1 %collective-permute-start.15 = (bf16[8,4,16,1280]{3,2,1,0:T(8,128)(2,1)S(1)}, bf16[8,4,16,1280]{3,2,1,0:T(8,128)(2,1)S(1)}, u32[]{:S(2)}, u32[]{:S(2)}) collective-permute-start(bf16[8,4,16,1280]{3,2,1,0:T(8,128)(2,1)S(1)} %weight_part.3), channel_id=1, source_target_pairs={{0,8},{8,0},{1,9},{9,1},{2,10},{10,2},{3,11},{11,3},{4,12},{12,4},... | collective-permute-start | bytes 3932168 | tf_op jit(solution)/shard_map/ppermute | solution.py:33
  103.7 18.2 %all-to-all-start.2 = ((bf16[4,16,1280]{2,1,0:T(8,128)(2,1)}), bf16[4,16,1280]{2,1,0:T(8,128)(2,1)S(1)}, u32[]{:S(2)}, u32[]{:S(2)}) async-start(bf16[4,16,1280]{2,1,0:T(8,128)(2,1)} %bitcast.17), calls=%async_computation.2 | async-start | bytes 327680 | tf_op jit(solution)/shard_map/all_to_all | solution.py:327
  (1 other events, 0.8 us)

commit v12 on v11

--- a/solution.py
+++ b/solution.py
@@ -324,9 +324,13 @@
     part = plus(mine, theirs).reshape(ctx, -1, n)
     part = lax.all_to_all(part, CTX, 0, 0, tiled=True)
     part = jnp.sum(part.astype(F32), axis=0).astype(BF).reshape(z_hi, -1, n)
-    part = lax.all_to_all(part, "zh", 0, 0, tiled=True)
+    my_zh = lax.axis_index("zh")
+    weight = 0.0
+    for step in range(z_hi):
+        piece = lax.dynamic_index_in_dim(part, (my_zh + step) % z_hi, 0, keepdims=False)
+        weight = weight + (shifted(piece, "zh", z_hi, step) if step else piece).astype(F32)
     tokens = rows * ctx * nx * nc * z_hi
-    weight = jnp.sum(part.astype(F32), axis=0) * (1.0 / math.sqrt(tokens))
+    weight = weight * (1.0 / math.sqrt(tokens))
     width = q.shape[1]
     return (
         dq[None],

time: 125 us -> 123 us (0.984)
  blocking collectives: 21.9 us -> 0 us
  waiting for transfers between devices: 30.3 us -> 41 us
  starting transfers between devices: 44.6 us -> 52.6 us
    all_to_all x1 -> x0, blocking collectives: 21.9 us -> none  [local(): part = lax.all_to_all(part, CTX, 0, 0, tiled=True)]
    ppermute x16 -> x19, starting transfers between devices: 24.4 us -> 36.2 us  [shifted(): return lax.ppermute(value, axis, pairs)]
    all_to_all x1, waiting for transfers between devices: 8.08 us -> 17.6 us  [local(): part = lax.all_to_all(part, CTX, 0, 0, tiled=True)]
    all_to_all x1, starting transfers between devices: 9.49 us -> 5.7 us  [local(): part = lax.all_to_all(part, CTX, 0, 0, tiled=True)]
    ppermute x16 -> x19, waiting for transfers between devices: 14.1 us -> 15.8 us  [shifted(): return lax.ppermute(value, axis, pairs)]
  transfers between devices with their start and end apart: 18 -> 21, of which waited for: 7 -> 8; matrix products, arithmetic and copies ran while one was open for 2% -> 2% of each run, Pallas kernels for 9% -> 10%
where the time goes in v12:
time: 123 us; the launch traced here: 121 us
  starting transfers between devices  52.6 us (43%)
  waiting for transfers between devices  41 us (33%)
  Pallas kernels  14.3 us (12%)
  local copies, waits for them, and re-layouts  7.9 us (6%)
  other arithmetic  3.91 us (3%)
    ppermute x19, starting transfers between devices, shifted(): return lax.ppermute(value, axis, pairs)  36.2 us
    all_to_all x1, waiting for transfers between devices, local(): part = lax.all_to_all(part, CTX, 0, 0, tiled=True)  17.6 us
    ppermute x19, waiting for transfers between devices, shifted(): return lax.ppermute(value, axis, pairs)  15.8 us
    all_to_all x1, starting transfers between devices, local(): dkv = lax.all_to_all(dkv, CTX, 0, 0, tiled=True)  10.8 us
    all_to_all x1, waiting for transfers between devices, local(): dkv = lax.all_to_all(dkv, CTX, 0, 0, tiled=True)  7.51 us
    pallas_call x1, Pallas kernels, attention(): pl.pallas_call(functools.partial(attention_kernel, ny, per, DOCS, hd ** (...  6.62 us
    all_to_all x1, starting transfers between devices, local(): part = lax.all_to_all(part, CTX, 0, 0, tiled=True)  5.7 us
    pallas_call x2, Pallas kernels, weight_part(): pl.pallas_call(functools.partial(weight_kernel, nx, z_hi), in_specs=[pl.B...  5.33 us
  transfers between devices with their start and end apart: 21, of which 8 were waited for; matrix products, arithmetic and copies ran while one was open for 2% of the time, Pallas kernels for 10%

profile of v12, /device:TPU:32, one launch (start us, length us, event | category | flops | bytes accessed | tf_op | source)
XLA Modules:
  0.0 120.6 jit_solution(16504699442906058005)
XLA Ops:
  1.5 1.9 %collective-permute-start = (bf16[256,256]{1,0:T(8,128)(2,1)S(1)}, bf16[256,256]{1,0:T(8,128)(2,1)S(1)}, u32[]{:S(2)}, u32[]{:S(2)}) collective-permute-start(bf16[256,256]{1,0:T(8,128)(2,1)S(1)} %get-tuple-element.52), channel_id=1, source_target_pairs={{0,1},{1,0},{2,3},{3,2},{4,5},{5,4},{6,7},{7,6},{8,9},{9,8},{10,11... | collective-permute-start | bytes 393224 | tf_op jit(solution)/shard_map/ppermute | solution.py:33
  3.5 1.6 %copy-done = bf16[1,256,4096]{2,1,0:T(8,128)(2,1)S(1)} copy-done((bf16[1,256,4096]{2,1,0:T(8,128)(2,1)S(1)}, bf16[1,256,4096]{2,1,0:T(8,128)(2,1)}, u32[]{:S(2)}) %copy-start) | copy-done | bytes 2097176
  5.1 2.4 %split_features.1 = (bf16[1024,256]{1,0:T(8,128)(2,1)S(1)}, bf16[1024,256]{1,0:T(8,128)(2,1)}, bf16[1024,256]{1,0:T(8,128)(2,1)}, bf16[1024,256]{1,0:T(8,128)(2,1)}) custom-call(s32[1]{0:T(128)} %bitcast.6.info, bf16[256,4096]{1,0:T(8,128)(2,1)S(1)} %bitcast.32, bf16[256,4096]{1,0:T(8,128)(2,1)S(1)} %bitcast.33, bf16[256,4096]{1,0:T(8,128)(2,1)S(1)} %bitcast.34, ...), custom_call_target="tpu_custom_call" | custom-call | tf_op jit(solution)/shard_map/split_features/pallas_call | solution.py:222
  8.5 2.2 %collective-permute-start.3 = (bf16[2,256,256]{2,1,0:T(8,128)(2,1)S(1)}, bf16[2,256,256]{2,1,0:T(8,128)(2,1)S(1)}, u32[]{:S(2)}, u32[]{:S(2)}) collective-permute-start(bf16[2,256,256]{2,1,0:T(8,128)(2,1)S(1)} %pad_maximum_fusion.refs_0_), channel_id=1, source_target_pairs={{0,6},{2,0},{4,2},{6,4},{1,7},{3,1},{5,3},{7,5},{8,14},{10,8},{12,... | collective-permute-start | bytes 786440 | tf_op jit(solution)/shard_map/ppermute | solution.py:33
  11.7 2.7 %collective-permute-start.6 = (bf16[1024,256]{1,0:T(8,128)(2,1)}, bf16[1024,256]{1,0:T(8,128)(2,1)S(1)}, u32[]{:S(2)}, u32[]{:S(2)}) collective-permute-start(bf16[1024,256]{1,0:T(8,128)(2,1)} %get-tuple-element.35), channel_id=1, source_target_pairs={{0,32},{16,48},{32,0},{48,16},{1,33},{17,49},{33,1},{49,17},{2,34}... | collective-permute-start | bytes 1572872 | tf_op jit(solution)/shard_map/ppermute | solution.py:33
  16.3 2.9 %collective-permute-start.4 = (bf16[256,256]{1,0:T(8,128)(2,1)S(1)}, bf16[256,256]{1,0:T(8,128)(2,1)S(1)}, u32[]{:S(2)}, u32[]{:S(2)}) collective-permute-start(bf16[256,256]{1,0:T(8,128)(2,1)S(1)} %slice_bitcast_fusion), channel_id=1, source_target_pairs={{0,6},{2,0},{4,2},{6,4},{1,7},{3,1},{5,3},{7,5},{8,14},{10,8},{12,... | collective-permute-start | bytes 393224 | tf_op jit(solution)/shard_map/ppermute | solution.py:33
  19.3 2.8 %collective-permute-done.2.refs_2_ = bf16[256,256]{1,0:T(8,128)(2,1)S(1)} collective-permute-done((bf16[256,256]{1,0:T(8,128)(2,1)S(1)}, bf16[256,256]{1,0:T(8,128)(2,1)S(1)}, u32[]{:S(2)}, u32[]{:S(2)}) %collective-permute-start.2) | collective-permute-done | bytes 131104 | tf_op jit(solution)/shard_map/ppermute | solution.py:33
  23.2 6.6 %attention_backward.1 = (bf16[256,1024]{1,0:T(8,128)(2,1)}, bf16[8,256,256]{2,1,0:T(8,128)(2,1)}) custom-call(s32[1]{0:T(128)} %bitcast.info, s32[1,2048]{1,0:T(1,128)S(1)} %copy-done.6, bf16[256,1024]{1,0:T(8,128)(2,1)S(1)} %bitcast.37, bf16[256,1024]{1,0:T(8,128)(2,1)} %bitcast.43, bf16[2,256,256]{2,1,0:T(8,128)(2,1)S(1)} %pad_maximum_fusion.refs_0_, ...), custom_call_target="tpu_custom_call" | custom-call | flops 2147483648 | bytes 4194304 | tf_op jit(solution)/shard_map/attention_backward/pallas_call | solution.py:169
  29.8 6.4 %collective-permute-done.6.refs_2_ = bf16[1024,256]{1,0:T(8,128)(2,1)S(1)} collective-permute-done((bf16[1024,256]{1,0:T(8,128)(2,1)}, bf16[1024,256]{1,0:T(8,128)(2,1)S(1)}, u32[]{:S(2)}, u32[]{:S(2)}) %collective-permute-start.6) | collective-permute-done | bytes 524320 | tf_op jit(solution)/shard_map/ppermute | solution.py:33
  37.0 10.8 %all-to-all-start = ((bf16[8,256,256]{2,1,0:T(8,128)(2,1)}), bf16[8,256,256]{2,1,0:T(8,128)(2,1)}, u32[]{:S(2)}, u32[]{:S(2)}) async-start(bf16[8,256,256]{2,1,0:T(8,128)(2,1)} %get-tuple-element.38), calls=%async_computation | async-start | bytes 2097152 | tf_op jit(solution)/shard_map/all_to_all | solution.py:312
  48.2 2.8 %collective-permute-start.9 = (bf16[256,1024]{1,0:T(8,128)(2,1)S(1)}, bf16[256,1024]{1,0:T(8,128)(2,1)S(1)}, u32[]{:S(2)}, u32[]{:S(2)}) collective-permute-start(bf16[256,1024]{1,0:T(8,128)(2,1)S(1)} %copy-done.1), channel_id=1, source_target_pairs={{0,48},{16,0},{32,16},{48,32},{1,49},{17,1},{33,17},{49,33},{2,50}... | collective-permute-start | bytes 1572872 | tf_op jit(solution)/shard_map/ppermute | solution.py:33
  51.0 7.5 %all-to-all-done = bf16[8,256,256]{2,1,0:T(8,128)(2,1)} async-done(((bf16[8,256,256]{2,1,0:T(8,128)(2,1)}), bf16[8,256,256]{2,1,0:T(8,128)(2,1)}, u32[]{:S(2)}, u32[]{:S(2)}) %all-to-all-start) | async-done | bytes 1048608 | tf_op jit(solution)/shard_map/all_to_all | solution.py:312
  60.7 1.9 %collective-permute-start.10 = (bf16[256,512]{1,0:T(8,128)(2,1)}, bf16[256,512]{1,0:T(8,128)(2,1)S(1)}, u32[]{:S(2)}, u32[]{:S(2)}) collective-permute-start(bf16[256,512]{1,0:T(8,128)(2,1)} %slice.31), channel_id=1, source_target_pairs={{0,16},{16,32},{32,48},{48,0},{1,17},{17,33},{33,49},{49,1},{2,18}... | collective-permute-start | bytes 786440 | tf_op jit(solution)/shard_map/ppermute | solution.py:33
  65.4 2.9 %collective-permute-start.13 = (bf16[256,256]{1,0:T(8,128)(2,1)S(1)}, bf16[256,256]{1,0:T(8,128)(2,1)}, u32[]{:S(2)}, u32[]{:S(2)}) collective-permute-start(bf16[256,256]{1,0:T(8,128)(2,1)S(1)} %reduce_sum.24.refs_9_), channel_id=1, source_target_pairs={{0,32},{16,48},{32,0},{48,16},{1,33},{17,49},{33,1},{49,17},{2,34}... | collective-permute-start | bytes 393224 | tf_op jit(solution)/shard_map/ppermute | solution.py:33
  69.4 2.1 %collective-permute-done.12.refs_10_ = bf16[256,256]{1,0:T(8,128)(2,1)} collective-permute-done((bf16[256,256]{1,0:T(8,128)(2,1)S(1)}, bf16[256,256]{1,0:T(8,128)(2,1)}, u32[]{:S(2)}, u32[]{:S(2)}) %collective-permute-start.12) | collective-permute-done | bytes 131104 | tf_op jit(solution)/shard_map/ppermute | solution.py:33
  71.5 1.9 %collective-permute-done.13.refs_11_ = bf16[256,256]{1,0:T(8,128)(2,1)} collective-permute-done((bf16[256,256]{1,0:T(8,128)(2,1)S(1)}, bf16[256,256]{1,0:T(8,128)(2,1)}, u32[]{:S(2)}, u32[]{:S(2)}) %collective-permute-start.13) | collective-permute-done | bytes 131104 | tf_op jit(solution)/shard_map/ppermute | solution.py:33
  74.5 2.7 %weight_part.3 = bf16[8,4,16,1280]{3,2,1,0:T(8,128)(2,1)S(1)} custom-call(s32[1]{0:T(128)} %bitcast.15.info, bf16[1024,256]{1,0:T(8,128)(2,1)S(1)} %get-tuple-element.40.refs_0_, bf16[1024,256]{1,0:T(8,128)(2,1)S(1)} %collective-permute-done.5.refs_1_, bf16[1024,256]{1,0:T(8,128)(2,1)S(1)} %collective-permute-done.6.refs_2_, ...), custom_call_target="tpu_custom_call" | custom-call | flops 1342177280 | bytes 6291456 | tf_op jit(solution)/shard_map/weight_part/pallas_call | solution.py:274
  77.3 2.6 %weight_part.2 = bf16[8,4,16,1280]{3,2,1,0:T(8,128)(2,1)S(1)} custom-call(s32[1]{0:T(128)} %bitcast.14.info, bf16[1024,256]{1,0:T(8,128)(2,1)S(1)} %get-tuple-element.40.refs_0_, bf16[1024,256]{1,0:T(8,128)(2,1)S(1)} %collective-permute-done.5.refs_1_, bf16[1024,256]{1,0:T(8,128)(2,1)S(1)} %collective-permute-done.6.refs_2_, ...), custom_call_target="tpu_custom_call" | custom-call | flops 1342177280 | bytes 6291456 | tf_op jit(solution)/shard_map/weight_part/pallas_call | solution.py:274
  81.7 5.7 %all-to-all-start.1 = ((bf16[8,64,1280]{2,1,0:T(8,128)(2,1)}), bf16[8,64,1280]{2,1,0:T(8,128)(2,1)S(1)}, u32[]{:S(2)}, u32[]{:S(2)}) async-start(bf16[8,64,1280]{2,1,0:T(8,128)(2,1)} %bitcast.16), calls=%async_computation.1 | async-start | bytes 2621440 | tf_op jit(solution)/shard_map/all_to_all | solution.py:325
  87.4 17.6 %all-to-all-done.1 = bf16[8,64,1280]{2,1,0:T(8,128)(2,1)S(1)} async-done(((bf16[8,64,1280]{2,1,0:T(8,128)(2,1)}), bf16[8,64,1280]{2,1,0:T(8,128)(2,1)S(1)}, u32[]{:S(2)}, u32[]{:S(2)}) %all-to-all-start.1) | async-done | bytes 1310752 | tf_op jit(solution)/shard_map/all_to_all | solution.py:325
  105.2 3.3 %collective-permute-start.16 = (bf16[16,1280]{1,0:T(8,128)(2,1)S(1)}, bf16[16,1280]{1,0:T(8,128)(2,1)S(1)}, u32[]{:S(2)}, u32[]{:S(2)}) collective-permute-start(bf16[16,1280]{1,0:T(8,128)(2,1)S(1)} %get-tuple-element.46), channel_id=1, source_target_pairs={{0,64},{64,128},{128,192},{192,0},{1,65},{65,129},{129,193},{193,1... | collective-permute-start | bytes 122888 | tf_op jit(solution)/shard_map/ppermute | solution.py:33
  108.6 5.7 %collective-permute-start.17 = (bf16[16,1280]{1,0:T(8,128)(2,1)S(1)}, bf16[16,1280]{1,0:T(8,128)(2,1)S(1)}, u32[]{:S(2)}, u32[]{:S(2)}) collective-permute-start(bf16[16,1280]{1,0:T(8,128)(2,1)S(1)} %get-tuple-element.48), channel_id=1, source_target_pairs={{0,128},{64,192},{128,0},{192,64},{1,129},{65,193},{129,1},{193,65... | collective-permute-start | bytes 122888 | tf_op jit(solution)/shard_map/ppermute | solution.py:33
  114.3 2.1 %collective-permute-start.18 = (bf16[16,1280]{1,0:T(8,128)(2,1)S(1)}, bf16[16,1280]{1,0:T(8,128)(2,1)S(1)}, u32[]{:S(2)}, u32[]{:S(2)}) collective-permute-start(bf16[16,1280]{1,0:T(8,128)(2,1)S(1)} %get-tuple-element.47), channel_id=1, source_target_pairs={{0,192},{64,0},{128,64},{192,128},{1,193},{65,1},{129,65},{193,129... | collective-permute-start | bytes 122888 | tf_op jit(solution)/shard_map/ppermute | solution.py:33
  117.1 2.2 %collective-permute-done.18 = bf16[16,1280]{1,0:T(8,128)(2,1)S(1)} collective-permute-done((bf16[16,1280]{1,0:T(8,128)(2,1)S(1)}, bf16[16,1280]{1,0:T(8,128)(2,1)S(1)}, u32[]{:S(2)}, u32[]{:S(2)}) %collective-permute-start.18) | collective-permute-done | bytes 40992 | tf_op jit(solution)/shard_map/ppermute | solution.py:33
  (50 shorter events, 18.1 us)
Async XLA Ops:
  1.5 5.9 %collective-permute-start = (bf16[256,256]{1,0:T(8,128)(2,1)S(1)}, bf16[256,256]{1,0:T(8,128)(2,1)S(1)}, u32[]{:S(2)}, u32[]{:S(2)}) collective-permute-start(bf16[256,256]{1,0:T(8,128)(2,1)S(1)} %get-tuple-element.52), channel_id=1, source_target_pairs={{0,1},{1,0},{2,3},{3,2},{4,5},{5,4},{6,7},{7,6},{8,9},{9,8},{10,11... | collective-permute-start | bytes 393224 | tf_op jit(solution)/shard_map/ppermute | solution.py:33
  5.0 17.1 %copy-start.6 = (s32[1,2048]{1,0:T(1,128)S(1)}, s32[1,2048]{1,0:T(1,128)}, u32[]{:S(2)}) copy-start(s32[1,2048]{1,0:T(1,128)} %docs_ref.1) | copy-start | bytes 24580
  7.5 8.4 %collective-permute-start.1 = (bf16[2,256,256]{2,1,0:T(8,128)(2,1)S(1)}, bf16[2,256,256]{2,1,0:T(8,128)(2,1)S(1)}, u32[]{:S(2)}, u32[]{:S(2)}) collective-permute-start(bf16[2,256,256]{2,1,0:T(8,128)(2,1)S(1)} %pad_maximum_fusion.refs_0_), channel_id=1, source_target_pairs={{0,2},{2,4},{4,6},{6,0},{1,3},{3,5},{5,7},{7,1},{8,10},{10,12},{12... | collective-permute-start | bytes 786440 | tf_op jit(solution)/shard_map/ppermute | solution.py:33
  8.5 7.8 %collective-permute-start.3 = (bf16[2,256,256]{2,1,0:T(8,128)(2,1)S(1)}, bf16[2,256,256]{2,1,0:T(8,128)(2,1)S(1)}, u32[]{:S(2)}, u32[]{:S(2)}) collective-permute-start(bf16[2,256,256]{2,1,0:T(8,128)(2,1)S(1)} %pad_maximum_fusion.refs_0_), channel_id=1, source_target_pairs={{0,6},{2,0},{4,2},{6,4},{1,7},{3,1},{5,3},{7,5},{8,14},{10,8},{12,... | collective-permute-start | bytes 786440 | tf_op jit(solution)/shard_map/ppermute | solution.py:33
  10.8 19.0 %collective-permute-start.5 = (bf16[1024,256]{1,0:T(8,128)(2,1)}, bf16[1024,256]{1,0:T(8,128)(2,1)S(1)}, u32[]{:S(2)}, u32[]{:S(2)}) collective-permute-start(bf16[1024,256]{1,0:T(8,128)(2,1)} %get-tuple-element.34), channel_id=1, source_target_pairs={{0,16},{16,32},{32,48},{48,0},{1,17},{17,33},{33,49},{49,1},{2,18}... | collective-permute-start | bytes 1572872 | tf_op jit(solution)/shard_map/ppermute | solution.py:33
  11.7 24.5 %collective-permute-start.6 = (bf16[1024,256]{1,0:T(8,128)(2,1)}, bf16[1024,256]{1,0:T(8,128)(2,1)S(1)}, u32[]{:S(2)}, u32[]{:S(2)}) collective-permute-start(bf16[1024,256]{1,0:T(8,128)(2,1)} %get-tuple-element.35), channel_id=1, source_target_pairs={{0,32},{16,48},{32,0},{48,16},{1,33},{17,49},{33,1},{49,17},{2,34}... | collective-permute-start | bytes 1572872 | tf_op jit(solution)/shard_map/ppermute | solution.py:33
  14.4 21.8 %collective-permute-start.7 = (bf16[1024,256]{1,0:T(8,128)(2,1)}, bf16[1024,256]{1,0:T(8,128)(2,1)S(1)}, u32[]{:S(2)}, u32[]{:S(2)}) collective-permute-start(bf16[1024,256]{1,0:T(8,128)(2,1)} %get-tuple-element.36), channel_id=1, source_target_pairs={{0,48},{16,0},{32,16},{48,32},{1,49},{17,1},{33,17},{49,33},{2,50}... | collective-permute-start | bytes 1572872 | tf_op jit(solution)/shard_map/ppermute | solution.py:33
  15.9 6.3 %collective-permute-start.2 = (bf16[256,256]{1,0:T(8,128)(2,1)S(1)}, bf16[256,256]{1,0:T(8,128)(2,1)S(1)}, u32[]{:S(2)}, u32[]{:S(2)}) collective-permute-start(bf16[256,256]{1,0:T(8,128)(2,1)S(1)} %slice_bitcast_fusion.1), channel_id=1, source_target_pairs={{0,2},{2,4},{4,6},{6,0},{1,3},{3,5},{5,7},{7,1},{8,10},{10,12},{12... | collective-permute-start | bytes 393224 | tf_op jit(solution)/shard_map/ppermute | solution.py:33
  16.3 5.8 %collective-permute-start.4 = (bf16[256,256]{1,0:T(8,128)(2,1)S(1)}, bf16[256,256]{1,0:T(8,128)(2,1)S(1)}, u32[]{:S(2)}, u32[]{:S(2)}) collective-permute-start(bf16[256,256]{1,0:T(8,128)(2,1)S(1)} %slice_bitcast_fusion), channel_id=1, source_target_pairs={{0,6},{2,0},{4,2},{6,4},{1,7},{3,1},{5,3},{7,5},{8,14},{10,8},{12,... | collective-permute-start | bytes 393224 | tf_op jit(solution)/shard_map/ppermute | solution.py:33
  29.8 18.0 %copy-start.1 = (bf16[256,1024]{1,0:T(8,128)(2,1)S(1)}, bf16[256,1024]{1,0:T(8,128)(2,1)}, u32[]{:S(2)}) copy-start(bf16[256,1024]{1,0:T(8,128)(2,1)} %get-tuple-element.37.refs_4_) | copy-start | bytes 1572868
  37.0 21.5 %all-to-all-start = ((bf16[8,256,256]{2,1,0:T(8,128)(2,1)}), bf16[8,256,256]{2,1,0:T(8,128)(2,1)}, u32[]{:S(2)}, u32[]{:S(2)}) async-start(bf16[8,256,256]{2,1,0:T(8,128)(2,1)} %get-tuple-element.38), calls=%async_computation | async-start | bytes 2097152 | tf_op jit(solution)/shard_map/all_to_all | solution.py:312
  47.8 12.1 %collective-permute-start.8 = (bf16[256,1024]{1,0:T(8,128)(2,1)S(1)}, bf16[256,1024]{1,0:T(8,128)(2,1)S(1)}, u32[]{:S(2)}, u32[]{:S(2)}) collective-permute-start(bf16[256,1024]{1,0:T(8,128)(2,1)S(1)} %copy-done.1), channel_id=1, source_target_pairs={{0,16},{16,32},{32,48},{48,0},{1,17},{17,33},{33,49},{49,1},{2,18}... | collective-permute-start | bytes 1572872 | tf_op jit(solution)/shard_map/ppermute | solution.py:33
  48.2 11.7 %collective-permute-start.9 = (bf16[256,1024]{1,0:T(8,128)(2,1)S(1)}, bf16[256,1024]{1,0:T(8,128)(2,1)S(1)}, u32[]{:S(2)}, u32[]{:S(2)}) collective-permute-start(bf16[256,1024]{1,0:T(8,128)(2,1)S(1)} %copy-done.1), channel_id=1, source_target_pairs={{0,48},{16,0},{32,16},{48,32},{1,49},{17,1},{33,17},{49,33},{2,50}... | collective-permute-start | bytes 1572872 | tf_op jit(solution)/shard_map/ppermute | solution.py:33
  60.7 12.7 %collective-permute-start.10 = (bf16[256,512]{1,0:T(8,128)(2,1)}, bf16[256,512]{1,0:T(8,128)(2,1)S(1)}, u32[]{:S(2)}, u32[]{:S(2)}) collective-permute-start(bf16[256,512]{1,0:T(8,128)(2,1)} %slice.31), channel_id=1, source_target_pairs={{0,16},{16,32},{32,48},{48,0},{1,17},{17,33},{33,49},{49,1},{2,18}... | collective-permute-start | bytes 786440 | tf_op jit(solution)/shard_map/ppermute | solution.py:33
  63.3 10.1 %collective-permute-start.11 = (bf16[256,512]{1,0:T(8,128)(2,1)}, bf16[256,512]{1,0:T(8,128)(2,1)}, u32[]{:S(2)}, u32[]{:S(2)}) collective-permute-start(bf16[256,512]{1,0:T(8,128)(2,1)} %slice.32), channel_id=1, source_target_pairs={{0,48},{16,0},{32,16},{48,32},{1,49},{17,1},{33,17},{49,33},{2,50}... | collective-permute-start | bytes 786440 | tf_op jit(solution)/shard_map/ppermute | solution.py:33
  64.8 6.7 %collective-permute-start.12 = (bf16[256,256]{1,0:T(8,128)(2,1)S(1)}, bf16[256,256]{1,0:T(8,128)(2,1)}, u32[]{:S(2)}, u32[]{:S(2)}) collective-permute-start(bf16[256,256]{1,0:T(8,128)(2,1)S(1)} %reduce_sum.24.refs_9_), channel_id=1, source_target_pairs={{0,16},{16,32},{32,48},{48,0},{1,17},{17,33},{33,49},{49,1},{2,18}... | collective-permute-start | bytes 393224 | tf_op jit(solution)/shard_map/ppermute | solution.py:33
  65.4 8.0 %collective-permute-start.13 = (bf16[256,256]{1,0:T(8,128)(2,1)S(1)}, bf16[256,256]{1,0:T(8,128)(2,1)}, u32[]{:S(2)}, u32[]{:S(2)}) collective-permute-start(bf16[256,256]{1,0:T(8,128)(2,1)S(1)} %reduce_sum.24.refs_9_), channel_id=1, source_target_pairs={{0,32},{16,48},{32,0},{48,16},{1,33},{17,49},{33,1},{49,17},{2,34}... | collective-permute-start | bytes 393224 | tf_op jit(solution)/shard_map/ppermute | solution.py:33
  68.3 5.1 %collective-permute-start.14 = (bf16[256,256]{1,0:T(8,128)(2,1)S(1)}, bf16[256,256]{1,0:T(8,128)(2,1)}, u32[]{:S(2)}, u32[]{:S(2)}) collective-permute-start(bf16[256,256]{1,0:T(8,128)(2,1)S(1)} %reduce_sum.24.refs_9_), channel_id=1, source_target_pairs={{0,48},{16,0},{32,16},{48,32},{1,49},{17,1},{33,17},{49,33},{2,50}... | collective-permute-start | bytes 393224 | tf_op jit(solution)/shard_map/ppermute | solution.py:33
  74.5 2.8 %copy-start.4 = (bf16[1024,256]{1,0:T(8,128)(2,1)S(1)}, bf16[1024,256]{1,0:T(8,128)(2,1)}, u32[]{:S(2)}) copy-start(bf16[1024,256]{1,0:T(8,128)(2,1)} %copy-done.2) | copy-start | bytes 1572868
  77.2 3.1 %collective-permute-start.15 = (bf16[8,4,16,1280]{3,2,1,0:T(8,128)(2,1)S(1)}, bf16[8,4,16,1280]{3,2,1,0:T(8,128)(2,1)S(1)}, u32[]{:S(2)}, u32[]{:S(2)}) collective-permute-start(bf16[8,4,16,1280]{3,2,1,0:T(8,128)(2,1)S(1)} %weight_part.3), channel_id=1, source_target_pairs={{0,8},{8,0},{1,9},{9,1},{2,10},{10,2},{3,11},{11,3},{4,12},{12,4},... | collective-permute-start | bytes 3932168 | tf_op jit(solution)/shard_map/ppermute | solution.py:33
  81.7 23.3 %all-to-all-start.1 = ((bf16[8,64,1280]{2,1,0:T(8,128)(2,1)}), bf16[8,64,1280]{2,1,0:T(8,128)(2,1)S(1)}, u32[]{:S(2)}, u32[]{:S(2)}) async-start(bf16[8,64,1280]{2,1,0:T(8,128)(2,1)} %bitcast.16), calls=%async_computation.1 | async-start | bytes 2621440 | tf_op jit(solution)/shard_map/all_to_all | solution.py:325
  105.2 11.8 %collective-permute-start.16 = (bf16[16,1280]{1,0:T(8,128)(2,1)S(1)}, bf16[16,1280]{1,0:T(8,128)(2,1)S(1)}, u32[]{:S(2)}, u32[]{:S(2)}) collective-permute-start(bf16[16,1280]{1,0:T(8,128)(2,1)S(1)} %get-tuple-element.46), channel_id=1, source_target_pairs={{0,64},{64,128},{128,192},{192,0},{1,65},{65,129},{129,193},{193,1... | collective-permute-start | bytes 122888 | tf_op jit(solution)/shard_map/ppermute | solution.py:33
  108.6 8.5 %collective-permute-start.17 = (bf16[16,1280]{1,0:T(8,128)(2,1)S(1)}, bf16[16,1280]{1,0:T(8,128)(2,1)S(1)}, u32[]{:S(2)}, u32[]{:S(2)}) collective-permute-start(bf16[16,1280]{1,0:T(8,128)(2,1)S(1)} %get-tuple-element.48), channel_id=1, source_target_pairs={{0,128},{64,192},{128,0},{192,64},{1,129},{65,193},{129,1},{193,65... | collective-permute-start | bytes 122888 | tf_op jit(solution)/shard_map/ppermute | solution.py:33
  114.3 5.0 %collective-permute-start.18 = (bf16[16,1280]{1,0:T(8,128)(2,1)S(1)}, bf16[16,1280]{1,0:T(8,128)(2,1)S(1)}, u32[]{:S(2)}, u32[]{:S(2)}) collective-permute-start(bf16[16,1280]{1,0:T(8,128)(2,1)S(1)} %get-tuple-element.47), channel_id=1, source_target_pairs={{0,192},{64,0},{128,64},{192,128},{1,193},{65,1},{129,65},{193,129... | collective-permute-start | bytes 122888 | tf_op jit(solution)/shard_map/ppermute | solution.py:33
  (4 other events, 4.5 us)

commit v13 on v12

--- a/solution.py
+++ b/solution.py
@@ -206,6 +206,25 @@
     )(place[None], docs, q, do, *kv)
 
 
+def halves_kernel(left_ref, right_ref, first_ref, second_ref):
+    half = first_ref.shape[1]
+    first_ref[...] = left_ref[:, :half]
+    second_ref[...] = right_ref[:, half:]
+
+
+def halves(left, right):
+    half = jax.ShapeDtypeStruct((left.shape[0], left.shape[1] // 2), left.dtype)
+    return pl.pallas_call(
+        halves_kernel,
+        in_specs=[pl.BlockSpec(memory_space=pltpu.VMEM)] * 2,
+        out_specs=[pl.BlockSpec(memory_space=pltpu.VMEM)] * 2,
+        out_shape=[half, half],
+        compiler_params=pltpu.CompilerParams(vmem_limit_bytes=4 * 2**20),
+        cost_estimate=pl.CostEstimate(flops=2**36, bytes_accessed=2**21, transcendentals=0),
+        name="halves",
+    )(left, right)
+
+
 def split_kernel(info, *refs):
     half = len(refs) // 2
     for src, dst in zip(refs[:half], refs[half:]):
@@ -309,12 +328,12 @@
     dq, dkv = attention(q, do, [pair, before, *far, after], doc_ids, place, ny)
     dq, dkv, features = lax.optimization_barrier((dq, dkv, features))
     left, right = shifted(dq, "x", nx, 1), shifted(dq, "x", nx, -1)
+    first, second = halves(left, right)
     dkv = lax.all_to_all(dkv, CTX, 0, 0, tiled=True)
+    dkv, first, second = lax.optimization_barrier((dkv, first, second))
     dkv_own = jnp.sum(dkv.astype(F32), axis=0).astype(BF)
     narrow = [dkv_own] + [shifted(dkv_own, "x", nx, s) for s in range(1, nx)]
-    left, right, dkv_own = lax.optimization_barrier((left, right, dkv_own))
-    half = dq.shape[1] // 2
-    far = shifted(left[:, :half], "x", nx, 1), shifted(right[:, half:], "x", nx, -1)
+    far = shifted(first, "x", nx, 1), shifted(second, "x", nx, -1)
     wide = [dq, left, *far, right]
 
     theirs = weight_part(features, wide, narrow, 1 - my_core, z_hi, ctx)

time: 123 us -> 122 us (level)
  starting transfers between devices: 52.6 us -> 49.8 us
  waiting for transfers between devices: 41 us -> 43.8 us
    ppermute x19, starting transfers between devices: 36.2 us -> 34.4 us  [shifted(): return lax.ppermute(value, axis, pairs)]
    ppermute x19, waiting for transfers between devices: 15.8 us -> 17.5 us  [shifted(): return lax.ppermute(value, axis, pairs)]
    slice x2 -> x0, local copies, waits for them, and re-layouts: 1.47 us -> none  [the longest x1 0.74 us: local(): right[:, half:]]
    squeeze x2, local copies, waits for them, and re-layouts: 0.02 us -> 1.33 us  [local(): far = (shifted(before[0], 'y', ny, 1), shifted(after[1], 'y', ny, -1))]
    unnamed x14 -> x16, local copies, waits for them, and re-layouts: 4.49 us -> 4.86 us
  transfers between devices with their start and end apart: 21 -> 21, of which waited for: 8 -> 11; matrix products, arithmetic and copies ran while one was open for 2% -> 3% of each run, Pallas kernels for 10% -> 10%
where the time goes in v13:
time: 122 us; the launch traced here: 121 us
  starting transfers between devices  49.8 us (41%)
  waiting for transfers between devices  43.8 us (36%)
  Pallas kernels  14.4 us (12%)
  local copies, waits for them, and re-layouts  8.1 us (7%)
  other arithmetic  3.92 us (3%)
    ppermute x19, starting transfers between devices, shifted(): return lax.ppermute(value, axis, pairs)  34.4 us
    all_to_all x1, waiting for transfers between devices, local(): part = lax.all_to_all(part, CTX, 0, 0, tiled=True)  18 us
    ppermute x19, waiting for transfers between devices, shifted(): return lax.ppermute(value, axis, pairs)  17.5 us
    all_to_all x1, starting transfers between devices, local(): dkv = lax.all_to_all(dkv, CTX, 0, 0, tiled=True)  10.6 us
    all_to_all x1, waiting for transfers between devices, local(): dkv = lax.all_to_all(dkv, CTX, 0, 0, tiled=True)  8.38 us
    pallas_call x1, Pallas kernels, attention(): pl.pallas_call(functools.partial(attention_kernel, ny, per, DOCS, hd ** (...  6.73 us
    pallas_call x2, Pallas kernels, weight_part(): pl.pallas_call(functools.partial(weight_kernel, nx, z_hi), in_specs=[pl.B...  5.28 us
    unnamed x16, local copies, waits for them, and re-layouts  4.86 us
  transfers between devices with their start and end apart: 21, of which 11 were waited for; matrix products, arithmetic and copies ran while one was open for 3% of the time, Pallas kernels for 10%

profile of v13, /device:TPU:32, one launch (start us, length us, event | category | flops | bytes accessed | tf_op | source)
XLA Modules:
  0.0 120.8 jit_solution(647892999195961188)
XLA Ops:
  1.5 1.9 %collective-permute-start = (bf16[256,256]{1,0:T(8,128)(2,1)S(1)}, bf16[256,256]{1,0:T(8,128)(2,1)S(1)}, u32[]{:S(2)}, u32[]{:S(2)}) collective-permute-start(bf16[256,256]{1,0:T(8,128)(2,1)S(1)} %get-tuple-element.56), channel_id=1, source_target_pairs={{0,1},{1,0},{2,3},{3,2},{4,5},{5,4},{6,7},{7,6},{8,9},{9,8},{10,11... | collective-permute-start | bytes 393224 | tf_op jit(solution)/shard_map/ppermute | solution.py:33
  3.5 1.6 %copy-done = bf16[1,256,4096]{2,1,0:T(8,128)(2,1)S(1)} copy-done((bf16[1,256,4096]{2,1,0:T(8,128)(2,1)S(1)}, bf16[1,256,4096]{2,1,0:T(8,128)(2,1)}, u32[]{:S(2)}) %copy-start) | copy-done | bytes 2097176
  5.1 2.3 %split_features.1 = (bf16[1024,256]{1,0:T(8,128)(2,1)S(1)}, bf16[1024,256]{1,0:T(8,128)(2,1)}, bf16[1024,256]{1,0:T(8,128)(2,1)}, bf16[1024,256]{1,0:T(8,128)(2,1)}) custom-call(s32[1]{0:T(128)} %bitcast.6.info, bf16[256,4096]{1,0:T(8,128)(2,1)S(1)} %bitcast.32, bf16[256,4096]{1,0:T(8,128)(2,1)S(1)} %bitcast.33, bf16[256,4096]{1,0:T(8,128)(2,1)S(1)} %bitcast.34, ...), custom_call_target="tpu_custom_call" | custom-call | tf_op jit(solution)/shard_map/split_features/pallas_call | solution.py:241
  8.5 2.2 %collective-permute-start.3 = (bf16[2,256,256]{2,1,0:T(8,128)(2,1)S(1)}, bf16[2,256,256]{2,1,0:T(8,128)(2,1)S(1)}, u32[]{:S(2)}, u32[]{:S(2)}) collective-permute-start(bf16[2,256,256]{2,1,0:T(8,128)(2,1)S(1)} %pad_maximum_fusion.refs_0_), channel_id=1, source_target_pairs={{0,6},{2,0},{4,2},{6,4},{1,7},{3,1},{5,3},{7,5},{8,14},{10,8},{12,... | collective-permute-start | bytes 786440 | tf_op jit(solution)/shard_map/ppermute | solution.py:33
  11.7 2.7 %collective-permute-start.6 = (bf16[1024,256]{1,0:T(8,128)(2,1)}, bf16[1024,256]{1,0:T(8,128)(2,1)S(1)}, u32[]{:S(2)}, u32[]{:S(2)}) collective-permute-start(bf16[1024,256]{1,0:T(8,128)(2,1)} %get-tuple-element.37), channel_id=1, source_target_pairs={{0,32},{16,48},{32,0},{48,16},{1,33},{17,49},{33,1},{49,17},{2,34}... | collective-permute-start | bytes 1572872 | tf_op jit(solution)/shard_map/ppermute | solution.py:33
  17.6 2.9 %collective-permute-start.4 = (bf16[256,256]{1,0:T(8,128)(2,1)}, bf16[256,256]{1,0:T(8,128)(2,1)}, u32[]{:S(2)}, u32[]{:S(2)}) collective-permute-start(bf16[256,256]{1,0:T(8,128)(2,1)} %slice_bitcast_fusion), channel_id=1, source_target_pairs={{0,6},{2,0},{4,2},{6,4},{1,7},{3,1},{5,3},{7,5},{8,14},{10,8},{12,... | collective-permute-start | bytes 393224 | tf_op jit(solution)/shard_map/ppermute | solution.py:33
  20.4 2.5 %collective-permute-done.2.refs_2_ = bf16[256,256]{1,0:T(8,128)(2,1)S(1)} collective-permute-done((bf16[256,256]{1,0:T(8,128)(2,1)}, bf16[256,256]{1,0:T(8,128)(2,1)S(1)}, u32[]{:S(2)}, u32[]{:S(2)}) %collective-permute-start.2) | collective-permute-done | bytes 131104 | tf_op jit(solution)/shard_map/ppermute | solution.py:33
  23.3 6.7 %attention_backward.1 = (bf16[256,1024]{1,0:T(8,128)(2,1)}, bf16[8,256,256]{2,1,0:T(8,128)(2,1)}) custom-call(s32[1]{0:T(128)} %bitcast.info, s32[1,2048]{1,0:T(1,128)S(1)} %copy-done.7, bf16[256,1024]{1,0:T(8,128)(2,1)S(1)} %bitcast.37, bf16[256,1024]{1,0:T(8,128)(2,1)} %bitcast.43, bf16[2,256,256]{2,1,0:T(8,128)(2,1)S(1)} %pad_maximum_fusion.refs_0_, ...), custom_call_target="tpu_custom_call" | custom-call | flops 2147483648 | bytes 4194304 | tf_op jit(solution)/shard_map/attention_backward/pallas_call | solution.py:169
  30.0 6.2 %collective-permute-done.6.refs_2_ = bf16[1024,256]{1,0:T(8,128)(2,1)S(1)} collective-permute-done((bf16[1024,256]{1,0:T(8,128)(2,1)}, bf16[1024,256]{1,0:T(8,128)(2,1)S(1)}, u32[]{:S(2)}, u32[]{:S(2)}) %collective-permute-start.6) | collective-permute-done | bytes 524320 | tf_op jit(solution)/shard_map/ppermute | solution.py:33
  37.6 1.9 %collective-permute-start.9 = (bf16[256,1024]{1,0:T(8,128)(2,1)}, bf16[256,1024]{1,0:T(8,128)(2,1)S(1)}, u32[]{:S(2)}, u32[]{:S(2)}) collective-permute-start(bf16[256,1024]{1,0:T(8,128)(2,1)} %get-tuple-element.39.refs_4_), channel_id=1, source_target_pairs={{0,48},{16,0},{32,16},{48,32},{1,49},{17,1},{33,17},{49,33},{2,50}... | collective-permute-start | bytes 1572872 | tf_op jit(solution)/shard_map/ppermute | solution.py:33
  39.5 10.6 %all-to-all-start = ((bf16[8,256,256]{2,1,0:T(8,128)(2,1)}), bf16[8,256,256]{2,1,0:T(8,128)(2,1)}, u32[]{:S(2)}, u32[]{:S(2)}) async-start(bf16[8,256,256]{2,1,0:T(8,128)(2,1)} %get-tuple-element.40), calls=%async_computation | async-start | bytes 2097152 | tf_op jit(solution)/shard_map/all_to_all | solution.py:332
  53.1 8.4 %all-to-all-done = bf16[8,256,256]{2,1,0:T(8,128)(2,1)} async-done(((bf16[8,256,256]{2,1,0:T(8,128)(2,1)}), bf16[8,256,256]{2,1,0:T(8,128)(2,1)}, u32[]{:S(2)}, u32[]{:S(2)}) %all-to-all-start) | async-done | bytes 1048608 | tf_op jit(solution)/shard_map/all_to_all | solution.py:332
  61.5 3.2 %collective-permute-start.11 = (bf16[256,512]{1,0:T(8,128)(2,1)}, bf16[256,512]{1,0:T(8,128)(2,1)}, u32[]{:S(2)}, u32[]{:S(2)}) collective-permute-start(bf16[256,512]{1,0:T(8,128)(2,1)} %copy-done.5), channel_id=1, source_target_pairs={{0,48},{16,0},{32,16},{48,32},{1,49},{17,1},{33,17},{49,33},{2,50}... | collective-permute-start | bytes 786440 | tf_op jit(solution)/shard_map/ppermute | solution.py:33
  66.2 1.7 %collective-permute-start.13 = (bf16[256,256]{1,0:T(8,128)(2,1)S(1)}, bf16[256,256]{1,0:T(8,128)(2,1)}, u32[]{:S(2)}, u32[]{:S(2)}) collective-permute-start(bf16[256,256]{1,0:T(8,128)(2,1)S(1)} %reduce_sum.24.refs_9_), channel_id=1, source_target_pairs={{0,32},{16,48},{32,0},{48,16},{1,33},{17,49},{33,1},{49,17},{2,34}... | collective-permute-start | bytes 393224 | tf_op jit(solution)/shard_map/ppermute | solution.py:33
  67.9 1.5 %collective-permute-start.14 = (bf16[256,256]{1,0:T(8,128)(2,1)S(1)}, bf16[256,256]{1,0:T(8,128)(2,1)}, u32[]{:S(2)}, u32[]{:S(2)}) collective-permute-start(bf16[256,256]{1,0:T(8,128)(2,1)S(1)} %reduce_sum.24.refs_9_), channel_id=1, source_target_pairs={{0,48},{16,0},{32,16},{48,32},{1,49},{17,1},{33,17},{49,33},{2,50}... | collective-permute-start | bytes 393224 | tf_op jit(solution)/shard_map/ppermute | solution.py:33
  69.4 4.4 %collective-permute-done.12.refs_10_ = bf16[256,256]{1,0:T(8,128)(2,1)} collective-permute-done((bf16[256,256]{1,0:T(8,128)(2,1)S(1)}, bf16[256,256]{1,0:T(8,128)(2,1)}, u32[]{:S(2)}, u32[]{:S(2)}) %collective-permute-start.12) | collective-permute-done | bytes 131104 | tf_op jit(solution)/shard_map/ppermute | solution.py:33
  75.8 2.6 %weight_part.3 = bf16[8,4,16,1280]{3,2,1,0:T(8,128)(2,1)S(1)} custom-call(s32[1]{0:T(128)} %bitcast.15.info, bf16[1024,256]{1,0:T(8,128)(2,1)S(1)} %get-tuple-element.44.refs_0_, bf16[1024,256]{1,0:T(8,128)(2,1)S(1)} %collective-permute-done.5.refs_1_, bf16[1024,256]{1,0:T(8,128)(2,1)S(1)} %collective-permute-done.6.refs_2_, ...), custom_call_target="tpu_custom_call" | custom-call | flops 1342177280 | bytes 6291456 | tf_op jit(solution)/shard_map/weight_part/pallas_call | solution.py:293
  78.5 2.6 %weight_part.2 = bf16[8,4,16,1280]{3,2,1,0:T(8,128)(2,1)S(1)} custom-call(s32[1]{0:T(128)} %bitcast.14.info, bf16[1024,256]{1,0:T(8,128)(2,1)S(1)} %get-tuple-element.44.refs_0_, bf16[1024,256]{1,0:T(8,128)(2,1)S(1)} %collective-permute-done.5.refs_1_, bf16[1024,256]{1,0:T(8,128)(2,1)S(1)} %collective-permute-done.6.refs_2_, ...), custom_call_target="tpu_custom_call" | custom-call | flops 1342177280 | bytes 6291456 | tf_op jit(solution)/shard_map/weight_part/pallas_call | solution.py:293
  83.0 4.7 %all-to-all-start.1 = ((bf16[8,64,1280]{2,1,0:T(8,128)(2,1)}), bf16[8,64,1280]{2,1,0:T(8,128)(2,1)S(1)}, u32[]{:S(2)}, u32[]{:S(2)}) async-start(bf16[8,64,1280]{2,1,0:T(8,128)(2,1)} %bitcast.16), calls=%async_computation.1 | async-start | bytes 2621440 | tf_op jit(solution)/shard_map/all_to_all | solution.py:344
  87.7 18.0 %all-to-all-done.1 = bf16[8,64,1280]{2,1,0:T(8,128)(2,1)S(1)} async-done(((bf16[8,64,1280]{2,1,0:T(8,128)(2,1)}), bf16[8,64,1280]{2,1,0:T(8,128)(2,1)S(1)}, u32[]{:S(2)}, u32[]{:S(2)}) %all-to-all-start.1) | async-done | bytes 1310752 | tf_op jit(solution)/shard_map/all_to_all | solution.py:344
  105.9 3.8 %collective-permute-start.16 = (bf16[16,1280]{1,0:T(8,128)(2,1)S(1)}, bf16[16,1280]{1,0:T(8,128)(2,1)S(1)}, u32[]{:S(2)}, u32[]{:S(2)}) collective-permute-start(bf16[16,1280]{1,0:T(8,128)(2,1)S(1)} %get-tuple-element.50), channel_id=1, source_target_pairs={{0,64},{64,128},{128,192},{192,0},{1,65},{65,129},{129,193},{193,1... | collective-permute-start | bytes 122888 | tf_op jit(solution)/shard_map/ppermute | solution.py:33
  109.6 4.6 %collective-permute-start.17 = (bf16[16,1280]{1,0:T(8,128)(2,1)S(1)}, bf16[16,1280]{1,0:T(8,128)(2,1)S(1)}, u32[]{:S(2)}, u32[]{:S(2)}) collective-permute-start(bf16[16,1280]{1,0:T(8,128)(2,1)S(1)} %get-tuple-element.52), channel_id=1, source_target_pairs={{0,128},{64,192},{128,0},{192,64},{1,129},{65,193},{129,1},{193,65... | collective-permute-start | bytes 122888 | tf_op jit(solution)/shard_map/ppermute | solution.py:33
  114.2 2.6 %collective-permute-start.18 = (bf16[16,1280]{1,0:T(8,128)(2,1)S(1)}, bf16[16,1280]{1,0:T(8,128)(2,1)S(1)}, u32[]{:S(2)}, u32[]{:S(2)}) collective-permute-start(bf16[16,1280]{1,0:T(8,128)(2,1)S(1)} %get-tuple-element.51), channel_id=1, source_target_pairs={{0,192},{64,0},{128,64},{192,128},{1,193},{65,1},{129,65},{193,129... | collective-permute-start | bytes 122888 | tf_op jit(solution)/shard_map/ppermute | solution.py:33
  117.7 1.8 %collective-permute-done.18 = bf16[16,1280]{1,0:T(8,128)(2,1)S(1)} collective-permute-done((bf16[16,1280]{1,0:T(8,128)(2,1)S(1)}, bf16[16,1280]{1,0:T(8,128)(2,1)S(1)}, u32[]{:S(2)}, u32[]{:S(2)}) %collective-permute-start.18) | collective-permute-done | bytes 40992 | tf_op jit(solution)/shard_map/ppermute | solution.py:33
  (51 shorter events, 18.5 us)
Async XLA Ops:
  1.5 5.9 %collective-permute-start = (bf16[256,256]{1,0:T(8,128)(2,1)S(1)}, bf16[256,256]{1,0:T(8,128)(2,1)S(1)}, u32[]{:S(2)}, u32[]{:S(2)}) collective-permute-start(bf16[256,256]{1,0:T(8,128)(2,1)S(1)} %get-tuple-element.56), channel_id=1, source_target_pairs={{0,1},{1,0},{2,3},{3,2},{4,5},{5,4},{6,7},{7,6},{8,9},{9,8},{10,11... | collective-permute-start | bytes 393224 | tf_op jit(solution)/shard_map/ppermute | solution.py:33
  5.0 18.2 %copy-start.4 = (bf16[1,256,1024]{2,1,0:T(8,128)(2,1)S(1)}, bf16[1,256,1024]{2,1,0:T(8,128)(2,1)}, u32[]{:S(2)}) copy-start(bf16[1,256,1024]{2,1,0:T(8,128)(2,1)} %param.7) | copy-start | bytes 1572868
  5.1 18.2 %copy-start.7 = (s32[1,2048]{1,0:T(1,128)S(1)}, s32[1,2048]{1,0:T(1,128)}, u32[]{:S(2)}) copy-start(s32[1,2048]{1,0:T(1,128)} %docs_ref.1) | copy-start | bytes 24580
  7.4 8.4 %collective-permute-start.1 = (bf16[2,256,256]{2,1,0:T(8,128)(2,1)S(1)}, bf16[2,256,256]{2,1,0:T(8,128)(2,1)S(1)}, u32[]{:S(2)}, u32[]{:S(2)}) collective-permute-start(bf16[2,256,256]{2,1,0:T(8,128)(2,1)S(1)} %pad_maximum_fusion.refs_0_), channel_id=1, source_target_pairs={{0,2},{2,4},{4,6},{6,0},{1,3},{3,5},{5,7},{7,1},{8,10},{10,12},{12... | collective-permute-start | bytes 786440 | tf_op jit(solution)/shard_map/ppermute | solution.py:33
  8.5 8.4 %collective-permute-start.3 = (bf16[2,256,256]{2,1,0:T(8,128)(2,1)S(1)}, bf16[2,256,256]{2,1,0:T(8,128)(2,1)S(1)}, u32[]{:S(2)}, u32[]{:S(2)}) collective-permute-start(bf16[2,256,256]{2,1,0:T(8,128)(2,1)S(1)} %pad_maximum_fusion.refs_0_), channel_id=1, source_target_pairs={{0,6},{2,0},{4,2},{6,4},{1,7},{3,1},{5,3},{7,5},{8,14},{10,8},{12,... | collective-permute-start | bytes 786440 | tf_op jit(solution)/shard_map/ppermute | solution.py:33
  10.7 19.3 %collective-permute-start.5 = (bf16[1024,256]{1,0:T(8,128)(2,1)}, bf16[1024,256]{1,0:T(8,128)(2,1)S(1)}, u32[]{:S(2)}, u32[]{:S(2)}) collective-permute-start(bf16[1024,256]{1,0:T(8,128)(2,1)} %get-tuple-element.36), channel_id=1, source_target_pairs={{0,16},{16,32},{32,48},{48,0},{1,17},{17,33},{33,49},{49,1},{2,18}... | collective-permute-start | bytes 1572872 | tf_op jit(solution)/shard_map/ppermute | solution.py:33
  11.7 24.5 %collective-permute-start.6 = (bf16[1024,256]{1,0:T(8,128)(2,1)}, bf16[1024,256]{1,0:T(8,128)(2,1)S(1)}, u32[]{:S(2)}, u32[]{:S(2)}) collective-permute-start(bf16[1024,256]{1,0:T(8,128)(2,1)} %get-tuple-element.37), channel_id=1, source_target_pairs={{0,32},{16,48},{32,0},{48,16},{1,33},{17,49},{33,1},{49,17},{2,34}... | collective-permute-start | bytes 1572872 | tf_op jit(solution)/shard_map/ppermute | solution.py:33
  14.4 21.8 %collective-permute-start.7 = (bf16[1024,256]{1,0:T(8,128)(2,1)}, bf16[1024,256]{1,0:T(8,128)(2,1)S(1)}, u32[]{:S(2)}, u32[]{:S(2)}) collective-permute-start(bf16[1024,256]{1,0:T(8,128)(2,1)} %get-tuple-element.38), channel_id=1, source_target_pairs={{0,48},{16,0},{32,16},{48,32},{1,49},{17,1},{33,17},{49,33},{2,50}... | collective-permute-start | bytes 1572872 | tf_op jit(solution)/shard_map/ppermute | solution.py:33
  16.5 6.4 %collective-permute-start.2 = (bf16[256,256]{1,0:T(8,128)(2,1)}, bf16[256,256]{1,0:T(8,128)(2,1)S(1)}, u32[]{:S(2)}, u32[]{:S(2)}) collective-permute-start(bf16[256,256]{1,0:T(8,128)(2,1)} %slice_bitcast_fusion.1), channel_id=1, source_target_pairs={{0,2},{2,4},{4,6},{6,0},{1,3},{3,5},{5,7},{7,1},{8,10},{10,12},{12... | collective-permute-start | bytes 393224 | tf_op jit(solution)/shard_map/ppermute | solution.py:33
  17.6 5.7 %collective-permute-start.4 = (bf16[256,256]{1,0:T(8,128)(2,1)}, bf16[256,256]{1,0:T(8,128)(2,1)}, u32[]{:S(2)}, u32[]{:S(2)}) collective-permute-start(bf16[256,256]{1,0:T(8,128)(2,1)} %slice_bitcast_fusion), channel_id=1, source_target_pairs={{0,6},{2,0},{4,2},{6,4},{1,7},{3,1},{5,3},{7,5},{8,14},{10,8},{12,... | collective-permute-start | bytes 393224 | tf_op jit(solution)/shard_map/ppermute | solution.py:33
  36.2 14.6 %collective-permute-start.8 = (bf16[256,1024]{1,0:T(8,128)(2,1)}, bf16[256,1024]{1,0:T(8,128)(2,1)S(1)}, u32[]{:S(2)}, u32[]{:S(2)}) collective-permute-start(bf16[256,1024]{1,0:T(8,128)(2,1)} %get-tuple-element.39.refs_4_), channel_id=1, source_target_pairs={{0,16},{16,32},{32,48},{48,0},{1,17},{17,33},{33,49},{49,1},{2,18}... | collective-permute-start | bytes 1572872 | tf_op jit(solution)/shard_map/ppermute | solution.py:33
  37.6 13.2 %collective-permute-start.9 = (bf16[256,1024]{1,0:T(8,128)(2,1)}, bf16[256,1024]{1,0:T(8,128)(2,1)S(1)}, u32[]{:S(2)}, u32[]{:S(2)}) collective-permute-start(bf16[256,1024]{1,0:T(8,128)(2,1)} %get-tuple-element.39.refs_4_), channel_id=1, source_target_pairs={{0,48},{16,0},{32,16},{48,32},{1,49},{17,1},{33,17},{49,33},{2,50}... | collective-permute-start | bytes 1572872 | tf_op jit(solution)/shard_map/ppermute | solution.py:33
  39.5 22.0 %all-to-all-start = ((bf16[8,256,256]{2,1,0:T(8,128)(2,1)}), bf16[8,256,256]{2,1,0:T(8,128)(2,1)}, u32[]{:S(2)}, u32[]{:S(2)}) async-start(bf16[8,256,256]{2,1,0:T(8,128)(2,1)} %get-tuple-element.40), calls=%async_computation | async-start | bytes 2097152 | tf_op jit(solution)/shard_map/all_to_all | solution.py:332
  53.1 21.7 %copy-start.1 = (bf16[256,1024]{1,0:T(8,128)(2,1)S(1)}, bf16[256,1024]{1,0:T(8,128)(2,1)}, u32[]{:S(2)}) copy-start(bf16[256,1024]{1,0:T(8,128)(2,1)} %get-tuple-element.39.refs_4_) | copy-start | bytes 1572868
  61.4 13.3 %collective-permute-start.10 = (bf16[256,512]{1,0:T(8,128)(2,1)}, bf16[256,512]{1,0:T(8,128)(2,1)S(1)}, u32[]{:S(2)}, u32[]{:S(2)}) collective-permute-start(bf16[256,512]{1,0:T(8,128)(2,1)} %copy-done.6), channel_id=1, source_target_pairs={{0,16},{16,32},{32,48},{48,0},{1,17},{17,33},{33,49},{49,1},{2,18}... | collective-permute-start | bytes 786440 | tf_op jit(solution)/shard_map/ppermute | solution.py:33
  61.5 13.2 %collective-permute-start.11 = (bf16[256,512]{1,0:T(8,128)(2,1)}, bf16[256,512]{1,0:T(8,128)(2,1)}, u32[]{:S(2)}, u32[]{:S(2)}) collective-permute-start(bf16[256,512]{1,0:T(8,128)(2,1)} %copy-done.5), channel_id=1, source_target_pairs={{0,48},{16,0},{32,16},{48,32},{1,49},{17,1},{33,17},{49,33},{2,50}... | collective-permute-start | bytes 786440 | tf_op jit(solution)/shard_map/ppermute | solution.py:33
  66.1 7.8 %collective-permute-start.12 = (bf16[256,256]{1,0:T(8,128)(2,1)S(1)}, bf16[256,256]{1,0:T(8,128)(2,1)}, u32[]{:S(2)}, u32[]{:S(2)}) collective-permute-start(bf16[256,256]{1,0:T(8,128)(2,1)S(1)} %reduce_sum.24.refs_9_), channel_id=1, source_target_pairs={{0,16},{16,32},{32,48},{48,0},{1,17},{17,33},{33,49},{49,1},{2,18}... | collective-permute-start | bytes 393224 | tf_op jit(solution)/shard_map/ppermute | solution.py:33
  66.2 7.7 %collective-permute-start.13 = (bf16[256,256]{1,0:T(8,128)(2,1)S(1)}, bf16[256,256]{1,0:T(8,128)(2,1)}, u32[]{:S(2)}, u32[]{:S(2)}) collective-permute-start(bf16[256,256]{1,0:T(8,128)(2,1)S(1)} %reduce_sum.24.refs_9_), channel_id=1, source_target_pairs={{0,32},{16,48},{32,0},{48,16},{1,33},{17,49},{33,1},{49,17},{2,34}... | collective-permute-start | bytes 393224 | tf_op jit(solution)/shard_map/ppermute | solution.py:33
  67.9 6.8 %collective-permute-start.14 = (bf16[256,256]{1,0:T(8,128)(2,1)S(1)}, bf16[256,256]{1,0:T(8,128)(2,1)}, u32[]{:S(2)}, u32[]{:S(2)}) collective-permute-start(bf16[256,256]{1,0:T(8,128)(2,1)S(1)} %reduce_sum.24.refs_9_), channel_id=1, source_target_pairs={{0,48},{16,0},{32,16},{48,32},{1,49},{17,1},{33,17},{49,33},{2,50}... | collective-permute-start | bytes 393224 | tf_op jit(solution)/shard_map/ppermute | solution.py:33
  78.4 3.1 %collective-permute-start.15 = (bf16[8,4,16,1280]{3,2,1,0:T(8,128)(2,1)S(1)}, bf16[8,4,16,1280]{3,2,1,0:T(8,128)(2,1)S(1)}, u32[]{:S(2)}, u32[]{:S(2)}) collective-permute-start(bf16[8,4,16,1280]{3,2,1,0:T(8,128)(2,1)S(1)} %weight_part.3), channel_id=1, source_target_pairs={{0,8},{8,0},{1,9},{9,1},{2,10},{10,2},{3,11},{11,3},{4,12},{12,4},... | collective-permute-start | bytes 3932168 | tf_op jit(solution)/shard_map/ppermute | solution.py:33
  83.0 22.7 %all-to-all-start.1 = ((bf16[8,64,1280]{2,1,0:T(8,128)(2,1)}), bf16[8,64,1280]{2,1,0:T(8,128)(2,1)S(1)}, u32[]{:S(2)}, u32[]{:S(2)}) async-start(bf16[8,64,1280]{2,1,0:T(8,128)(2,1)} %bitcast.16), calls=%async_computation.1 | async-start | bytes 2621440 | tf_op jit(solution)/shard_map/all_to_all | solution.py:344
  105.9 11.6 %collective-permute-start.16 = (bf16[16,1280]{1,0:T(8,128)(2,1)S(1)}, bf16[16,1280]{1,0:T(8,128)(2,1)S(1)}, u32[]{:S(2)}, u32[]{:S(2)}) collective-permute-start(bf16[16,1280]{1,0:T(8,128)(2,1)S(1)} %get-tuple-element.50), channel_id=1, source_target_pairs={{0,64},{64,128},{128,192},{192,0},{1,65},{65,129},{129,193},{193,1... | collective-permute-start | bytes 122888 | tf_op jit(solution)/shard_map/ppermute | solution.py:33
  109.6 8.1 %collective-permute-start.17 = (bf16[16,1280]{1,0:T(8,128)(2,1)S(1)}, bf16[16,1280]{1,0:T(8,128)(2,1)S(1)}, u32[]{:S(2)}, u32[]{:S(2)}) collective-permute-start(bf16[16,1280]{1,0:T(8,128)(2,1)S(1)} %get-tuple-element.52), channel_id=1, source_target_pairs={{0,128},{64,192},{128,0},{192,64},{1,129},{65,193},{129,1},{193,65... | collective-permute-start | bytes 122888 | tf_op jit(solution)/shard_map/ppermute | solution.py:33
  114.2 5.2 %collective-permute-start.18 = (bf16[16,1280]{1,0:T(8,128)(2,1)S(1)}, bf16[16,1280]{1,0:T(8,128)(2,1)S(1)}, u32[]{:S(2)}, u32[]{:S(2)}) collective-permute-start(bf16[16,1280]{1,0:T(8,128)(2,1)S(1)} %get-tuple-element.51), channel_id=1, source_target_pairs={{0,192},{64,0},{128,64},{192,128},{1,193},{65,1},{129,65},{193,129... | collective-permute-start | bytes 122888 | tf_op jit(solution)/shard_map/ppermute | solution.py:33
  (5 other events, 4.9 us)

commit v14 on v13

--- a/solution.py
+++ b/solution.py
@@ -330,9 +330,9 @@
     left, right = shifted(dq, "x", nx, 1), shifted(dq, "x", nx, -1)
     first, second = halves(left, right)
     dkv = lax.all_to_all(dkv, CTX, 0, 0, tiled=True)
-    dkv, first, second = lax.optimization_barrier((dkv, first, second))
     dkv_own = jnp.sum(dkv.astype(F32), axis=0).astype(BF)
     narrow = [dkv_own] + [shifted(dkv_own, "x", nx, s) for s in range(1, nx)]
+    dkv_own, first, second = lax.optimization_barrier((dkv_own, first, second))
     far = shifted(first, "x", nx, 1), shifted(second, "x", nx, -1)
     wide = [dq, left, *far, right]
 
@@ -344,20 +344,23 @@
     part = lax.all_to_all(part, CTX, 0, 0, tiled=True)
     part = jnp.sum(part.astype(F32), axis=0).astype(BF).reshape(z_hi, -1, n)
     my_zh = lax.axis_index("zh")
-    weight = 0.0
+    pieces = []
     for step in range(z_hi):
         piece = lax.dynamic_index_in_dim(part, (my_zh + step) % z_hi, 0, keepdims=False)
-        weight = weight + (shifted(piece, "zh", z_hi, step) if step else piece).astype(F32)
-    tokens = rows * ctx * nx * nc * z_hi
-    weight = weight * (1.0 / math.sqrt(tokens))
+        pieces.append(shifted(piece, "zh", z_hi, step) if step else piece)
+    factor = 1.0 / math.sqrt(rows * ctx * nx * nc * z_hi)
     width = q.shape[1]
+
+    def weight(first, last):
+        return sum(piece[:, first:last].astype(F32) for piece in pieces) * factor
+
     return (
         dq[None],
         dkv_own[None, :, :hd],
         dkv_own[None, :, hd:],
-        weight[:, :width],
-        weight[:, width : width + hd],
-        weight[:, width + hd :],
+        weight(0, width),
+        weight(width, width + hd),
+        weight(width + hd, n),
     )
 
 

time: 122 us -> 123 us (level)
  other arithmetic: 3.92 us -> 5.16 us
    slice x2 -> x0, local copies, waits for them, and re-layouts: 1.24 us -> none  [the longest x1 0.63 us: local(): weight[:, :width]]
    mul x1 -> x2, other arithmetic: 0.03 us -> 1.26 us  [weight(): return sum((piece[:, first:last].astype(F32) for piece in pieces)) * factor]
  transfers between devices with their start and end apart: 21 -> 21, of which waited for: 11 -> 11; matrix products, arithmetic and copies ran while one was open for 3% -> 2% of each run, Pallas kernels for 10% -> 10%
where the time goes in v14:
time: 123 us; the launch traced here: 121 us
  starting transfers between devices  50 us (41%)
  waiting for transfers between devices  43.8 us (36%)
  Pallas kernels  14.4 us (12%)
  local copies, waits for them, and re-layouts  6.87 us (6%)
  other arithmetic  5.16 us (4%)
    ppermute x19, starting transfers between devices, shifted(): return lax.ppermute(value, axis, pairs)  33.6 us
    all_to_all x1, waiting for transfers between devices, local(): part = lax.all_to_all(part, CTX, 0, 0, tiled=True)  18 us
    ppermute x19, waiting for transfers between devices, shifted(): return lax.ppermute(value, axis, pairs)  17.5 us
    all_to_all x1, starting transfers between devices, local(): dkv = lax.all_to_all(dkv, CTX, 0, 0, tiled=True)  11.3 us
    all_to_all x1, waiting for transfers between devices, local(): dkv = lax.all_to_all(dkv, CTX, 0, 0, tiled=True)  8.38 us
    pallas_call x1, Pallas kernels, attention(): pl.pallas_call(functools.partial(attention_kernel, ny, per, DOCS, hd ** (...  6.73 us
    pallas_call x2, Pallas kernels, weight_part(): pl.pallas_call(functools.partial(weight_kernel, nx, z_hi), in_specs=[pl.B...  5.28 us
    all_to_all x1, starting transfers between devices, local(): part = lax.all_to_all(part, CTX, 0, 0, tiled=True)  5.15 us
  transfers between devices with their start and end apart: 21, of which 11 were waited for; matrix products, arithmetic and copies ran while one was open for 2% of the time, Pallas kernels for 10%

profile of v14, /device:TPU:32, one launch (start us, length us, event | category | flops | bytes accessed | tf_op | source)
XLA Modules:
  0.0 121.0 jit_solution(5755148252988989421)
XLA Ops:
  1.5 1.9 %collective-permute-start = (bf16[256,256]{1,0:T(8,128)(2,1)S(1)}, bf16[256,256]{1,0:T(8,128)(2,1)S(1)}, u32[]{:S(2)}, u32[]{:S(2)}) collective-permute-start(bf16[256,256]{1,0:T(8,128)(2,1)S(1)} %get-tuple-element.59), channel_id=1, source_target_pairs={{0,1},{1,0},{2,3},{3,2},{4,5},{5,4},{6,7},{7,6},{8,9},{9,8},{10,11... | collective-permute-start | bytes 393224 | tf_op jit(solution)/shard_map/ppermute | solution.py:33
  3.5 1.6 %copy-done = bf16[1,256,4096]{2,1,0:T(8,128)(2,1)S(1)} copy-done((bf16[1,256,4096]{2,1,0:T(8,128)(2,1)S(1)}, bf16[1,256,4096]{2,1,0:T(8,128)(2,1)}, u32[]{:S(2)}) %copy-start) | copy-done | bytes 2097176
  5.1 2.3 %split_features.1 = (bf16[1024,256]{1,0:T(8,128)(2,1)S(1)}, bf16[1024,256]{1,0:T(8,128)(2,1)}, bf16[1024,256]{1,0:T(8,128)(2,1)}, bf16[1024,256]{1,0:T(8,128)(2,1)}) custom-call(s32[1]{0:T(128)} %bitcast.6.info, bf16[256,4096]{1,0:T(8,128)(2,1)S(1)} %bitcast.31, bf16[256,4096]{1,0:T(8,128)(2,1)S(1)} %bitcast.32, bf16[256,4096]{1,0:T(8,128)(2,1)S(1)} %bitcast.33, ...), custom_call_target="tpu_custom_call" | custom-call | tf_op jit(solution)/shard_map/split_features/pallas_call | solution.py:241
  8.5 2.2 %collective-permute-start.3 = (bf16[2,256,256]{2,1,0:T(8,128)(2,1)S(1)}, bf16[2,256,256]{2,1,0:T(8,128)(2,1)S(1)}, u32[]{:S(2)}, u32[]{:S(2)}) collective-permute-start(bf16[2,256,256]{2,1,0:T(8,128)(2,1)S(1)} %pad_maximum_fusion.refs_0_), channel_id=1, source_target_pairs={{0,6},{2,0},{4,2},{6,4},{1,7},{3,1},{5,3},{7,5},{8,14},{10,8},{12,... | collective-permute-start | bytes 786440 | tf_op jit(solution)/shard_map/ppermute | solution.py:33
  11.7 2.7 %collective-permute-start.6 = (bf16[1024,256]{1,0:T(8,128)(2,1)}, bf16[1024,256]{1,0:T(8,128)(2,1)S(1)}, u32[]{:S(2)}, u32[]{:S(2)}) collective-permute-start(bf16[1024,256]{1,0:T(8,128)(2,1)} %get-tuple-element.37), channel_id=1, source_target_pairs={{0,32},{16,48},{32,0},{48,16},{1,33},{17,49},{33,1},{49,17},{2,34}... | collective-permute-start | bytes 1572872 | tf_op jit(solution)/shard_map/ppermute | solution.py:33
  17.6 2.9 %collective-permute-start.4 = (bf16[256,256]{1,0:T(8,128)(2,1)}, bf16[256,256]{1,0:T(8,128)(2,1)}, u32[]{:S(2)}, u32[]{:S(2)}) collective-permute-start(bf16[256,256]{1,0:T(8,128)(2,1)} %slice_bitcast_fusion), channel_id=1, source_target_pairs={{0,6},{2,0},{4,2},{6,4},{1,7},{3,1},{5,3},{7,5},{8,14},{10,8},{12,... | collective-permute-start | bytes 393224 | tf_op jit(solution)/shard_map/ppermute | solution.py:33
  20.4 2.5 %collective-permute-done.2.refs_2_ = bf16[256,256]{1,0:T(8,128)(2,1)S(1)} collective-permute-done((bf16[256,256]{1,0:T(8,128)(2,1)}, bf16[256,256]{1,0:T(8,128)(2,1)S(1)}, u32[]{:S(2)}, u32[]{:S(2)}) %collective-permute-start.2) | collective-permute-done | bytes 131104 | tf_op jit(solution)/shard_map/ppermute | solution.py:33
  23.3 6.7 %attention_backward.1 = (bf16[256,1024]{1,0:T(8,128)(2,1)}, bf16[8,256,256]{2,1,0:T(8,128)(2,1)}) custom-call(s32[1]{0:T(128)} %bitcast.info, s32[1,2048]{1,0:T(1,128)S(1)} %copy-done.7, bf16[256,1024]{1,0:T(8,128)(2,1)S(1)} %bitcast.36, bf16[256,1024]{1,0:T(8,128)(2,1)} %bitcast.41, bf16[2,256,256]{2,1,0:T(8,128)(2,1)S(1)} %pad_maximum_fusion.refs_0_, ...), custom_call_target="tpu_custom_call" | custom-call | flops 2147483648 | bytes 4194304 | tf_op jit(solution)/shard_map/attention_backward/pallas_call | solution.py:169
  30.0 6.2 %collective-permute-done.6.refs_2_ = bf16[1024,256]{1,0:T(8,128)(2,1)S(1)} collective-permute-done((bf16[1024,256]{1,0:T(8,128)(2,1)}, bf16[1024,256]{1,0:T(8,128)(2,1)S(1)}, u32[]{:S(2)}, u32[]{:S(2)}) %collective-permute-start.6) | collective-permute-done | bytes 524320 | tf_op jit(solution)/shard_map/ppermute | solution.py:33
  37.6 1.9 %collective-permute-start.9 = (bf16[256,1024]{1,0:T(8,128)(2,1)}, bf16[256,1024]{1,0:T(8,128)(2,1)S(1)}, u32[]{:S(2)}, u32[]{:S(2)}) collective-permute-start(bf16[256,1024]{1,0:T(8,128)(2,1)} %get-tuple-element.39.refs_4_), channel_id=1, source_target_pairs={{0,48},{16,0},{32,16},{48,32},{1,49},{17,1},{33,17},{49,33},{2,50}... | collective-permute-start | bytes 1572872 | tf_op jit(solution)/shard_map/ppermute | solution.py:33
  39.5 11.3 %all-to-all-start = ((bf16[8,256,256]{2,1,0:T(8,128)(2,1)}), bf16[8,256,256]{2,1,0:T(8,128)(2,1)}, u32[]{:S(2)}, u32[]{:S(2)}) async-start(bf16[8,256,256]{2,1,0:T(8,128)(2,1)} %get-tuple-element.40), calls=%async_computation | async-start | bytes 2097152 | tf_op jit(solution)/shard_map/all_to_all | solution.py:332
  53.1 8.4 %all-to-all-done = bf16[8,256,256]{2,1,0:T(8,128)(2,1)} async-done(((bf16[8,256,256]{2,1,0:T(8,128)(2,1)}), bf16[8,256,256]{2,1,0:T(8,128)(2,1)}, u32[]{:S(2)}, u32[]{:S(2)}) %all-to-all-start) | async-done | bytes 1048608 | tf_op jit(solution)/shard_map/all_to_all | solution.py:332
  63.1 3.2 %collective-permute-start.11 = (bf16[256,512]{1,0:T(8,128)(2,1)}, bf16[256,512]{1,0:T(8,128)(2,1)}, u32[]{:S(2)}, u32[]{:S(2)}) collective-permute-start(bf16[256,512]{1,0:T(8,128)(2,1)} %copy-done.5), channel_id=1, source_target_pairs={{0,48},{16,0},{32,16},{48,32},{1,49},{17,1},{33,17},{49,33},{2,50}... | collective-permute-start | bytes 786440 | tf_op jit(solution)/shard_map/ppermute | solution.py:33
  66.3 1.5 %collective-permute-start.13 = (bf16[256,256]{1,0:T(8,128)(2,1)S(1)}, bf16[256,256]{1,0:T(8,128)(2,1)}, u32[]{:S(2)}, u32[]{:S(2)}) collective-permute-start(bf16[256,256]{1,0:T(8,128)(2,1)S(1)} %reduce_sum.24.refs_9_), channel_id=1, source_target_pairs={{0,32},{16,48},{32,0},{48,16},{1,33},{17,49},{33,1},{49,17},{2,34}... | collective-permute-start | bytes 393224 | tf_op jit(solution)/shard_map/ppermute | solution.py:33
  67.8 1.8 %collective-permute-start.14 = (bf16[256,256]{1,0:T(8,128)(2,1)S(1)}, bf16[256,256]{1,0:T(8,128)(2,1)}, u32[]{:S(2)}, u32[]{:S(2)}) collective-permute-start(bf16[256,256]{1,0:T(8,128)(2,1)S(1)} %reduce_sum.24.refs_9_), channel_id=1, source_target_pairs={{0,48},{16,0},{32,16},{48,32},{1,49},{17,1},{33,17},{49,33},{2,50}... | collective-permute-start | bytes 393224 | tf_op jit(solution)/shard_map/ppermute | solution.py:33
  69.6 4.4 %collective-permute-done.12.refs_10_ = bf16[256,256]{1,0:T(8,128)(2,1)} collective-permute-done((bf16[256,256]{1,0:T(8,128)(2,1)S(1)}, bf16[256,256]{1,0:T(8,128)(2,1)}, u32[]{:S(2)}, u32[]{:S(2)}) %collective-permute-start.12) | collective-permute-done | bytes 131104 | tf_op jit(solution)/shard_map/ppermute | solution.py:33
  76.0 2.6 %weight_part.3 = bf16[8,4,16,1280]{3,2,1,0:T(8,128)(2,1)S(1)} custom-call(s32[1]{0:T(128)} %bitcast.15.info, bf16[1024,256]{1,0:T(8,128)(2,1)S(1)} %get-tuple-element.44.refs_0_, bf16[1024,256]{1,0:T(8,128)(2,1)S(1)} %collective-permute-done.5.refs_1_, bf16[1024,256]{1,0:T(8,128)(2,1)S(1)} %collective-permute-done.6.refs_2_, ...), custom_call_target="tpu_custom_call" | custom-call | flops 1342177280 | bytes 6291456 | tf_op jit(solution)/shard_map/weight_part/pallas_call | solution.py:293
  78.7 2.6 %weight_part.2 = bf16[8,4,16,1280]{3,2,1,0:T(8,128)(2,1)S(1)} custom-call(s32[1]{0:T(128)} %bitcast.14.info, bf16[1024,256]{1,0:T(8,128)(2,1)S(1)} %get-tuple-element.44.refs_0_, bf16[1024,256]{1,0:T(8,128)(2,1)S(1)} %collective-permute-done.5.refs_1_, bf16[1024,256]{1,0:T(8,128)(2,1)S(1)} %collective-permute-done.6.refs_2_, ...), custom_call_target="tpu_custom_call" | custom-call | flops 1342177280 | bytes 6291456 | tf_op jit(solution)/shard_map/weight_part/pallas_call | solution.py:293
  83.1 5.2 %all-to-all-start.1 = ((bf16[8,64,1280]{2,1,0:T(8,128)(2,1)}), bf16[8,64,1280]{2,1,0:T(8,128)(2,1)S(1)}, u32[]{:S(2)}, u32[]{:S(2)}) async-start(bf16[8,64,1280]{2,1,0:T(8,128)(2,1)} %bitcast.16), calls=%async_computation.1 | async-start | bytes 2621440 | tf_op jit(solution)/shard_map/all_to_all | solution.py:344
  88.3 18.0 %all-to-all-done.1 = bf16[8,64,1280]{2,1,0:T(8,128)(2,1)S(1)} async-done(((bf16[8,64,1280]{2,1,0:T(8,128)(2,1)}), bf16[8,64,1280]{2,1,0:T(8,128)(2,1)S(1)}, u32[]{:S(2)}, u32[]{:S(2)}) %all-to-all-start.1) | async-done | bytes 1310752 | tf_op jit(solution)/shard_map/all_to_all | solution.py:344
  106.5 3.3 %collective-permute-start.16 = (bf16[16,1280]{1,0:T(8,128)(2,1)S(1)}, bf16[16,1280]{1,0:T(8,128)(2,1)S(1)}, u32[]{:S(2)}, u32[]{:S(2)}) collective-permute-start(bf16[16,1280]{1,0:T(8,128)(2,1)S(1)} %get-tuple-element.55), channel_id=1, source_target_pairs={{0,64},{64,128},{128,192},{192,0},{1,65},{65,129},{129,193},{193,1... | collective-permute-start | bytes 122888 | tf_op jit(solution)/shard_map/ppermute | solution.py:33
  109.8 4.5 %collective-permute-start.17 = (bf16[16,1280]{1,0:T(8,128)(2,1)S(1)}, bf16[16,1280]{1,0:T(8,128)(2,1)S(1)}, u32[]{:S(2)}, u32[]{:S(2)}) collective-permute-start(bf16[16,1280]{1,0:T(8,128)(2,1)S(1)} %get-tuple-element.54), channel_id=1, source_target_pairs={{0,128},{64,192},{128,0},{192,64},{1,129},{65,193},{129,1},{193,65... | collective-permute-start | bytes 122888 | tf_op jit(solution)/shard_map/ppermute | solution.py:33
  114.3 2.1 %collective-permute-start.18 = (bf16[16,1280]{1,0:T(8,128)(2,1)S(1)}, bf16[16,1280]{1,0:T(8,128)(2,1)S(1)}, u32[]{:S(2)}, u32[]{:S(2)}) collective-permute-start(bf16[16,1280]{1,0:T(8,128)(2,1)S(1)} %get-tuple-element.53), channel_id=1, source_target_pairs={{0,192},{64,0},{128,64},{192,128},{1,193},{65,1},{129,65},{193,129... | collective-permute-start | bytes 122888 | tf_op jit(solution)/shard_map/ppermute | solution.py:33
  117.1 1.6 %collective-permute-done.17 = bf16[16,1280]{1,0:T(8,128)(2,1)S(1)} collective-permute-done((bf16[16,1280]{1,0:T(8,128)(2,1)S(1)}, bf16[16,1280]{1,0:T(8,128)(2,1)S(1)}, u32[]{:S(2)}, u32[]{:S(2)}) %collective-permute-start.17) | collective-permute-done | bytes 40992 | tf_op jit(solution)/shard_map/ppermute | solution.py:33
  (50 shorter events, 18.8 us)
Async XLA Ops:
  1.5 5.9 %collective-permute-start = (bf16[256,256]{1,0:T(8,128)(2,1)S(1)}, bf16[256,256]{1,0:T(8,128)(2,1)S(1)}, u32[]{:S(2)}, u32[]{:S(2)}) collective-permute-start(bf16[256,256]{1,0:T(8,128)(2,1)S(1)} %get-tuple-element.59), channel_id=1, source_target_pairs={{0,1},{1,0},{2,3},{3,2},{4,5},{5,4},{6,7},{7,6},{8,9},{9,8},{10,11... | collective-permute-start | bytes 393224 | tf_op jit(solution)/shard_map/ppermute | solution.py:33
  5.0 18.2 %copy-start.4 = (bf16[1,256,1024]{2,1,0:T(8,128)(2,1)S(1)}, bf16[1,256,1024]{2,1,0:T(8,128)(2,1)}, u32[]{:S(2)}) copy-start(bf16[1,256,1024]{2,1,0:T(8,128)(2,1)} %param.7) | copy-start | bytes 1572868
  5.1 18.2 %copy-start.7 = (s32[1,2048]{1,0:T(1,128)S(1)}, s32[1,2048]{1,0:T(1,128)}, u32[]{:S(2)}) copy-start(s32[1,2048]{1,0:T(1,128)} %docs_ref.1) | copy-start | bytes 24580
  7.4 8.4 %collective-permute-start.1 = (bf16[2,256,256]{2,1,0:T(8,128)(2,1)S(1)}, bf16[2,256,256]{2,1,0:T(8,128)(2,1)S(1)}, u32[]{:S(2)}, u32[]{:S(2)}) collective-permute-start(bf16[2,256,256]{2,1,0:T(8,128)(2,1)S(1)} %pad_maximum_fusion.refs_0_), channel_id=1, source_target_pairs={{0,2},{2,4},{4,6},{6,0},{1,3},{3,5},{5,7},{7,1},{8,10},{10,12},{12... | collective-permute-start | bytes 786440 | tf_op jit(solution)/shard_map/ppermute | solution.py:33
  8.5 8.4 %collective-permute-start.3 = (bf16[2,256,256]{2,1,0:T(8,128)(2,1)S(1)}, bf16[2,256,256]{2,1,0:T(8,128)(2,1)S(1)}, u32[]{:S(2)}, u32[]{:S(2)}) collective-permute-start(bf16[2,256,256]{2,1,0:T(8,128)(2,1)S(1)} %pad_maximum_fusion.refs_0_), channel_id=1, source_target_pairs={{0,6},{2,0},{4,2},{6,4},{1,7},{3,1},{5,3},{7,5},{8,14},{10,8},{12,... | collective-permute-start | bytes 786440 | tf_op jit(solution)/shard_map/ppermute | solution.py:33
  10.7 19.3 %collective-permute-start.5 = (bf16[1024,256]{1,0:T(8,128)(2,1)}, bf16[1024,256]{1,0:T(8,128)(2,1)S(1)}, u32[]{:S(2)}, u32[]{:S(2)}) collective-permute-start(bf16[1024,256]{1,0:T(8,128)(2,1)} %get-tuple-element.36), channel_id=1, source_target_pairs={{0,16},{16,32},{32,48},{48,0},{1,17},{17,33},{33,49},{49,1},{2,18}... | collective-permute-start | bytes 1572872 | tf_op jit(solution)/shard_map/ppermute | solution.py:33
  11.7 24.5 %collective-permute-start.6 = (bf16[1024,256]{1,0:T(8,128)(2,1)}, bf16[1024,256]{1,0:T(8,128)(2,1)S(1)}, u32[]{:S(2)}, u32[]{:S(2)}) collective-permute-start(bf16[1024,256]{1,0:T(8,128)(2,1)} %get-tuple-element.37), channel_id=1, source_target_pairs={{0,32},{16,48},{32,0},{48,16},{1,33},{17,49},{33,1},{49,17},{2,34}... | collective-permute-start | bytes 1572872 | tf_op jit(solution)/shard_map/ppermute | solution.py:33
  14.4 21.8 %collective-permute-start.7 = (bf16[1024,256]{1,0:T(8,128)(2,1)}, bf16[1024,256]{1,0:T(8,128)(2,1)S(1)}, u32[]{:S(2)}, u32[]{:S(2)}) collective-permute-start(bf16[1024,256]{1,0:T(8,128)(2,1)} %get-tuple-element.38), channel_id=1, source_target_pairs={{0,48},{16,0},{32,16},{48,32},{1,49},{17,1},{33,17},{49,33},{2,50}... | collective-permute-start | bytes 1572872 | tf_op jit(solution)/shard_map/ppermute | solution.py:33
  16.5 6.4 %collective-permute-start.2 = (bf16[256,256]{1,0:T(8,128)(2,1)}, bf16[256,256]{1,0:T(8,128)(2,1)S(1)}, u32[]{:S(2)}, u32[]{:S(2)}) collective-permute-start(bf16[256,256]{1,0:T(8,128)(2,1)} %slice_bitcast_fusion.1), channel_id=1, source_target_pairs={{0,2},{2,4},{4,6},{6,0},{1,3},{3,5},{5,7},{7,1},{8,10},{10,12},{12... | collective-permute-start | bytes 393224 | tf_op jit(solution)/shard_map/ppermute | solution.py:33
  17.6 5.7 %collective-permute-start.4 = (bf16[256,256]{1,0:T(8,128)(2,1)}, bf16[256,256]{1,0:T(8,128)(2,1)}, u32[]{:S(2)}, u32[]{:S(2)}) collective-permute-start(bf16[256,256]{1,0:T(8,128)(2,1)} %slice_bitcast_fusion), channel_id=1, source_target_pairs={{0,6},{2,0},{4,2},{6,4},{1,7},{3,1},{5,3},{7,5},{8,14},{10,8},{12,... | collective-permute-start | bytes 393224 | tf_op jit(solution)/shard_map/ppermute | solution.py:33
  36.2 14.6 %collective-permute-start.8 = (bf16[256,1024]{1,0:T(8,128)(2,1)}, bf16[256,1024]{1,0:T(8,128)(2,1)S(1)}, u32[]{:S(2)}, u32[]{:S(2)}) collective-permute-start(bf16[256,1024]{1,0:T(8,128)(2,1)} %get-tuple-element.39.refs_4_), channel_id=1, source_target_pairs={{0,16},{16,32},{32,48},{48,0},{1,17},{17,33},{33,49},{49,1},{2,18}... | collective-permute-start | bytes 1572872 | tf_op jit(solution)/shard_map/ppermute | solution.py:33
  37.6 13.2 %collective-permute-start.9 = (bf16[256,1024]{1,0:T(8,128)(2,1)}, bf16[256,1024]{1,0:T(8,128)(2,1)S(1)}, u32[]{:S(2)}, u32[]{:S(2)}) collective-permute-start(bf16[256,1024]{1,0:T(8,128)(2,1)} %get-tuple-element.39.refs_4_), channel_id=1, source_target_pairs={{0,48},{16,0},{32,16},{48,32},{1,49},{17,1},{33,17},{49,33},{2,50}... | collective-permute-start | bytes 1572872 | tf_op jit(solution)/shard_map/ppermute | solution.py:33
  39.5 22.0 %all-to-all-start = ((bf16[8,256,256]{2,1,0:T(8,128)(2,1)}), bf16[8,256,256]{2,1,0:T(8,128)(2,1)}, u32[]{:S(2)}, u32[]{:S(2)}) async-start(bf16[8,256,256]{2,1,0:T(8,128)(2,1)} %get-tuple-element.40), calls=%async_computation | async-start | bytes 2097152 | tf_op jit(solution)/shard_map/all_to_all | solution.py:332
  53.1 21.8 %copy-start.1 = (bf16[256,1024]{1,0:T(8,128)(2,1)S(1)}, bf16[256,1024]{1,0:T(8,128)(2,1)}, u32[]{:S(2)}) copy-start(bf16[256,1024]{1,0:T(8,128)(2,1)} %get-tuple-element.39.refs_4_) | copy-start | bytes 1572868
  62.8 12.1 %collective-permute-start.10 = (bf16[256,512]{1,0:T(8,128)(2,1)}, bf16[256,512]{1,0:T(8,128)(2,1)S(1)}, u32[]{:S(2)}, u32[]{:S(2)}) collective-permute-start(bf16[256,512]{1,0:T(8,128)(2,1)} %copy-done.6), channel_id=1, source_target_pairs={{0,16},{16,32},{32,48},{48,0},{1,17},{17,33},{33,49},{49,1},{2,18}... | collective-permute-start | bytes 786440 | tf_op jit(solution)/shard_map/ppermute | solution.py:33
  63.1 11.8 %collective-permute-start.11 = (bf16[256,512]{1,0:T(8,128)(2,1)}, bf16[256,512]{1,0:T(8,128)(2,1)}, u32[]{:S(2)}, u32[]{:S(2)}) collective-permute-start(bf16[256,512]{1,0:T(8,128)(2,1)} %copy-done.5), channel_id=1, source_target_pairs={{0,48},{16,0},{32,16},{48,32},{1,49},{17,1},{33,17},{49,33},{2,50}... | collective-permute-start | bytes 786440 | tf_op jit(solution)/shard_map/ppermute | solution.py:33
  66.3 7.7 %collective-permute-start.12 = (bf16[256,256]{1,0:T(8,128)(2,1)S(1)}, bf16[256,256]{1,0:T(8,128)(2,1)}, u32[]{:S(2)}, u32[]{:S(2)}) collective-permute-start(bf16[256,256]{1,0:T(8,128)(2,1)S(1)} %reduce_sum.24.refs_9_), channel_id=1, source_target_pairs={{0,16},{16,32},{32,48},{48,0},{1,17},{17,33},{33,49},{49,1},{2,18}... | collective-permute-start | bytes 393224 | tf_op jit(solution)/shard_map/ppermute | solution.py:33
  66.3 7.7 %collective-permute-start.13 = (bf16[256,256]{1,0:T(8,128)(2,1)S(1)}, bf16[256,256]{1,0:T(8,128)(2,1)}, u32[]{:S(2)}, u32[]{:S(2)}) collective-permute-start(bf16[256,256]{1,0:T(8,128)(2,1)S(1)} %reduce_sum.24.refs_9_), channel_id=1, source_target_pairs={{0,32},{16,48},{32,0},{48,16},{1,33},{17,49},{33,1},{49,17},{2,34}... | collective-permute-start | bytes 393224 | tf_op jit(solution)/shard_map/ppermute | solution.py:33
  67.8 7.1 %collective-permute-start.14 = (bf16[256,256]{1,0:T(8,128)(2,1)S(1)}, bf16[256,256]{1,0:T(8,128)(2,1)}, u32[]{:S(2)}, u32[]{:S(2)}) collective-permute-start(bf16[256,256]{1,0:T(8,128)(2,1)S(1)} %reduce_sum.24.refs_9_), channel_id=1, source_target_pairs={{0,48},{16,0},{32,16},{48,32},{1,49},{17,1},{33,17},{49,33},{2,50}... | collective-permute-start | bytes 393224 | tf_op jit(solution)/shard_map/ppermute | solution.py:33
  78.6 3.1 %collective-permute-start.15 = (bf16[8,4,16,1280]{3,2,1,0:T(8,128)(2,1)S(1)}, bf16[8,4,16,1280]{3,2,1,0:T(8,128)(2,1)S(1)}, u32[]{:S(2)}, u32[]{:S(2)}) collective-permute-start(bf16[8,4,16,1280]{3,2,1,0:T(8,128)(2,1)S(1)} %weight_part.3), channel_id=1, source_target_pairs={{0,8},{8,0},{1,9},{9,1},{2,10},{10,2},{3,11},{11,3},{4,12},{12,4},... | collective-permute-start | bytes 3932168 | tf_op jit(solution)/shard_map/ppermute | solution.py:33
  83.1 23.1 %all-to-all-start.1 = ((bf16[8,64,1280]{2,1,0:T(8,128)(2,1)}), bf16[8,64,1280]{2,1,0:T(8,128)(2,1)S(1)}, u32[]{:S(2)}, u32[]{:S(2)}) async-start(bf16[8,64,1280]{2,1,0:T(8,128)(2,1)} %bitcast.16), calls=%async_computation.1 | async-start | bytes 2621440 | tf_op jit(solution)/shard_map/all_to_all | solution.py:344
  106.5 10.6 %collective-permute-start.16 = (bf16[16,1280]{1,0:T(8,128)(2,1)S(1)}, bf16[16,1280]{1,0:T(8,128)(2,1)S(1)}, u32[]{:S(2)}, u32[]{:S(2)}) collective-permute-start(bf16[16,1280]{1,0:T(8,128)(2,1)S(1)} %get-tuple-element.55), channel_id=1, source_target_pairs={{0,64},{64,128},{128,192},{192,0},{1,65},{65,129},{129,193},{193,1... | collective-permute-start | bytes 122888 | tf_op jit(solution)/shard_map/ppermute | solution.py:33
  109.8 8.8 %collective-permute-start.17 = (bf16[16,1280]{1,0:T(8,128)(2,1)S(1)}, bf16[16,1280]{1,0:T(8,128)(2,1)S(1)}, u32[]{:S(2)}, u32[]{:S(2)}) collective-permute-start(bf16[16,1280]{1,0:T(8,128)(2,1)S(1)} %get-tuple-element.54), channel_id=1, source_target_pairs={{0,128},{64,192},{128,0},{192,64},{1,129},{65,193},{129,1},{193,65... | collective-permute-start | bytes 122888 | tf_op jit(solution)/shard_map/ppermute | solution.py:33
  114.3 5.4 %collective-permute-start.18 = (bf16[16,1280]{1,0:T(8,128)(2,1)S(1)}, bf16[16,1280]{1,0:T(8,128)(2,1)S(1)}, u32[]{:S(2)}, u32[]{:S(2)}) collective-permute-start(bf16[16,1280]{1,0:T(8,128)(2,1)S(1)} %get-tuple-element.53), channel_id=1, source_target_pairs={{0,192},{64,0},{128,64},{192,128},{1,193},{65,1},{129,65},{193,129... | collective-permute-start | bytes 122888 | tf_op jit(solution)/shard_map/ppermute | solution.py:33
  (5 other events, 4.9 us)
